TPU v7x, 32 devices: a whole 2x2x4 slice. The times are simulated.
32 devices in a mesh: seq: 4 (over y, x), fsdp: 8 (over z, core).
Axes of the slice: x: 2, y: 2, z: 4, core: 2. Of those that a mesh axis runs over, the one named last changes fastest.
Arguments:
- tokens: bfloat16 [8, 1024, 2048], P('fsdp', 'seq'), may hold values from -6 to 6
- positions: int32 [8, 1024], P('fsdp'), may hold values from 0 to 1023, as said below
- attn_gain: bfloat16 [2048], P(('seq', 'fsdp')), may hold values from 0.099609375 to 1.8984375
- query_weight: bfloat16 [2048, 2048], P(('seq', 'fsdp')), may hold values from -0.25 to 0.25
- key_weight: bfloat16 [2048, 256], P(('seq', 'fsdp')), may hold values from -0.125 to 0.125
- value_weight: bfloat16 [2048, 256], P(('seq', 'fsdp')), may hold values from -0.125 to 0.125
- output_weight: bfloat16 [2048, 2048], P(('seq', 'fsdp')), may hold values from -0.5 to 0.5
- ffn_gain: bfloat16 [2048], P(('seq', 'fsdp')), may hold values from 0.099609375 to 1.8984375
- gate_weight: bfloat16 [2048, 5632], P(('seq', 'fsdp')), may hold values from -0.125 to 0.125
- up_weight: bfloat16 [2048, 5632], P(('seq', 'fsdp')), may hold values from -0.125 to 0.125
- down_weight: bfloat16 [5632, 2048], P(('seq', 'fsdp')), may hold values from -0.078125 to 0.078125
- cotangent: bfloat16 [8, 1024, 2048], P('fsdp', 'seq'), may hold values from -6 to 6
Outputs:
- block_out: bfloat16 [8, 1024, 2048], P('fsdp', 'seq')
- grad_tokens: float32 [8, 1024, 2048], P('fsdp', 'seq')
- grad_attn_gain: float32 [2048], P(('seq', 'fsdp'))
- grad_query: float32 [2048, 2048], P(('seq', 'fsdp'))
- grad_key: float32 [2048, 256], P(('seq', 'fsdp'))
- grad_value: float32 [2048, 256], P(('seq', 'fsdp'))
- grad_output: float32 [2048, 2048], P(('seq', 'fsdp'))
- grad_ffn_gain: float32 [2048], P(('seq', 'fsdp'))
- grad_gate: float32 [2048, 5632], P(('seq', 'fsdp'))
- grad_up: float32 [2048, 5632], P(('seq', 'fsdp'))
- grad_down: float32 [5632, 2048], P(('seq', 'fsdp'))
Inputs may be any that keep to these rules, and one draw needn't show every extreme that they name: Each sequence's positions are 0 to 1023, each once, in whole blocks of 256: entries j * 256 to (j + 1) * 256 - 1 hold i * 256 to (i + 1) * 256 - 1 in rising order for some i.
All inputs are finite; a program needn't handle non-finite values.
Results may differ from a plain program's by a relative error of at most 0.02.
Values may be sent and summed in bfloat16 or wider, within the bound.
No kernel may reach another device: no remote copies, remote signals or barrier semaphores. Data moves between devices by JAX's collectives and lax.ppermute only.
A program may use at most 384 MiB of HBM per device.

v0:
```python
import math

import jax
import jax.numpy as jnp
from jax import lax
from jax.sharding import PartitionSpec as P

HEADS = 32
KV_HEADS = 4
HEAD_DIM = 64


EPSILON = 1e-05
MASK_FILL = -1e30


def rope_tables(where_at):
    half_dim = HEAD_DIM // 2
    frequency = 1.0 / 10000.0 ** (jnp.arange(half_dim, dtype=jnp.float32) * 2.0 / HEAD_DIM)
    angles = where_at.astype(jnp.float32)[:, None] * frequency[None, :]
    return (
        jnp.concatenate([jnp.cos(angles), jnp.cos(angles)], -1),
        jnp.concatenate([jnp.sin(angles), jnp.sin(angles)], -1),
    )


def rotate(values, cosine, sine_table):
    half_dim = values.shape[-1] // 2
    turned = jnp.concatenate([-values[..., half_dim:], values[..., :half_dim]], -1)
    return values * cosine + turned * sine_table


def unrotate(gradient, cosine, sine_table):
    half_dim = gradient.shape[-1] // 2
    scaled = gradient * sine_table
    turned_back = jnp.concatenate([scaled[..., half_dim:], -scaled[..., :half_dim]], -1)
    return gradient * cosine + turned_back


def swiglu_back(grad_hidden, gate_rows, up_rows, gate_silu):
    gate_sigmoid = jax.nn.sigmoid(gate_rows)
    grad_gaterows = (
        grad_hidden * up_rows * gate_sigmoid * (1.0 + gate_rows * (1.0 - gate_sigmoid))
    ).astype(jnp.bfloat16)
    grad_uprows = (grad_hidden * gate_silu).astype(jnp.bfloat16)
    return (grad_gaterows, grad_uprows)


def shards(
    tokens,
    positions,
    attn_gain,
    query_weight,
    key_weight,
    value_weight,
    output_weight,
    ffn_gain,
    gate_weight,
    up_weight,
    down_weight,
    cotangent,
):
    span_rows = tokens.shape[1]
    model_width = tokens.shape[2]
    group_size = HEADS // KV_HEADS
    kv_width = KV_HEADS * HEAD_DIM
    score_scale = 1.0 / math.sqrt(HEAD_DIM)
    all_pos = positions[0]
    seq_len = all_pos.shape[0]
    own_pos = lax.dynamic_slice_in_dim(all_pos, lax.axis_index("seq") * span_rows, span_rows)
    gain_one, gain_two, query_full, key_full, value_full, output_full = (
        lax.all_gather(attn_gain, ("seq", "fsdp"), axis=0, tiled=True),
        lax.all_gather(ffn_gain, ("seq", "fsdp"), axis=0, tiled=True),
        lax.all_gather(query_weight, ("seq", "fsdp"), axis=0, tiled=True),
        lax.all_gather(key_weight, ("seq", "fsdp"), axis=0, tiled=True),
        lax.all_gather(value_weight, ("seq", "fsdp"), axis=0, tiled=True),
        lax.all_gather(output_weight, ("seq", "fsdp"), axis=0, tiled=True),
    )
    token_rows = tokens[0].astype(jnp.float32)
    inv_one = lax.rsqrt(jnp.mean(token_rows * token_rows, -1, keepdims=True) + EPSILON)
    scaled_one = token_rows * inv_one
    normed_one = (scaled_one * gain_one.astype(jnp.float32)).astype(jnp.bfloat16)
    query_proj = jnp.dot(normed_one, query_full, preferred_element_type=jnp.float32)
    key_proj = jnp.dot(normed_one, key_full, preferred_element_type=jnp.float32)
    value_rows = jnp.dot(normed_one, value_full, preferred_element_type=jnp.float32).astype(
        jnp.bfloat16
    )
    cosine, sine_table = rope_tables(own_pos)
    query_rot = rotate(
        query_proj.reshape(span_rows, HEADS, HEAD_DIM), cosine[:, None], sine_table[:, None]
    ).astype(jnp.bfloat16)
    key_rot = (
        rotate(
            key_proj.reshape(span_rows, KV_HEADS, HEAD_DIM), cosine[:, None], sine_table[:, None]
        )
        .astype(jnp.bfloat16)
        .reshape(span_rows, kv_width)
    )
    query_heads = query_rot.reshape(span_rows, KV_HEADS, group_size, HEAD_DIM).transpose(1, 2, 0, 3)
    running_max = jnp.full((KV_HEADS, group_size, span_rows), MASK_FILL, jnp.float32)
    key_piece = lax.all_gather(key_rot, "seq", axis=0, tiled=True)
    value_piece = lax.all_gather(value_rows, "seq", axis=0, tiled=True)
    piece_rows = key_piece.shape[0]
    key_pos = all_pos
    key_heads = key_piece.reshape(piece_rows, KV_HEADS, HEAD_DIM)
    value_heads = value_piece.reshape(piece_rows, KV_HEADS, HEAD_DIM)
    scores = (
        jnp.einsum("kgqd,jkd->kgqj", query_heads, key_heads, preferred_element_type=jnp.float32)
        * score_scale
    )
    allowed = key_pos[None, :] <= own_pos[:, None]
    masked = jnp.where(allowed, scores, MASK_FILL)
    new_max = jnp.maximum(running_max, jnp.max(masked, -1))
    weights = jnp.where(allowed, jnp.exp(scores - new_max[..., None]), 0.0)
    running_sum = jnp.sum(weights, -1)
    summed = jnp.einsum(
        "kgqj,jkd->kgqd",
        weights.astype(jnp.bfloat16),
        value_heads,
        preferred_element_type=jnp.float32,
    )
    running_max, running_sum, summed = (new_max, running_sum, summed)
    attended = summed / running_sum[..., None]
    log_total = running_max + jnp.log(running_sum)
    attended_low = (
        attended.transpose(2, 0, 1, 3).reshape(span_rows, model_width).astype(jnp.bfloat16)
    )
    middle = token_rows + jnp.dot(attended_low, output_full, preferred_element_type=jnp.float32)
    inv_two = lax.rsqrt(jnp.mean(middle * middle, -1, keepdims=True) + EPSILON)
    scaled_two = middle * inv_two
    normed_two = (scaled_two * gain_two.astype(jnp.float32)).astype(jnp.bfloat16)
    upstream = cotangent[0]
    gate_full, up_full, down_full = (
        lax.all_gather(gate_weight, ("seq", "fsdp"), axis=0, tiled=True),
        lax.all_gather(up_weight, ("seq", "fsdp"), axis=0, tiled=True),
        lax.all_gather(down_weight, ("seq", "fsdp"), axis=0, tiled=True),
    )
    gate_rows = jnp.dot(normed_two, gate_full, preferred_element_type=jnp.float32)
    up_rows = jnp.dot(normed_two, up_full, preferred_element_type=jnp.float32)
    gate_silu = jax.nn.silu(gate_rows)
    hidden = (gate_silu * up_rows).astype(jnp.bfloat16)
    block_out = (middle + jnp.dot(hidden, down_full, preferred_element_type=jnp.float32)).astype(
        jnp.bfloat16
    )
    gate_full, up_full, down_full = (
        lax.all_gather(gate_weight, ("seq", "fsdp"), axis=0, tiled=True),
        lax.all_gather(up_weight, ("seq", "fsdp"), axis=0, tiled=True),
        lax.all_gather(down_weight, ("seq", "fsdp"), axis=0, tiled=True),
    )
    grad_down = jnp.dot(hidden.T, upstream, preferred_element_type=jnp.float32)
    grad_hidden = jnp.dot(upstream, down_full.T, preferred_element_type=jnp.float32)
    grad_gaterows, grad_uprows = swiglu_back(grad_hidden, gate_rows, up_rows, gate_silu)
    grad_gate = jnp.dot(normed_two.T, grad_gaterows, preferred_element_type=jnp.float32)
    grad_up = jnp.dot(normed_two.T, grad_uprows, preferred_element_type=jnp.float32)
    grad_normtwo = jnp.dot(
        grad_gaterows, gate_full.T, preferred_element_type=jnp.float32
    ) + jnp.dot(grad_uprows, up_full.T, preferred_element_type=jnp.float32)
    ffn_results = (
        lax.psum_scatter(grad_gate, ("seq", "fsdp"), scatter_dimension=0, tiled=True),
        lax.psum_scatter(grad_up, ("seq", "fsdp"), scatter_dimension=0, tiled=True),
        lax.psum_scatter(grad_down, ("seq", "fsdp"), scatter_dimension=0, tiled=True),
    )
    grad_gain_two = jnp.sum(grad_normtwo * scaled_two, 0)
    scaled_grad_two = grad_normtwo * gain_two.astype(jnp.float32)
    grad_middle = upstream.astype(jnp.float32) + inv_two * (
        scaled_grad_two - scaled_two * jnp.mean(scaled_grad_two * scaled_two, -1, keepdims=True)
    )
    gain_one, query_full, key_full, value_full, output_full = (
        lax.all_gather(attn_gain, ("seq", "fsdp"), axis=0, tiled=True),
        lax.all_gather(query_weight, ("seq", "fsdp"), axis=0, tiled=True),
        lax.all_gather(key_weight, ("seq", "fsdp"), axis=0, tiled=True),
        lax.all_gather(value_weight, ("seq", "fsdp"), axis=0, tiled=True),
        lax.all_gather(output_weight, ("seq", "fsdp"), axis=0, tiled=True),
    )
    grad_branch = grad_middle.astype(jnp.bfloat16)
    grad_output = jnp.dot(attended_low.T, grad_branch, preferred_element_type=jnp.float32)
    grad_attended = jnp.dot(grad_branch, output_full.T, preferred_element_type=jnp.float32).astype(
        jnp.bfloat16
    )
    grad_heads = grad_attended.reshape(span_rows, KV_HEADS, group_size, HEAD_DIM).transpose(
        1, 2, 0, 3
    )
    row_delta = jnp.sum(grad_heads.astype(jnp.float32) * attended, -1)
    key_all, value_all = (
        lax.all_gather(key_rot, "seq", axis=0, tiled=True),
        lax.all_gather(value_rows, "seq", axis=0, tiled=True),
    )
    block_span = min(512, seq_len)
    block_count = seq_len // block_span
    key_blocks = key_all.reshape(block_count, block_span, KV_HEADS, HEAD_DIM)
    value_blocks = value_all.reshape(block_count, block_span, KV_HEADS, HEAD_DIM)
    pos_blocks = all_pos.reshape(block_count, block_span)

    def backstep(grad_query_acc, block_data):
        key_heads, value_heads, key_pos = block_data
        scores = (
            jnp.einsum("kgqd,jkd->kgqj", query_heads, key_heads, preferred_element_type=jnp.float32)
            * score_scale
        )
        allowed = key_pos[None, :] <= own_pos[:, None]
        probabilities = jnp.where(allowed, jnp.exp(scores - log_total[..., None]), 0.0)
        grad_vblock = jnp.einsum(
            "kgqj,kgqd->jkd",
            probabilities.astype(jnp.bfloat16),
            grad_heads,
            preferred_element_type=jnp.float32,
        )
        grad_probs = jnp.einsum(
            "kgqd,jkd->kgqj", grad_heads, value_heads, preferred_element_type=jnp.float32
        )
        grad_scores = (probabilities * (grad_probs - row_delta[..., None])).astype(jnp.bfloat16)
        grad_query_acc = (
            grad_query_acc
            + jnp.einsum(
                "kgqj,jkd->kgqd", grad_scores, key_heads, preferred_element_type=jnp.float32
            )
            * score_scale
        )
        grad_kblock = (
            jnp.einsum(
                "kgqj,kgqd->jkd", grad_scores, query_heads, preferred_element_type=jnp.float32
            )
            * score_scale
        )
        return (grad_query_acc, (grad_kblock, grad_vblock))

    start_query = jnp.zeros((KV_HEADS, group_size, span_rows, HEAD_DIM), jnp.float32)
    grad_qrot, (grad_kblocks, grad_vblocks) = lax.scan(
        backstep, start_query, (key_blocks, value_blocks, pos_blocks)
    )
    grad_key_own, grad_value_own = (
        lax.psum_scatter(
            grad_kblocks.reshape(seq_len, kv_width).astype(jnp.bfloat16),
            "seq",
            scatter_dimension=0,
            tiled=True,
        ).astype(jnp.float32),
        lax.psum_scatter(
            grad_vblocks.reshape(seq_len, kv_width).astype(jnp.bfloat16),
            "seq",
            scatter_dimension=0,
            tiled=True,
        ).astype(jnp.float32),
    )
    grad_kproj = (
        unrotate(
            grad_key_own.reshape(span_rows, KV_HEADS, HEAD_DIM),
            cosine[:, None],
            sine_table[:, None],
        )
        .reshape(span_rows, kv_width)
        .astype(jnp.bfloat16)
    )
    grad_vrows = grad_value_own.astype(jnp.bfloat16)
    grad_qproj = (
        unrotate(
            grad_qrot.transpose(2, 0, 1, 3).reshape(span_rows, HEADS, HEAD_DIM),
            cosine[:, None],
            sine_table[:, None],
        )
        .reshape(span_rows, model_width)
        .astype(jnp.bfloat16)
    )
    grad_query = jnp.dot(normed_one.T, grad_qproj, preferred_element_type=jnp.float32)
    grad_key = jnp.dot(normed_one.T, grad_kproj, preferred_element_type=jnp.float32)
    grad_value = jnp.dot(normed_one.T, grad_vrows, preferred_element_type=jnp.float32)
    grad_normone = (
        jnp.dot(grad_qproj, query_full.T, preferred_element_type=jnp.float32)
        + jnp.dot(grad_kproj, key_full.T, preferred_element_type=jnp.float32)
        + jnp.dot(grad_vrows, value_full.T, preferred_element_type=jnp.float32)
    )
    grad_gain_one = jnp.sum(grad_normone * scaled_one, 0)
    scaled_grad_one = grad_normone * gain_one.astype(jnp.float32)
    grad_rows = grad_middle + inv_one * (
        scaled_grad_one - scaled_one * jnp.mean(scaled_grad_one * scaled_one, -1, keepdims=True)
    )
    attn_results = (
        lax.psum_scatter(grad_gain_one, ("seq", "fsdp"), scatter_dimension=0, tiled=True),
        lax.psum_scatter(grad_gain_two, ("seq", "fsdp"), scatter_dimension=0, tiled=True),
        lax.psum_scatter(grad_query, ("seq", "fsdp"), scatter_dimension=0, tiled=True),
        lax.psum_scatter(grad_key, ("seq", "fsdp"), scatter_dimension=0, tiled=True),
        lax.psum_scatter(grad_value, ("seq", "fsdp"), scatter_dimension=0, tiled=True),
        lax.psum_scatter(grad_output, ("seq", "fsdp"), scatter_dimension=0, tiled=True),
    )
    return (
        block_out[None],
        grad_rows[None],
        attn_results[0],
        attn_results[2],
        attn_results[3],
        attn_results[4],
        attn_results[5],
        attn_results[1],
        ffn_results[0],
        ffn_results[1],
        ffn_results[2],
    )


def solution(mesh):
    return jax.shard_map(
        shards,
        mesh=mesh,
        in_specs=(
            P("fsdp", "seq", None),
            P("fsdp", None),
            P(("seq", "fsdp")),
            P(("seq", "fsdp"), None),
            P(("seq", "fsdp"), None),
            P(("seq", "fsdp"), None),
            P(("seq", "fsdp"), None),
            P(("seq", "fsdp")),
            P(("seq", "fsdp"), None),
            P(("seq", "fsdp"), None),
            P(("seq", "fsdp"), None),
            P("fsdp", "seq", None),
        ),
        out_specs=(
            P("fsdp", "seq", None),
            P("fsdp", "seq", None),
            P(("seq", "fsdp")),
            P(("seq", "fsdp"), None),
            P(("seq", "fsdp"), None),
            P(("seq", "fsdp"), None),
            P(("seq", "fsdp"), None),
            P(("seq", "fsdp")),
            P(("seq", "fsdp"), None),
            P(("seq", "fsdp"), None),
            P(("seq", "fsdp"), None),
        ),
        check_vma=False,
    )
```

profile of v0, /device:TPU:0, one launch (start us, length us, event | category | flops | bytes accessed | tf_op | source)
XLA Modules:
  0.0 3035.1 jit_solution(1454719289485478778)
XLA Ops:
  12.5 42.1 %all-reduce.5 = (bf16[2048]{0:T(1024)(128)(2,1)S(1)}, bf16[2048]{0:T(1024)(128)(2,1)S(1)}) all-reduce(bf16[2048]{0:T(1024)(128)(2,1)S(1)} %dynamic-update-slice, bf16[2048]{0:T(1024)(128)(2,1)S(1)} %dynamic-update-slice.1), channel_id=1, replica_groups=mesh['seq'=4,'fsdp'=8] {'seq','fsdp'}, use_global_device_ids=true, to_apply=%add | all-reduce | flops 4096 | bytes 16384
  56.7 10.9 all-gather.12.cloned.1.call-done
  69.4 10.2 all_gather.48
  81.1 42.3 %all-gather.10.cloned.1.call-done = bf16[2048,256]{1,0:T(8,128)(2,1)} async-done(((bf16[64,256]{1,0:T(8,128)(2,1)}), bf16[2048,256]{1,0:T(8,128)(2,1)}) %all-gather.10.cloned.1.call-update) | async-done | bytes 1048592 | tf_op jit(solution)/shard_map/all_gather | solution.py:75
  127.6 16.5 all_gather.46
  147.6 56.6 %all-gather.8.cloned.1.call-done = bf16[2048,2048]{1,0:T(8,128)(2,1)} async-done(((bf16[64,2048]{1,0:T(8,128)(2,1)}), bf16[2048,2048]{1,0:T(8,128)(2,1)}) %all-gather.8.cloned.1.call-update) | async-done | bytes 8388624 | tf_op jit(solution)/shard_map/all_gather | solution.py:74
  204.2 12.3 copy.46
  216.5 5.9 fusion.64
  223.7 13.8 select_reduce_fusion
  237.5 15.3 fusion.26
  252.8 16.8 fusion.57
  269.6 13.5 all-gather.14.cloned.1.call-done
  283.1 6.2 multiply_reduce_fusion.3
  290.9 138.2 %all-gather.16.cloned.1.call-done = bf16[2048,5632]{1,0:T(8,128)(2,1)} async-done(((bf16[64,5632]{1,0:T(8,128)(2,1)}), bf16[2048,5632]{1,0:T(8,128)(2,1)}) %all-gather.16.cloned.1.call-update) | async-done | bytes 23068688 | tf_op jit(solution)/shard_map/all_gather | solution.py:134
  429.1 13.1 fusion.86
  442.2 132.5 %all-gather.18.cloned.1.call-done = bf16[2048,5632]{1,0:T(8,128)(2,1)} async-done(((bf16[64,5632]{1,0:T(8,128)(2,1)}), bf16[2048,5632]{1,0:T(8,128)(2,1)}) %all-gather.18.cloned.1.call-update) | async-done | bytes 23068688 | tf_op jit(solution)/shard_map/all_gather | solution.py:135
  574.7 13.2 fusion.87
  587.9 132.5 %all-gather.20.cloned.1.call-done = bf16[5632,2048]{1,0:T(8,128)(2,1)} async-done(((bf16[176,2048]{1,0:T(8,128)(2,1)}), bf16[5632,2048]{1,0:T(8,128)(2,1)}) %all-gather.20.cloned.1.call-update) | async-done | bytes 23068688 | tf_op jit(solution)/shard_map/all_gather | solution.py:136
  720.4 18.5 multiply_convert_fusion
  738.8 12.6 fusion.88
  751.4 14.8 multiply_reduce_fusion
  770.5 6.7 convolution_convert_fusion
  781.4 68.7 %while.15 = (s32[]{:T(128)}, f32[4,8,256,64]{2,3,1,0:T(8,128)}, bf16[2,512,4,64]{1,3,2,0:T(8,128)(2,1)}, bf16[2,512,4,64]{1,3,2,0:T(8,128)(2,1)}, s32[2,512]{1,0...) while((s32[]{:T(128)}, f32[4,8,256,64]{2,3,1,0:T(8,128)}, ...), condition=%wide.region_7.8_spmd.clone, body=%wide.region_6.7_spmd.clone.sunk | while | flops 2728132608 | bytes 191733088 | solution.py:228
  784.8 4.8 copy-done.1
  789.6 8.5 fusion.158
  798.1 6.4 select_add_fusion.2
  807.2 8.3 fusion.160
  818.9 4.8 copy-done.1
  823.6 8.5 fusion.158
  832.1 7.0 select_add_fusion.2
  841.8 8.3 fusion.160
  854.3 21.5 reduce-scatter.10.cloned.1.call-done
  879.8 24.4 reduce-scatter.12.cloned.1.call-done
  909.9 8.3 fusion.66
  918.2 10.1 fusion.68
  928.4 19.6 fusion.90
  948.1 19.8 fusion.91
  968.1 19.6 fusion.58
  989.8 6.0 fusion.89
  995.8 12.2 fusion.40
  1011.6 39.7 %all-reduce.4 = (f32[2048]{0:T(1024)S(1)}, f32[2048]{0:T(1024)S(1)}) all-reduce(f32[2048]{0:T(1024)S(1)} %get-tuple-element.155, f32[2048]{0:T(1024)S(1)} %copy-done.34), channel_id=4, replica_groups=mesh['seq'=4,'fsdp'=8] {'seq','fsdp'}, use_global_device_ids=true, to_apply=%region_12.13.clone | all-reduce | flops 4096 | bytes 32768
  1052.5 3.5 fusion.46
  1055.9 124.9 %reduce-scatter.18.cloned.1.call-done = f32[64,256]{1,0:T(8,128)} async-done(((f32[2048,256]{1,0:T(8,128)}), f32[64,256]{1,0:T(8,128)}) %reduce-scatter.18.cloned.1.call-update) | async-done | bytes 65552 | tf_op jit(solution)/shard_map/reduce_scatter | solution.py:282
  1180.9 185.5 %reduce-scatter.14.cloned.1.call-done = f32[64,2048]{1,0:T(8,128)} async-done(((f32[2048,2048]{1,0:T(8,128)}), f32[64,2048]{1,0:T(8,128)}) %reduce-scatter.14.cloned.1.call-update) | async-done | bytes 524304 | tf_op jit(solution)/shard_map/reduce_scatter | solution.py:280
  1366.4 187.2 %reduce-scatter.20.cloned.1.call-done = f32[64,2048]{1,0:T(8,128)} async-done(((f32[2048,2048]{1,0:T(8,128)}), f32[64,2048]{1,0:T(8,128)}) %reduce-scatter.20.cloned.1.call-update) | async-done | bytes 524304 | tf_op jit(solution)/shard_map/reduce_scatter | solution.py:283
  1553.6 492.4 %reduce-scatter.22.cloned.1.call-done = f32[64,5632]{1,0:T(8,128)} async-done(((f32[2048,5632]{1,0:T(8,128)}), f32[64,5632]{1,0:T(8,128)}) %reduce-scatter.22.cloned.1.call-update) | async-done | bytes 1441808 | tf_op jit(solution)/shard_map/reduce_scatter | solution.py:159
  2046.0 491.2 %reduce-scatter.24.cloned.1.call-done = f32[64,5632]{1,0:T(8,128)} async-done(((f32[2048,5632]{1,0:T(8,128)}), f32[64,5632]{1,0:T(8,128)}) %reduce-scatter.24.cloned.1.call-update) | async-done | bytes 1441808 | tf_op jit(solution)/shard_map/reduce_scatter | solution.py:160
  2537.2 491.2 %reduce-scatter.26.cloned.1.call-done = f32[176,2048]{1,0:T(8,128)} async-done(((f32[5632,2048]{1,0:T(8,128)}), f32[176,2048]{1,0:T(8,128)}) %reduce-scatter.26.cloned.1.call-update) | async-done | bytes 1441808 | tf_op jit(solution)/shard_map/reduce_scatter | solution.py:161
  (185 shorter events, 62.1 us)
Async XLA Ops:
  7.2 4.9 copy-start.35
  7.2 5.1 copy-start.36
  7.2 47.5 %copy-start.33 = (s32[1,1024]{1,0:T(1,128)S(1)}, s32[1,1024]{1,0:T(1,128)}, u32[]{:S(2)}) copy-start(s32[1,1024]{1,0:T(1,128)} %param.15) | copy-start | bytes 12292
  7.2 49.0 %copy-start.3 = (bf16[1,256,2048]{2,1,0:T(8,128)(2,1)S(1)}, bf16[1,256,2048]{2,1,0:T(8,128)(2,1)}, u32[]{:S(2)}) copy-start(bf16[1,256,2048]{2,1,0:T(8,128)(2,1)} %param.14) | copy-start | bytes 3145732
  7.2 60.5 %all-gather.12.cloned.1.call-start = ((), (), s32[]{:S(2)}) async-start(), calls=%async_computation.11 | async-start | bytes 1081344 | tf_op jit(solution)/shard_map/all_gather | solution.py:76
  8.0 115.4 %all-gather.10.cloned.1.call-start = ((), (), s32[]{:S(2)}) async-start(), calls=%async_computation.10 | async-start | bytes 1081344 | tf_op jit(solution)/shard_map/all_gather | solution.py:75
  8.7 195.5 %all-gather.8.cloned.1.call-start = ((), (), s32[]{:S(2)}) async-start(), calls=%async_computation.9 | async-start | bytes 8650752 | tf_op jit(solution)/shard_map/all_gather | solution.py:74
  9.4 273.7 %all-gather.14.cloned.1.call-start = ((), (), s32[]{:S(2)}) async-start(), calls=%async_computation.12 | async-start | bytes 8650752 | tf_op jit(solution)/shard_map/all_gather | solution.py:77
  10.0 419.1 %all-gather.16.cloned.1.call-start = ((), (), s32[]{:S(2)}) async-start(), calls=%async_computation.13 | async-start | bytes 23789568 | tf_op jit(solution)/shard_map/all_gather | solution.py:134
  10.6 564.0 %all-gather.18.cloned.1.call-start = ((), (), s32[]{:S(2)}) async-start(), calls=%async_computation.14 | async-start | bytes 23789568 | tf_op jit(solution)/shard_map/all_gather | solution.py:135
  11.2 709.2 %all-gather.20.cloned.1.call-start = ((), (), s32[]{:S(2)}) async-start(), calls=%async_computation.15 | async-start | bytes 23789568 | tf_op jit(solution)/shard_map/all_gather | solution.py:136
  11.9 863.9 %reduce-scatter.10.cloned.1.call-start = ((), (), s32[]{:S(2)}) async-start(), calls=%async_computation.16 | async-start | bytes 655360 | tf_op jit(solution)/shard_map/reduce_scatter | solution.py:232
  54.7 161.8 %copy-start.26 = (f32[2048]{0:T(1024)}, f32[2048]{0:T(1024)S(1)}, u32[]{:S(2)}) copy-start(f32[2048]{0:T(1024)S(1)} %convert_element_type.124) | copy-start | bytes 24580
  54.7 14.7 copy-start.28
  56.2 71.3 %copy-start.17 = (f32[256,64]{0,1:T(8,128)}, f32[256,64]{0,1:T(8,128)S(1)}, u32[]{:S(2)}) copy-start(f32[256,64]{0,1:T(8,128)S(1)} %pad_maximum_fusion.3) | copy-start | bytes 196612
  56.2 71.3 %copy-start.14 = (f32[256,64]{0,1:T(8,128)}, f32[256,64]{0,1:T(8,128)S(1)}, u32[]{:S(2)}) copy-start(f32[256,64]{0,1:T(8,128)S(1)} %pad_maximum_fusion.2) | copy-start | bytes 196612
  56.5 160.0 %copy-start.30 = (f32[256]{0:T(256)}, f32[256]{0:T(256)S(1)}, u32[]{:S(2)}) copy-start(f32[256]{0:T(256)S(1)} %add_rsqrt_fusion.1) | copy-start | bytes 3076
  237.5 15.3 copy-start.25
  290.8 283.8 %copy-start.9 = (bf16[256,2048]{1,0:T(8,128)(2,1)}, bf16[256,2048]{1,0:T(8,128)(2,1)S(1)}, u32[]{:S(2)}) copy-start(bf16[256,2048]{1,0:T(8,128)(2,1)S(1)} %multiply_convert_fusion.3) | copy-start | bytes 3145732
  751.4 14.8 copy-start.12
  778.7 2.7 copy-start.29
  783.8 5.8 copy-start.1
  798.0 6.4 copy-start
  798.0 6.4 copy-start.22
  804.5 2.7 copy-start.32
  807.1 8.3 copy-start.23
  817.8 5.8 copy-start.1
  832.1 7.0 copy-start
  832.1 7.0 copy-start.22
  841.8 8.3 copy-start.23
  851.8 24.0 copy-start.19
  852.7 24.1 copy-start.16
  852.7 51.5 %reduce-scatter.12.cloned.1.call-start = ((), (), s32[]{:S(2)}) async-start(), calls=%async_computation.17 | async-start | bytes 655360 | tf_op jit(solution)/shard_map/reduce_scatter | solution.py:238
  853.3 24.4 copy-start.4
  853.3 24.4 copy-start.27
  853.3 24.4 copy-start.31
  854.2 201.7 %reduce-scatter.16.cloned.1.call-start = ((), (), s32[]{:S(2)}) async-start(), calls=%async_computation.19 | async-start | bytes 2162688 | tf_op jit(solution)/shard_map/reduce_scatter | solution.py:281
  879.7 28.0 copy-start.2
  879.7 301.1 %reduce-scatter.18.cloned.1.call-start = ((), (), s32[]{:S(2)}) async-start(), calls=%async_computation.20 | async-start | bytes 2162688 | tf_op jit(solution)/shard_map/reduce_scatter | solution.py:282
  907.3 459.1 %reduce-scatter.14.cloned.1.call-start = ((), (), s32[]{:S(2)}) async-start(), calls=%async_computation.18 | async-start | bytes 17301504 | tf_op jit(solution)/shard_map/reduce_scatter | solution.py:280
  918.2 635.4 %reduce-scatter.20.cloned.1.call-start = ((), (), s32[]{:S(2)}) async-start(), calls=%async_computation.21 | async-start | bytes 17301504 | tf_op jit(solution)/shard_map/reduce_scatter | solution.py:283
  928.3 1117.7 %reduce-scatter.22.cloned.1.call-start = ((), (), s32[]{:S(2)}) async-start(), calls=%async_computation.22 | async-start | bytes 47579136 | tf_op jit(solution)/shard_map/reduce_scatter | solution.py:159
  948.0 1589.2 %reduce-scatter.24.cloned.1.call-start = ((), (), s32[]{:S(2)}) async-start(), calls=%async_computation.23 | async-start | bytes 47579136 | tf_op jit(solution)/shard_map/reduce_scatter | solution.py:160
  967.9 2060.5 %reduce-scatter.26.cloned.1.call-start = ((), (), s32[]{:S(2)}) async-start(), calls=%async_computation.24 | async-start | bytes 47579136 | tf_op jit(solution)/shard_map/reduce_scatter | solution.py:161
  989.8 6.0 copy-start.8
  989.8 6.0 copy-start.10
  995.8 12.2 copy-start.11
  1009.3 43.2 %copy-start.6 = (f32[256,2048]{1,0:T(8,128)S(1)}, f32[256,2048]{1,0:T(8,128)}, u32[]{:S(2)}) copy-start(f32[256,2048]{1,0:T(8,128)} %copy-done.5) | copy-start | bytes 6291460
  (11 other events, 19.8 us)
Sparse Core Ops, SparseCore 0:
  11.1 56.5 all-gather.11
  70.7 52.6 all-gather.9
  126.4 77.8 all-gather.7
  207.1 75.9 all-gather.13
  285.8 143.2 all-gather.15
  431.8 142.8 all-gather.17
  577.5 142.8 all-gather.19
  852.8 22.9 reduce-scatter.9
  879.4 24.7 reduce-scatter.11
  906.9 137.1 reduce-scatter.15
  1047.1 133.7 reduce-scatter.17
  1183.6 182.7 reduce-scatter.13
  1369.3 184.3 reduce-scatter.19
  1556.4 489.5 reduce-scatter.21
  2048.7 488.4 reduce-scatter.23
  2539.9 488.4 reduce-scatter.25
where the time goes:
time: 3040 us
  waiting for transfers between devices  2550 us (84%)
  matrix products  285 us (9%)
  blocking collectives  109 us (4%)
  local copies, waits for them, and re-layouts  40.2 us (1%)
  other arithmetic  35.5 us (1%)
    reduce_scatter x1, waiting for transfers between devices, shards(): lax.psum_scatter(grad_gate, ('seq', 'fsdp'), scatter_dimension=0, tiled=T...  492 us
    reduce_scatter x1, waiting for transfers between devices, shards(): lax.psum_scatter(grad_up, ('seq', 'fsdp'), scatter_dimension=0, tiled=True)  491 us
    reduce_scatter x1, waiting for transfers between devices, shards(): lax.psum_scatter(grad_down, ('seq', 'fsdp'), scatter_dimension=0, tiled=T...  491 us
    reduce_scatter x1, waiting for transfers between devices, shards(): lax.psum_scatter(grad_output, ('seq', 'fsdp'), scatter_dimension=0, tiled...  187 us
    reduce_scatter x1, waiting for transfers between devices, shards(): lax.psum_scatter(grad_query, ('seq', 'fsdp'), scatter_dimension=0, tiled=...  186 us
    all_gather x1, waiting for transfers between devices, shards(): lax.all_gather(gate_weight, ('seq', 'fsdp'), axis=0, tiled=True)  138 us
    all_gather x1, waiting for transfers between devices, shards(): lax.all_gather(up_weight, ('seq', 'fsdp'), axis=0, tiled=True)  132 us
    all_gather x1, waiting for transfers between devices, shards(): lax.all_gather(down_weight, ('seq', 'fsdp'), axis=0, tiled=True)  132 us
  transfers between devices with their start and end apart: 16, of which 15 were waited for; matrix products, arithmetic and copies ran while one was open for 7% of the time, Pallas kernels for 0%

commit v1 on v0

v1 whole, which is shorter than its diff:
```python
import functools
import math

import jax
import jax.numpy as jnp
from jax import lax
from jax.experimental import pallas as pl
from jax.experimental.pallas import tpu as pltpu
from jax.sharding import PartitionSpec as P

HEADS = 32
KV_HEADS = 4
HEAD_DIM = 64
HALF = HEAD_DIM // 2
GROUP = HEADS // KV_HEADS
EPSILON = 1e-05
SCALE = 1.0 / math.sqrt(HEAD_DIM)
LOW = jnp.bfloat16
FULL = jnp.float32


def dot(a, b, dims=((1,), (0,)), out=FULL):
    return lax.dot_general(a, b, (dims, ((), ())), preferred_element_type=out)


def rope_tables(where_at):
    frequency = 1.0 / 10000.0 ** (jnp.arange(HALF, dtype=FULL) * 2.0 / HEAD_DIM)
    angles = frequency[:, None] * where_at.astype(FULL)[None, :]
    return jnp.cos(angles), jnp.sin(angles)


def attend_kernel(heads, kvs, span, order_ref, rank_ref, qkv_ref, cos_ref, sin_ref,
                  qrot_ref, kv_ref, att_ref, mix_ref, lse_ref, keys_ref):
    count = cos_ref.shape[1] // span
    qw, kw = heads * HEAD_DIM, kvs * HEAD_DIM
    cosine, sine = cos_ref[...], sin_ref[...]

    def rotated(row):
        one, two = qkv_ref[row:row + HALF, :], qkv_ref[row + HALF:row + HEAD_DIM, :]
        return jnp.concatenate([one * cosine - two * sine, two * cosine + one * sine], 0)

    for h in range(heads):
        qrot_ref[h * HEAD_DIM:(h + 1) * HEAD_DIM, :] = rotated(h * HEAD_DIM).astype(LOW)
    for k in range(kvs):
        turned = rotated(qw + k * HEAD_DIM).astype(LOW)
        kv_ref[k * HEAD_DIM:(k + 1) * HEAD_DIM, :] = turned
        keys_ref[k] = (turned.astype(FULL) * SCALE).T.astype(LOW)
    kv_ref[kw:, :] = qkv_ref[qw + kw:, :].astype(LOW)

    def one_block(qb, _):
        cols = pl.ds(pl.multiple_of(qb * span, span), span)
        rank = rank_ref[qb]

        def step(at, state, diagonal):
            rows = pl.ds(pl.multiple_of(order_ref[at] * span, span), span)
            out = []
            for h in range(heads):
                top, total, mixed = state[h]
                k = h * kvs // heads
                scores = dot(keys_ref[k, rows, :], qrot_ref[h * HEAD_DIM:(h + 1) * HEAD_DIM, cols])
                if diagonal:
                    key_at = lax.broadcasted_iota(jnp.int32, (span, span), 0)
                    query_at = lax.broadcasted_iota(jnp.int32, (span, span), 1)
                    scores = jnp.where(key_at <= query_at, scores, -1e30)
                new_top = jnp.maximum(top, jnp.max(scores, 0, keepdims=True))
                weights = jnp.exp(scores - new_top)
                fade = jnp.exp(top - new_top)
                total = total * fade + jnp.sum(weights, 0, keepdims=True)
                values = kv_ref[kw + k * HEAD_DIM:kw + (k + 1) * HEAD_DIM, rows]
                mixed = mixed * fade + dot(values, weights.astype(LOW))
                out.append((new_top, total, mixed))
            return out

        start = [(jnp.full((1, span), -1e30, FULL), jnp.zeros((1, span), FULL),
                  jnp.zeros((HEAD_DIM, span), FULL)) for _ in range(heads)]
        state = lax.fori_loop(0, rank, lambda at, st: step(at, st, False), start)
        state = step(rank, state, True)
        for h in range(heads):
            top, total, mixed = state[h]
            mixed = mixed / total
            mix_ref[h * HEAD_DIM:(h + 1) * HEAD_DIM, cols] = mixed
            att_ref[h * HEAD_DIM:(h + 1) * HEAD_DIM, cols] = mixed.astype(LOW)
            lse_ref[h:h + 1, cols] = top + jnp.log(total)
        return 0

    lax.fori_loop(0, count, one_block, 0)


def attend(order, rank, qkv, cosine, sine, heads, kvs, span):
    tokens = qkv.shape[1]
    qw, kw = heads * HEAD_DIM, kvs * HEAD_DIM
    vmem = pl.BlockSpec(memory_space=pltpu.VMEM)
    smem = pl.BlockSpec(memory_space=pltpu.SMEM)
    return pl.pallas_call(
        functools.partial(attend_kernel, heads, kvs, span),
        out_shape=(
            jax.ShapeDtypeStruct((qw, tokens), LOW),
            jax.ShapeDtypeStruct((2 * kw, tokens), LOW),
            jax.ShapeDtypeStruct((qw, tokens), LOW),
            jax.ShapeDtypeStruct((qw, tokens), FULL),
            jax.ShapeDtypeStruct((heads, tokens), FULL),
        ),
        in_specs=[smem, smem, vmem, vmem, vmem],
        out_specs=(vmem,) * 5,
        scratch_shapes=[pltpu.VMEM((kvs, tokens, HEAD_DIM), LOW)],
        compiler_params=pltpu.CompilerParams(vmem_limit_bytes=40 << 20),
        cost_estimate=pl.CostEstimate(
            flops=4 * qw * tokens * tokens, bytes_accessed=12 * qw * tokens, transcendentals=heads * tokens * tokens
        ),
        name="attend",
    )(order, rank, qkv, cosine, sine)


def attend_back_kernel(heads, kvs, span, order_ref, rank_ref, qrot_ref, kv_ref, grad_ref, mix_ref, lse_ref,
                       cos_ref, sin_ref, out_ref, keys_ref, values_ref, delta_ref, dkv_ref):
    count = cos_ref.shape[1] // span
    qw, kw = heads * HEAD_DIM, kvs * HEAD_DIM
    for k in range(kvs):
        keys_ref[k] = (kv_ref[k * HEAD_DIM:(k + 1) * HEAD_DIM, :].astype(FULL) * SCALE).T.astype(LOW)
        values_ref[k] = kv_ref[kw + k * HEAD_DIM:kw + (k + 1) * HEAD_DIM, :].astype(FULL).T.astype(LOW)
    for h in range(heads):
        rows = slice(h * HEAD_DIM, (h + 1) * HEAD_DIM)
        delta_ref[h:h + 1, :] = jnp.sum(grad_ref[rows, :].astype(FULL) * mix_ref[rows, :], 0, keepdims=True)
    dkv_ref[...] = jnp.zeros_like(dkv_ref)

    def one_block(qb, _):
        cols = pl.ds(pl.multiple_of(qb * span, span), span)
        rank = rank_ref[qb]

        def step(at, state, diagonal):
            rows = pl.ds(pl.multiple_of(order_ref[at] * span, span), span)
            out = []
            dkeys = [None] * kvs
            dvalues = [None] * kvs
            for h in range(heads):
                k = h * kvs // heads
                mine = slice(h * HEAD_DIM, (h + 1) * HEAD_DIM)
                query = qrot_ref[mine, cols]
                grad = grad_ref[mine, cols]
                scores = dot(keys_ref[k, rows, :], query)
                weights = jnp.exp(scores - lse_ref[h:h + 1, cols])
                if diagonal:
                    key_at = lax.broadcasted_iota(jnp.int32, (span, span), 0)
                    query_at = lax.broadcasted_iota(jnp.int32, (span, span), 1)
                    weights = jnp.where(key_at <= query_at, weights, 0.0)
                grad_probs = dot(values_ref[k, rows, :], grad)
                grad_scores = (weights * (grad_probs - delta_ref[h:h + 1, cols])).astype(LOW)
                key_t = kv_ref[k * HEAD_DIM:(k + 1) * HEAD_DIM, rows]
                out.append(state[h] + dot(key_t, grad_scores))
                dk = dot(query, grad_scores, ((1,), (1,)))
                dv = dot(grad, weights.astype(LOW), ((1,), (1,)))
                dkeys[k] = dk if dkeys[k] is None else dkeys[k] + dk
                dvalues[k] = dv if dvalues[k] is None else dvalues[k] + dv
            for k in range(kvs):
                mine = slice(k * HEAD_DIM, (k + 1) * HEAD_DIM)
                dkv_ref[mine, rows] += dkeys[k]
                mine = slice(kw + k * HEAD_DIM, kw + (k + 1) * HEAD_DIM)
                dkv_ref[mine, rows] += dvalues[k]
            return out

        state = [jnp.zeros((HEAD_DIM, span), FULL) for _ in range(heads)]
        state = lax.fori_loop(0, rank, lambda at, st: step(at, st, False), state)
        state = step(rank, state, True)
        cosine, sine = cos_ref[:, cols], sin_ref[:, cols]
        for h in range(heads):
            one, two = state[h][:HALF] * SCALE, state[h][HALF:] * SCALE
            out_ref[h * HEAD_DIM:h * HEAD_DIM + HALF, cols] = (one * cosine + two * sine).astype(LOW)
            out_ref[h * HEAD_DIM + HALF:(h + 1) * HEAD_DIM, cols] = (two * cosine - one * sine).astype(LOW)
        return 0

    lax.fori_loop(0, count, one_block, 0)
    cosine, sine = cos_ref[...], sin_ref[...]
    for k in range(kvs):
        top = k * HEAD_DIM
        one, two = dkv_ref[top:top + HALF, :] * SCALE, dkv_ref[top + HALF:top + HEAD_DIM, :] * SCALE
        out_ref[qw + top:qw + top + HALF, :] = (one * cosine + two * sine).astype(LOW)
        out_ref[qw + top + HALF:qw + top + HEAD_DIM, :] = (two * cosine - one * sine).astype(LOW)
    out_ref[qw + kw:, :] = dkv_ref[kw:, :].astype(LOW)


def attend_back(order, rank, qrot, kv, grad, mix, lse, cosine, sine, heads, kvs, span):
    tokens = qrot.shape[1]
    qw, kw = heads * HEAD_DIM, kvs * HEAD_DIM
    vmem = pl.BlockSpec(memory_space=pltpu.VMEM)
    smem = pl.BlockSpec(memory_space=pltpu.SMEM)
    return pl.pallas_call(
        functools.partial(attend_back_kernel, heads, kvs, span),
        out_shape=jax.ShapeDtypeStruct((qw + 2 * kw, tokens), LOW),
        in_specs=[smem, smem] + [vmem] * 7,
        out_specs=vmem,
        scratch_shapes=[
            pltpu.VMEM((kvs, tokens, HEAD_DIM), LOW),
            pltpu.VMEM((kvs, tokens, HEAD_DIM), LOW),
            pltpu.VMEM((heads, tokens), FULL),
            pltpu.VMEM((2 * kw, tokens), FULL),
        ],
        compiler_params=pltpu.CompilerParams(vmem_limit_bytes=40 << 20),
        cost_estimate=pl.CostEstimate(
            flops=10 * qw * tokens * tokens, bytes_accessed=12 * qw * tokens, transcendentals=heads * tokens * tokens
        ),
        name="attend_back",
    )(order, rank, qrot, kv, grad, mix, lse, cosine, sine)


def layer(seq_size, fsdp_size, tokens, positions, attn_gain, query_weight, key_weight, value_weight, output_weight,
          ffn_gain, gate_weight, up_weight, down_weight, cotangent):
    span, width = tokens.shape[1:]
    heads = HEADS // seq_size
    kvs = max(1, KV_HEADS // seq_size)
    shared = max(1, seq_size // KV_HEADS)
    qw, kw = heads * HEAD_DIM, kvs * HEAD_DIM
    own_rows = query_weight.shape[0]
    hidden_own = gate_weight.shape[1] // seq_size
    here = lax.axis_index("seq")

    def swap(x, j):
        return lax.ppermute(x, "seq", [(i, i ^ j) for i in range(seq_size)])

    def seq_gather(x):
        if seq_size != 4:
            return jnp.concatenate([x] + [swap(x, j) for j in range(1, seq_size)], 0)
        half = x.shape[0] // 2
        a, b = x[:half], x[half:]
        ax, by = swap(a, 1), swap(b, 2)
        ay, bx = swap(a, 2), swap(b, 1)
        ad, bd = swap(ax, 2), swap(by, 1)
        return jnp.concatenate([a, b, ax, bx, ay, by, ad, bd], 0)

    def seq_scatter(x):
        blocks = [x[j * span:(j + 1) * span] for j in range(seq_size)]
        if seq_size != 4:
            total = blocks[0].astype(FULL)
            for j in range(1, seq_size):
                total = total + swap(blocks[j], j).astype(FULL)
            return total
        half = span // 2
        a, b = [blk[:half] for blk in blocks], [blk[half:] for blk in blocks]
        da, db = swap(a[3], 2), swap(b[3], 1)
        ya, xb = swap(a[2], 2), swap(b[1], 1)
        xa = swap((a[1].astype(FULL) + da.astype(FULL)).astype(LOW), 1)
        yb = swap((b[2].astype(FULL) + db.astype(FULL)).astype(LOW), 2)
        return jnp.concatenate([
            a[0].astype(FULL) + ya.astype(FULL) + xa.astype(FULL),
            b[0].astype(FULL) + xb.astype(FULL) + yb.astype(FULL),
        ], 0)

    def spread(pieces_for):
        got = [pieces_for(here)] + [swap(pieces_for(here ^ j), j) for j in range(1, seq_size)]
        stack = jnp.stack(got)
        return jnp.concatenate(
            [lax.dynamic_index_in_dim(stack, here ^ t, 0, False) for t in range(seq_size)], 0
        )

    def collect(x):
        blocks = x.reshape(seq_size, own_rows, x.shape[1])
        got = jnp.stack([lax.dynamic_index_in_dim(blocks, here, 0, False)] + [
            swap(lax.dynamic_index_in_dim(blocks, here ^ j, 0, False), j) for j in range(1, seq_size)
        ])
        return jnp.stack([lax.dynamic_index_in_dim(got, here ^ t, 0, False) for t in range(seq_size)])

    def fsdp_gather(x):
        return lax.all_gather(x, "fsdp", axis=0, tiled=True)

    def fsdp_scatter(x):
        return lax.psum_scatter(x, "fsdp", scatter_dimension=0, tiled=True)

    def shuffled(x):
        return x.reshape(span, seq_size, fsdp_size, own_rows).swapaxes(1, 2).reshape(span, width)

    def unshuffled(x):
        return x.reshape(span, fsdp_size, seq_size, own_rows).swapaxes(1, 2).reshape(span, width)

    gain_one, gain_two = attn_gain.astype(FULL)[:, None], ffn_gain.astype(FULL)[:, None]

    def with_gain(weight, gain):
        return (weight.astype(FULL) * gain).astype(LOW)

    query_low, key_low, value_low = (with_gain(w, gain_one) for w in (query_weight, key_weight, value_weight))
    gate_low, up_low = (with_gain(w, gain_two) for w in (gate_weight, up_weight))

    def qkv_for(t):
        first = (t * heads // GROUP) * HEAD_DIM
        return jnp.concatenate([
            lax.dynamic_slice_in_dim(query_low, t * qw, qw, 1),
            lax.dynamic_slice_in_dim(key_low, first, kw, 1),
            lax.dynamic_slice_in_dim(value_low, first, kw, 1),
        ], 1)

    def gate_up_for(t):
        return jnp.concatenate([
            lax.dynamic_slice_in_dim(gate_low, t * hidden_own, hidden_own, 1),
            lax.dynamic_slice_in_dim(up_low, t * hidden_own, hidden_own, 1),
        ], 1)

    token_rows = tokens[0].astype(FULL)
    inv_one = lax.rsqrt(jnp.mean(token_rows * token_rows, -1, keepdims=True) + EPSILON)
    scaled_one = token_rows * inv_one
    normed_one = seq_gather(shuffled(scaled_one.astype(LOW)))
    qkv_full = fsdp_gather(spread(qkv_for))
    output_full = fsdp_gather(output_weight)
    gate_up_full = fsdp_gather(spread(gate_up_for))
    down_full = fsdp_gather(down_weight)
    upstream = seq_gather(cotangent[0])

    count = positions.shape[1] // span
    where_at = positions[0].reshape(count, span)
    where_at = jnp.stack([lax.dynamic_index_in_dim(where_at, here ^ j, 0, False) for j in range(count)])
    rank = where_at[:, 0] // span
    order = jnp.argsort(rank).astype(jnp.int32)
    cosine, sine = rope_tables(where_at.reshape(-1))

    qkv = dot(qkv_full, normed_one, ((0,), (1,)))
    qrot, kv, attended, mix, lse = attend(order, rank, qkv, cosine, sine, heads, kvs, span)
    branch = seq_scatter(dot(attended, output_full, ((0,), (0,)), LOW))
    middle = token_rows + branch

    inv_two = lax.rsqrt(jnp.mean(middle * middle, -1, keepdims=True) + EPSILON)
    scaled_two = middle * inv_two
    normed_two = seq_gather(shuffled(scaled_two.astype(LOW)))
    gate_full, up_full = gate_up_full[:, :hidden_own], gate_up_full[:, hidden_own:]
    gate_rows = dot(normed_two, gate_full)
    up_rows = dot(normed_two, up_full)
    sigmoid = jax.nn.sigmoid(gate_rows)
    silu = gate_rows * sigmoid
    hidden = (silu * up_rows).astype(LOW)
    grad_hidden = dot(upstream, down_full, ((1,), (1,)))
    grad_gaterows = (grad_hidden * up_rows * sigmoid * (1.0 + gate_rows * (1.0 - sigmoid))).astype(LOW)
    grad_uprows = (grad_hidden * silu).astype(LOW)
    grad_down = fsdp_scatter(dot(hidden, upstream, ((0,), (0,)), LOW))
    grad_gate = fsdp_scatter(dot(normed_two, grad_gaterows, ((0,), (0,)), LOW))
    grad_up = fsdp_scatter(dot(normed_two, grad_uprows, ((0,), (0,)), LOW))
    grad_two = (dot(grad_gaterows, gate_full, ((1,), (1,))) + dot(grad_uprows, up_full, ((1,), (1,)))).astype(LOW)
    scaled_grad = unshuffled(seq_scatter(grad_two))
    block_out = (middle + seq_scatter(dot(hidden, down_full, out=LOW))).astype(LOW)
    grad_middle = cotangent[0].astype(FULL) + inv_two * (
        scaled_grad - scaled_two * jnp.mean(scaled_grad * scaled_two, -1, keepdims=True)
    )

    grad_branch = seq_gather(grad_middle.astype(LOW))
    grad_output = fsdp_scatter(dot(attended, grad_branch, out=LOW))
    grad_attended = dot(output_full, grad_branch, ((1,), (1,)), LOW)
    grad_qkv = attend_back(order, rank, qrot, kv, grad_attended, mix, lse, cosine, sine, heads, kvs, span)
    grad_qkv_weight = fsdp_scatter(dot(normed_one, grad_qkv, ((0,), (1,)), LOW))
    grad_one = dot(grad_qkv, qkv_full, ((0,), (1,)), LOW)
    scaled_grad = unshuffled(seq_scatter(grad_one))
    grad_tokens = grad_middle + inv_one * (
        scaled_grad - scaled_one * jnp.mean(scaled_grad * scaled_one, -1, keepdims=True)
    )

    def whole_rows(x):
        return x.swapaxes(0, 1).reshape(own_rows, -1)

    grad_gate, grad_up = (whole_rows(collect(g).astype(FULL)) for g in (grad_gate, grad_up))
    got = collect(grad_qkv_weight).astype(FULL)
    grad_query = whole_rows(got[:, :, :qw])

    def of_heads(x):
        return whole_rows(x.reshape(seq_size // shared, shared, own_rows, kw).sum(1))

    grad_key, grad_value = of_heads(got[:, :, qw:qw + kw]), of_heads(got[:, :, qw + kw:])
    grad_attn_gain = (
        jnp.sum(grad_query * query_weight.astype(FULL), 1)
        + jnp.sum(grad_key * key_weight.astype(FULL), 1)
        + jnp.sum(grad_value * value_weight.astype(FULL), 1)
    )
    grad_ffn_gain = jnp.sum(grad_gate * gate_weight.astype(FULL), 1) + jnp.sum(grad_up * up_weight.astype(FULL), 1)
    return (
        block_out[None],
        grad_tokens[None],
        grad_attn_gain,
        grad_query * gain_one,
        grad_key * gain_one,
        grad_value * gain_one,
        grad_output.astype(FULL),
        grad_ffn_gain,
        grad_gate * gain_two,
        grad_up * gain_two,
        grad_down.astype(FULL),
    )


def solution(mesh):
    rows, vector, matrix = P("fsdp", "seq", None), P(("seq", "fsdp")), P(("seq", "fsdp"), None)
    return jax.shard_map(
        functools.partial(layer, mesh.shape["seq"], mesh.shape["fsdp"]),
        mesh=mesh,
        in_specs=(
            rows, P("fsdp", None), vector, matrix, matrix, matrix, matrix, vector, matrix, matrix, matrix, rows,
        ),
        out_specs=(rows, rows, vector, matrix, matrix, matrix, matrix, vector, matrix, matrix, matrix),
        check_vma=False,
    )
```

time: 3040 us -> 723 us (0.24)
  waiting for transfers between devices: 2550 us -> 335 us
  matrix products: 285 us -> 128 us
  blocking collectives: 109 us -> 0 us
  starting transfers between devices: 1.22 us -> 70.3 us
  Pallas kernels: 0 us -> 50.3 us
    reduce_scatter x9 -> x5, waiting for transfers between devices: 2020 us -> 103 us  [fsdp_scatter(): return lax.psum_scatter(x, 'fsdp', scatter_dimension=0, tiled=True)]
    all_gather x7 -> x4, waiting for transfers between devices: 526 us -> 13.5 us  [fsdp_gather(): return lax.all_gather(x, 'fsdp', axis=0, tiled=True)]
    ppermute x0 -> x63, waiting for transfers between devices: none -> 218 us  [swap(): return lax.ppermute(x, 'seq', [(i, i ^ j) for i in range(seq_size)])]
    dot_general x33 -> x15, matrix products: 285 us -> 128 us  [dot(): return lax.dot_general(a, b, (dims, ((), ())), preferred_element_type=out)]
    unnamed x2 -> x0, blocking collectives: 81.8 us -> none
    ppermute x0 -> x63, starting transfers between devices: none -> 69.8 us  [swap(): return lax.ppermute(x, 'seq', [(i, i ^ j) for i in range(seq_size)])]
    pallas_call x0 -> x2, Pallas kernels: none -> 50.3 us  [the longest x1 26 us: attend_back(): pl.pallas_call(functools.partial(attend_back_kernel, heads, kvs, span), o...]
  transfers between devices with their start and end apart: 16 -> 72, of which waited for: 15 -> 41; matrix products, arithmetic and copies ran while one was open for 7% -> 22% of each run, Pallas kernels for 0% -> 3%
where the time goes in v1:
time: 723 us; the launch traced here: 715 us
  waiting for transfers between devices  335 us (46%)
  matrix products  128 us (18%)
  starting transfers between devices  70.3 us (10%)
  local copies, waits for them, and re-layouts  64 us (9%)
  other arithmetic  51 us (7%)
  Pallas kernels  50.3 us (7%)
  between operations  15.5 us (2%)
    ppermute x63, waiting for transfers between devices, swap(): return lax.ppermute(x, 'seq', [(i, i ^ j) for i in range(seq_size)])  218 us
    dot_general x15, matrix products, dot(): return lax.dot_general(a, b, (dims, ((), ())), preferred_element_type=out)  128 us
    reduce_scatter x5, waiting for transfers between devices, fsdp_scatter(): return lax.psum_scatter(x, 'fsdp', scatter_dimension=0, tiled=True)  103 us
    ppermute x63, starting transfers between devices, swap(): return lax.ppermute(x, 'seq', [(i, i ^ j) for i in range(seq_size)])  69.8 us
    unnamed x101, local copies, waits for them, and re-layouts  26.3 us
    pallas_call x1, Pallas kernels, attend_back(): pl.pallas_call(functools.partial(attend_back_kernel, heads, kvs, span), o...  26 us
    pallas_call x1, Pallas kernels, attend(): pl.pallas_call(functools.partial(attend_kernel, heads, kvs, span), out_sh...  24.2 us
  transfers between devices with their start and end apart: 72, of which 41 were waited for; matrix products, arithmetic and copies ran while one was open for 22% of the time, Pallas kernels for 3%

profile of v1, /device:TPU:0, one launch (start us, length us, event | category | flops | bytes accessed | tf_op | source)
XLA Modules:
  0.0 714.7 jit_solution(14285094052073941089)
XLA Ops:
  27.1 7.6 %collective-permute-done.21 = bf16[64,2816]{1,0:T(8,128)(2,1)S(1)} collective-permute-done((bf16[64,2816]{1,0:T(8,128)(2,1)S(1)}, bf16[64,2816]{1,0:T(8,128)(2,1)S(1)}, u32[]{:S(2)}, u32[]{:S(2)}) %collective-permute-start.21) | collective-permute-done | bytes 360480 | tf_op jit(solution)/shard_map/ppermute | solution.py:217
  34.7 5.6 collective-permute-done.22
  55.6 4.7 collective-permute-done.3
  61.3 9.1 %collective-permute-done.6 = bf16[128,2048]{0,1:T(8,128)(2,1)S(1)} collective-permute-done((bf16[128,2048]{0,1:T(8,128)(2,1)}, bf16[128,2048]{0,1:T(8,128)(2,1)S(1)}, u32[]{:S(2)}, u32[]{:S(2)}) %collective-permute-start.6) | collective-permute-done | bytes 524320 | tf_op jit(solution)/shard_map/ppermute | solution.py:217
  80.5 5.5 fusion.38.qkv_ref
  86.0 24.2 %attend.1 = (bf16[512,1024]{1,0:T(8,128)(2,1)S(1)}, bf16[128,1024]{1,0:T(8,128)(2,1)S(1)}, bf16[512,1024]{1,0:T(8,128)(2,1)S(1)}, f32[512,1024]{1,0:T(8,128)S(1)}, f32[8,1024]{1,0:T(8,128)S(1)}) custom-call(s32[4]{0:T(128)S(1)} %get-tuple-element.17.order_ref, s32[4]{0:T(128)S(1)} %and_select_fusion.rank_ref, f32[640,1024]{1,0:T(8,128)S(1)} %fusion.38.qkv_ref, ...), custom_call_target="tpu_custom_call" | custom-call | flops 2147483648 | bytes 6291456 | tf_op jit(solution)/shard_map/attend/pallas_call | solution.py:94
  112.6 4.0 fusion.39
  122.9 9.5 %collective-permute-done.10 = bf16[128,2048]{1,0:T(8,128)(2,1)S(1)} collective-permute-done((bf16[128,2048]{1,0:T(8,128)(2,1)S(1)}, bf16[128,2048]{1,0:T(8,128)(2,1)S(1)}, u32[]{:S(2)}, u32[]{:S(2)}) %collective-permute-start.10) | collective-permute-done | bytes 524320 | tf_op jit(solution)/shard_map/ppermute | solution.py:217
  133.8 12.1 %collective-permute-done.30 = bf16[128,2048]{1,0:T(8,128)(2,1)S(1)} collective-permute-done((bf16[128,2048]{1,0:T(8,128)(2,1)S(1)}, bf16[128,2048]{1,0:T(8,128)(2,1)S(1)}, u32[]{:S(2)}, u32[]{:S(2)}) %collective-permute-start.30) | collective-permute-done | bytes 524320 | tf_op jit(solution)/shard_map/ppermute | solution.py:217
  149.4 5.6 collective-permute-done.9
  158.3 10.1 %collective-permute-done.11 = bf16[128,2048]{1,0:T(8,128)(2,1)S(1)} collective-permute-done((bf16[128,2048]{1,0:T(8,128)(2,1)S(1)}, bf16[128,2048]{1,0:T(8,128)(2,1)S(1)}, u32[]{:S(2)}, u32[]{:S(2)}) %collective-permute-start.11) | collective-permute-done | bytes 524320 | tf_op jit(solution)/shard_map/ppermute | solution.py:217
  172.1 4.8 collective-permute-done.34
  181.4 3.8 collective-permute-done.12
  202.8 7.1 collective-permute-done.15
  213.3 7.4 %collective-permute-done.16 = bf16[128,2048]{0,1:T(8,128)(2,1)S(1)} collective-permute-done((bf16[128,2048]{0,1:T(8,128)(2,1)S(1)}, bf16[128,2048]{0,1:T(8,128)(2,1)S(1)}, u32[]{:S(2)}, u32[]{:S(2)}) %collective-permute-start.16) | collective-permute-done | bytes 524320 | tf_op jit(solution)/shard_map/ppermute | solution.py:217
  223.9 3.8 collective-permute-done.19
  229.5 11.8 %fusion.41 = f32[1024,1408]{1,0:T(8,128)} fusion(bf16[1024,2048]{1,0:T(8,128)(2,1)} %constant_dynamic-update-slice_fusion.16, bf16[1408,2048]{1,0:T(8,128)(2,1)} %all-gather.11.cloned.1.call-done), kind=kOutput, calls=%fused_computation.214 | convolution fusion | flops 5905580032 | bytes 15728640 | tf_op jit(solution)/shard_map/dot_general | solution.py:23
  241.3 13.5 %all-gather.9.cloned.1.call-done = bf16[2048,2816]{1,0:T(8,128)(2,1)} async-done(((bf16[256,2816]{1,0:T(8,128)(2,1)}), bf16[2048,2816]{1,0:T(8,128)(2,1)}) %all-gather.9.cloned.1.call-update) | async-done | bytes 11534352 | tf_op jit(solution)/shard_map/all_gather | solution.py:262
  254.9 12.4 %fusion.3 = f32[1024,1408]{1,0:T(8,128)} fusion(bf16[1024,2048]{0,1:T(8,128)(2,1)} %constant_dynamic-update-slice_fusion.8, bf16[2048,2816]{1,0:T(8,128)(2,1)} %all-gather.9.cloned.1.call-done), kind=kOutput, calls=%fused_computation.8 | convolution fusion | flops 5905580032 | bytes 15728640 | tf_op jit(solution)/shard_map/dot_general | solution.py:23
  267.3 15.5 %multiply_convert_fusion.1 = (bf16[1024,1408]{1,0:T(8,128)(2,1)}, bf16[1024,1408]{1,0:T(8,128)(2,1)}, bf16[1024,1408]{1,0:T(8,128)(2,1)}) fusion(f32[1024,1408]{1,0:T(8,128)} %fusion.41, f32[1024,1408]{1,0:T(8,128)} %fusion.3, bf16[1024,2048]{0,1:T(8,128)(2,1)} %constant_dynamic-update-slice_fusion.8, bf16[2048,2816]{1,0:T(8,128)(2,1)S(1)} %copy-done.32), kind=kOutput, calls=%fused_computation.2 | convolution fusion | flops 5927206912 | bytes 30146560 | tf_op jit(solution)/shard_map/dot_general | solution.py:23
  282.8 10.3 %fusion.1 = f32[1024,2048]{1,0:T(8,128)} fusion(bf16[1024,1408]{1,0:T(8,128)(2,1)} %get-tuple-element.26, bf16[2048,2816]{1,0:T(8,128)(2,1)S(1)} %copy-done.32), kind=kOutput, calls=%fused_computation.6 | convolution fusion | flops 5905580032 | bytes 17039360 | tf_op jit(solution)/shard_map/dot_general | solution.py:23
  293.1 10.2 %add_convert_fusion = bf16[1024,2048]{1,0:T(8,128)(2,1)S(1)} fusion(f32[1024,2048]{1,0:T(8,128)} %fusion.1, bf16[1024,1408]{1,0:T(8,128)(2,1)} %get-tuple-element.25, bf16[2048,2816]{1,0:T(8,128)(2,1)S(1)} %copy-done.32), kind=kOutput, calls=%fused_computation | convolution fusion | flops 5909774336 | bytes 21233664 | tf_op jit(solution)/shard_map/dot_general | solution.py:23
  307.1 11.3 %collective-permute-done.37 = bf16[128,2048]{1,0:T(8,128)(2,1)S(1)} collective-permute-done((bf16[128,2048]{1,0:T(8,128)(2,1)S(1)}, bf16[128,2048]{1,0:T(8,128)(2,1)S(1)}, u32[]{:S(2)}, u32[]{:S(2)}) %collective-permute-start.37) | collective-permute-done | bytes 524320 | tf_op jit(solution)/shard_map/ppermute | solution.py:217
  320.6 8.3 %collective-permute-done.36 = bf16[128,2048]{1,0:T(8,128)(2,1)S(1)} collective-permute-done((bf16[128,2048]{1,0:T(8,128)(2,1)S(1)}, bf16[128,2048]{1,0:T(8,128)(2,1)S(1)}, u32[]{:S(2)}, u32[]{:S(2)}) %collective-permute-start.36) | collective-permute-done | bytes 524320 | tf_op jit(solution)/shard_map/ppermute | solution.py:217
  328.9 4.5 collective-permute-done.38
  335.4 6.9 collective-permute-done.39
  348.0 3.5 fusion.17
  363.1 10.8 %collective-permute-done.45 = bf16[128,2048]{1,0:T(8,128)(2,1)S(1)} collective-permute-done((bf16[128,2048]{1,0:T(8,128)(2,1)S(1)}, bf16[128,2048]{1,0:T(8,128)(2,1)S(1)}, u32[]{:S(2)}, u32[]{:S(2)}) %collective-permute-start.45) | collective-permute-done | bytes 524320 | tf_op jit(solution)/shard_map/ppermute | solution.py:217
  377.0 9.7 %collective-permute-done.43 = bf16[128,2048]{1,0:T(8,128)(2,1)S(1)} collective-permute-done((bf16[128,2048]{1,0:T(8,128)(2,1)S(1)}, bf16[128,2048]{1,0:T(8,128)(2,1)S(1)}, u32[]{:S(2)}, u32[]{:S(2)}) %collective-permute-start.43) | collective-permute-done | bytes 524320 | tf_op jit(solution)/shard_map/ppermute | solution.py:217
  386.8 5.4 collective-permute-done.46
  396.9 26.0 %attend_back.1 = bf16[640,1024]{1,0:T(8,128)(2,1)S(1)} custom-call(s32[4]{0:T(128)S(1)} %get-tuple-element.17.order_ref, s32[4]{0:T(128)S(1)} %and_select_fusion.rank_ref, bf16[512,1024]{1,0:T(8,128)(2,1)S(1)} %copy-done.3, bf16[128,1024]{1,0:T(8,128)(2,1)S(1)} %get-tuple-element.20.kv_ref, bf16[512,1024]{1,0:T(8,128)(2,1)S(1)} %convolution_bitcast_fusion.grad_ref, ...), custom_call_target="tpu_custom_call" | custom-call | flops 5368709120 | bytes 6291456 | tf_op jit(solution)/shard_map/attend_back/pallas_call | solution.py:186
  423.0 4.8 fusion.43
  428.0 5.8 fusion.44
  433.9 10.9 %fusion.45 = bf16[2048,1408]{1,0:T(8,128)(2,1)} fusion(bf16[1024,2048]{0,1:T(8,128)(2,1)} %constant_dynamic-update-slice_fusion.8, bf16[1024,1408]{1,0:T(8,128)(2,1)} %get-tuple-element.25), kind=kOutput, calls=%fused_computation.218 | convolution fusion | flops 5905580032 | bytes 12845056 | tf_op jit(solution)/shard_map/dot_general | solution.py:23
  444.9 11.0 %fusion.46 = bf16[2048,1408]{1,0:T(8,128)(2,1)} fusion(bf16[1024,2048]{0,1:T(8,128)(2,1)} %constant_dynamic-update-slice_fusion.8, bf16[1024,1408]{1,0:T(8,128)(2,1)} %get-tuple-element.26), kind=kOutput, calls=%fused_computation.219 | convolution fusion | flops 5905580032 | bytes 12845056 | tf_op jit(solution)/shard_map/dot_general | solution.py:23
  455.9 10.5 %fusion.47 = bf16[1408,2048]{1,0:T(8,128)(2,1)} fusion(bf16[1024,1408]{1,0:T(8,128)(2,1)} %get-tuple-element.27, bf16[1024,2048]{1,0:T(8,128)(2,1)} %constant_dynamic-update-slice_fusion.16), kind=kOutput, calls=%fused_computation.220 | convolution fusion | flops 5905580032 | bytes 12845056 | tf_op jit(solution)/shard_map/dot_general | solution.py:23
  466.5 9.6 %fusion.40 = bf16[1024,2048]{1,0:T(8,128)(2,1)S(1)} fusion(bf16[1024,1408]{1,0:T(8,128)(2,1)} %get-tuple-element.27, bf16[1408,2048]{1,0:T(8,128)(2,1)} %all-gather.11.cloned.1.call-done), kind=kOutput, calls=%fused_computation.213 | convolution fusion | flops 5905580032 | bytes 12845056 | tf_op jit(solution)/shard_map/dot_general | solution.py:23
  479.5 3.7 fusion.42
  493.0 9.0 %collective-permute-done.49 = bf16[128,2048]{1,0:T(8,128)(2,1)S(1)} collective-permute-done((bf16[128,2048]{1,0:T(8,128)(2,1)S(1)}, bf16[128,2048]{1,0:T(8,128)(2,1)S(1)}, u32[]{:S(2)}, u32[]{:S(2)}) %collective-permute-start.49) | collective-permute-done | bytes 524320 | tf_op jit(solution)/shard_map/ppermute | solution.py:217
  502.5 10.7 %collective-permute-done.24 = bf16[128,2048]{1,0:T(8,128)(2,1)S(1)} collective-permute-done((bf16[128,2048]{1,0:T(8,128)(2,1)S(1)}, bf16[128,2048]{1,0:T(8,128)(2,1)S(1)}, u32[]{:S(2)}, u32[]{:S(2)}) %collective-permute-start.24) | collective-permute-done | bytes 524320 | tf_op jit(solution)/shard_map/ppermute | solution.py:217
  517.2 7.2 %collective-permute-done.48 = bf16[128,2048]{1,0:T(8,128)(2,1)S(1)} collective-permute-done((bf16[128,2048]{1,0:T(8,128)(2,1)S(1)}, bf16[128,2048]{1,0:T(8,128)(2,1)S(1)}, u32[]{:S(2)}, u32[]{:S(2)}) %collective-permute-start.48) | collective-permute-done | bytes 524320 | tf_op jit(solution)/shard_map/ppermute | solution.py:217
  525.9 9.0 %collective-permute-done.52 = bf16[128,2048]{1,0:T(8,128)(2,1)S(1)} collective-permute-done((bf16[128,2048]{1,0:T(8,128)(2,1)S(1)}, bf16[128,2048]{1,0:T(8,128)(2,1)S(1)}, u32[]{:S(2)}, u32[]{:S(2)}) %collective-permute-start.52) | collective-permute-done | bytes 524320 | tf_op jit(solution)/shard_map/ppermute | solution.py:217
  534.9 11.1 %collective-permute-done.50 = bf16[128,2048]{1,0:T(8,128)(2,1)S(1)} collective-permute-done((bf16[128,2048]{1,0:T(8,128)(2,1)S(1)}, bf16[128,2048]{1,0:T(8,128)(2,1)S(1)}, u32[]{:S(2)}, u32[]{:S(2)}) %collective-permute-start.50) | collective-permute-done | bytes 524320 | tf_op jit(solution)/shard_map/ppermute | solution.py:217
  552.2 4.6 collective-permute-done.53
  573.5 6.5 fusion.11
  590.0 41.2 %reduce-scatter.12.cloned.1.call-done = bf16[256,1408]{1,0:T(8,128)(2,1)} async-done(((bf16[2048,1408]{1,0:T(8,128)(2,1)}), bf16[256,1408]{1,0:T(8,128)(2,1)}) %reduce-scatter.12.cloned.1.call-update) | async-done | bytes 720912 | tf_op jit(solution)/shard_map/reduce_scatter | solution.py:265
  635.4 61.4 %reduce-scatter.14.cloned.1.call-done = bf16[176,2048]{1,0:T(8,128)(2,1)} async-done(((bf16[1408,2048]{1,0:T(8,128)(2,1)}), bf16[176,2048]{1,0:T(8,128)(2,1)}) %reduce-scatter.14.cloned.1.call-update) | async-done | bytes 720912 | tf_op jit(solution)/shard_map/reduce_scatter | solution.py:265
  701.1 3.5 collective-permute-done.60
  (334 shorter events, 193.6 us)
Async XLA Ops:
  7.2 73.3 %all-gather.5.cloned.1.call-start = ((), (), s32[]{:S(2)}) async-start(), calls=%async_computation.5 | async-start | bytes 2949120 | tf_op jit(solution)/shard_map/all_gather | solution.py:262
  21.2 91.4 %all-gather.7.cloned.1.call-start = ((), (), s32[]{:S(2)}) async-start(), calls=%async_computation.6 | async-start | bytes 2359296 | tf_op jit(solution)/shard_map/all_gather | solution.py:262
  21.9 207.6 %all-gather.11.cloned.1.call-start = ((), (), s32[]{:S(2)}) async-start(), calls=%async_computation.8 | async-start | bytes 6488064 | tf_op jit(solution)/shard_map/all_gather | solution.py:262
  22.7 232.2 %all-gather.9.cloned.1.call-start = ((), (), s32[]{:S(2)}) async-start(), calls=%async_computation.7 | async-start | bytes 12976128 | tf_op jit(solution)/shard_map/all_gather | solution.py:262
  41.8 527.1 %reduce-scatter.6.cloned.1.call-start = ((), (), s32[]{:S(2)}) async-start(), calls=%async_computation.9 | async-start | bytes 2949120 | tf_op jit(solution)/shard_map/reduce_scatter | solution.py:265
  44.1 30.3 %collective-permute-start.5 = (bf16[128,2048]{0,1:T(8,128)(2,1)}, bf16[128,2048]{0,1:T(8,128)(2,1)}, u32[]{:S(2)}, u32[]{:S(2)}) collective-permute-start(bf16[128,2048]{0,1:T(8,128)(2,1)} %bitcast.11), channel_id=1, source_target_pairs={{0,16},{8,24},{16,0},{24,8},{1,17},{9,25},{17,1},{25,9},{2,18},{10... | collective-permute-start | bytes 1572872 | tf_op jit(solution)/shard_map/ppermute | solution.py:217
  46.6 23.8 %collective-permute-start.6 = (bf16[128,2048]{0,1:T(8,128)(2,1)}, bf16[128,2048]{0,1:T(8,128)(2,1)S(1)}, u32[]{:S(2)}, u32[]{:S(2)}) collective-permute-start(bf16[128,2048]{0,1:T(8,128)(2,1)} %bitcast.12), channel_id=1, source_target_pairs={{0,16},{8,24},{16,0},{24,8},{1,17},{9,25},{17,1},{25,9},{2,18},{10... | collective-permute-start | bytes 1572872 | tf_op jit(solution)/shard_map/ppermute | solution.py:217
  48.2 25.4 %collective-permute-start.4 = (bf16[128,2048]{0,1:T(8,128)(2,1)}, bf16[128,2048]{0,1:T(8,128)(2,1)S(1)}, u32[]{:S(2)}, u32[]{:S(2)}) collective-permute-start(bf16[128,2048]{0,1:T(8,128)(2,1)} %bitcast.12), channel_id=1, source_target_pairs={{0,8},{8,0},{16,24},{24,16},{1,9},{9,1},{17,25},{25,17},{2,10},{10... | collective-permute-start | bytes 1572872 | tf_op jit(solution)/shard_map/ppermute | solution.py:217
  60.2 17.1 %collective-permute-start.7 = (bf16[128,2048]{0,1:T(8,128)(2,1)}, bf16[128,2048]{0,1:T(8,128)(2,1)S(1)}, u32[]{:S(2)}, u32[]{:S(2)}) collective-permute-start(bf16[128,2048]{0,1:T(8,128)(2,1)} %collective-permute-done.3), channel_id=1, source_target_pairs={{0,16},{8,24},{16,0},{24,8},{1,17},{9,25},{17,1},{25,9},{2,18},{10... | collective-permute-start | bytes 1572872 | tf_op jit(solution)/shard_map/ppermute | solution.py:217
  118.7 29.6 %collective-permute-start.33 = (bf16[128,2048]{1,0:T(8,128)(2,1)S(1)}, bf16[128,2048]{1,0:T(8,128)(2,1)}, u32[]{:S(2)}, u32[]{:S(2)}) collective-permute-start(bf16[128,2048]{1,0:T(8,128)(2,1)S(1)} %get-tuple-element.64), channel_id=1, source_target_pairs={{0,16},{8,24},{16,0},{24,8},{1,17},{9,25},{17,1},{25,9},{2,18},{10... | collective-permute-start | bytes 1572872 | tf_op jit(solution)/shard_map/ppermute | solution.py:217
  119.8 27.4 %collective-permute-start.31 = (bf16[128,2048]{1,0:T(8,128)(2,1)S(1)}, bf16[128,2048]{1,0:T(8,128)(2,1)S(1)}, u32[]{:S(2)}, u32[]{:S(2)}) collective-permute-start(bf16[128,2048]{1,0:T(8,128)(2,1)S(1)} %get-tuple-element.64), channel_id=1, source_target_pairs={{0,8},{8,0},{16,24},{24,16},{1,9},{9,1},{17,25},{25,17},{2,10},{10... | collective-permute-start | bytes 1572872 | tf_op jit(solution)/shard_map/ppermute | solution.py:217
  121.0 24.9 %collective-permute-start.30 = (bf16[128,2048]{1,0:T(8,128)(2,1)S(1)}, bf16[128,2048]{1,0:T(8,128)(2,1)S(1)}, u32[]{:S(2)}, u32[]{:S(2)}) collective-permute-start(bf16[128,2048]{1,0:T(8,128)(2,1)S(1)} %get-tuple-element.65), channel_id=1, source_target_pairs={{0,8},{8,0},{16,24},{24,16},{1,9},{9,1},{17,25},{25,17},{2,10},{10... | collective-permute-start | bytes 1572872 | tf_op jit(solution)/shard_map/ppermute | solution.py:217
  121.9 33.1 %collective-permute-start.9 = (bf16[128,2048]{1,0:T(8,128)(2,1)S(1)}, bf16[128,2048]{1,0:T(8,128)(2,1)S(1)}, u32[]{:S(2)}, u32[]{:S(2)}) collective-permute-start(bf16[128,2048]{1,0:T(8,128)(2,1)S(1)} %get-tuple-element.48), channel_id=1, source_target_pairs={{0,16},{8,24},{16,0},{24,8},{1,17},{9,25},{17,1},{25,9},{2,18},{10... | collective-permute-start | bytes 1572872 | tf_op jit(solution)/shard_map/ppermute | solution.py:217
  132.5 24.7 %collective-permute-start.13 = (bf16[128,2048]{1,0:T(8,128)(2,1)S(1)}, bf16[128,2048]{1,0:T(8,128)(2,1)S(1)}, u32[]{:S(2)}, u32[]{:S(2)}) collective-permute-start(bf16[128,2048]{1,0:T(8,128)(2,1)S(1)} %get-tuple-element.49), channel_id=1, source_target_pairs={{0,8},{8,0},{16,24},{24,16},{1,9},{9,1},{17,25},{25,17},{2,10},{10... | collective-permute-start | bytes 1572872 | tf_op jit(solution)/shard_map/ppermute | solution.py:217
  145.9 22.5 %collective-permute-start.11 = (bf16[128,2048]{1,0:T(8,128)(2,1)S(1)}, bf16[128,2048]{1,0:T(8,128)(2,1)S(1)}, u32[]{:S(2)}, u32[]{:S(2)}) collective-permute-start(bf16[128,2048]{1,0:T(8,128)(2,1)S(1)} %add_convert_fusion.8), channel_id=1, source_target_pairs={{0,8},{8,0},{16,24},{24,16},{1,9},{9,1},{17,25},{25,17},{2,10},{10... | collective-permute-start | bytes 1572872 | tf_op jit(solution)/shard_map/ppermute | solution.py:217
  147.2 23.7 %collective-permute-start.32 = (bf16[128,2048]{1,0:T(8,128)(2,1)S(1)}, bf16[128,2048]{1,0:T(8,128)(2,1)S(1)}, u32[]{:S(2)}, u32[]{:S(2)}) collective-permute-start(bf16[128,2048]{1,0:T(8,128)(2,1)S(1)} %get-tuple-element.65), channel_id=1, source_target_pairs={{0,16},{8,24},{16,0},{24,8},{1,17},{9,25},{17,1},{25,9},{2,18},{10... | collective-permute-start | bytes 1572872 | tf_op jit(solution)/shard_map/ppermute | solution.py:217
  148.3 28.6 %collective-permute-start.34 = (bf16[128,2048]{1,0:T(8,128)(2,1)S(1)}, bf16[128,2048]{1,0:T(8,128)(2,1)S(1)}, u32[]{:S(2)}, u32[]{:S(2)}) collective-permute-start(bf16[128,2048]{1,0:T(8,128)(2,1)S(1)} %collective-permute-done.30), channel_id=1, source_target_pairs={{0,16},{8,24},{16,0},{24,8},{1,17},{9,25},{17,1},{25,9},{2,18},{10... | collective-permute-start | bytes 1572872 | tf_op jit(solution)/shard_map/ppermute | solution.py:217
  155.0 42.5 %collective-permute-start.35 = (bf16[128,2048]{1,0:T(8,128)(2,1)}, bf16[128,2048]{1,0:T(8,128)(2,1)}, u32[]{:S(2)}, u32[]{:S(2)}) collective-permute-start(bf16[128,2048]{1,0:T(8,128)(2,1)} %collective-permute-done.33), channel_id=1, source_target_pairs={{0,8},{8,0},{16,24},{24,16},{1,9},{9,1},{17,25},{25,17},{2,10},{10... | collective-permute-start | bytes 1572872 | tf_op jit(solution)/shard_map/ppermute | solution.py:217
  157.2 28.1 %collective-permute-start.12 = (bf16[128,2048]{1,0:T(8,128)(2,1)}, bf16[128,2048]{1,0:T(8,128)(2,1)}, u32[]{:S(2)}, u32[]{:S(2)}) collective-permute-start(bf16[128,2048]{1,0:T(8,128)(2,1)} %get-tuple-element.50), channel_id=1, source_target_pairs={{0,8},{8,0},{16,24},{24,16},{1,9},{9,1},{17,25},{25,17},{2,10},{10... | collective-permute-start | bytes 1572872 | tf_op jit(solution)/shard_map/ppermute | solution.py:217
  199.4 22.7 %collective-permute-start.17 = (bf16[128,2048]{0,1:T(8,128)(2,1)S(1)}, bf16[128,2048]{0,1:T(8,128)(2,1)S(1)}, u32[]{:S(2)}, u32[]{:S(2)}) collective-permute-start(bf16[128,2048]{0,1:T(8,128)(2,1)S(1)} %bitcast.181), channel_id=1, source_target_pairs={{0,16},{8,24},{16,0},{24,8},{1,17},{9,25},{17,1},{25,9},{2,18},{10... | collective-permute-start | bytes 1572872 | tf_op jit(solution)/shard_map/ppermute | solution.py:217
  200.7 19.9 %collective-permute-start.16 = (bf16[128,2048]{0,1:T(8,128)(2,1)S(1)}, bf16[128,2048]{0,1:T(8,128)(2,1)S(1)}, u32[]{:S(2)}, u32[]{:S(2)}) collective-permute-start(bf16[128,2048]{0,1:T(8,128)(2,1)S(1)} %bitcast.184), channel_id=1, source_target_pairs={{0,8},{8,0},{16,24},{24,16},{1,9},{9,1},{17,25},{25,17},{2,10},{10... | collective-permute-start | bytes 1572872 | tf_op jit(solution)/shard_map/ppermute | solution.py:217
  209.9 17.8 %collective-permute-start.19 = (bf16[128,2048]{0,1:T(8,128)(2,1)S(1)}, bf16[128,2048]{0,1:T(8,128)(2,1)S(1)}, u32[]{:S(2)}, u32[]{:S(2)}) collective-permute-start(bf16[128,2048]{0,1:T(8,128)(2,1)S(1)} %collective-permute-done.15), channel_id=1, source_target_pairs={{0,16},{8,24},{16,0},{24,8},{1,17},{9,25},{17,1},{25,9},{2,18},{10... | collective-permute-start | bytes 1572872 | tf_op jit(solution)/shard_map/ppermute | solution.py:217
  211.7 17.0 %collective-permute-start.20 = (bf16[128,2048]{0,1:T(8,128)(2,1)S(1)}, bf16[128,2048]{0,1:T(8,128)(2,1)S(1)}, u32[]{:S(2)}, u32[]{:S(2)}) collective-permute-start(bf16[128,2048]{0,1:T(8,128)(2,1)S(1)} %collective-permute-done.18), channel_id=1, source_target_pairs={{0,8},{8,0},{16,24},{24,16},{1,9},{9,1},{17,25},{25,17},{2,10},{10... | collective-permute-start | bytes 1572872 | tf_op jit(solution)/shard_map/ppermute | solution.py:217
  305.1 23.8 %collective-permute-start.36 = (bf16[128,2048]{1,0:T(8,128)(2,1)S(1)}, bf16[128,2048]{1,0:T(8,128)(2,1)S(1)}, u32[]{:S(2)}, u32[]{:S(2)}) collective-permute-start(bf16[128,2048]{1,0:T(8,128)(2,1)S(1)} %get-tuple-element.36), channel_id=1, source_target_pairs={{0,16},{8,24},{16,0},{24,8},{1,17},{9,25},{17,1},{25,9},{2,18},{10... | collective-permute-start | bytes 1572872 | tf_op jit(solution)/shard_map/ppermute | solution.py:217
  305.6 23.3 %collective-permute-start.40 = (bf16[128,2048]{1,0:T(8,128)(2,1)S(1)}, bf16[128,2048]{1,0:T(8,128)(2,1)S(1)}, u32[]{:S(2)}, u32[]{:S(2)}) collective-permute-start(bf16[128,2048]{1,0:T(8,128)(2,1)S(1)} %get-tuple-element.37), channel_id=1, source_target_pairs={{0,8},{8,0},{16,24},{24,16},{1,9},{9,1},{17,25},{25,17},{2,10},{10... | collective-permute-start | bytes 1572872 | tf_op jit(solution)/shard_map/ppermute | solution.py:217
  320.0 22.3 %collective-permute-start.39 = (bf16[128,2048]{1,0:T(8,128)(2,1)S(1)}, bf16[128,2048]{1,0:T(8,128)(2,1)S(1)}, u32[]{:S(2)}, u32[]{:S(2)}) collective-permute-start(bf16[128,2048]{1,0:T(8,128)(2,1)S(1)} %get-tuple-element.38), channel_id=1, source_target_pairs={{0,8},{8,0},{16,24},{24,16},{1,9},{9,1},{17,25},{25,17},{2,10},{10... | collective-permute-start | bytes 1572872 | tf_op jit(solution)/shard_map/ppermute | solution.py:217
  362.1 24.6 %collective-permute-start.43 = (bf16[128,2048]{1,0:T(8,128)(2,1)S(1)}, bf16[128,2048]{1,0:T(8,128)(2,1)S(1)}, u32[]{:S(2)}, u32[]{:S(2)}) collective-permute-start(bf16[128,2048]{1,0:T(8,128)(2,1)S(1)} %get-tuple-element.62), channel_id=1, source_target_pairs={{0,8},{8,0},{16,24},{24,16},{1,9},{9,1},{17,25},{25,17},{2,10},{10... | collective-permute-start | bytes 1572872 | tf_op jit(solution)/shard_map/ppermute | solution.py:217
  362.6 24.1 %collective-permute-start.44 = (bf16[128,2048]{1,0:T(8,128)(2,1)S(1)}, bf16[128,2048]{1,0:T(8,128)(2,1)S(1)}, u32[]{:S(2)}, u32[]{:S(2)}) collective-permute-start(bf16[128,2048]{1,0:T(8,128)(2,1)S(1)} %get-tuple-element.63), channel_id=1, source_target_pairs={{0,16},{8,24},{16,0},{24,8},{1,17},{9,25},{17,1},{25,9},{2,18},{10... | collective-permute-start | bytes 1572872 | tf_op jit(solution)/shard_map/ppermute | solution.py:217
  373.9 19.6 %collective-permute-start.47 = (bf16[128,2048]{1,0:T(8,128)(2,1)S(1)}, bf16[128,2048]{1,0:T(8,128)(2,1)S(1)}, u32[]{:S(2)}, u32[]{:S(2)}) collective-permute-start(bf16[128,2048]{1,0:T(8,128)(2,1)S(1)} %collective-permute-done.45), channel_id=1, source_target_pairs={{0,8},{8,0},{16,24},{24,16},{1,9},{9,1},{17,25},{25,17},{2,10},{10... | collective-permute-start | bytes 1572872 | tf_op jit(solution)/shard_map/ppermute | solution.py:217
  427.7 152.3 %reduce-scatter.8.cloned.1.call-start = ((), (), s32[]{:S(2)}) async-start(), calls=%async_computation.10 | async-start | bytes 2359296 | tf_op jit(solution)/shard_map/reduce_scatter | solution.py:265
  433.9 151.3 %reduce-scatter.10.cloned.1.call-start = ((), (), s32[]{:S(2)}) async-start(), calls=%async_computation.11 | async-start | bytes 6488064 | tf_op jit(solution)/shard_map/reduce_scatter | solution.py:265
  444.8 186.4 %reduce-scatter.12.cloned.1.call-start = ((), (), s32[]{:S(2)}) async-start(), calls=%async_computation.12 | async-start | bytes 6488064 | tf_op jit(solution)/shard_map/reduce_scatter | solution.py:265
  455.9 240.9 %reduce-scatter.14.cloned.1.call-start = ((), (), s32[]{:S(2)}) async-start(), calls=%async_computation.13 | async-start | bytes 6488064 | tf_op jit(solution)/shard_map/reduce_scatter | solution.py:265
  484.3 17.6 %collective-permute-start.49 = (bf16[128,2048]{1,0:T(8,128)(2,1)S(1)}, bf16[128,2048]{1,0:T(8,128)(2,1)S(1)}, u32[]{:S(2)}, u32[]{:S(2)}) collective-permute-start(bf16[128,2048]{1,0:T(8,128)(2,1)S(1)} %get-tuple-element.33), channel_id=1, source_target_pairs={{0,16},{8,24},{16,0},{24,8},{1,17},{9,25},{17,1},{25,9},{2,18},{10... | collective-permute-start | bytes 1572872 | tf_op jit(solution)/shard_map/ppermute | solution.py:217
  484.8 28.4 %collective-permute-start.24 = (bf16[128,2048]{1,0:T(8,128)(2,1)S(1)}, bf16[128,2048]{1,0:T(8,128)(2,1)S(1)}, u32[]{:S(2)}, u32[]{:S(2)}) collective-permute-start(bf16[128,2048]{1,0:T(8,128)(2,1)S(1)} %get-tuple-element.42), channel_id=1, source_target_pairs={{0,16},{8,24},{16,0},{24,8},{1,17},{9,25},{17,1},{25,9},{2,18},{10... | collective-permute-start | bytes 1572872 | tf_op jit(solution)/shard_map/ppermute | solution.py:217
  486.4 28.3 %collective-permute-start.28 = (bf16[128,2048]{1,0:T(8,128)(2,1)S(1)}, bf16[128,2048]{1,0:T(8,128)(2,1)S(1)}, u32[]{:S(2)}, u32[]{:S(2)}) collective-permute-start(bf16[128,2048]{1,0:T(8,128)(2,1)S(1)} %get-tuple-element.43), channel_id=1, source_target_pairs={{0,8},{8,0},{16,24},{24,16},{1,9},{9,1},{17,25},{25,17},{2,10},{10... | collective-permute-start | bytes 1572872 | tf_op jit(solution)/shard_map/ppermute | solution.py:217
  490.9 24.3 %collective-permute-start.26 = (bf16[128,2048]{1,0:T(8,128)(2,1)S(1)}, bf16[128,2048]{1,0:T(8,128)(2,1)S(1)}, u32[]{:S(2)}, u32[]{:S(2)}) collective-permute-start(bf16[128,2048]{1,0:T(8,128)(2,1)S(1)} %add_convert_fusion.6), channel_id=1, source_target_pairs={{0,8},{8,0},{16,24},{24,16},{1,9},{9,1},{17,25},{25,17},{2,10},{10... | collective-permute-start | bytes 1572872 | tf_op jit(solution)/shard_map/ppermute | solution.py:217
  492.4 57.2 %collective-permute-start.27 = (bf16[128,2048]{1,0:T(8,128)(2,1)}, bf16[128,2048]{1,0:T(8,128)(2,1)}, u32[]{:S(2)}, u32[]{:S(2)}) collective-permute-start(bf16[128,2048]{1,0:T(8,128)(2,1)} %get-tuple-element.44), channel_id=1, source_target_pairs={{0,8},{8,0},{16,24},{24,16},{1,9},{9,1},{17,25},{25,17},{2,10},{10... | collective-permute-start | bytes 1572872 | tf_op jit(solution)/shard_map/ppermute | solution.py:217
  501.9 22.5 %collective-permute-start.48 = (bf16[128,2048]{1,0:T(8,128)(2,1)S(1)}, bf16[128,2048]{1,0:T(8,128)(2,1)S(1)}, u32[]{:S(2)}, u32[]{:S(2)}) collective-permute-start(bf16[128,2048]{1,0:T(8,128)(2,1)S(1)} %get-tuple-element.30), channel_id=1, source_target_pairs={{0,16},{8,24},{16,0},{24,8},{1,17},{9,25},{17,1},{25,9},{2,18},{10... | collective-permute-start | bytes 1572872 | tf_op jit(solution)/shard_map/ppermute | solution.py:217
  513.2 21.8 %collective-permute-start.52 = (bf16[128,2048]{1,0:T(8,128)(2,1)S(1)}, bf16[128,2048]{1,0:T(8,128)(2,1)S(1)}, u32[]{:S(2)}, u32[]{:S(2)}) collective-permute-start(bf16[128,2048]{1,0:T(8,128)(2,1)S(1)} %get-tuple-element.31), channel_id=1, source_target_pairs={{0,8},{8,0},{16,24},{24,16},{1,9},{9,1},{17,25},{25,17},{2,10},{10... | collective-permute-start | bytes 1572872 | tf_op jit(solution)/shard_map/ppermute | solution.py:217
  514.7 31.4 %collective-permute-start.50 = (bf16[128,2048]{1,0:T(8,128)(2,1)S(1)}, bf16[128,2048]{1,0:T(8,128)(2,1)S(1)}, u32[]{:S(2)}, u32[]{:S(2)}) collective-permute-start(bf16[128,2048]{1,0:T(8,128)(2,1)S(1)} %add_convert_fusion.2), channel_id=1, source_target_pairs={{0,8},{8,0},{16,24},{24,16},{1,9},{9,1},{17,25},{25,17},{2,10},{10... | collective-permute-start | bytes 1572872 | tf_op jit(solution)/shard_map/ppermute | solution.py:217
  516.8 32.8 %collective-permute-start.29 = (bf16[128,2048]{1,0:T(8,128)(2,1)}, bf16[128,2048]{1,0:T(8,128)(2,1)}, u32[]{:S(2)}, u32[]{:S(2)}) collective-permute-start(bf16[128,2048]{1,0:T(8,128)(2,1)} %get-tuple-element.41), channel_id=1, source_target_pairs={{0,16},{8,24},{16,0},{24,8},{1,17},{9,25},{17,1},{25,9},{2,18},{10... | collective-permute-start | bytes 1572872 | tf_op jit(solution)/shard_map/ppermute | solution.py:217
  524.4 27.8 %collective-permute-start.51 = (bf16[128,2048]{1,0:T(8,128)(2,1)}, bf16[128,2048]{1,0:T(8,128)(2,1)}, u32[]{:S(2)}, u32[]{:S(2)}) collective-permute-start(bf16[128,2048]{1,0:T(8,128)(2,1)} %get-tuple-element.32), channel_id=1, source_target_pairs={{0,8},{8,0},{16,24},{24,16},{1,9},{9,1},{17,25},{25,17},{2,10},{10... | collective-permute-start | bytes 1572872 | tf_op jit(solution)/shard_map/ppermute | solution.py:217
  586.4 112.7 %collective-permute-start.59 = (bf16[64,1408]{1,0:T(8,128)(2,1)S(1)}, bf16[64,1408]{1,0:T(8,128)(2,1)S(1)}, u32[]{:S(2)}, u32[]{:S(2)}) collective-permute-start(bf16[64,1408]{1,0:T(8,128)(2,1)S(1)} %get-tuple-element.83), channel_id=1, source_target_pairs={{0,24},{8,16},{16,8},{24,0},{1,25},{9,17},{17,9},{25,1},{2,26},{10... | collective-permute-start | bytes 540680 | tf_op jit(solution)/shard_map/ppermute | solution.py:217
  588.0 112.6 %collective-permute-start.58 = (bf16[64,1408]{1,0:T(8,128)(2,1)S(1)}, bf16[64,1408]{1,0:T(8,128)(2,1)S(1)}, u32[]{:S(2)}, u32[]{:S(2)}) collective-permute-start(bf16[64,1408]{1,0:T(8,128)(2,1)S(1)} %get-tuple-element.84), channel_id=1, source_target_pairs={{0,16},{8,24},{16,0},{24,8},{1,17},{9,25},{17,1},{25,9},{2,18},{10... | collective-permute-start | bytes 540680 | tf_op jit(solution)/shard_map/ppermute | solution.py:217
  589.4 111.2 %collective-permute-start.57 = (bf16[64,1408]{1,0:T(8,128)(2,1)S(1)}, bf16[64,1408]{1,0:T(8,128)(2,1)S(1)}, u32[]{:S(2)}, u32[]{:S(2)}) collective-permute-start(bf16[64,1408]{1,0:T(8,128)(2,1)S(1)} %get-tuple-element.85), channel_id=1, source_target_pairs={{0,8},{8,0},{16,24},{24,16},{1,9},{9,1},{17,25},{25,17},{2,10},{10... | collective-permute-start | bytes 540680 | tf_op jit(solution)/shard_map/ppermute | solution.py:217
  632.5 68.7 %collective-permute-start.62 = (bf16[64,1408]{1,0:T(8,128)(2,1)S(1)}, bf16[64,1408]{1,0:T(8,128)(2,1)S(1)}, u32[]{:S(2)}, u32[]{:S(2)}) collective-permute-start(bf16[64,1408]{1,0:T(8,128)(2,1)S(1)} %get-tuple-element.75), channel_id=1, source_target_pairs={{0,24},{8,16},{16,8},{24,0},{1,25},{9,17},{17,9},{25,1},{2,26},{10... | collective-permute-start | bytes 540680 | tf_op jit(solution)/shard_map/ppermute | solution.py:217
  634.9 66.2 %collective-permute-start.61 = (bf16[64,1408]{1,0:T(8,128)(2,1)S(1)}, bf16[64,1408]{1,0:T(8,128)(2,1)S(1)}, u32[]{:S(2)}, u32[]{:S(2)}) collective-permute-start(bf16[64,1408]{1,0:T(8,128)(2,1)S(1)} %get-tuple-element.76), channel_id=1, source_target_pairs={{0,16},{8,24},{16,0},{24,8},{1,17},{9,25},{17,1},{25,9},{2,18},{10... | collective-permute-start | bytes 540680 | tf_op jit(solution)/shard_map/ppermute | solution.py:217
  (60 other events, 690.2 us)
Sparse Core Ops, SparseCore 0:
  21.3 33.2 all-gather.4
  56.2 28.0 all-gather.6
  86.0 59.9 all-gather.10
  148.0 106.7 all-gather.8
  427.9 34.9 reduce-scatter.5
  465.0 34.6 reduce-scatter.7
  502.1 63.5 reduce-scatter.9
  568.0 63.2 reduce-scatter.11
  633.5 63.2 reduce-scatter.13

commit v2 on v1

v2 whole, which is shorter than its diff:
```python
import functools
import math

import jax
import jax.numpy as jnp
from jax import lax
from jax.experimental import pallas as pl
from jax.experimental.pallas import tpu as pltpu
from jax.sharding import PartitionSpec as P

HEADS = 32
KV_HEADS = 4
HEAD_DIM = 64
HALF = HEAD_DIM // 2
GROUP = HEADS // KV_HEADS
EPSILON = 1e-05
SCALE = 1.0 / math.sqrt(HEAD_DIM)
LOW = jnp.bfloat16
FULL = jnp.float32
VMEM = pl.BlockSpec(memory_space=pltpu.VMEM)
ANY = pl.BlockSpec(memory_space=pltpu.HBM)
SMEM = pl.BlockSpec(memory_space=pltpu.SMEM)
PARAMS = pltpu.CompilerParams(vmem_limit_bytes=60 << 20)
NN, NT, TN = ((1,), (0,)), ((1,), (1,)), ((0,), (0,))


def dot(a, b, dims=NN):
    return lax.dot_general(a, b, (dims, ((), ())), preferred_element_type=FULL)


def like(shape, dtype=LOW):
    return jax.ShapeDtypeStruct(shape, dtype)


def rope_tables(where_at):
    frequency = 1.0 / 10000.0 ** (jnp.arange(HALF, dtype=FULL) * 2.0 / HEAD_DIM)
    angles = frequency[:, None] * where_at.astype(FULL)[None, :]
    return jnp.cos(angles), jnp.sin(angles)


def regroup(x, outer, inner, rows):
    return jnp.concatenate(
        [x[:, (o * inner + i) * rows:(o * inner + i + 1) * rows] for i in range(inner) for o in range(outer)], 1
    )


def join(pieces, whole_ref):
    at = 0
    for piece in pieces:
        whole_ref[at:at + piece.shape[0], :] = piece[...]
        at += piece.shape[0]


def fetch(pieces, whole_ref, sems):
    copies, at = [], 0
    for i, piece in enumerate(pieces):
        rows = piece.shape[0]
        copies.append(pltpu.make_async_copy(piece, whole_ref.at[pl.ds(at, rows)], sems.at[i]))
        at += rows
    for copy in copies:
        copy.start()
    for copy in copies:
        copy.wait()


def arrivals(count):
    return pltpu.SemaphoreType.DMA((count,))


def call_own(kernel, out_shape, *args):
    return pl.pallas_call(
        kernel, out_shape=out_shape, in_specs=[VMEM] * len(args),
        out_specs=jax.tree.map(lambda _: VMEM, out_shape), compiler_params=PARAMS, name=kernel.func.__name__,
    )(*args)


def added(refs):
    total = refs[0][...].astype(FULL)
    for ref in refs[1:]:
        total = total + ref[...].astype(FULL)
    return total


def regroup_kernel(grid, x_ref, *out_refs):
    x = regroup(x_ref[...].astype(FULL), *grid).astype(LOW)
    rows = out_refs[0].shape[0]
    for i, ref in enumerate(out_refs):
        ref[...] = x[i * rows:(i + 1) * rows]


def middle_kernel(grid, parts, *refs):
    tokens_ref, refs = refs[0], refs[1:]
    per = (len(refs) - 2 - parts) // parts
    middle_ref, inv_ref, *normed_refs = refs[per * parts:]
    rows = normed_refs[0].shape[0]
    for i in range(parts):
        at = slice(i * rows, (i + 1) * rows)
        middle = tokens_ref[at, :].astype(FULL) + added(refs[i * per:(i + 1) * per])
        inv = lax.rsqrt(jnp.mean(middle * middle, -1, keepdims=True) + EPSILON)
        middle_ref[at, :] = middle
        inv_ref[at, :] = inv
        normed_refs[i][...] = regroup(middle * inv, *grid).astype(LOW)


def grad_middle_kernel(grid, parts, *refs):
    upstream_ref, middle_ref, inv_ref, refs = refs[0], refs[1], refs[2], refs[3:]
    per = (len(refs) - 1 - parts) // parts
    out_ref, *low_refs = refs[per * parts:]
    rows = low_refs[0].shape[0]
    for i in range(parts):
        at = slice(i * rows, (i + 1) * rows)
        inv = inv_ref[at, :]
        normed = middle_ref[at, :] * inv
        grad = regroup(added(refs[i * per:(i + 1) * per]), *grid)
        grad = upstream_ref[at, :].astype(FULL) + inv * (grad - normed * jnp.mean(grad * normed, -1, keepdims=True))
        out_ref[at, :] = grad
        low_refs[i][...] = grad.astype(LOW)


def grad_tokens_kernel(grid, parts, *refs):
    tokens_ref, grad_ref, refs, out_ref = refs[0], refs[1], refs[2:-1], refs[-1]
    per = len(refs) // parts
    rows = out_ref.shape[0] // parts
    for i in range(parts):
        at = slice(i * rows, (i + 1) * rows)
        tokens = tokens_ref[at, :].astype(FULL)
        normed = tokens * lax.rsqrt(jnp.mean(tokens * tokens, -1, keepdims=True) + EPSILON)
        grad = regroup(added(refs[i * per:(i + 1) * per]), *grid)
        out_ref[at, :] = grad_ref[at, :] + grad - normed * jnp.mean(grad * normed, -1, keepdims=True)


def block_out_kernel(parts, *refs):
    middle_ref, refs, out_ref = refs[0], refs[1:-1], refs[-1]
    per = len(refs) // parts
    rows = out_ref.shape[0] // parts
    for i in range(parts):
        at = slice(i * rows, (i + 1) * rows)
        out_ref[at, :] = (middle_ref[at, :] + added(refs[i * per:(i + 1) * per])).astype(LOW)


def rows_of(pieces):
    return sum(p.shape[0] for p in pieces)


def whole(shape):
    return pl.BlockSpec(shape, lambda i: (0,) * len(shape))


def columns(rows, width):
    return pl.BlockSpec((rows, width), lambda i: (0, i))


def by_rows(height, width):
    return pl.BlockSpec((height, width), lambda i: (i, 0))


def hidden_kernel(count, chunk, *refs):
    pieces, (weight_ref, slope_ref, hidden_ref, normed_ref, sems) = refs[:count], refs[count:]

    @pl.when(pl.program_id(0) == 0)
    def _():
        fetch(pieces, normed_ref, sems)

    both = dot(normed_ref[...], weight_ref[...])
    gate, up = both[:, :chunk], both[:, chunk:]
    sigmoid = jax.nn.sigmoid(gate)
    silu = gate * sigmoid
    slope = up * sigmoid * (1.0 + gate * (1.0 - sigmoid))
    slope_ref[...] = jnp.concatenate([slope, silu], 1).astype(LOW)
    hidden_ref[...] = (silu * up).T.astype(LOW)


def hidden_of(pieces, weight, chunk):
    tokens, (width, both) = rows_of(pieces), weight.shape
    return pl.pallas_call(
        functools.partial(hidden_kernel, len(pieces), chunk),
        grid=(both // (2 * chunk),),
        in_specs=[ANY] * len(pieces) + [columns(width, 2 * chunk)],
        out_specs=(columns(tokens, 2 * chunk), by_rows(chunk, tokens)),
        out_shape=(like((tokens, both)), like((both // 2, tokens))),
        scratch_shapes=[pltpu.VMEM((tokens, width), LOW), arrivals(len(pieces))],
        compiler_params=PARAMS,
        name="hidden_of",
    )(*pieces, weight)


def grad_down_kernel(count, *refs):
    pieces, (hidden_ref, out_ref, block_ref) = refs[:count], refs[count:]
    join(pieces, block_ref)
    out_ref[...] = dot(hidden_ref[...], block_ref[...]).astype(LOW)


def grad_down_of(hidden, pieces, block=256):
    tokens, width = rows_of(pieces), pieces[0].shape[1]
    return pl.pallas_call(
        functools.partial(grad_down_kernel, len(pieces)),
        grid=(width // block,),
        in_specs=[columns(p.shape[0], block) for p in pieces] + [whole(hidden.shape)],
        out_specs=columns(hidden.shape[0], block),
        out_shape=like((hidden.shape[0], width)),
        scratch_shapes=[pltpu.VMEM((tokens, block), LOW)],
        compiler_params=PARAMS,
        name="grad_down_of",
    )(*pieces, hidden)


def grad_gate_up_kernel(count, chunk, places_ref, *refs):
    pieces, refs = refs[:count], refs[count:]
    *blocks, slope_ref, out_ref, down_ref, upstream_ref, sems, block_sems = refs
    step, steps = pl.program_id(0), pl.num_programs(0)

    @pl.when(step == 0)
    def _():
        copies = []
        for i, block in enumerate(blocks):
            rows = block.shape[0]
            there = pl.ds(pl.multiple_of(places_ref[i] * rows, math.gcd(rows, 16)), rows)
            copies.append(pltpu.make_async_copy(block, down_ref.at[there], block_sems.at[i]))
        for copy in copies:
            copy.start()
        fetch(pieces, upstream_ref, sems)
        for copy in copies:
            copy.wait()

    def work(chunks):
        rows = pl.ds(pl.multiple_of(step * 2 * chunk, 2 * chunk), chunks * chunk)
        grad = dot(upstream_ref[...], down_ref[rows, :], NT)
        each = [grad[:, c * chunk:(c + 1) * chunk] for c in range(chunks) for _ in range(2)]
        width = chunks * 2 * chunk
        out_ref[:, :width] = (jnp.concatenate(each, 1) * slope_ref[:, :width].astype(FULL)).astype(LOW)

    odd = down_ref.shape[0] // chunk % 2

    @pl.when(step < steps - odd)
    def _():
        work(2)

    if odd:

        @pl.when(step == steps - 1)
        def _():
            work(1)


def grad_gate_up_of(pieces, places, blocks, slope, chunk):
    tokens, width = rows_of(pieces), pieces[0].shape[1]
    depth = rows_of(blocks)
    return pl.pallas_call(
        functools.partial(grad_gate_up_kernel, len(pieces), chunk),
        grid=(pl.cdiv(depth, 2 * chunk),),
        in_specs=[SMEM] + [ANY] * (len(pieces) + len(blocks)) + [columns(tokens, 4 * chunk)],
        out_specs=(columns(tokens, 4 * chunk), whole((depth, width))),
        out_shape=(like(slope.shape), like((depth, width))),
        scratch_shapes=[pltpu.VMEM((tokens, width), LOW), arrivals(len(pieces)), arrivals(len(blocks))],
        compiler_params=PARAMS,
        name="grad_gate_up_of",
    )(places, *pieces, *blocks, slope)


def grad_rows_kernel(first, grad_ref, weight_ref, *out_refs):
    grad = dot(grad_ref[...], weight_ref[:, first:], NT).astype(LOW)
    rows = out_refs[0].shape[0]
    for i, ref in enumerate(out_refs):
        ref[...] = grad[i * rows:(i + 1) * rows]


def grad_rows_of(grad, weight, piece_rows, block=256):
    tokens, width = grad.shape[0], weight.shape[0]
    count = tokens // piece_rows
    return pl.pallas_call(
        functools.partial(grad_rows_kernel, weight.shape[1] - grad.shape[1]),
        grid=(width // block,),
        in_specs=[whole(grad.shape), by_rows(block, weight.shape[1])],
        out_specs=(columns(piece_rows, block),) * count,
        out_shape=(like((piece_rows, width)),) * count,
        compiler_params=PARAMS,
        name="grad_rows_of",
    )(grad, weight)


def grad_weight_kernel(count, *refs):
    pieces, (grad_ref, out_ref, block_ref) = refs[:count], refs[count:]
    join(pieces, block_ref)
    out_ref[...] = dot(block_ref[...], grad_ref[...], TN).astype(LOW)


def grad_weight_of(pieces, grad, block=256):
    tokens, width = rows_of(pieces), pieces[0].shape[1]
    return pl.pallas_call(
        functools.partial(grad_weight_kernel, len(pieces)),
        grid=(width // block,),
        in_specs=[columns(p.shape[0], block) for p in pieces] + [whole(grad.shape)],
        out_specs=by_rows(block, grad.shape[1]),
        out_shape=like((width, grad.shape[1])),
        scratch_shapes=[pltpu.VMEM((tokens, block), LOW)],
        compiler_params=PARAMS,
        name="grad_weight_of",
    )(*pieces, grad)


def rows_kernel(left_ref, weight_ref, *refs):
    *out_refs, turned_ref = refs

    @pl.when(pl.program_id(0) == 0)
    def _():
        turned_ref[...] = left_ref[...].T

    weight = weight_ref[...].reshape(turned_ref.shape[1], weight_ref.shape[-1])
    out = dot(turned_ref[...], weight).astype(LOW)
    rows = out_refs[0].shape[0]
    for i, ref in enumerate(out_refs):
        ref[...] = out[i * rows:(i + 1) * rows]


def rows_of_product(left, weight, piece_rows, inner=None, block=256):
    depth, tokens = left.shape
    count = tokens // piece_rows
    if inner is None:
        width, spec = weight.shape[1], columns(depth, block)
    else:
        seq_size, fsdp_size, own_rows = inner
        width = weight.shape[0]
        per = width // seq_size // block
        weight = weight.reshape(fsdp_size, seq_size, own_rows, -1)
        spec = pl.BlockSpec((fsdp_size, 1, own_rows, block), lambda i: (0, i // per, 0, i % per))
    return pl.pallas_call(
        rows_kernel,
        grid=(width // block,),
        in_specs=[whole(left.shape), spec],
        out_specs=(columns(piece_rows, block),) * count,
        out_shape=(like((piece_rows, width)),) * count,
        scratch_shapes=[pltpu.VMEM((tokens, depth), LOW)],
        compiler_params=PARAMS,
        name="rows_of_product",
    )(left, weight)


def attention_weights_kernel(count, inner, *refs):
    tokens, grads = refs[:count], refs[count:2 * count]
    grad_qkv_ref, attended_ref, out_ref, block_ref = refs[2 * count:]
    seq_size, fsdp_size, own_rows = inner
    step, block = pl.program_id(0), block_ref.shape[1]
    across = out_ref.shape[1] - grad_qkv_ref.shape[0]
    join(tokens, block_ref)
    there = pl.ds(pl.multiple_of(step * block, block), block)
    out_ref[there, across:] = dot(grad_qkv_ref[...], block_ref[...]).T.astype(LOW)
    join(grads, block_ref)
    got = dot(attended_ref[...], block_ref[...]).astype(LOW)
    part = step * block // across
    first = step * block % across
    for f in range(fsdp_size):
        rows = pl.ds(pl.multiple_of((f * seq_size + part) * own_rows, own_rows), own_rows)
        out_ref[rows, pl.ds(pl.multiple_of(first, 128), block)] = got[f * own_rows:(f + 1) * own_rows]


def attention_weights_of(tokens, grads, grad_qkv, attended, inner, block=256):
    count, width = len(tokens), tokens[0].shape[1]
    shape = (width, grad_qkv.shape[0] + width // inner[0])
    return pl.pallas_call(
        functools.partial(attention_weights_kernel, count, inner),
        grid=(width // block,),
        in_specs=[columns(p.shape[0], block) for p in (*tokens, *grads)]
        + [whole(grad_qkv.shape), whole(attended.shape)],
        out_specs=whole(shape),
        out_shape=like(shape),
        scratch_shapes=[pltpu.VMEM((rows_of(tokens), block), LOW)],
        compiler_params=PARAMS,
        name="attention_weights_of",
    )(*tokens, *grads, grad_qkv, attended)


def attend_kernel(heads, kvs, span, pieces, order_ref, rank_ref, *refs):
    token_refs, refs = refs[:pieces], refs[pieces:]
    weight_ref, cos_ref, sin_ref, qrot_ref, kv_ref, att_ref, mix_ref, lse_ref, inv_ref, *scratch = refs
    keys_ref, qkv_ref, tokens_ref, sems = scratch
    fetch(token_refs, tokens_ref, sems)
    count = cos_ref.shape[1] // span
    for at in range(0, tokens_ref.shape[0], span):
        there = slice(at, at + span)
        values = tokens_ref[there, :].astype(FULL)
        inv = lax.rsqrt(jnp.mean(values * values, -1, keepdims=True) + EPSILON)
        qkv_ref[:, there] = (dot(tokens_ref[there, :], weight_ref[:, -qkv_ref.shape[0]:]) * inv).T
        inv_ref[:, there] = jnp.broadcast_to(inv, (span, 128)).T[:1]
    qw, kw = heads * HEAD_DIM, kvs * HEAD_DIM
    cosine, sine = cos_ref[...], sin_ref[...]

    def rotated(row):
        one, two = qkv_ref[row:row + HALF, :], qkv_ref[row + HALF:row + HEAD_DIM, :]
        return jnp.concatenate([one * cosine - two * sine, two * cosine + one * sine], 0)

    for h in range(heads):
        qrot_ref[h * HEAD_DIM:(h + 1) * HEAD_DIM, :] = rotated(h * HEAD_DIM).astype(LOW)
    for k in range(kvs):
        turned = rotated(qw + k * HEAD_DIM).astype(LOW)
        kv_ref[k * HEAD_DIM:(k + 1) * HEAD_DIM, :] = turned
        keys_ref[k] = (turned.astype(FULL) * SCALE).T.astype(LOW)
    kv_ref[kw:, :] = qkv_ref[qw + kw:, :].astype(LOW)

    def one_block(qb, _):
        cols = pl.ds(pl.multiple_of(qb * span, span), span)
        rank = rank_ref[qb]

        def step(at, state, diagonal):
            rows = pl.ds(pl.multiple_of(order_ref[at] * span, span), span)
            out = []
            for h in range(heads):
                top, total, mixed = state[h]
                k = h * kvs // heads
                scores = dot(keys_ref[k, rows, :], qrot_ref[h * HEAD_DIM:(h + 1) * HEAD_DIM, cols])
                if diagonal:
                    key_at = lax.broadcasted_iota(jnp.int32, (span, span), 0)
                    query_at = lax.broadcasted_iota(jnp.int32, (span, span), 1)
                    scores = jnp.where(key_at <= query_at, scores, -1e30)
                new_top = jnp.maximum(top, jnp.max(scores, 0, keepdims=True))
                weights = jnp.exp(scores - new_top)
                fade = jnp.exp(top - new_top)
                total = total * fade + jnp.sum(weights, 0, keepdims=True)
                values = kv_ref[kw + k * HEAD_DIM:kw + (k + 1) * HEAD_DIM, rows]
                mixed = mixed * fade + dot(values, weights.astype(LOW))
                out.append((new_top, total, mixed))
            return out

        start = [(jnp.full((1, span), -1e30, FULL), jnp.zeros((1, span), FULL),
                  jnp.zeros((HEAD_DIM, span), FULL)) for _ in range(heads)]
        state = lax.fori_loop(0, rank, lambda at, st: step(at, st, False), start)
        state = step(rank, state, True)
        for h in range(heads):
            top, total, mixed = state[h]
            mixed = mixed / total
            mix_ref[h * HEAD_DIM:(h + 1) * HEAD_DIM, cols] = mixed
            att_ref[h * HEAD_DIM:(h + 1) * HEAD_DIM, cols] = mixed.astype(LOW)
            lse_ref[h:h + 1, cols] = top + jnp.log(total)
        return 0

    lax.fori_loop(0, count, one_block, 0)


def attend(order, rank, pieces, weight, cosine, sine, heads, kvs, span):
    tokens = cosine.shape[1]
    qw, kw = heads * HEAD_DIM, kvs * HEAD_DIM
    return pl.pallas_call(
        functools.partial(attend_kernel, heads, kvs, span, len(pieces)),
        out_shape=(
            like((qw, tokens)), like((2 * kw, tokens)), like((qw, tokens)), like((qw, tokens), FULL),
            like((heads, tokens), FULL), like((1, tokens), FULL),
        ),
        in_specs=[SMEM, SMEM] + [ANY] * len(pieces) + [VMEM] * 3,
        out_specs=(VMEM,) * 6,
        scratch_shapes=[
            pltpu.VMEM((kvs, tokens, HEAD_DIM), LOW),
            pltpu.VMEM((qw + 2 * kw, tokens), FULL),
            pltpu.VMEM((tokens, weight.shape[0]), LOW),
            arrivals(len(pieces)),
        ],
        compiler_params=PARAMS,
        name="attend",
    )(order, rank, *pieces, weight, cosine, sine)


def attend_back_kernel(heads, kvs, span, pieces, order_ref, rank_ref, *refs):
    branch_refs, refs = refs[:pieces], refs[pieces:]
    output_ref, qrot_ref, kv_ref, mix_ref, lse_ref, cos_ref, sin_ref, inv_ref, out_ref, turned_ref, *scratch = refs
    keys_ref, values_ref, delta_ref, dkv_ref, grad_ref, branch_ref, sems = scratch
    count = cos_ref.shape[1] // span
    qw, kw = heads * HEAD_DIM, kvs * HEAD_DIM
    fetch(branch_refs, branch_ref, sems)
    seq_size, across = output_ref.shape[1], branch_ref.shape[1] // output_ref.shape[1]
    for at in range(0, branch_ref.shape[0], span):
        total = 0.0
        for part in range(seq_size):
            weight = output_ref[:, part, :, :across].reshape(qw, across)
            total = total + dot(weight, branch_ref[at:at + span, part * across:(part + 1) * across], NT)
        grad_ref[:, at:at + span] = total.astype(LOW)
    qw, kw = heads * HEAD_DIM, kvs * HEAD_DIM
    for k in range(kvs):
        keys_ref[k] = (kv_ref[k * HEAD_DIM:(k + 1) * HEAD_DIM, :].astype(FULL) * SCALE).T.astype(LOW)
        values_ref[k] = kv_ref[kw + k * HEAD_DIM:kw + (k + 1) * HEAD_DIM, :].astype(FULL).T.astype(LOW)
    for h in range(heads):
        rows = slice(h * HEAD_DIM, (h + 1) * HEAD_DIM)
        delta_ref[h:h + 1, :] = jnp.sum(grad_ref[rows, :].astype(FULL) * mix_ref[rows, :], 0, keepdims=True)
    dkv_ref[...] = jnp.zeros_like(dkv_ref)

    def one_block(qb, _):
        cols = pl.ds(pl.multiple_of(qb * span, span), span)
        rank = rank_ref[qb]

        def step(at, state, diagonal):
            rows = pl.ds(pl.multiple_of(order_ref[at] * span, span), span)
            out = []
            dkeys = [None] * kvs
            dvalues = [None] * kvs
            for h in range(heads):
                k = h * kvs // heads
                mine = slice(h * HEAD_DIM, (h + 1) * HEAD_DIM)
                query = qrot_ref[mine, cols]
                grad = grad_ref[mine, cols]
                scores = dot(keys_ref[k, rows, :], query)
                weights = jnp.exp(scores - lse_ref[h:h + 1, cols])
                if diagonal:
                    key_at = lax.broadcasted_iota(jnp.int32, (span, span), 0)
                    query_at = lax.broadcasted_iota(jnp.int32, (span, span), 1)
                    weights = jnp.where(key_at <= query_at, weights, 0.0)
                grad_probs = dot(values_ref[k, rows, :], grad)
                grad_scores = (weights * (grad_probs - delta_ref[h:h + 1, cols])).astype(LOW)
                key_t = kv_ref[k * HEAD_DIM:(k + 1) * HEAD_DIM, rows]
                out.append(state[h] + dot(key_t, grad_scores))
                dk = dot(query, grad_scores, NT)
                dv = dot(grad, weights.astype(LOW), NT)
                dkeys[k] = dk if dkeys[k] is None else dkeys[k] + dk
                dvalues[k] = dv if dvalues[k] is None else dvalues[k] + dv
            for k in range(kvs):
                mine = slice(k * HEAD_DIM, (k + 1) * HEAD_DIM)
                dkv_ref[mine, rows] += dkeys[k]
                mine = slice(kw + k * HEAD_DIM, kw + (k + 1) * HEAD_DIM)
                dkv_ref[mine, rows] += dvalues[k]
            return out

        state = [jnp.zeros((HEAD_DIM, span), FULL) for _ in range(heads)]
        state = lax.fori_loop(0, rank, lambda at, st: step(at, st, False), state)
        state = step(rank, state, True)
        scale = inv_ref[:, cols] * SCALE
        cosine, sine = cos_ref[:, cols], sin_ref[:, cols]
        for h in range(heads):
            one, two = state[h][:HALF] * scale, state[h][HALF:] * scale
            out_ref[h * HEAD_DIM:h * HEAD_DIM + HALF, cols] = (one * cosine + two * sine).astype(LOW)
            out_ref[h * HEAD_DIM + HALF:(h + 1) * HEAD_DIM, cols] = (two * cosine - one * sine).astype(LOW)
        return 0

    lax.fori_loop(0, count, one_block, 0)
    cosine, sine = cos_ref[...], sin_ref[...]
    scale = inv_ref[...] * SCALE
    for k in range(kvs):
        top = k * HEAD_DIM
        one, two = dkv_ref[top:top + HALF, :] * scale, dkv_ref[top + HALF:top + HEAD_DIM, :] * scale
        out_ref[qw + top:qw + top + HALF, :] = (one * cosine + two * sine).astype(LOW)
        out_ref[qw + top + HALF:qw + top + HEAD_DIM, :] = (two * cosine - one * sine).astype(LOW)
    out_ref[qw + kw:, :] = (dkv_ref[kw:, :] * inv_ref[...]).astype(LOW)
    turned_ref[...] = out_ref[...].T


def attend_back(order, rank, pieces, output, qrot, kv, mix, lse, cosine, sine, inv, heads, kvs, span):
    tokens = cosine.shape[1]
    qw, kw = heads * HEAD_DIM, kvs * HEAD_DIM
    return pl.pallas_call(
        functools.partial(attend_back_kernel, heads, kvs, span, len(pieces)),
        out_shape=(like((qw + 2 * kw, tokens)), like((tokens, qw + 2 * kw))),
        in_specs=[SMEM, SMEM] + [ANY] * len(pieces) + [VMEM] * 8,
        out_specs=(VMEM, VMEM),
        scratch_shapes=[
            pltpu.VMEM((kvs, tokens, HEAD_DIM), LOW),
            pltpu.VMEM((kvs, tokens, HEAD_DIM), LOW),
            pltpu.VMEM((heads, tokens), FULL),
            pltpu.VMEM((2 * kw, tokens), FULL),
            pltpu.VMEM((qw, tokens), LOW),
            pltpu.VMEM((tokens, pieces[0].shape[1]), LOW),
            arrivals(len(pieces)),
        ],
        compiler_params=PARAMS,
        name="attend_back",
    )(order, rank, *pieces, output, qrot, kv, mix, lse, cosine, sine, inv)


def layer(seq_size, fsdp_size, tokens, positions, attn_gain, query_weight, key_weight, value_weight, output_weight,
          ffn_gain, gate_weight, up_weight, down_weight, cotangent):
    span, width = tokens.shape[1:]
    heads = HEADS // seq_size
    kvs = max(1, KV_HEADS // seq_size)
    shared = max(1, seq_size // KV_HEADS)
    qw, kw = heads * HEAD_DIM, kvs * HEAD_DIM
    own_rows = query_weight.shape[0]
    hidden_own = gate_weight.shape[1] // seq_size
    chunk = 128 if hidden_own % 128 == 0 else 64
    parts = 2 if seq_size == 4 else 1
    piece_rows = span // parts
    into, back = (seq_size, fsdp_size, own_rows), (fsdp_size, seq_size, own_rows)
    here = lax.axis_index("seq")

    def after(x, *others):
        return lax.optimization_barrier((x, *others))[0]

    def swap(x, j):
        return lax.ppermute(x, "seq", [(i, i ^ j) for i in range(seq_size)])

    def seq_gather(own):
        if parts == 1:
            return [own[0]] + [swap(own[0], j) for j in range(1, seq_size)]
        a, b = own
        ax, by = swap(a, 1), swap(b, 2)
        ay, bx = swap(a, 2), swap(b, 1)
        ad, bd = swap(ax, 2), swap(by, 1)
        return [a, b, ax, bx, ay, by, ad, bd]

    def seq_scatter(pieces):
        if parts == 1:
            return (), [pieces[0]] + [swap(pieces[j], j) for j in range(1, seq_size)]
        a, b = pieces[::2], pieces[1::2]
        da, db = swap(a[3], 2), swap(b[3], 1)
        ya, xb = swap(a[2], 2), swap(b[1], 1)
        xa = swap((a[1].astype(FULL) + da.astype(FULL)).astype(LOW), 1)
        yb = swap((b[2].astype(FULL) + db.astype(FULL)).astype(LOW), 2)
        return (da, db), [a[0], ya, xa, b[0], xb, yb]

    def direct_scatter(pieces):
        if parts == 1:
            return seq_scatter(pieces)[1]
        a, b = pieces[::2], pieces[1::2]
        return [a[0]] + [swap(a[j], j) for j in (1, 2, 3)] + [b[0]] + [swap(b[j], j) for j in (1, 2, 3)]

    def spread(pieces_for):
        got = [pieces_for(here)] + [swap(pieces_for(here ^ j), j) for j in range(1, seq_size)]
        stack = jnp.stack(got)
        return jnp.concatenate(
            [lax.dynamic_index_in_dim(stack, here ^ t, 0, False) for t in range(seq_size)], 0
        )

    def collect(x):
        blocks = x.reshape(seq_size, own_rows, x.shape[1])
        got = jnp.stack([lax.dynamic_index_in_dim(blocks, here, 0, False)] + [
            swap(lax.dynamic_index_in_dim(blocks, here ^ j, 0, False), j) for j in range(1, seq_size)
        ])
        return jnp.stack([lax.dynamic_index_in_dim(got, here ^ t, 0, False) for t in range(seq_size)])

    def fsdp_gather(x):
        return lax.all_gather(x, "fsdp", axis=0, tiled=True)

    def fsdp_scatter(x):
        return lax.psum_scatter(x, "fsdp", scatter_dimension=0, tiled=True)

    gain_one, gain_two = attn_gain.astype(FULL)[:, None], ffn_gain.astype(FULL)[:, None]

    def with_gain(weight, gain):
        return (weight.astype(FULL) * gain).astype(LOW)

    query_low, key_low, value_low = (with_gain(w, gain_one) for w in (query_weight, key_weight, value_weight))

    def qkv_for(t):
        first = (t * heads // GROUP) * HEAD_DIM
        return jnp.concatenate([
            lax.dynamic_slice_in_dim(query_low, t * qw, qw, 1),
            lax.dynamic_slice_in_dim(key_low, first, kw, 1),
            lax.dynamic_slice_in_dim(value_low, first, kw, 1),
        ], 1)

    own_tokens = tokens[0]
    own_pieces = call_own(
        functools.partial(regroup_kernel, into), (like((piece_rows, width)),) * parts, own_tokens
    )
    token_pieces = seq_gather(own_pieces)
    output_own = output_weight.reshape(own_rows, seq_size, -1).swapaxes(0, 1).reshape(seq_size * own_rows, -1)
    projections = fsdp_gather(jnp.concatenate([output_own, spread(qkv_for)], 1))
    gate_weight, up_weight = lax.optimization_barrier((gate_weight, up_weight, *own_pieces))[:2]
    gate_low, up_low = with_gain(gate_weight, gain_two), with_gain(up_weight, gain_two)

    def gate_up_for(t):
        gate = lax.dynamic_slice_in_dim(gate_low, t * hidden_own, hidden_own, 1)
        up = lax.dynamic_slice_in_dim(up_low, t * hidden_own, hidden_own, 1)
        return jnp.concatenate(
            [x[:, c:c + chunk] for c in range(0, hidden_own, chunk) for x in (gate, up)], 1
        )

    gate_up_own = spread(gate_up_for)
    gate_up_full = fsdp_gather(gate_up_own)
    down_full = fsdp_gather(down_weight)
    own_upstream = after(cotangent[0], gate_up_own, *token_pieces)
    upstream = [own_upstream] + [swap(own_upstream, j) for j in range(1, seq_size)]

    count = positions.shape[1] // span
    where_at = positions[0].reshape(count, span)
    where_at = jnp.stack([lax.dynamic_index_in_dim(where_at, here ^ j, 0, False) for j in range(count)])
    rank = where_at[:, 0] // span
    order = jnp.argsort(rank).astype(jnp.int32)
    cosine, sine = rope_tables(where_at.reshape(-1))

    qrot, kv, attended, mix, lse, inv_one = attend(
        order, rank, token_pieces, projections, cosine, sine, heads, kvs, span
    )
    attended, *upstream = lax.optimization_barrier((attended, *upstream))
    branch = seq_scatter(rows_of_product(attended, projections, piece_rows, into))[1]
    middle, inv_two, *own_pieces = call_own(
        functools.partial(middle_kernel, into, parts),
        (like((span, width), FULL), like((span, 1), FULL)) + (like((piece_rows, width)),) * parts,
        own_tokens, *branch,
    )

    normed_pieces = seq_gather(own_pieces)
    slope, hidden = hidden_of(normed_pieces, gate_up_full, chunk)
    part_down = grad_down_of(hidden, upstream)
    grad_down = fsdp_scatter(part_down)
    grad_gate_up, down_full = grad_gate_up_of(
        [after(upstream[0], part_down), *upstream[1:]], jnp.zeros((1,), jnp.int32), [down_full], slope, chunk
    )
    first, grad_pieces = seq_scatter(grad_rows_of(grad_gate_up, gate_up_full, piece_rows))
    part_gate_up = grad_weight_of([after(normed_pieces[0], *first), *normed_pieces[1:]], grad_gate_up)
    grad_gate_up_own = fsdp_scatter(after(part_gate_up, part_down))
    out_pieces = rows_of_product(after(hidden, part_gate_up), down_full, piece_rows)
    grad_pieces[0] = after(grad_pieces[0], out_pieces[0], grad_down)
    grad_middle, *own_pieces = call_own(
        functools.partial(grad_middle_kernel, back, parts),
        (like((span, width), FULL),) + (like((piece_rows, width)),) * parts,
        cotangent[0], middle, inv_two, *grad_pieces,
    )

    branch_pieces = seq_gather(own_pieces)
    out_pieces = direct_scatter(lax.optimization_barrier((*out_pieces, *branch_pieces))[:len(out_pieces)])
    grad_qkv, grad_qkv_turned = attend_back(
        order, rank, branch_pieces, projections.reshape(fsdp_size, seq_size, own_rows, -1), qrot, kv, mix, lse,
        cosine, sine, inv_one, heads, kvs, span,
    )
    grad_qkv, *out_pieces = lax.optimization_barrier((grad_qkv, *out_pieces))
    part_projections = attention_weights_of(token_pieces, branch_pieces, grad_qkv, attended, into)
    grad_pieces = grad_rows_of(after(grad_qkv_turned, part_projections), projections, piece_rows)
    grad_pieces = seq_scatter(grad_pieces)[1]
    grad_projections = fsdp_scatter(after(part_projections, grad_gate_up_own))
    grad_qkv_own = grad_projections[:, -qw - 2 * kw:]
    grad_output = grad_projections[:, :-qw - 2 * kw].reshape(seq_size, own_rows, -1).swapaxes(0, 1)
    grad_output = grad_output.reshape(own_rows, width)
    block_out = call_own(
        functools.partial(block_out_kernel, parts), like((span, width)), middle, *out_pieces
    )
    grad_tokens = call_own(
        functools.partial(grad_tokens_kernel, back, parts), like((span, width), FULL),
        own_tokens, grad_middle, *grad_pieces,
    )

    def whole_rows(x):
        return x.swapaxes(0, 1).reshape(own_rows, -1)

    got = collect(grad_gate_up_own).astype(FULL).reshape(seq_size, own_rows, -1, 2, chunk)
    grad_gate, grad_up = whole_rows(got[:, :, :, 0]), whole_rows(got[:, :, :, 1])
    got = collect(grad_qkv_own).astype(FULL)
    grad_query = whole_rows(got[:, :, :qw])

    def of_heads(x):
        return whole_rows(x.reshape(seq_size // shared, shared, own_rows, kw).sum(1))

    grad_key, grad_value = of_heads(got[:, :, qw:qw + kw]), of_heads(got[:, :, qw + kw:])
    grad_attn_gain = (
        jnp.sum(grad_query * query_weight.astype(FULL), 1)
        + jnp.sum(grad_key * key_weight.astype(FULL), 1)
        + jnp.sum(grad_value * value_weight.astype(FULL), 1)
    )
    grad_ffn_gain = jnp.sum(grad_gate * gate_weight.astype(FULL), 1) + jnp.sum(grad_up * up_weight.astype(FULL), 1)
    return (
        block_out[None],
        grad_tokens[None],
        grad_attn_gain,
        grad_query * gain_one,
        grad_key * gain_one,
        grad_value * gain_one,
        grad_output.astype(FULL),
        grad_ffn_gain,
        grad_gate * gain_two,
        grad_up * gain_two,
        grad_down.astype(FULL),
    )


def solution(mesh):
    rows, vector, matrix = P("fsdp", "seq", None), P(("seq", "fsdp")), P(("seq", "fsdp"), None)
    return jax.shard_map(
        functools.partial(layer, mesh.shape["seq"], mesh.shape["fsdp"]),
        mesh=mesh,
        in_specs=(
            rows, P("fsdp", None), vector, matrix, matrix, matrix, matrix, vector, matrix, matrix, matrix, rows,
        ),
        out_specs=(rows, rows, vector, matrix, matrix, matrix, matrix, vector, matrix, matrix, matrix),
        check_vma=False,
    )
```

time: 723 us -> 538 us (0.74)
  Pallas kernels: 50.3 us -> 218 us
  waiting for transfers between devices: 335 us -> 190 us
  matrix products: 128 us -> 0 us
  local copies, waits for them, and re-layouts: 64 us -> 16.3 us
  other arithmetic: 51 us -> 24.5 us
    pallas_call x2 -> x16, Pallas kernels: 50.3 us -> 218 us  [the longest x1 34.8 us: attend_back(): pl.pallas_call(functools.partial(attend_back_kernel, heads, kvs, span, le...]
    dot_general x15 -> x0, matrix products: 128 us -> none  [dot(): return lax.dot_general(a, b, (dims, ((), ())), preferred_element_type=out)]
    reduce_scatter x5 -> x3, waiting for transfers between devices: 103 us -> 0.04 us  [fsdp_scatter(): return lax.psum_scatter(x, 'fsdp', scatter_dimension=0, tiled=True)]
    ppermute x63 -> x57, waiting for transfers between devices: 218 us -> 178 us  [swap(): return lax.ppermute(x, 'seq', [(i, i ^ j) for i in range(seq_size)])]
    unnamed x101 -> x129, local copies, waits for them, and re-layouts: 26.3 us -> 6.4 us
    add x7 -> x0, other arithmetic: 14.1 us -> none  [the longest x1 6.51 us: layer(): grad_middle + inv_one * (scaled_grad - scaled_one * jnp.mean(scaled_grad...]
    reshape x5 -> x1, local copies, waits for them, and re-layouts: 12.7 us -> 0.02 us  [layer(): output_weight.reshape(own_rows, seq_size, -1).swapaxes(0, 1)]
    concatenate x6 -> x2, local copies, waits for them, and re-layouts: 8.55 us -> 0.07 us  [gate_up_for(): jnp.concatenate([x[:, c:c + chunk] for c in range(0, hidden_own, chunk) f...]
  transfers between devices with their start and end apart: 72 -> 63, of which waited for: 41 -> 31; matrix products, arithmetic and copies ran while one was open for 22% -> 5% of each run, Pallas kernels for 3% -> 41%
where the time goes in v2:
time: 538 us; the launch traced here: 530 us
  Pallas kernels  218 us (41%)
  waiting for transfers between devices  190 us (35%)
  starting transfers between devices  65.2 us (12%)
  other arithmetic  24.5 us (5%)
  local copies, waits for them, and re-layouts  16.3 us (3%)
  between operations  15.8 us (3%)
    ppermute x57, waiting for transfers between devices, swap(): return lax.ppermute(x, 'seq', [(i, i ^ j) for i in range(seq_size)])  178 us
    ppermute x57, starting transfers between devices, swap(): return lax.ppermute(x, 'seq', [(i, i ^ j) for i in range(seq_size)])  64.9 us
    pallas_call x1, Pallas kernels, attend_back(): pl.pallas_call(functools.partial(attend_back_kernel, heads, kvs, span, le...  34.8 us
    pallas_call x1, Pallas kernels, attend(): pl.pallas_call(functools.partial(attend_kernel, heads, kvs, span, len(pie...  33.7 us
    pallas_call x2, Pallas kernels, grad_rows_of(): pl.pallas_call(functools.partial(grad_rows_kernel, weight.shape[1] - grad...  26.8 us
    pallas_call x5, Pallas kernels, call_own(): pl.pallas_call(kernel, out_shape=out_shape, in_specs=[VMEM] * len(args),...  23.3 us
    pallas_call x2, Pallas kernels, rows_of_product(): pl.pallas_call(rows_kernel, grid=(width // block,), in_specs=[whole(left....  20.9 us
    pallas_call x1, Pallas kernels, hidden_of(): pl.pallas_call(functools.partial(hidden_kernel, len(pieces), chunk), grid...  19.8 us
  transfers between devices with their start and end apart: 63, of which 31 were waited for; matrix products, arithmetic and copies ran while one was open for 5% of the time, Pallas kernels for 41%

profile of v2, /device:TPU:0, one launch (start us, length us, event | category | flops | bytes accessed | tf_op | source)
XLA Modules:
  0.0 529.9 jit_solution(7263496953554094268)
XLA Ops:
  10.2 2.9 collective-permute-start.6
  15.7 2.0 collective-permute-done.7
  17.7 2.5 collective-permute-done.8
  21.3 2.6 regroup_kernel.1
  28.8 7.9 %collective-permute-done.9 = bf16[64,2816]{1,0:T(8,128)(2,1)S(1)} collective-permute-done((bf16[64,2816]{1,0:T(8,128)(2,1)S(1)}, bf16[64,2816]{1,0:T(8,128)(2,1)S(1)}, u32[]{:S(2)}, u32[]{:S(2)}) %collective-permute-start.9) | collective-permute-done | bytes 360480 | tf_op jit(solution)/shard_map/ppermute | solution.py:582
  36.7 4.9 collective-permute-done.11
  49.6 10.8 %collective-permute-done.refs_2_ = bf16[128,2048]{1,0:T(8,128)(2,1)S(1)} collective-permute-done((bf16[128,2048]{1,0:T(8,128)(2,1)S(1)}, bf16[128,2048]{1,0:T(8,128)(2,1)S(1)}, u32[]{:S(2)}, u32[]{:S(2)}) %collective-permute-start) | collective-permute-done | bytes 524320 | tf_op jit(solution)/shard_map/ppermute | solution.py:582
  62.8 9.8 %collective-permute-done.2.refs_4_ = bf16[128,2048]{1,0:T(8,128)(2,1)S(1)} collective-permute-done((bf16[128,2048]{1,0:T(8,128)(2,1)S(1)}, bf16[128,2048]{1,0:T(8,128)(2,1)S(1)}, u32[]{:S(2)}, u32[]{:S(2)}) %collective-permute-start.2) | collective-permute-done | bytes 524320 | tf_op jit(solution)/shard_map/ppermute | solution.py:582
  72.6 18.6 %collective-permute-done.4.refs_6_ = bf16[128,2048]{1,0:T(8,128)(2,1)S(1)} collective-permute-done((bf16[128,2048]{1,0:T(8,128)(2,1)S(1)}, bf16[128,2048]{1,0:T(8,128)(2,1)S(1)}, u32[]{:S(2)}, u32[]{:S(2)}) %collective-permute-start.4) | collective-permute-done | bytes 524320 | tf_op jit(solution)/shard_map/ppermute | solution.py:582
  91.3 1.9 collective-permute-start.14
  98.4 33.7 %attend.1 = (bf16[512,1024]{1,0:T(8,128)(2,1)}, bf16[128,1024]{1,0:T(8,128)(2,1)}, bf16[512,1024]{1,0:T(8,128)(2,1)}, f32[512,1024]{1,0:T(8,128)}, f32[8,1024]{1,0:T(8,128)}, /*index=5*/f32[1,1024]{1,0:T(1,128)}) custom-call(s32[4]{0:T(128)} %get-tuple-element.97.order_ref, s32[4]{0:T(128)} %copy-done.50, bf16[128,2048]{1,0:T(8,128)(2,1)} %get-tuple-element.98.refs_0_, ...), custom_call_target="tpu_custom_call" | custom-call | tf_op jit(solution)/shard_map/attend/pallas_call | solution.py:441
  132.1 8.6 %rows_of_product.2 = (bf16[128,2048]{1,0:T(8,128)(2,1)}, bf16[128,2048]{1,0:T(8,128)(2,1)}, bf16[128,2048]{1,0:T(8,128)(2,1)}, bf16[128,2048]{1,0:T(8,128)(2,1)}...) custom-call(bf16[512,1024]{1,0:T(8,128)(2,1)} %get-tuple-element.104, ...), custom_call_target="tpu_custom_call" | custom-call | tf_op jit(solution)/shard_map/rows_of_product/pallas_call | solution.py:326
  140.7 2.1 collective-permute-start.16
  144.9 6.7 %collective-permute-done.16 = bf16[128,2048]{1,0:T(8,128)(2,1)S(1)} collective-permute-done((bf16[128,2048]{1,0:T(8,128)(2,1)}, bf16[128,2048]{1,0:T(8,128)(2,1)S(1)}, u32[]{:S(2)}, u32[]{:S(2)}) %collective-permute-start.16) | collective-permute-done | bytes 524320 | tf_op jit(solution)/shard_map/ppermute | solution.py:582
  153.4 1.8 collective-permute-start.20
  155.2 2.4 collective-permute-done.15.refs_2_
  157.6 2.4 collective-permute-done.18.refs_5_
  160.1 11.2 %collective-permute-done.17.refs_3_ = bf16[128,2048]{1,0:T(8,128)(2,1)S(1)} collective-permute-done((bf16[128,2048]{1,0:T(8,128)(2,1)S(1)}, bf16[128,2048]{1,0:T(8,128)(2,1)S(1)}, u32[]{:S(2)}, u32[]{:S(2)}) %collective-permute-start.17) | collective-permute-done | bytes 524320 | tf_op jit(solution)/shard_map/ppermute | solution.py:582
  172.3 4.9 middle_kernel.1
  177.7 1.8 collective-permute-start.23
  181.3 5.5 %collective-permute-done.21.refs_2_ = bf16[128,2048]{1,0:T(8,128)(2,1)S(1)} collective-permute-done((bf16[128,2048]{1,0:T(8,128)(2,1)}, bf16[128,2048]{1,0:T(8,128)(2,1)S(1)}, u32[]{:S(2)}, u32[]{:S(2)}) %collective-permute-start.21) | collective-permute-done | bytes 524320 | tf_op jit(solution)/shard_map/ppermute | solution.py:582
  188.7 3.9 collective-permute-done.23.refs_4_
  192.5 5.6 %collective-permute-done.25.refs_6_ = bf16[128,2048]{1,0:T(8,128)(2,1)S(1)} collective-permute-done((bf16[128,2048]{1,0:T(8,128)(2,1)S(1)}, bf16[128,2048]{1,0:T(8,128)(2,1)S(1)}, u32[]{:S(2)}, u32[]{:S(2)}) %collective-permute-start.25) | collective-permute-done | bytes 524320 | tf_op jit(solution)/shard_map/ppermute | solution.py:582
  199.1 19.8 %hidden_of.1 = (bf16[1024,2816]{1,0:T(8,128)(2,1)}, bf16[1408,1024]{1,0:T(8,128)(2,1)}) custom-call(bf16[128,2048]{1,0:T(8,128)(2,1)} %get-tuple-element.128.refs_0_, bf16[128,2048]{1,0:T(8,128)(2,1)} %get-tuple-element.120.refs_1_, bf16[128,2048]{1,0:T(8,128)(2,1)} %copy-done.18, bf16[128,2048]{1,0:T(8,128)(2,1)} %copy-done.23, ...), custom_call_target="tpu_custom_call" | custom-call | tf_op jit(solution)/shard_map/hidden_of/pallas_call | solution.py:175
  218.9 11.9 %grad_down_of.1 = bf16[1408,2048]{1,0:T(8,128)(2,1)} custom-call(bf16[256,2048]{1,0:T(8,128)(2,1)} %bitcast.86, bf16[256,2048]{1,0:T(8,128)(2,1)} %collective-permute-done.12.refs_1_, bf16[256,2048]{1,0:T(8,128)(2,1)} %copy-done.3, bf16[256,2048]{1,0:T(8,128)(2,1)} %copy-done.2, bf16[1408,1024]{1,0:T(8,128)(2,1)} %get-tuple-element.129.refs_4_.left_ref), custom_call_target="tpu_custom_call" | custom-call | tf_op jit(solution)/shard_map/grad_down_of/pallas_call | solution.py:195
  230.9 11.1 %all-gather.8.cloned.1.call-done.refs_4_ = bf16[1408,2048]{1,0:T(8,128)(2,1)} async-done(((bf16[176,2048]{1,0:T(8,128)(2,1)}), bf16[1408,2048]{1,0:T(8,128)(2,1)}) %all-gather.8.cloned.1.call-update) | async-done | bytes 5767184 | tf_op jit(solution)/shard_map/all_gather | solution.py:624
  242.0 16.4 %grad_gate_up_of.1 = (bf16[1024,2816]{1,0:T(8,128)(2,1)}, bf16[1408,2048]{1,0:T(8,128)(2,1)}) custom-call(s32[1]{0:T(128)} %constant.144.clone.1.places_ref, bf16[256,2048]{1,0:T(8,128)(2,1)} %bitcast.87, bf16[256,2048]{1,0:T(8,128)(2,1)} %collective-permute-done.12.refs_1_, bf16[256,2048]{1,0:T(8,128)(2,1)} %copy-done.3, bf16[256,2048]{1,0:T(8,128)(2,1)} %copy-done.2, ...), custom_call_target="tpu_custom_call" | custom-call | tf_op jit(solution)/shard_map/grad_gate_up_of/pallas_call | solution.py:248
  258.4 17.6 %grad_rows_of.2 = (bf16[128,2048]{1,0:T(8,128)(2,1)}, bf16[128,2048]{1,0:T(8,128)(2,1)}, bf16[128,2048]{1,0:T(8,128)(2,1)}, bf16[128,2048]{1,0:T(8,128)(2,1)}, b...) custom-call(bf16[1024,2816]{1,0:T(8,128)(2,1)} %get-tuple-element.12, ...), custom_call_target="tpu_custom_call" | custom-call | tf_op jit(solution)/shard_map/grad_rows_of/pallas_call | solution.py:270
  279.0 11.3 %collective-permute-done.27 = bf16[128,2048]{1,0:T(8,128)(2,1)S(1)} collective-permute-done((bf16[128,2048]{1,0:T(8,128)(2,1)}, bf16[128,2048]{1,0:T(8,128)(2,1)S(1)}, u32[]{:S(2)}, u32[]{:S(2)}) %collective-permute-start.27) | collective-permute-done | bytes 524320 | tf_op jit(solution)/shard_map/ppermute | solution.py:582
  291.6 18.2 %grad_weight_of.1 = bf16[2048,2816]{1,0:T(8,128)(2,1)} custom-call(bf16[128,2048]{1,0:T(8,128)(2,1)} %get-tuple-element.128.refs_0_, bf16[128,2048]{1,0:T(8,128)(2,1)} %get-tuple-element.120.refs_1_, bf16[128,2048]{1,0:T(8,128)(2,1)} %copy-done.18, bf16[128,2048]{1,0:T(8,128)(2,1)} %copy-done.23, bf16[128,2048]{1,0:T(8,128)(2,1)} %copy-done.21, ...), custom_call_target="tpu_custom_call" | custom-call | tf_op jit(solution)/shard_map/grad_weight_of/pallas_call | solution.py:289
  315.2 12.3 %rows_of_product.3 = (bf16[128,2048]{1,0:T(8,128)(2,1)}, bf16[128,2048]{1,0:T(8,128)(2,1)}, bf16[128,2048]{1,0:T(8,128)(2,1)}, bf16[128,2048]{1,0:T(8,128)(2,1)}...) custom-call(bf16[1408,1024]{1,0:T(8,128)(2,1)} %get-tuple-element.12, ...), custom_call_target="tpu_custom_call" | custom-call | tf_op jit(solution)/shard_map/rows_of_product/pallas_call | solution.py:326
  327.6 7.2 %collective-permute-done.30.refs_5_ = bf16[128,2048]{1,0:T(8,128)(2,1)S(1)} collective-permute-done((bf16[128,2048]{1,0:T(8,128)(2,1)}, bf16[128,2048]{1,0:T(8,128)(2,1)S(1)}, u32[]{:S(2)}, u32[]{:S(2)}) %collective-permute-start.30) | collective-permute-done | bytes 524320 | tf_op jit(solution)/shard_map/ppermute | solution.py:582
  335.8 5.7 %grad_middle_kernel.1 = (f32[256,2048]{1,0:T(8,128)}, bf16[128,2048]{1,0:T(8,128)(2,1)}, bf16[128,2048]{1,0:T(8,128)(2,1)}) custom-call(bf16[256,2048]{1,0:T(8,128)(2,1)} %bitcast.88, f32[256,2048]{1,0:T(8,128)} %get-tuple-element.113.refs_1_.refs_0_, f32[256,1]{1,0:T(8,128)} %get-tuple-element.114.refs_2_, bf16[128,2048]{1,0:T(8,128)(2,1)} %get-tuple-element.132.refs_3_, ...), custom_call_target="tpu_custom_call" | custom-call | tf_op jit(solution)/shard_map/grad_middle_kernel/pallas_call | solution.py:71
  345.5 11.0 %collective-permute-done.33.refs_2_.refs_10_ = bf16[128,2048]{1,0:T(8,128)(2,1)S(1)} collective-permute-done((bf16[128,2048]{1,0:T(8,128)(2,1)}, bf16[128,2048]{1,0:T(8,128)(2,1)S(1)}, u32[]{:S(2)}, u32[]{:S(2)}) %collective-permute-start.33) | collective-permute-done | bytes 524320 | tf_op jit(solution)/shard_map/ppermute | solution.py:582
  359.4 9.8 %collective-permute-done.35.refs_4_.refs_12_ = bf16[128,2048]{1,0:T(8,128)(2,1)S(1)} collective-permute-done((bf16[128,2048]{1,0:T(8,128)(2,1)}, bf16[128,2048]{1,0:T(8,128)(2,1)S(1)}, u32[]{:S(2)}, u32[]{:S(2)}) %collective-permute-start.35) | collective-permute-done | bytes 524320 | tf_op jit(solution)/shard_map/ppermute | solution.py:582
  369.3 8.2 %collective-permute-done.37.refs_6_.refs_14_ = bf16[128,2048]{1,0:T(8,128)(2,1)S(1)} collective-permute-done((bf16[128,2048]{1,0:T(8,128)(2,1)S(1)}, bf16[128,2048]{1,0:T(8,128)(2,1)S(1)}, u32[]{:S(2)}, u32[]{:S(2)}) %collective-permute-start.37) | collective-permute-done | bytes 524320 | tf_op jit(solution)/shard_map/ppermute | solution.py:582
  382.9 9.7 %collective-permute-done.39.refs_2_ = bf16[128,2048]{1,0:T(8,128)(2,1)S(1)} collective-permute-done((bf16[128,2048]{1,0:T(8,128)(2,1)}, bf16[128,2048]{1,0:T(8,128)(2,1)S(1)}, u32[]{:S(2)}, u32[]{:S(2)}) %collective-permute-start.39) | collective-permute-done | bytes 524320 | tf_op jit(solution)/shard_map/ppermute | solution.py:582
  394.0 34.8 %attend_back.1 = (bf16[640,1024]{1,0:T(8,128)(2,1)}, bf16[1024,640]{1,0:T(8,128)(2,1)}) custom-call(s32[4]{0:T(128)} %get-tuple-element.97.order_ref, s32[4]{0:T(128)} %copy-done.50, bf16[128,2048]{1,0:T(8,128)(2,1)} %get-tuple-element.138.refs_0_.refs_8_, bf16[128,2048]{1,0:T(8,128)(2,1)} %get-tuple-element.139.refs_1_.refs_9_, ...), custom_call_target="tpu_custom_call" | custom-call | tf_op jit(solution)/shard_map/attend_back/pallas_call | solution.py:544
  428.8 12.4 %attention_weights_of.1 = bf16[2048,1152]{1,0:T(8,128)(2,1)} custom-call(bf16[128,2048]{1,0:T(8,128)(2,1)} %get-tuple-element.98.refs_0_, bf16[128,2048]{1,0:T(8,128)(2,1)} %get-tuple-element.99.refs_1_, bf16[128,2048]{1,0:T(8,128)(2,1)} %copy-done.8, bf16[128,2048]{1,0:T(8,128)(2,1)} %copy-done.11, bf16[128,2048]{1,0:T(8,128)(2,1)} %copy-done.10, ...), custom_call_target="tpu_custom_call" | custom-call | tf_op jit(solution)/shard_map/attention_weights_of/pallas_call | solution.py:359
  441.3 9.2 %grad_rows_of.3 = (bf16[128,2048]{1,0:T(8,128)(2,1)}, bf16[128,2048]{1,0:T(8,128)(2,1)}, bf16[128,2048]{1,0:T(8,128)(2,1)}, bf16[128,2048]{1,0:T(8,128)(2,1)}, b...) custom-call(bf16[1024,640]{1,0:T(8,128)(2,1)} %get-tuple-element.172, ...), custom_call_target="tpu_custom_call" | custom-call | tf_op jit(solution)/shard_map/grad_rows_of/pallas_call | solution.py:270
  454.7 11.0 %collective-permute-done.46 = bf16[128,2048]{1,0:T(8,128)(2,1)S(1)} collective-permute-done((bf16[128,2048]{1,0:T(8,128)(2,1)}, bf16[128,2048]{1,0:T(8,128)(2,1)S(1)}, u32[]{:S(2)}, u32[]{:S(2)}) %collective-permute-start.46) | collective-permute-done | bytes 524320 | tf_op jit(solution)/shard_map/ppermute | solution.py:582
  471.7 9.1 %collective-permute-done.45.refs_3_ = bf16[128,2048]{1,0:T(8,128)(2,1)S(1)} collective-permute-done((bf16[128,2048]{1,0:T(8,128)(2,1)}, bf16[128,2048]{1,0:T(8,128)(2,1)S(1)}, u32[]{:S(2)}, u32[]{:S(2)}) %collective-permute-start.45) | collective-permute-done | bytes 524320 | tf_op jit(solution)/shard_map/ppermute | solution.py:582
  484.2 4.4 block_out_kernel.1
  489.6 5.6 %grad_tokens_kernel.1 = f32[256,2048]{1,0:T(8,128)} custom-call(bf16[256,2048]{1,0:T(8,128)(2,1)} %bitcast.94, f32[256,2048]{1,0:T(8,128)} %get-tuple-element.169.refs_1_, bf16[128,2048]{1,0:T(8,128)(2,1)} %get-tuple-element.173.refs_2_, bf16[128,2048]{1,0:T(8,128)(2,1)} %copy-done.30, bf16[128,2048]{1,0:T(8,128)(2,1)} %copy-done.32, ...), custom_call_target="tpu_custom_call" | custom-call | tf_op jit(solution)/shard_map/grad_tokens_kernel/pallas_call | solution.py:71
  497.2 2.9 maximum_convert_fusion
  500.1 2.2 fusion.10
  506.0 3.9 broadcast_multiply_fusion
  511.5 2.2 collective-permute-start.53
  (299 shorter events, 91.5 us)
Async XLA Ops:
  7.2 91.2 %all-gather.4.cloned.1.call-start = ((), (), s32[]{:S(2)}) async-start(), calls=%async_computation.3 | async-start | bytes 5308416 | tf_op jit(solution)/shard_map/all_gather | solution.py:624
  21.2 177.0 %all-gather.6.cloned.1.call-start = ((), (), s32[]{:S(2)}) async-start(), calls=%async_computation.4 | async-start | bytes 12976128 | tf_op jit(solution)/shard_map/all_gather | solution.py:624
  25.9 15.8 %collective-permute-start.11 = (bf16[64,2816]{1,0:T(8,128)(2,1)S(1)}, bf16[64,2816]{1,0:T(8,128)(2,1)S(1)}, u32[]{:S(2)}, u32[]{:S(2)}) collective-permute-start(bf16[64,2816]{1,0:T(8,128)(2,1)S(1)} %get-tuple-element.282), channel_id=1, source_target_pairs={{0,24},{8,16},{16,8},{24,0},{1,25},{9,17},{17,9},{25,1},{2,26},{10... | collective-permute-start | bytes 1081352 | tf_op jit(solution)/shard_map/ppermute | solution.py:582
  27.4 15.6 %collective-permute-start.10 = (bf16[64,2816]{1,0:T(8,128)(2,1)S(1)}, bf16[64,2816]{1,0:T(8,128)(2,1)S(1)}, u32[]{:S(2)}, u32[]{:S(2)}) collective-permute-start(bf16[64,2816]{1,0:T(8,128)(2,1)S(1)} %get-tuple-element.283), channel_id=1, source_target_pairs={{0,16},{8,24},{16,0},{24,8},{1,17},{9,25},{17,1},{25,9},{2,18},{10... | collective-permute-start | bytes 1081352 | tf_op jit(solution)/shard_map/ppermute | solution.py:582
  44.5 197.5 %all-gather.8.cloned.1.call-start = ((), (), s32[]{:S(2)}) async-start(), calls=%async_computation.5 | async-start | bytes 6488064 | tf_op jit(solution)/shard_map/all_gather | solution.py:624
  45.3 282.2 %reduce-scatter.4.cloned.1.call-start = ((), (), s32[]{:S(2)}) async-start(), calls=%async_computation.6 | async-start | bytes 6488064 | tf_op jit(solution)/shard_map/reduce_scatter | solution.py:627
  45.5 14.9 %collective-permute-start = (bf16[128,2048]{1,0:T(8,128)(2,1)S(1)}, bf16[128,2048]{1,0:T(8,128)(2,1)S(1)}, u32[]{:S(2)}, u32[]{:S(2)}) collective-permute-start(bf16[128,2048]{1,0:T(8,128)(2,1)S(1)} %copy-done.6), channel_id=1, source_target_pairs={{0,8},{8,0},{16,24},{24,16},{1,9},{9,1},{17,25},{25,17},{2,10},{10... | collective-permute-start | bytes 1572872 | tf_op jit(solution)/shard_map/ppermute | solution.py:582
  46.5 15.4 %collective-permute-start.3 = (bf16[128,2048]{1,0:T(8,128)(2,1)S(1)}, bf16[128,2048]{1,0:T(8,128)(2,1)S(1)}, u32[]{:S(2)}, u32[]{:S(2)}) collective-permute-start(bf16[128,2048]{1,0:T(8,128)(2,1)S(1)} %copy-done.7), channel_id=1, source_target_pairs={{0,16},{8,24},{16,0},{24,8},{1,17},{9,25},{17,1},{25,9},{2,18},{10... | collective-permute-start | bytes 1572872 | tf_op jit(solution)/shard_map/ppermute | solution.py:582
  47.9 24.7 %collective-permute-start.2 = (bf16[128,2048]{1,0:T(8,128)(2,1)S(1)}, bf16[128,2048]{1,0:T(8,128)(2,1)S(1)}, u32[]{:S(2)}, u32[]{:S(2)}) collective-permute-start(bf16[128,2048]{1,0:T(8,128)(2,1)S(1)} %copy-done.6), channel_id=1, source_target_pairs={{0,16},{8,24},{16,0},{24,8},{1,17},{9,25},{17,1},{25,9},{2,18},{10... | collective-permute-start | bytes 1572872 | tf_op jit(solution)/shard_map/ppermute | solution.py:582
  48.5 24.1 %collective-permute-start.1 = (bf16[128,2048]{1,0:T(8,128)(2,1)S(1)}, bf16[128,2048]{1,0:T(8,128)(2,1)S(1)}, u32[]{:S(2)}, u32[]{:S(2)}) collective-permute-start(bf16[128,2048]{1,0:T(8,128)(2,1)S(1)} %copy-done.7), channel_id=1, source_target_pairs={{0,8},{8,0},{16,24},{24,16},{1,9},{9,1},{17,25},{25,17},{2,10},{10... | collective-permute-start | bytes 1572872 | tf_op jit(solution)/shard_map/ppermute | solution.py:582
  60.4 30.8 %collective-permute-start.4 = (bf16[128,2048]{1,0:T(8,128)(2,1)S(1)}, bf16[128,2048]{1,0:T(8,128)(2,1)S(1)}, u32[]{:S(2)}, u32[]{:S(2)}) collective-permute-start(bf16[128,2048]{1,0:T(8,128)(2,1)S(1)} %collective-permute-done.refs_2_), channel_id=1, source_target_pairs={{0,16},{8,24},{16,0},{24,8},{1,17},{9,25},{17,1},{25,9},{2,18},{10... | collective-permute-start | bytes 1572872 | tf_op jit(solution)/shard_map/ppermute | solution.py:582
  61.9 29.3 %collective-permute-start.5 = (bf16[128,2048]{1,0:T(8,128)(2,1)S(1)}, bf16[128,2048]{1,0:T(8,128)(2,1)S(1)}, u32[]{:S(2)}, u32[]{:S(2)}) collective-permute-start(bf16[128,2048]{1,0:T(8,128)(2,1)S(1)} %collective-permute-done.3.refs_5_), channel_id=1, source_target_pairs={{0,8},{8,0},{16,24},{24,16},{1,9},{9,1},{17,25},{25,17},{2,10},{10... | collective-permute-start | bytes 1572872 | tf_op jit(solution)/shard_map/ppermute | solution.py:582
  91.3 40.8 %collective-permute-start.14 = (bf16[256,2048]{1,0:T(8,128)(2,1)S(1)}, bf16[256,2048]{1,0:T(8,128)(2,1)S(1)}, u32[]{:S(2)}, u32[]{:S(2)}) collective-permute-start(bf16[256,2048]{1,0:T(8,128)(2,1)S(1)} %bitcast.89), channel_id=1, source_target_pairs={{0,24},{8,16},{16,8},{24,0},{1,25},{9,17},{17,9},{25,1},{2,26},{10... | collective-permute-start | bytes 3145736 | tf_op jit(solution)/shard_map/ppermute | solution.py:582
  93.2 38.9 %collective-permute-start.13 = (bf16[256,2048]{1,0:T(8,128)(2,1)S(1)}, bf16[256,2048]{1,0:T(8,128)(2,1)S(1)}, u32[]{:S(2)}, u32[]{:S(2)}) collective-permute-start(bf16[256,2048]{1,0:T(8,128)(2,1)S(1)} %bitcast.90), channel_id=1, source_target_pairs={{0,16},{8,24},{16,0},{24,8},{1,17},{9,25},{17,1},{25,9},{2,18},{10... | collective-permute-start | bytes 3145736 | tf_op jit(solution)/shard_map/ppermute | solution.py:582
  93.5 38.6 %collective-permute-start.12 = (bf16[256,2048]{1,0:T(8,128)(2,1)S(1)}, bf16[256,2048]{1,0:T(8,128)(2,1)}, u32[]{:S(2)}, u32[]{:S(2)}) collective-permute-start(bf16[256,2048]{1,0:T(8,128)(2,1)S(1)} %bitcast.91), channel_id=1, source_target_pairs={{0,8},{8,0},{16,24},{24,16},{1,9},{9,1},{17,25},{25,17},{2,10},{10... | collective-permute-start | bytes 3145736 | tf_op jit(solution)/shard_map/ppermute | solution.py:582
  143.1 14.5 %collective-permute-start.15 = (bf16[128,2048]{1,0:T(8,128)(2,1)}, bf16[128,2048]{1,0:T(8,128)(2,1)S(1)}, u32[]{:S(2)}, u32[]{:S(2)}) collective-permute-start(bf16[128,2048]{1,0:T(8,128)(2,1)} %get-tuple-element.106), channel_id=1, source_target_pairs={{0,16},{8,24},{16,0},{24,8},{1,17},{9,25},{17,1},{25,9},{2,18},{10... | collective-permute-start | bytes 1572872 | tf_op jit(solution)/shard_map/ppermute | solution.py:582
  143.5 16.6 %collective-permute-start.18 = (bf16[128,2048]{1,0:T(8,128)(2,1)}, bf16[128,2048]{1,0:T(8,128)(2,1)S(1)}, u32[]{:S(2)}, u32[]{:S(2)}) collective-permute-start(bf16[128,2048]{1,0:T(8,128)(2,1)} %get-tuple-element.110), channel_id=1, source_target_pairs={{0,8},{8,0},{16,24},{24,16},{1,9},{9,1},{17,25},{25,17},{2,10},{10... | collective-permute-start | bytes 1572872 | tf_op jit(solution)/shard_map/ppermute | solution.py:582
  152.8 18.5 %collective-permute-start.17 = (bf16[128,2048]{1,0:T(8,128)(2,1)S(1)}, bf16[128,2048]{1,0:T(8,128)(2,1)S(1)}, u32[]{:S(2)}, u32[]{:S(2)}) collective-permute-start(bf16[128,2048]{1,0:T(8,128)(2,1)S(1)} %add_convert_fusion.5), channel_id=1, source_target_pairs={{0,8},{8,0},{16,24},{24,16},{1,9},{9,1},{17,25},{25,17},{2,10},{10... | collective-permute-start | bytes 1572872 | tf_op jit(solution)/shard_map/ppermute | solution.py:582
  153.4 17.9 %collective-permute-start.20 = (bf16[128,2048]{1,0:T(8,128)(2,1)S(1)}, bf16[128,2048]{1,0:T(8,128)(2,1)S(1)}, u32[]{:S(2)}, u32[]{:S(2)}) collective-permute-start(bf16[128,2048]{1,0:T(8,128)(2,1)S(1)} %add_convert_fusion.4), channel_id=1, source_target_pairs={{0,16},{8,24},{16,0},{24,8},{1,17},{9,25},{17,1},{25,9},{2,18},{10... | collective-permute-start | bytes 1572872 | tf_op jit(solution)/shard_map/ppermute | solution.py:582
  177.7 14.8 %collective-permute-start.23 = (bf16[128,2048]{1,0:T(8,128)(2,1)}, bf16[128,2048]{1,0:T(8,128)(2,1)S(1)}, u32[]{:S(2)}, u32[]{:S(2)}) collective-permute-start(bf16[128,2048]{1,0:T(8,128)(2,1)} %get-tuple-element.128.refs_0_), channel_id=1, source_target_pairs={{0,16},{8,24},{16,0},{24,8},{1,17},{9,25},{17,1},{25,9},{2,18},{10... | collective-permute-start | bytes 1572872 | tf_op jit(solution)/shard_map/ppermute | solution.py:582
  230.9 210.4 %reduce-scatter.6.cloned.1.call-start = ((), (), s32[]{:S(2)}) async-start(), calls=%async_computation.7 | async-start | bytes 12976128 | tf_op jit(solution)/shard_map/reduce_scatter | solution.py:627
  276.0 14.3 %collective-permute-start.27 = (bf16[128,2048]{1,0:T(8,128)(2,1)}, bf16[128,2048]{1,0:T(8,128)(2,1)S(1)}, u32[]{:S(2)}, u32[]{:S(2)}) collective-permute-start(bf16[128,2048]{1,0:T(8,128)(2,1)} %get-tuple-element.126), channel_id=1, source_target_pairs={{0,16},{8,24},{16,0},{24,8},{1,17},{9,25},{17,1},{25,9},{2,18},{10... | collective-permute-start | bytes 1572872 | tf_op jit(solution)/shard_map/ppermute | solution.py:582
  277.6 14.0 %collective-permute-start.28 = (bf16[128,2048]{1,0:T(8,128)(2,1)}, bf16[128,2048]{1,0:T(8,128)(2,1)S(1)}, u32[]{:S(2)}, u32[]{:S(2)}) collective-permute-start(bf16[128,2048]{1,0:T(8,128)(2,1)} %get-tuple-element.127), channel_id=1, source_target_pairs={{0,8},{8,0},{16,24},{24,16},{1,9},{9,1},{17,25},{25,17},{2,10},{10... | collective-permute-start | bytes 1572872 | tf_op jit(solution)/shard_map/ppermute | solution.py:582
  309.9 200.5 %reduce-scatter.8.cloned.1.call-start = ((), (), s32[]{:S(2)}) async-start(), calls=%async_computation.8 | async-start | bytes 5308416 | tf_op jit(solution)/shard_map/reduce_scatter | solution.py:627
  309.9 17.6 %collective-permute-start.29 = (bf16[128,2048]{1,0:T(8,128)(2,1)}, bf16[128,2048]{1,0:T(8,128)(2,1)S(1)}, u32[]{:S(2)}, u32[]{:S(2)}) collective-permute-start(bf16[128,2048]{1,0:T(8,128)(2,1)} %get-tuple-element.133), channel_id=1, source_target_pairs={{0,16},{8,24},{16,0},{24,8},{1,17},{9,25},{17,1},{25,9},{2,18},{10... | collective-permute-start | bytes 1572872 | tf_op jit(solution)/shard_map/ppermute | solution.py:582
  310.5 17.1 %collective-permute-start.31 = (bf16[128,2048]{1,0:T(8,128)(2,1)}, bf16[128,2048]{1,0:T(8,128)(2,1)S(1)}, u32[]{:S(2)}, u32[]{:S(2)}) collective-permute-start(bf16[128,2048]{1,0:T(8,128)(2,1)} %get-tuple-element.136), channel_id=1, source_target_pairs={{0,8},{8,0},{16,24},{24,16},{1,9},{9,1},{17,25},{25,17},{2,10},{10... | collective-permute-start | bytes 1572872 | tf_op jit(solution)/shard_map/ppermute | solution.py:582
  312.9 21.8 %collective-permute-start.30 = (bf16[128,2048]{1,0:T(8,128)(2,1)}, bf16[128,2048]{1,0:T(8,128)(2,1)S(1)}, u32[]{:S(2)}, u32[]{:S(2)}) collective-permute-start(bf16[128,2048]{1,0:T(8,128)(2,1)} %add_convert_fusion.3), channel_id=1, source_target_pairs={{0,8},{8,0},{16,24},{24,16},{1,9},{9,1},{17,25},{25,17},{2,10},{10... | collective-permute-start | bytes 1572872 | tf_op jit(solution)/shard_map/ppermute | solution.py:582
  313.6 21.2 %collective-permute-start.32 = (bf16[128,2048]{1,0:T(8,128)(2,1)S(1)}, bf16[128,2048]{1,0:T(8,128)(2,1)S(1)}, u32[]{:S(2)}, u32[]{:S(2)}) collective-permute-start(bf16[128,2048]{1,0:T(8,128)(2,1)S(1)} %add_convert_fusion.2), channel_id=1, source_target_pairs={{0,16},{8,24},{16,0},{24,8},{1,17},{9,25},{17,1},{25,9},{2,18},{10... | collective-permute-start | bytes 1572872 | tf_op jit(solution)/shard_map/ppermute | solution.py:582
  341.5 15.1 %collective-permute-start.33 = (bf16[128,2048]{1,0:T(8,128)(2,1)}, bf16[128,2048]{1,0:T(8,128)(2,1)S(1)}, u32[]{:S(2)}, u32[]{:S(2)}) collective-permute-start(bf16[128,2048]{1,0:T(8,128)(2,1)} %get-tuple-element.138.refs_0_.refs_8_), channel_id=1, source_target_pairs={{0,8},{8,0},{16,24},{24,16},{1,9},{9,1},{17,25},{25,17},{2,10},{10... | collective-permute-start | bytes 1572872 | tf_op jit(solution)/shard_map/ppermute | solution.py:582
  343.0 15.1 %collective-permute-start.36 = (bf16[128,2048]{1,0:T(8,128)(2,1)}, bf16[128,2048]{1,0:T(8,128)(2,1)S(1)}, u32[]{:S(2)}, u32[]{:S(2)}) collective-permute-start(bf16[128,2048]{1,0:T(8,128)(2,1)} %get-tuple-element.139.refs_1_.refs_9_), channel_id=1, source_target_pairs={{0,16},{8,24},{16,0},{24,8},{1,17},{9,25},{17,1},{25,9},{2,18},{10... | collective-permute-start | bytes 1572872 | tf_op jit(solution)/shard_map/ppermute | solution.py:582
  344.4 24.9 %collective-permute-start.35 = (bf16[128,2048]{1,0:T(8,128)(2,1)}, bf16[128,2048]{1,0:T(8,128)(2,1)S(1)}, u32[]{:S(2)}, u32[]{:S(2)}) collective-permute-start(bf16[128,2048]{1,0:T(8,128)(2,1)} %get-tuple-element.138.refs_0_.refs_8_), channel_id=1, source_target_pairs={{0,16},{8,24},{16,0},{24,8},{1,17},{9,25},{17,1},{25,9},{2,18},{10... | collective-permute-start | bytes 1572872 | tf_op jit(solution)/shard_map/ppermute | solution.py:582
  345.0 24.3 %collective-permute-start.34 = (bf16[128,2048]{1,0:T(8,128)(2,1)}, bf16[128,2048]{1,0:T(8,128)(2,1)S(1)}, u32[]{:S(2)}, u32[]{:S(2)}) collective-permute-start(bf16[128,2048]{1,0:T(8,128)(2,1)} %get-tuple-element.139.refs_1_.refs_9_), channel_id=1, source_target_pairs={{0,8},{8,0},{16,24},{24,16},{1,9},{9,1},{17,25},{25,17},{2,10},{10... | collective-permute-start | bytes 1572872 | tf_op jit(solution)/shard_map/ppermute | solution.py:582
  356.6 20.9 %collective-permute-start.37 = (bf16[128,2048]{1,0:T(8,128)(2,1)S(1)}, bf16[128,2048]{1,0:T(8,128)(2,1)S(1)}, u32[]{:S(2)}, u32[]{:S(2)}) collective-permute-start(bf16[128,2048]{1,0:T(8,128)(2,1)S(1)} %collective-permute-done.33.refs_2_.refs_10_), channel_id=1, source_target_pairs={{0,16},{8,24},{16,0},{24,8},{1,17},{9,25},{17,1},{25,9},{2,18},{10... | collective-permute-start | bytes 1572872 | tf_op jit(solution)/shard_map/ppermute | solution.py:582
  358.0 19.4 %collective-permute-start.38 = (bf16[128,2048]{1,0:T(8,128)(2,1)S(1)}, bf16[128,2048]{1,0:T(8,128)(2,1)S(1)}, u32[]{:S(2)}, u32[]{:S(2)}) collective-permute-start(bf16[128,2048]{1,0:T(8,128)(2,1)S(1)} %collective-permute-done.36.refs_5_.refs_13_), channel_id=1, source_target_pairs={{0,8},{8,0},{16,24},{24,16},{1,9},{9,1},{17,25},{25,17},{2,10},{10... | collective-permute-start | bytes 1572872 | tf_op jit(solution)/shard_map/ppermute | solution.py:582
  377.4 15.1 %collective-permute-start.39 = (bf16[128,2048]{1,0:T(8,128)(2,1)}, bf16[128,2048]{1,0:T(8,128)(2,1)S(1)}, u32[]{:S(2)}, u32[]{:S(2)}) collective-permute-start(bf16[128,2048]{1,0:T(8,128)(2,1)} %get-tuple-element.154), channel_id=1, source_target_pairs={{0,8},{8,0},{16,24},{24,16},{1,9},{9,1},{17,25},{25,17},{2,10},{10... | collective-permute-start | bytes 1572872 | tf_op jit(solution)/shard_map/ppermute | solution.py:582
  378.1 50.7 %collective-permute-start.40 = (bf16[128,2048]{1,0:T(8,128)(2,1)}, bf16[128,2048]{1,0:T(8,128)(2,1)}, u32[]{:S(2)}, u32[]{:S(2)}) collective-permute-start(bf16[128,2048]{1,0:T(8,128)(2,1)} %get-tuple-element.155), channel_id=1, source_target_pairs={{0,16},{8,24},{16,0},{24,8},{1,17},{9,25},{17,1},{25,9},{2,18},{10... | collective-permute-start | bytes 1572872 | tf_op jit(solution)/shard_map/ppermute | solution.py:582
  379.4 49.4 %collective-permute-start.41 = (bf16[128,2048]{1,0:T(8,128)(2,1)}, bf16[128,2048]{1,0:T(8,128)(2,1)}, u32[]{:S(2)}, u32[]{:S(2)}) collective-permute-start(bf16[128,2048]{1,0:T(8,128)(2,1)} %get-tuple-element.156), channel_id=1, source_target_pairs={{0,24},{8,16},{16,8},{24,0},{1,25},{9,17},{17,9},{25,1},{2,26},{10... | collective-permute-start | bytes 1572872 | tf_op jit(solution)/shard_map/ppermute | solution.py:582
  381.0 47.8 %collective-permute-start.42 = (bf16[128,2048]{1,0:T(8,128)(2,1)}, bf16[128,2048]{1,0:T(8,128)(2,1)}, u32[]{:S(2)}, u32[]{:S(2)}) collective-permute-start(bf16[128,2048]{1,0:T(8,128)(2,1)} %get-tuple-element.158), channel_id=1, source_target_pairs={{0,8},{8,0},{16,24},{24,16},{1,9},{9,1},{17,25},{25,17},{2,10},{10... | collective-permute-start | bytes 1572872 | tf_op jit(solution)/shard_map/ppermute | solution.py:582
  381.6 47.2 %collective-permute-start.43 = (bf16[128,2048]{1,0:T(8,128)(2,1)}, bf16[128,2048]{1,0:T(8,128)(2,1)}, u32[]{:S(2)}, u32[]{:S(2)}) collective-permute-start(bf16[128,2048]{1,0:T(8,128)(2,1)} %get-tuple-element.159), channel_id=1, source_target_pairs={{0,16},{8,24},{16,0},{24,8},{1,17},{9,25},{17,1},{25,9},{2,18},{10... | collective-permute-start | bytes 1572872 | tf_op jit(solution)/shard_map/ppermute | solution.py:582
  392.6 36.2 %collective-permute-start.44 = (bf16[128,2048]{1,0:T(8,128)(2,1)}, bf16[128,2048]{1,0:T(8,128)(2,1)}, u32[]{:S(2)}, u32[]{:S(2)}) collective-permute-start(bf16[128,2048]{1,0:T(8,128)(2,1)} %get-tuple-element.160), channel_id=1, source_target_pairs={{0,24},{8,16},{16,8},{24,0},{1,25},{9,17},{17,9},{25,1},{2,26},{10... | collective-permute-start | bytes 1572872 | tf_op jit(solution)/shard_map/ppermute | solution.py:582
  450.5 15.1 %collective-permute-start.46 = (bf16[128,2048]{1,0:T(8,128)(2,1)}, bf16[128,2048]{1,0:T(8,128)(2,1)S(1)}, u32[]{:S(2)}, u32[]{:S(2)}) collective-permute-start(bf16[128,2048]{1,0:T(8,128)(2,1)} %get-tuple-element.176), channel_id=1, source_target_pairs={{0,16},{8,24},{16,0},{24,8},{1,17},{9,25},{17,1},{25,9},{2,18},{10... | collective-permute-start | bytes 1572872 | tf_op jit(solution)/shard_map/ppermute | solution.py:582
  451.3 17.2 %collective-permute-start.49 = (bf16[128,2048]{1,0:T(8,128)(2,1)}, bf16[128,2048]{1,0:T(8,128)(2,1)S(1)}, u32[]{:S(2)}, u32[]{:S(2)}) collective-permute-start(bf16[128,2048]{1,0:T(8,128)(2,1)} %get-tuple-element.180), channel_id=1, source_target_pairs={{0,8},{8,0},{16,24},{24,16},{1,9},{9,1},{17,25},{25,17},{2,10},{10... | collective-permute-start | bytes 1572872 | tf_op jit(solution)/shard_map/ppermute | solution.py:582
  452.8 28.0 %collective-permute-start.45 = (bf16[128,2048]{1,0:T(8,128)(2,1)}, bf16[128,2048]{1,0:T(8,128)(2,1)S(1)}, u32[]{:S(2)}, u32[]{:S(2)}) collective-permute-start(bf16[128,2048]{1,0:T(8,128)(2,1)} %get-tuple-element.174), channel_id=1, source_target_pairs={{0,16},{8,24},{16,0},{24,8},{1,17},{9,25},{17,1},{25,9},{2,18},{10... | collective-permute-start | bytes 1572872 | tf_op jit(solution)/shard_map/ppermute | solution.py:582
  454.1 27.4 %collective-permute-start.48 = (bf16[128,2048]{1,0:T(8,128)(2,1)}, bf16[128,2048]{1,0:T(8,128)(2,1)S(1)}, u32[]{:S(2)}, u32[]{:S(2)}) collective-permute-start(bf16[128,2048]{1,0:T(8,128)(2,1)} %get-tuple-element.178), channel_id=1, source_target_pairs={{0,8},{8,0},{16,24},{24,16},{1,9},{9,1},{17,25},{25,17},{2,10},{10... | collective-permute-start | bytes 1572872 | tf_op jit(solution)/shard_map/ppermute | solution.py:582
  467.0 21.6 %collective-permute-start.47 = (bf16[128,2048]{1,0:T(8,128)(2,1)S(1)}, bf16[128,2048]{1,0:T(8,128)(2,1)S(1)}, u32[]{:S(2)}, u32[]{:S(2)}) collective-permute-start(bf16[128,2048]{1,0:T(8,128)(2,1)S(1)} %add_convert_fusion.1), channel_id=1, source_target_pairs={{0,8},{8,0},{16,24},{24,16},{1,9},{9,1},{17,25},{25,17},{2,10},{10... | collective-permute-start | bytes 1572872 | tf_op jit(solution)/shard_map/ppermute | solution.py:582
  468.6 20.0 %collective-permute-start.50 = (bf16[128,2048]{1,0:T(8,128)(2,1)S(1)}, bf16[128,2048]{1,0:T(8,128)(2,1)S(1)}, u32[]{:S(2)}, u32[]{:S(2)}) collective-permute-start(bf16[128,2048]{1,0:T(8,128)(2,1)S(1)} %add_convert_fusion), channel_id=1, source_target_pairs={{0,16},{8,24},{16,0},{24,8},{1,17},{9,25},{17,1},{25,9},{2,18},{10... | collective-permute-start | bytes 1572872 | tf_op jit(solution)/shard_map/ppermute | solution.py:582
  470.4 24.8 %collective-permute-start.56 = (bf16[64,2816]{1,0:T(8,128)(2,1)}, bf16[64,2816]{1,0:T(8,128)(2,1)}, u32[]{:S(2)}, u32[]{:S(2)}) collective-permute-start(bf16[64,2816]{1,0:T(8,128)(2,1)} %get-tuple-element.194), channel_id=1, source_target_pairs={{0,24},{8,16},{16,8},{24,0},{1,25},{9,17},{17,9},{25,1},{2,26},{10... | collective-permute-start | bytes 1081352 | tf_op jit(solution)/shard_map/ppermute | solution.py:582
  480.8 14.4 %collective-permute-start.55 = (bf16[64,2816]{1,0:T(8,128)(2,1)}, bf16[64,2816]{1,0:T(8,128)(2,1)}, u32[]{:S(2)}, u32[]{:S(2)}) collective-permute-start(bf16[64,2816]{1,0:T(8,128)(2,1)} %get-tuple-element.195), channel_id=1, source_target_pairs={{0,16},{8,24},{16,0},{24,8},{1,17},{9,25},{17,1},{25,9},{2,18},{10... | collective-permute-start | bytes 1081352 | tf_op jit(solution)/shard_map/ppermute | solution.py:582
  (68 other events, 728.6 us)
Sparse Core Ops, SparseCore 0:
  21.3 51.1 all-gather.3
  74.7 106.8 all-gather.5
  183.2 58.7 all-gather.7
  244.2 63.5 reduce-scatter.3
  310.0 117.5 reduce-scatter.5
  441.4 53.0 reduce-scatter.7

commit v3 on v2

--- a/solution.py
+++ b/solution.py
@@ -6,6 +6,7 @@
 from jax import lax
 from jax.experimental import pallas as pl
 from jax.experimental.pallas import tpu as pltpu
+from jax.sharding import Mesh
 from jax.sharding import PartitionSpec as P
 
 HEADS = 32
@@ -15,6 +16,7 @@
 GROUP = HEADS // KV_HEADS
 EPSILON = 1e-05
 SCALE = 1.0 / math.sqrt(HEAD_DIM)
+FSDP = ("chip", "core")
 LOW = jnp.bfloat16
 FULL = jnp.float32
 VMEM = pl.BlockSpec(memory_space=pltpu.VMEM)
@@ -67,11 +69,12 @@
     return pltpu.SemaphoreType.DMA((count,))
 
 
-def call_own(kernel, out_shape, *args):
-    return pl.pallas_call(
-        kernel, out_shape=out_shape, in_specs=[VMEM] * len(args),
-        out_specs=jax.tree.map(lambda _: VMEM, out_shape), compiler_params=PARAMS, name=kernel.func.__name__,
-    )(*args)
+def call_own(kernel, out_shape, *args, scalars=()):
+    return pl.pallas_call(
+        kernel, out_shape=out_shape, in_specs=[SMEM] * len(scalars) + [VMEM] * len(args),
+        out_specs=jax.tree.map(lambda _: VMEM, out_shape), compiler_params=PARAMS,
+        name=getattr(kernel, "func", kernel).__name__,
+    )(*scalars, *args)
 
 
 def added(refs):
@@ -104,8 +107,8 @@
 
 def grad_middle_kernel(grid, parts, *refs):
     upstream_ref, middle_ref, inv_ref, refs = refs[0], refs[1], refs[2], refs[3:]
+    out_ref, *low_refs = refs[-1 - parts:]
     per = (len(refs) - 1 - parts) // parts
-    out_ref, *low_refs = refs[per * parts:]
     rows = low_refs[0].shape[0]
     for i in range(parts):
         at = slice(i * rows, (i + 1) * rows)
@@ -129,13 +132,54 @@
         out_ref[at, :] = grad_ref[at, :] + grad - normed * jnp.mean(grad * normed, -1, keepdims=True)
 
 
-def block_out_kernel(parts, *refs):
-    middle_ref, refs, out_ref = refs[0], refs[1:-1], refs[-1]
-    per = len(refs) // parts
-    rows = out_ref.shape[0] // parts
-    for i in range(parts):
-        at = slice(i * rows, (i + 1) * rows)
-        out_ref[at, :] = (middle_ref[at, :] + added(refs[i * per:(i + 1) * per])).astype(LOW)
+def block_out_kernel(middle_ref, *refs):
+    refs[-1][...] = (middle_ref[...] + added(refs[:-1])).astype(LOW)
+
+
+def as_row(column):
+    return jnp.broadcast_to(column, (column.shape[0], 128)).T[:1]
+
+
+def finish_gate_up_kernel(here_ref, *refs):
+    *pieces, gate_ref, up_ref, gain_ref, grad_gate_ref, grad_up_ref, grad_gain_ref = refs
+    gain, total = gain_ref[...], 0.0
+    across, chunk = gate_ref.shape[1] // len(pieces), 128
+    for j, piece in enumerate(pieces):
+        first = (here_ref[0] ^ j) * across
+        for c in range(across // chunk):
+            there = pl.ds(pl.multiple_of(first + c * chunk, chunk), chunk)
+            for i, (weight_ref, out_ref) in enumerate(((gate_ref, grad_gate_ref), (up_ref, grad_up_ref))):
+                grad = piece[:, (2 * c + i) * chunk:(2 * c + i + 1) * chunk].astype(FULL)
+                out_ref[:, there] = grad * gain
+                total = total + grad * weight_ref[:, there].astype(FULL)
+    grad_gain_ref[...] = as_row(jnp.sum(total, 1, keepdims=True))
+
+
+def finish_projections_kernel(here_ref, *refs):
+    *pieces, own_ref, query_ref, key_ref, value_ref, gain_ref = refs[:-5]
+    grad_query_ref, grad_key_ref, grad_value_ref, grad_output_ref, grad_gain_ref = refs[-5:]
+    gain, count = gain_ref[...], len(pieces)
+    rows = gain.shape[0]
+    qw, kw = query_ref.shape[1] // count, key_ref.shape[1] // count
+    total = 0.0
+    for j, piece in enumerate(pieces):
+        there = pl.ds(pl.multiple_of((here_ref[0] ^ j) * qw, qw), qw)
+        grad = piece[:, :qw].astype(FULL)
+        grad_query_ref[:, there] = grad * gain
+        total = total + jnp.sum(grad * query_ref[:, there].astype(FULL), 1, keepdims=True)
+    for first, weight_ref, out_ref in ((qw, key_ref, grad_key_ref), (qw + kw, value_ref, grad_value_ref)):
+        grad = [jnp.zeros((rows, kw), FULL)] * count
+        for j, piece in enumerate(pieces):
+            mine = piece[:, first:first + kw].astype(FULL)
+            for t in range(count):
+                grad[t] = jnp.where(here_ref[0] == t ^ j, mine, grad[t])
+        grad = jnp.concatenate(grad, 1)
+        out_ref[...] = grad * gain
+        total = total + jnp.sum(grad * weight_ref[...].astype(FULL), 1, keepdims=True)
+    across = grad_output_ref.shape[1] // count
+    for part in range(count):
+        grad_output_ref[:, part * across:(part + 1) * across] = own_ref[part * rows:(part + 1) * rows, :across].astype(FULL)
+    grad_gain_ref[...] = as_row(total)
 
 
 def rows_of(pieces):
@@ -176,9 +220,9 @@
         functools.partial(hidden_kernel, len(pieces), chunk),
         grid=(both // (2 * chunk),),
         in_specs=[ANY] * len(pieces) + [columns(width, 2 * chunk)],
-        out_specs=(columns(tokens, 2 * chunk), by_rows(chunk, tokens)),
-        out_shape=(like((tokens, both)), like((both // 2, tokens))),
-        scratch_shapes=[pltpu.VMEM((tokens, width), LOW), arrivals(len(pieces))],
+        out_specs=(columns(tokens, 2 * chunk), by_rows(chunk, tokens), whole((tokens, width))),
+        out_shape=(like((tokens, both)), like((both // 2, tokens)), like((tokens, width))),
+        scratch_shapes=[arrivals(len(pieces))],
         compiler_params=PARAMS,
         name="hidden_of",
     )(*pieces, weight)
@@ -204,33 +248,20 @@
     )(*pieces, hidden)
 
 
-def grad_gate_up_kernel(count, chunk, places_ref, *refs):
-    pieces, refs = refs[:count], refs[count:]
-    *blocks, slope_ref, out_ref, down_ref, upstream_ref, sems, block_sems = refs
+def grad_gate_up_kernel(count, chunk, odd, *refs):
+    pieces, (down_ref, slope_ref, out_ref, upstream_ref, sems) = refs[:count], refs[count:]
     step, steps = pl.program_id(0), pl.num_programs(0)
 
     @pl.when(step == 0)
     def _():
-        copies = []
-        for i, block in enumerate(blocks):
-            rows = block.shape[0]
-            there = pl.ds(pl.multiple_of(places_ref[i] * rows, math.gcd(rows, 16)), rows)
-            copies.append(pltpu.make_async_copy(block, down_ref.at[there], block_sems.at[i]))
-        for copy in copies:
-            copy.start()
         fetch(pieces, upstream_ref, sems)
-        for copy in copies:
-            copy.wait()
 
     def work(chunks):
-        rows = pl.ds(pl.multiple_of(step * 2 * chunk, 2 * chunk), chunks * chunk)
-        grad = dot(upstream_ref[...], down_ref[rows, :], NT)
+        grad = dot(upstream_ref[...], down_ref[:chunks * chunk, :], NT)
         each = [grad[:, c * chunk:(c + 1) * chunk] for c in range(chunks) for _ in range(2)]
         width = chunks * 2 * chunk
         out_ref[:, :width] = (jnp.concatenate(each, 1) * slope_ref[:, :width].astype(FULL)).astype(LOW)
 
-    odd = down_ref.shape[0] // chunk % 2
-
     @pl.when(step < steps - odd)
     def _():
         work(2)
@@ -242,19 +273,18 @@
             work(1)
 
 
-def grad_gate_up_of(pieces, places, blocks, slope, chunk):
-    tokens, width = rows_of(pieces), pieces[0].shape[1]
-    depth = rows_of(blocks)
-    return pl.pallas_call(
-        functools.partial(grad_gate_up_kernel, len(pieces), chunk),
+def grad_gate_up_of(pieces, down, slope, chunk):
+    (tokens, width), depth = (rows_of(pieces), pieces[0].shape[1]), down.shape[0]
+    return pl.pallas_call(
+        functools.partial(grad_gate_up_kernel, len(pieces), chunk, depth // chunk % 2),
         grid=(pl.cdiv(depth, 2 * chunk),),
-        in_specs=[SMEM] + [ANY] * (len(pieces) + len(blocks)) + [columns(tokens, 4 * chunk)],
-        out_specs=(columns(tokens, 4 * chunk), whole((depth, width))),
-        out_shape=(like(slope.shape), like((depth, width))),
-        scratch_shapes=[pltpu.VMEM((tokens, width), LOW), arrivals(len(pieces)), arrivals(len(blocks))],
+        in_specs=[ANY] * len(pieces) + [by_rows(2 * chunk, width), columns(tokens, 4 * chunk)],
+        out_specs=columns(tokens, 4 * chunk),
+        out_shape=like(slope.shape),
+        scratch_shapes=[pltpu.VMEM((tokens, width), LOW), arrivals(len(pieces))],
         compiler_params=PARAMS,
         name="grad_gate_up_of",
-    )(places, *pieces, *blocks, slope)
+    )(*pieces, down, slope)
 
 
 def grad_rows_kernel(first, grad_ref, weight_ref, *out_refs):
@@ -264,7 +294,7 @@
         ref[...] = grad[i * rows:(i + 1) * rows]
 
 
-def grad_rows_of(grad, weight, piece_rows, block=256):
+def grad_rows_of(grad, weight, piece_rows, block=512):
     tokens, width = grad.shape[0], weight.shape[0]
     count = tokens // piece_rows
     return pl.pallas_call(
@@ -278,24 +308,28 @@
     )(grad, weight)
 
 
-def grad_weight_kernel(count, *refs):
-    pieces, (grad_ref, out_ref, block_ref) = refs[:count], refs[count:]
-    join(pieces, block_ref)
-    out_ref[...] = dot(block_ref[...], grad_ref[...], TN).astype(LOW)
-
-
-def grad_weight_of(pieces, grad, block=256):
-    tokens, width = rows_of(pieces), pieces[0].shape[1]
-    return pl.pallas_call(
-        functools.partial(grad_weight_kernel, len(pieces)),
-        grid=(width // block,),
-        in_specs=[columns(p.shape[0], block) for p in pieces] + [whole(grad.shape)],
-        out_specs=by_rows(block, grad.shape[1]),
-        out_shape=like((width, grad.shape[1])),
-        scratch_shapes=[pltpu.VMEM((tokens, block), LOW)],
+def grad_weight_kernel(core_ref, left_ref, other_left_ref, grad_ref, other_grad_ref, out_ref):
+    got = dot(left_ref[...], grad_ref[...], TN) + dot(other_left_ref[...], other_grad_ref[...], TN)
+    out_ref[...] = got.astype(LOW)
+
+
+def grad_weight_of(left, other_left, grad, other_grad, core, chips):
+    tokens, width = left.shape
+    block = width // chips // 2
+    mine = pl.BlockSpec((tokens, block), lambda i, core_ref: (0, i * 2 + core_ref[0]))
+    every = pl.BlockSpec(grad.shape, lambda i, core_ref: (0, 0))
+    return pl.pallas_call(
+        grad_weight_kernel,
+        grid_spec=pltpu.PrefetchScalarGridSpec(
+            num_scalar_prefetch=1,
+            grid=(chips,),
+            in_specs=[mine, mine, every, every],
+            out_specs=pl.BlockSpec((block, grad.shape[1]), lambda i, core_ref: (i, 0)),
+        ),
+        out_shape=like((width // 2, grad.shape[1])),
         compiler_params=PARAMS,
         name="grad_weight_of",
-    )(*pieces, grad)
+    )(core, left, other_left, grad, other_grad)
 
 
 def rows_kernel(left_ref, weight_ref, *refs):
@@ -312,7 +346,7 @@
         ref[...] = out[i * rows:(i + 1) * rows]
 
 
-def rows_of_product(left, weight, piece_rows, inner=None, block=256):
+def rows_of_product(left, weight, piece_rows, inner=None, block=512):
     depth, tokens = left.shape
     count = tokens // piece_rows
     if inner is None:
@@ -320,6 +354,7 @@
     else:
         seq_size, fsdp_size, own_rows = inner
         width = weight.shape[0]
+        block = min(block, width // seq_size)
         per = width // seq_size // block
         weight = weight.reshape(fsdp_size, seq_size, own_rows, -1)
         spec = pl.BlockSpec((fsdp_size, 1, own_rows, block), lambda i: (0, i // per, 0, i % per))
@@ -353,8 +388,9 @@
         out_ref[rows, pl.ds(pl.multiple_of(first, 128), block)] = got[f * own_rows:(f + 1) * own_rows]
 
 
-def attention_weights_of(tokens, grads, grad_qkv, attended, inner, block=256):
+def attention_weights_of(tokens, grads, grad_qkv, attended, inner, block=512):
     count, width = len(tokens), tokens[0].shape[1]
+    block = min(block, width // inner[0])
     shape = (width, grad_qkv.shape[0] + width // inner[0])
     return pl.pallas_call(
         functools.partial(attention_weights_kernel, count, inner),
@@ -596,15 +632,13 @@
         a, b = pieces[::2], pieces[1::2]
         da, db = swap(a[3], 2), swap(b[3], 1)
         ya, xb = swap(a[2], 2), swap(b[1], 1)
-        xa = swap((a[1].astype(FULL) + da.astype(FULL)).astype(LOW), 1)
-        yb = swap((b[2].astype(FULL) + db.astype(FULL)).astype(LOW), 2)
+        da = (a[1].astype(FULL) + da.astype(FULL)).astype(LOW)
+        db = (b[2].astype(FULL) + db.astype(FULL)).astype(LOW)
+        xa, yb = swap(da, 1), swap(db, 2)
         return (da, db), [a[0], ya, xa, b[0], xb, yb]
 
-    def direct_scatter(pieces):
-        if parts == 1:
-            return seq_scatter(pieces)[1]
-        a, b = pieces[::2], pieces[1::2]
-        return [a[0]] + [swap(a[j], j) for j in (1, 2, 3)] + [b[0]] + [swap(b[j], j) for j in (1, 2, 3)]
+    def direct_scatter(blocks):
+        return [blocks[0]] + [swap(blocks[j], j) for j in range(1, seq_size)]
 
     def spread(pieces_for):
         got = [pieces_for(here)] + [swap(pieces_for(here ^ j), j) for j in range(1, seq_size)]
@@ -615,16 +649,25 @@
 
     def collect(x):
         blocks = x.reshape(seq_size, own_rows, x.shape[1])
-        got = jnp.stack([lax.dynamic_index_in_dim(blocks, here, 0, False)] + [
+        return [lax.dynamic_index_in_dim(blocks, here, 0, False)] + [
             swap(lax.dynamic_index_in_dim(blocks, here ^ j, 0, False), j) for j in range(1, seq_size)
-        ])
-        return jnp.stack([lax.dynamic_index_in_dim(got, here ^ t, 0, False) for t in range(seq_size)])
+        ]
+
+    def in_order(got):
+        got = jnp.stack(got)
+        return jnp.stack([lax.dynamic_index_in_dim(got, here ^ t, 0, False) for t in range(seq_size)]).astype(FULL)
 
     def fsdp_gather(x):
-        return lax.all_gather(x, "fsdp", axis=0, tiled=True)
+        return lax.all_gather(x, FSDP, axis=0, tiled=True)
+
+    def exchange(x):
+        return lax.ppermute(x, "core", [(0, 1), (1, 0)])
+
+    def chip_scatter(x):
+        return lax.psum_scatter(x.reshape(-1, x.shape[-1]), "chip", scatter_dimension=0, tiled=True)
 
     def fsdp_scatter(x):
-        return lax.psum_scatter(x, "fsdp", scatter_dimension=0, tiled=True)
+        return lax.psum_scatter(x, FSDP, scatter_dimension=0, tiled=True)
 
     gain_one, gain_two = attn_gain.astype(FULL)[:, None], ffn_gain.astype(FULL)[:, None]
 
@@ -683,17 +726,18 @@
     )
 
     normed_pieces = seq_gather(own_pieces)
-    slope, hidden = hidden_of(normed_pieces, gate_up_full, chunk)
+    slope, hidden, normed = hidden_of(normed_pieces, gate_up_full, chunk)
     part_down = grad_down_of(hidden, upstream)
     grad_down = fsdp_scatter(part_down)
-    grad_gate_up, down_full = grad_gate_up_of(
-        [after(upstream[0], part_down), *upstream[1:]], jnp.zeros((1,), jnp.int32), [down_full], slope, chunk
-    )
+    grad_gate_up = grad_gate_up_of([after(upstream[0], part_down), *upstream[1:]], down_full, slope, chunk)
     first, grad_pieces = seq_scatter(grad_rows_of(grad_gate_up, gate_up_full, piece_rows))
-    part_gate_up = grad_weight_of([after(normed_pieces[0], *first), *normed_pieces[1:]], grad_gate_up)
-    grad_gate_up_own = fsdp_scatter(after(part_gate_up, part_down))
-    out_pieces = rows_of_product(after(hidden, part_gate_up), down_full, piece_rows)
-    grad_pieces[0] = after(grad_pieces[0], out_pieces[0], grad_down)
+    place, core = (at.astype(jnp.int32).reshape(1) for at in (here, lax.axis_index("core")))
+    part_gate_up = grad_weight_of(
+        after(normed, *first), exchange(normed), grad_gate_up, exchange(grad_gate_up), core, fsdp_size // 2
+    )
+    part_gate_up, *grad_pieces = lax.optimization_barrier((part_gate_up, *grad_pieces))
+    grad_gate_up_own = chip_scatter(part_gate_up)
+    grad_pieces[0] = after(grad_pieces[0], grad_down)
     grad_middle, *own_pieces = call_own(
         functools.partial(grad_middle_kernel, back, parts),
         (like((span, width), FULL),) + (like((piece_rows, width)),) * parts,
@@ -701,7 +745,9 @@
     )
 
     branch_pieces = seq_gather(own_pieces)
-    out_pieces = direct_scatter(lax.optimization_barrier((*out_pieces, *branch_pieces))[:len(out_pieces)])
+    out_pieces = rows_of_product(after(hidden, own_pieces[0]), down_full, span)
+    out_pieces = lax.optimization_barrier((*out_pieces, *branch_pieces))[:seq_size]
+    out_pieces = direct_scatter(out_pieces)
     grad_qkv, grad_qkv_turned = attend_back(
         order, rank, branch_pieces, projections.reshape(fsdp_size, seq_size, own_rows, -1), qrot, kv, mix, lse,
         cosine, sine, inv_one, heads, kvs, span,
@@ -709,59 +755,78 @@
     grad_qkv, *out_pieces = lax.optimization_barrier((grad_qkv, *out_pieces))
     part_projections = attention_weights_of(token_pieces, branch_pieces, grad_qkv, attended, into)
     grad_pieces = grad_rows_of(after(grad_qkv_turned, part_projections), projections, piece_rows)
+    grad_projections = fsdp_scatter(after(part_projections, grad_gate_up_own, grad_pieces[0]))
     grad_pieces = seq_scatter(grad_pieces)[1]
-    grad_projections = fsdp_scatter(after(part_projections, grad_gate_up_own))
-    grad_qkv_own = grad_projections[:, -qw - 2 * kw:]
-    grad_output = grad_projections[:, :-qw - 2 * kw].reshape(seq_size, own_rows, -1).swapaxes(0, 1)
-    grad_output = grad_output.reshape(own_rows, width)
-    block_out = call_own(
-        functools.partial(block_out_kernel, parts), like((span, width)), middle, *out_pieces
-    )
+    got = collect(after(grad_gate_up_own, *grad_pieces))
+    block_out = call_own(block_out_kernel, like((span, width)), middle, *out_pieces)
+
+
+    def whole_rows(x):
+        return x.swapaxes(0, 1).reshape(own_rows, -1)
+
+    if chunk == 128:
+        rows_like = like((own_rows, gate_weight.shape[1]), FULL)
+        grad_gate, grad_up, grad_ffn_gain = call_own(
+            finish_gate_up_kernel, (rows_like, rows_like, like((1, own_rows), FULL)),
+            *got, gate_weight, up_weight, gain_two, scalars=(place,),
+        )
+    else:
+        got = in_order(got).reshape(seq_size, own_rows, -1, 2, chunk)
+        grad_gate, grad_up = whole_rows(got[:, :, :, 0]), whole_rows(got[:, :, :, 1])
+        grad_ffn_gain = jnp.sum(grad_gate * gate_weight.astype(FULL) + grad_up * up_weight.astype(FULL), 1)
+        grad_gate, grad_up = grad_gate * gain_two, grad_up * gain_two
     grad_tokens = call_own(
         functools.partial(grad_tokens_kernel, back, parts), like((span, width), FULL),
         own_tokens, grad_middle, *grad_pieces,
     )
-
-    def whole_rows(x):
-        return x.swapaxes(0, 1).reshape(own_rows, -1)
-
-    got = collect(grad_gate_up_own).astype(FULL).reshape(seq_size, own_rows, -1, 2, chunk)
-    grad_gate, grad_up = whole_rows(got[:, :, :, 0]), whole_rows(got[:, :, :, 1])
-    got = collect(grad_qkv_own).astype(FULL)
-    grad_query = whole_rows(got[:, :, :qw])
-
-    def of_heads(x):
-        return whole_rows(x.reshape(seq_size // shared, shared, own_rows, kw).sum(1))
-
-    grad_key, grad_value = of_heads(got[:, :, qw:qw + kw]), of_heads(got[:, :, qw + kw:])
-    grad_attn_gain = (
-        jnp.sum(grad_query * query_weight.astype(FULL), 1)
-        + jnp.sum(grad_key * key_weight.astype(FULL), 1)
-        + jnp.sum(grad_value * value_weight.astype(FULL), 1)
-    )
-    grad_ffn_gain = jnp.sum(grad_gate * gate_weight.astype(FULL), 1) + jnp.sum(grad_up * up_weight.astype(FULL), 1)
+    grad_projections = after(grad_projections, grad_tokens, block_out, grad_ffn_gain)
+    got = collect(grad_projections[:, -qw - 2 * kw:])
+    if shared == 1 and kvs == 1:
+        grad_query, grad_key, grad_value, grad_output, grad_attn_gain = call_own(
+            finish_projections_kernel,
+            tuple(like(w.shape, FULL) for w in (query_weight, key_weight, value_weight, output_weight))
+            + (like((1, own_rows), FULL),),
+            *got, grad_projections, query_weight, key_weight, value_weight, gain_one, scalars=(place,),
+        )
+    else:
+        grad_output = grad_projections[:, :-qw - 2 * kw].reshape(seq_size, own_rows, -1).swapaxes(0, 1)
+        grad_output = grad_output.reshape(own_rows, width).astype(FULL)
+        got = in_order(got)
+        grad_query = whole_rows(got[:, :, :qw])
+
+        def of_heads(x):
+            return whole_rows(x.reshape(seq_size // shared, shared, own_rows, kw).sum(1))
+
+        grad_key, grad_value = of_heads(got[:, :, qw:qw + kw]), of_heads(got[:, :, qw + kw:])
+        grads = (grad_query, grad_key, grad_value)
+        grad_attn_gain = sum(
+            jnp.sum(g * w.astype(FULL), 1) for g, w in zip(grads, (query_weight, key_weight, value_weight))
+        )
+        grad_query, grad_key, grad_value = (g * gain_one for g in grads)
     return (
         block_out[None],
         grad_tokens[None],
-        grad_attn_gain,
-        grad_query * gain_one,
-        grad_key * gain_one,
-        grad_value * gain_one,
-        grad_output.astype(FULL),
-        grad_ffn_gain,
-        grad_gate * gain_two,
-        grad_up * gain_two,
+        grad_attn_gain.reshape(-1),
+        grad_query,
+        grad_key,
+        grad_value,
+        grad_output,
+        grad_ffn_gain.reshape(-1),
+        grad_gate,
+        grad_up,
         grad_down.astype(FULL),
     )
 
 
 def solution(mesh):
-    rows, vector, matrix = P("fsdp", "seq", None), P(("seq", "fsdp")), P(("seq", "fsdp"), None)
+    seq_size, fsdp_size = mesh.shape["seq"], mesh.shape["fsdp"]
+    split = Mesh(mesh.devices.reshape(seq_size, fsdp_size // 2, 2), ("seq", "chip", "core"))
+    rows, vector, matrix = P(FSDP, "seq", None), P(("seq", *FSDP)), P(("seq", *FSDP), None)
     return jax.shard_map(
-        functools.partial(layer, mesh.shape["seq"], mesh.shape["fsdp"]),
-        mesh=mesh,
+        functools.partial(layer, seq_size, fsdp_size),
+        mesh=split,
         in_specs=(
-            rows, P("fsdp", None), vector, matrix, matrix, matrix, matrix, vector, matrix, matrix, matrix, rows,
+            rows, P(FSDP, None), vector, matrix, matrix, matrix, matrix, vector, matrix, matrix, matrix, rows,
         ),
         out_specs=(rows, rows, vector, matrix, matrix, matrix, matrix, vector, matrix, matrix, matrix),
         check_vma=False,

time: 538 us -> 506 us (0.941)
  other arithmetic: 24.5 us -> 12.3 us
  waiting for transfers between devices: 190 us -> 179 us
    all_gather x3, waiting for transfers between devices: 11.1 us -> 0.04 us  [fsdp_gather(): return lax.all_gather(x, FSDP, axis=0, tiled=True)]
    mul x3 -> x0, other arithmetic: 5.69 us -> none  [the longest x1 3.86 us: layer(): grad_up * gain_two]
    pallas_call x7 -> x9, Pallas kernels: 57.9 us -> 63.2 us  [the longest x7 30.2 us: call_own(): pl.pallas_call(kernel, out_shape=out_shape, in_specs=[SMEM] * len(scalars...]
    ppermute x57 -> x54, starting transfers between devices: 64.9 us -> 60.2 us  [swap(): return lax.ppermute(x, 'seq', [(i, i ^ j) for i in range(seq_size)])]
    ppermute x57 -> x54, waiting for transfers between devices: 178 us -> 178 us  [swap(): return lax.ppermute(x, 'seq', [(i, i ^ j) for i in range(seq_size)])]
  transfers between devices with their start and end apart: 63 -> 62, of which waited for: 31 -> 29; matrix products, arithmetic and copies ran while one was open for 5% -> 3% of each run, Pallas kernels for 41% -> 43%
where the time goes in v3:
time: 506 us; the launch traced here: 498 us
  Pallas kernels  219 us (43%)
  waiting for transfers between devices  179 us (35%)
  starting transfers between devices  61 us (12%)
  between operations  15.4 us (3%)
  other arithmetic  12.3 us (2%)
  local copies, waits for them, and re-layouts  12 us (2%)
    ppermute x54, waiting for transfers between devices, swap(): return lax.ppermute(x, 'seq', [(i, i ^ j) for i in range(seq_size)])  178 us
    ppermute x54, starting transfers between devices, swap(): return lax.ppermute(x, 'seq', [(i, i ^ j) for i in range(seq_size)])  60.2 us
    pallas_call x1, Pallas kernels, attend_back(): pl.pallas_call(functools.partial(attend_back_kernel, heads, kvs, span, le...  34.9 us
    pallas_call x1, Pallas kernels, attend(): pl.pallas_call(functools.partial(attend_kernel, heads, kvs, span, len(pie...  34.2 us
    pallas_call x7, Pallas kernels, call_own(): pl.pallas_call(kernel, out_shape=out_shape, in_specs=[SMEM] * len(scalars...  30.2 us
    pallas_call x2, Pallas kernels, grad_rows_of(): pl.pallas_call(functools.partial(grad_rows_kernel, weight.shape[1] - grad...  24.9 us
    pallas_call x1, Pallas kernels, hidden_of(): pl.pallas_call(functools.partial(hidden_kernel, len(pieces), chunk), grid...  21 us
    pallas_call x1, Pallas kernels, grad_weight_of(): pl.pallas_call(grad_weight_kernel, grid_spec=pltpu.PrefetchScalarGridSpec...  18.7 us
  transfers between devices with their start and end apart: 62, of which 29 were waited for; matrix products, arithmetic and copies ran while one was open for 3% of the time, Pallas kernels for 43%

profile of v3, /device:TPU:0, one launch (start us, length us, event | category | flops | bytes accessed | tf_op | source)
XLA Modules:
  0.0 498.1 jit_solution(14117037338170756329)
XLA Ops:
  10.2 3.9 collective-permute-start.8
  15.0 1.7 collective-permute-done.8
  16.7 1.9 collective-permute-done.7
  20.4 2.6 regroup_kernel.1
  24.4 1.6 collective-permute-start.11
  27.9 8.8 %collective-permute-done.11 = bf16[64,2816]{1,0:T(8,128)(2,1)S(1)} collective-permute-done((bf16[64,2816]{1,0:T(8,128)(2,1)S(1)}, bf16[64,2816]{1,0:T(8,128)(2,1)S(1)}, u32[]{:S(2)}, u32[]{:S(2)}) %collective-permute-start.11) | collective-permute-done | bytes 360480 | tf_op jit(solution)/shard_map/ppermute | solution.py:618
  36.7 5.5 %collective-permute-done.10 = bf16[64,2816]{1,0:T(8,128)(2,1)S(1)} collective-permute-done((bf16[64,2816]{1,0:T(8,128)(2,1)S(1)}, bf16[64,2816]{1,0:T(8,128)(2,1)S(1)}, u32[]{:S(2)}, u32[]{:S(2)}) %collective-permute-start.10) | collective-permute-done | bytes 360480 | tf_op jit(solution)/shard_map/ppermute | solution.py:618
  49.1 10.8 %collective-permute-done.refs_2_ = bf16[128,2048]{1,0:T(8,128)(2,1)S(1)} collective-permute-done((bf16[128,2048]{1,0:T(8,128)(2,1)S(1)}, bf16[128,2048]{1,0:T(8,128)(2,1)S(1)}, u32[]{:S(2)}, u32[]{:S(2)}) %collective-permute-start) | collective-permute-done | bytes 524320 | tf_op jit(solution)/shard_map/ppermute | solution.py:618
  61.9 9.2 %collective-permute-done.1.refs_3_ = bf16[128,2048]{1,0:T(8,128)(2,1)S(1)} collective-permute-done((bf16[128,2048]{1,0:T(8,128)(2,1)S(1)}, bf16[128,2048]{1,0:T(8,128)(2,1)S(1)}, u32[]{:S(2)}, u32[]{:S(2)}) %collective-permute-start.1) | collective-permute-done | bytes 524320 | tf_op jit(solution)/shard_map/ppermute | solution.py:618
  72.4 10.1 %collective-permute-done.4.refs_6_ = bf16[128,2048]{1,0:T(8,128)(2,1)S(1)} collective-permute-done((bf16[128,2048]{1,0:T(8,128)(2,1)S(1)}, bf16[128,2048]{1,0:T(8,128)(2,1)S(1)}, u32[]{:S(2)}, u32[]{:S(2)}) %collective-permute-start.4) | collective-permute-done | bytes 524320 | tf_op jit(solution)/shard_map/ppermute | solution.py:618
  83.1 1.6 collective-permute-start.13
  89.6 34.2 %attend.1 = (bf16[512,1024]{1,0:T(8,128)(2,1)}, bf16[128,1024]{1,0:T(8,128)(2,1)}, bf16[512,1024]{1,0:T(8,128)(2,1)}, f32[512,1024]{1,0:T(8,128)}, f32[8,1024]{1,0:T(8,128)}, /*index=5*/f32[1,1024]{1,0:T(1,128)}) custom-call(s32[4]{0:T(128)} %get-tuple-element.100.order_ref, s32[4]{0:T(128)} %copy-done.51, bf16[128,2048]{1,0:T(8,128)(2,1)} %get-tuple-element.101.refs_0_, ...), custom_call_target="tpu_custom_call" | custom-call | tf_op jit(solution)/shard_map/attend/pallas_call | solution.py:477
  123.8 5.6 %collective-permute-done.13.refs_2_ = bf16[256,2048]{1,0:T(8,128)(2,1)S(1)} collective-permute-done((bf16[256,2048]{1,0:T(8,128)(2,1)S(1)}, bf16[256,2048]{1,0:T(8,128)(2,1)S(1)}, u32[]{:S(2)}, u32[]{:S(2)}) %collective-permute-start.13) | collective-permute-done | bytes 1048608 | tf_op jit(solution)/shard_map/ppermute | solution.py:618
  129.4 6.5 %rows_of_product.2 = (bf16[128,2048]{1,0:T(8,128)(2,1)}, bf16[128,2048]{1,0:T(8,128)(2,1)}, bf16[128,2048]{1,0:T(8,128)(2,1)}, bf16[128,2048]{1,0:T(8,128)(2,1)}...) custom-call(bf16[512,1024]{1,0:T(8,128)(2,1)} %get-tuple-element.107, ...), custom_call_target="tpu_custom_call" | custom-call | tf_op jit(solution)/shard_map/rows_of_product/pallas_call | solution.py:361
  135.9 1.6 collective-permute-start.16
  140.0 11.0 %collective-permute-done.16 = bf16[128,2048]{1,0:T(8,128)(2,1)S(1)} collective-permute-done((bf16[128,2048]{1,0:T(8,128)(2,1)}, bf16[128,2048]{1,0:T(8,128)(2,1)S(1)}, u32[]{:S(2)}, u32[]{:S(2)}) %collective-permute-start.16) | collective-permute-done | bytes 524320 | tf_op jit(solution)/shard_map/ppermute | solution.py:618
  152.2 1.6 collective-permute-start.17
  154.6 7.7 %collective-permute-done.15.refs_2_ = bf16[128,2048]{1,0:T(8,128)(2,1)S(1)} collective-permute-done((bf16[128,2048]{1,0:T(8,128)(2,1)}, bf16[128,2048]{1,0:T(8,128)(2,1)S(1)}, u32[]{:S(2)}, u32[]{:S(2)}) %collective-permute-start.15) | collective-permute-done | bytes 524320 | tf_op jit(solution)/shard_map/ppermute | solution.py:618
  163.8 7.4 %collective-permute-done.17.refs_3_ = bf16[128,2048]{1,0:T(8,128)(2,1)S(1)} collective-permute-done((bf16[128,2048]{1,0:T(8,128)(2,1)S(1)}, bf16[128,2048]{1,0:T(8,128)(2,1)S(1)}, u32[]{:S(2)}, u32[]{:S(2)}) %collective-permute-start.17) | collective-permute-done | bytes 524320 | tf_op jit(solution)/shard_map/ppermute | solution.py:618
  172.2 4.9 middle_kernel.1
  181.1 11.0 %collective-permute-done.21.refs_2_ = bf16[128,2048]{1,0:T(8,128)(2,1)S(1)} collective-permute-done((bf16[128,2048]{1,0:T(8,128)(2,1)}, bf16[128,2048]{1,0:T(8,128)(2,1)S(1)}, u32[]{:S(2)}, u32[]{:S(2)}) %collective-permute-start.21) | collective-permute-done | bytes 524320 | tf_op jit(solution)/shard_map/ppermute | solution.py:618
  194.2 9.2 %collective-permute-done.22.refs_3_ = bf16[128,2048]{1,0:T(8,128)(2,1)S(1)} collective-permute-done((bf16[128,2048]{1,0:T(8,128)(2,1)}, bf16[128,2048]{1,0:T(8,128)(2,1)S(1)}, u32[]{:S(2)}, u32[]{:S(2)}) %collective-permute-start.22) | collective-permute-done | bytes 524320 | tf_op jit(solution)/shard_map/ppermute | solution.py:618
  203.9 6.4 %collective-permute-done.25.refs_6_ = bf16[128,2048]{1,0:T(8,128)(2,1)S(1)} collective-permute-done((bf16[128,2048]{1,0:T(8,128)(2,1)S(1)}, bf16[128,2048]{1,0:T(8,128)(2,1)S(1)}, u32[]{:S(2)}, u32[]{:S(2)}) %collective-permute-start.25) | collective-permute-done | bytes 524320 | tf_op jit(solution)/shard_map/ppermute | solution.py:618
  211.3 21.0 %hidden_of.1 = (bf16[1024,2816]{1,0:T(8,128)(2,1)}, bf16[1408,1024]{1,0:T(8,128)(2,1)}, bf16[1024,2048]{1,0:T(8,128)(2,1)}) custom-call(bf16[128,2048]{1,0:T(8,128)(2,1)} %get-tuple-element.118.refs_0_, bf16[128,2048]{1,0:T(8,128)(2,1)} %get-tuple-element.119.refs_1_, bf16[128,2048]{1,0:T(8,128)(2,1)} %copy-done.30, bf16[128,2048]{1,0:T(8,128)(2,1)} %copy-done.32, ...), custom_call_target="tpu_custom_call" | custom-call | tf_op jit(solution)/shard_map/hidden_of/pallas_call | solution.py:219
  232.4 11.8 %grad_down_of.1 = bf16[1408,2048]{1,0:T(8,128)(2,1)} custom-call(bf16[256,2048]{1,0:T(8,128)(2,1)} %bitcast.71, bf16[256,2048]{1,0:T(8,128)(2,1)} %copy-done.1, bf16[256,2048]{1,0:T(8,128)(2,1)} %copy-done.2, bf16[256,2048]{1,0:T(8,128)(2,1)} %collective-permute-done.14.refs_3_, bf16[1408,1024]{1,0:T(8,128)(2,1)} %get-tuple-element.152.refs_4_.left_ref), custom_call_target="tpu_custom_call" | custom-call | tf_op jit(solution)/shard_map/grad_down_of/pallas_call | solution.py:239
  244.3 14.3 %grad_gate_up_of.1.grad_ref = bf16[1024,2816]{1,0:T(8,128)(2,1)} custom-call(bf16[256,2048]{1,0:T(8,128)(2,1)} %bitcast.72, bf16[256,2048]{1,0:T(8,128)(2,1)} %copy-done.1, bf16[256,2048]{1,0:T(8,128)(2,1)} %copy-done.2, bf16[256,2048]{1,0:T(8,128)(2,1)} %collective-permute-done.14.refs_3_, ...), custom_call_target="tpu_custom_call" | custom-call | tf_op jit(solution)/shard_map/grad_gate_up_of/pallas_call | solution.py:278
  259.2 17.2 %grad_rows_of.2 = (bf16[128,2048]{1,0:T(8,128)(2,1)}, bf16[128,2048]{1,0:T(8,128)(2,1)}, bf16[128,2048]{1,0:T(8,128)(2,1)}, bf16[128,2048]{1,0:T(8,128)(2,1)}, b...) custom-call(bf16[1024,2816]{1,0:T(8,128)(2,1)} %grad_gate_up_of.1.gr, ...), custom_call_target="tpu_custom_call" | custom-call | tf_op jit(solution)/shard_map/grad_rows_of/pallas_call | solution.py:300
  276.4 1.6 collective-permute-start.27
  279.8 11.6 %collective-permute-done.27 = bf16[128,2048]{1,0:T(8,128)(2,1)S(1)} collective-permute-done((bf16[128,2048]{1,0:T(8,128)(2,1)}, bf16[128,2048]{1,0:T(8,128)(2,1)S(1)}, u32[]{:S(2)}, u32[]{:S(2)}) %collective-permute-start.27) | collective-permute-done | bytes 524320 | tf_op jit(solution)/shard_map/ppermute | solution.py:618
  294.9 1.6 collective-permute-start.34
  296.5 18.7 %grad_weight_of.1 = bf16[1024,2816]{1,0:T(8,128)(2,1)} custom-call(s32[1]{0:T(128)} %bitcast.21.core_ref, bf16[1024,2048]{1,0:T(8,128)(2,1)} %get-tuple-element.132.left_ref, bf16[1024,2048]{1,0:T(8,128)(2,1)} %collective-permute-done.29.other_left_ref, bf16[1024,2816]{1,0:T(8,128)(2,1)} %grad_gate_up_of.1.grad_ref, ...), custom_call_target="tpu_custom_call" | custom-call | tf_op jit(solution)/shard_map/grad_weight_of/pallas_call | solution.py:321
  316.5 6.0 %grad_middle_kernel.1 = (f32[256,2048]{1,0:T(8,128)}, bf16[128,2048]{1,0:T(8,128)(2,1)}, bf16[128,2048]{1,0:T(8,128)(2,1)}) custom-call(bf16[256,2048]{1,0:T(8,128)(2,1)} %bitcast.73, f32[256,2048]{1,0:T(8,128)} %get-tuple-element.116.refs_1_.middle_ref, f32[256,1]{1,0:T(8,128)} %get-tuple-element.117.refs_2_, bf16[128,2048]{1,0:T(8,128)(2,1)} %get-tuple-element.138.refs_3_, ...), custom_call_target="tpu_custom_call" | custom-call | tf_op jit(solution)/shard_map/grad_middle_kernel/pallas_call | solution.py:73
  326.5 11.0 %collective-permute-done.35.refs_2_.refs_10_ = bf16[128,2048]{1,0:T(8,128)(2,1)S(1)} collective-permute-done((bf16[128,2048]{1,0:T(8,128)(2,1)}, bf16[128,2048]{1,0:T(8,128)(2,1)S(1)}, u32[]{:S(2)}, u32[]{:S(2)}) %collective-permute-start.35) | collective-permute-done | bytes 524320 | tf_op jit(solution)/shard_map/ppermute | solution.py:618
  339.6 11.5 %rows_of_product.3 = (bf16[256,2048]{1,0:T(8,128)(2,1)}, bf16[256,2048]{1,0:T(8,128)(2,1)}, bf16[256,2048]{1,0:T(8,128)(2,1)}, bf16[256,2048]{1,0:T(8,128)(2,1)}) custom-call(bf16[1408,1024]{1,0:T(8,128)(2,1)} %get-tuple-element.152.refs_4_.left_ref, bf16[1408,2048]{1,0:T(8,128)(2,1)} %all-gather.8.cloned.1.call-done.refs_4_.weight_ref), custom_call_target="tpu_custom_call" | custom-call | tf_op jit(solution)/shard_map/rows_of_product/pallas_call | solution.py:361
  351.2 5.8 %collective-permute-done.39.refs_6_.refs_14_ = bf16[128,2048]{1,0:T(8,128)(2,1)S(1)} collective-permute-done((bf16[128,2048]{1,0:T(8,128)(2,1)S(1)}, bf16[128,2048]{1,0:T(8,128)(2,1)S(1)}, u32[]{:S(2)}, u32[]{:S(2)}) %collective-permute-start.39) | collective-permute-done | bytes 524320 | tf_op jit(solution)/shard_map/ppermute | solution.py:618
  360.5 34.9 %attend_back.1 = (bf16[640,1024]{1,0:T(8,128)(2,1)}, bf16[1024,640]{1,0:T(8,128)(2,1)}) custom-call(s32[4]{0:T(128)} %get-tuple-element.100.order_ref, s32[4]{0:T(128)} %copy-done.51, bf16[128,2048]{1,0:T(8,128)(2,1)} %get-tuple-element.144.refs_0_.refs_8_, bf16[128,2048]{1,0:T(8,128)(2,1)} %get-tuple-element.145.refs_1_.refs_9_, ...), custom_call_target="tpu_custom_call" | custom-call | tf_op jit(solution)/shard_map/attend_back/pallas_call | solution.py:580
  395.4 6.6 %collective-permute-done.42.refs_2_ = bf16[256,2048]{1,0:T(8,128)(2,1)} collective-permute-done((bf16[256,2048]{1,0:T(8,128)(2,1)}, bf16[256,2048]{1,0:T(8,128)(2,1)}, u32[]{:S(2)}, u32[]{:S(2)}) %collective-permute-start.42) | collective-permute-done | bytes 1048608 | tf_op jit(solution)/shard_map/ppermute | solution.py:618
  402.0 10.5 %attention_weights_of.1 = bf16[2048,1152]{1,0:T(8,128)(2,1)} custom-call(bf16[128,2048]{1,0:T(8,128)(2,1)} %get-tuple-element.101.refs_0_, bf16[128,2048]{1,0:T(8,128)(2,1)} %get-tuple-element.102.refs_1_, bf16[128,2048]{1,0:T(8,128)(2,1)} %copy-done.7, bf16[128,2048]{1,0:T(8,128)(2,1)} %copy-done.9, bf16[128,2048]{1,0:T(8,128)(2,1)} %copy-done.10, ...), custom_call_target="tpu_custom_call" | custom-call | tf_op jit(solution)/shard_map/attention_weights_of/pallas_call | solution.py:395
  412.5 7.8 %grad_rows_of.3 = (bf16[128,2048]{1,0:T(8,128)(2,1)}, bf16[128,2048]{1,0:T(8,128)(2,1)}, bf16[128,2048]{1,0:T(8,128)(2,1)}, bf16[128,2048]{1,0:T(8,128)(2,1)}, b...) custom-call(bf16[1024,640]{1,0:T(8,128)(2,1)} %get-tuple-element.168, ...), custom_call_target="tpu_custom_call" | custom-call | tf_op jit(solution)/shard_map/grad_rows_of/pallas_call | solution.py:300
  425.4 10.8 %collective-permute-done.45 = bf16[128,2048]{1,0:T(8,128)(2,1)S(1)} collective-permute-done((bf16[128,2048]{1,0:T(8,128)(2,1)S(1)}, bf16[128,2048]{1,0:T(8,128)(2,1)S(1)}, u32[]{:S(2)}, u32[]{:S(2)}) %collective-permute-start.45) | collective-permute-done | bytes 524320 | tf_op jit(solution)/shard_map/ppermute | solution.py:618
  438.8 8.6 %collective-permute-done.44.refs_3_ = bf16[128,2048]{1,0:T(8,128)(2,1)S(1)} collective-permute-done((bf16[128,2048]{1,0:T(8,128)(2,1)S(1)}, bf16[128,2048]{1,0:T(8,128)(2,1)S(1)}, u32[]{:S(2)}, u32[]{:S(2)}) %collective-permute-start.44) | collective-permute-done | bytes 524320 | tf_op jit(solution)/shard_map/ppermute | solution.py:618
  448.6 7.8 %collective-permute-done.46.refs_4_ = bf16[128,2048]{1,0:T(8,128)(2,1)S(1)} collective-permute-done((bf16[128,2048]{1,0:T(8,128)(2,1)S(1)}, bf16[128,2048]{1,0:T(8,128)(2,1)S(1)}, u32[]{:S(2)}, u32[]{:S(2)}) %collective-permute-start.46) | collective-permute-done | bytes 524320 | tf_op jit(solution)/shard_map/ppermute | solution.py:618
  461.8 4.4 block_out_kernel.1
  466.2 5.6 %grad_tokens_kernel.1 = f32[256,2048]{1,0:T(8,128)} custom-call(bf16[256,2048]{1,0:T(8,128)(2,1)} %bitcast.70, f32[256,2048]{1,0:T(8,128)} %get-tuple-element.165.refs_1_, bf16[128,2048]{1,0:T(8,128)(2,1)} %get-tuple-element.169.refs_2_, bf16[128,2048]{1,0:T(8,128)(2,1)} %copy-done.23, bf16[128,2048]{1,0:T(8,128)(2,1)} %copy-done.26, ...), custom_call_target="tpu_custom_call" | custom-call | tf_op jit(solution)/shard_map/grad_tokens_kernel/pallas_call | solution.py:73
  471.8 2.3 collective-permute-done.51.refs_2_
  475.0 4.2 finish_gate_up_kernel.1
  482.5 1.9 collective-permute-start.55
  488.5 2.5 finish_projections_kernel.1
  (280 shorter events, 78.0 us)
Async XLA Ops:
  7.2 82.4 %all-gather.4.cloned.1.call-start = ((), (), s32[]{:S(2)}) async-start(), calls=%async_computation.3 | async-start | bytes 5308416 | tf_op jit(solution)/shard_map/all_gather | solution.py:661
  20.3 190.1 %all-gather.6.cloned.1.call-start = ((), (), s32[]{:S(2)}) async-start(), calls=%async_computation.4 | async-start | bytes 12976128 | tf_op jit(solution)/shard_map/all_gather | solution.py:661
  25.9 16.3 %collective-permute-start.10 = (bf16[64,2816]{1,0:T(8,128)(2,1)S(1)}, bf16[64,2816]{1,0:T(8,128)(2,1)S(1)}, u32[]{:S(2)}, u32[]{:S(2)}) collective-permute-start(bf16[64,2816]{1,0:T(8,128)(2,1)S(1)} %get-tuple-element.279), channel_id=1, source_target_pairs={{0,16},{8,24},{16,0},{24,8},{1,17},{9,25},{17,1},{25,9},{2,18},{10... | collective-permute-start | bytes 1081352 | tf_op jit(solution)/shard_map/ppermute | solution.py:618
  26.7 15.7 %collective-permute-start.9 = (bf16[64,2816]{1,0:T(8,128)(2,1)S(1)}, bf16[64,2816]{1,0:T(8,128)(2,1)S(1)}, u32[]{:S(2)}, u32[]{:S(2)}) collective-permute-start(bf16[64,2816]{1,0:T(8,128)(2,1)S(1)} %get-tuple-element.277), channel_id=1, source_target_pairs={{0,8},{8,0},{16,24},{24,16},{1,9},{9,1},{17,25},{25,17},{2,10},{10... | collective-permute-start | bytes 1081352 | tf_op jit(solution)/shard_map/ppermute | solution.py:618
  44.0 200.3 %all-gather.8.cloned.1.call-start = ((), (), s32[]{:S(2)}) async-start(), calls=%async_computation.5 | async-start | bytes 6488064 | tf_op jit(solution)/shard_map/all_gather | solution.py:661
  44.7 271.8 %reduce-scatter.4.cloned.1.call-start = ((), (), s32[]{:S(2)}) async-start(), calls=%async_computation.6 | async-start | bytes 6488064 | tf_op jit(solution)/shard_map/reduce_scatter | solution.py:670
  47.0 24.0 %collective-permute-start.1 = (bf16[128,2048]{1,0:T(8,128)(2,1)S(1)}, bf16[128,2048]{1,0:T(8,128)(2,1)S(1)}, u32[]{:S(2)}, u32[]{:S(2)}) collective-permute-start(bf16[128,2048]{1,0:T(8,128)(2,1)S(1)} %copy-done.6), channel_id=1, source_target_pairs={{0,8},{8,0},{16,24},{24,16},{1,9},{9,1},{17,25},{25,17},{2,10},{10... | collective-permute-start | bytes 1572872 | tf_op jit(solution)/shard_map/ppermute | solution.py:618
  48.4 24.0 %collective-permute-start.2 = (bf16[128,2048]{1,0:T(8,128)(2,1)S(1)}, bf16[128,2048]{1,0:T(8,128)(2,1)S(1)}, u32[]{:S(2)}, u32[]{:S(2)}) collective-permute-start(bf16[128,2048]{1,0:T(8,128)(2,1)S(1)} %copy-done.5), channel_id=1, source_target_pairs={{0,16},{8,24},{16,0},{24,8},{1,17},{9,25},{17,1},{25,9},{2,18},{10... | collective-permute-start | bytes 1572872 | tf_op jit(solution)/shard_map/ppermute | solution.py:618
  59.8 22.7 %collective-permute-start.4 = (bf16[128,2048]{1,0:T(8,128)(2,1)S(1)}, bf16[128,2048]{1,0:T(8,128)(2,1)S(1)}, u32[]{:S(2)}, u32[]{:S(2)}) collective-permute-start(bf16[128,2048]{1,0:T(8,128)(2,1)S(1)} %collective-permute-done.refs_2_), channel_id=1, source_target_pairs={{0,16},{8,24},{16,0},{24,8},{1,17},{9,25},{17,1},{25,9},{2,18},{10... | collective-permute-start | bytes 1572872 | tf_op jit(solution)/shard_map/ppermute | solution.py:618
  61.2 21.3 %collective-permute-start.5 = (bf16[128,2048]{1,0:T(8,128)(2,1)S(1)}, bf16[128,2048]{1,0:T(8,128)(2,1)S(1)}, u32[]{:S(2)}, u32[]{:S(2)}) collective-permute-start(bf16[128,2048]{1,0:T(8,128)(2,1)S(1)} %collective-permute-done.3.refs_5_), channel_id=1, source_target_pairs={{0,8},{8,0},{16,24},{24,16},{1,9},{9,1},{17,25},{25,17},{2,10},{10... | collective-permute-start | bytes 1572872 | tf_op jit(solution)/shard_map/ppermute | solution.py:618
  82.5 41.2 %collective-permute-start.12 = (bf16[256,2048]{1,0:T(8,128)(2,1)S(1)}, bf16[256,2048]{1,0:T(8,128)(2,1)S(1)}, u32[]{:S(2)}, u32[]{:S(2)}) collective-permute-start(bf16[256,2048]{1,0:T(8,128)(2,1)S(1)} %bitcast.74), channel_id=1, source_target_pairs={{0,8},{8,0},{16,24},{24,16},{1,9},{9,1},{17,25},{25,17},{2,10},{10... | collective-permute-start | bytes 3145736 | tf_op jit(solution)/shard_map/ppermute | solution.py:618
  83.1 46.3 %collective-permute-start.13 = (bf16[256,2048]{1,0:T(8,128)(2,1)S(1)}, bf16[256,2048]{1,0:T(8,128)(2,1)S(1)}, u32[]{:S(2)}, u32[]{:S(2)}) collective-permute-start(bf16[256,2048]{1,0:T(8,128)(2,1)S(1)} %bitcast.75), channel_id=1, source_target_pairs={{0,16},{8,24},{16,0},{24,8},{1,17},{9,25},{17,1},{25,9},{2,18},{10... | collective-permute-start | bytes 3145736 | tf_op jit(solution)/shard_map/ppermute | solution.py:618
  84.7 44.7 %collective-permute-start.14 = (bf16[256,2048]{1,0:T(8,128)(2,1)S(1)}, bf16[256,2048]{1,0:T(8,128)(2,1)}, u32[]{:S(2)}, u32[]{:S(2)}) collective-permute-start(bf16[256,2048]{1,0:T(8,128)(2,1)S(1)} %bitcast.76), channel_id=1, source_target_pairs={{0,24},{8,16},{16,8},{24,0},{1,25},{9,17},{17,9},{25,1},{2,26},{10... | collective-permute-start | bytes 3145736 | tf_op jit(solution)/shard_map/ppermute | solution.py:618
  135.9 15.1 %collective-permute-start.16 = (bf16[128,2048]{1,0:T(8,128)(2,1)}, bf16[128,2048]{1,0:T(8,128)(2,1)S(1)}, u32[]{:S(2)}, u32[]{:S(2)}) collective-permute-start(bf16[128,2048]{1,0:T(8,128)(2,1)} %get-tuple-element.111), channel_id=1, source_target_pairs={{0,16},{8,24},{16,0},{24,8},{1,17},{9,25},{17,1},{25,9},{2,18},{10... | collective-permute-start | bytes 1572872 | tf_op jit(solution)/shard_map/ppermute | solution.py:618
  137.5 16.4 %collective-permute-start.19 = (bf16[128,2048]{1,0:T(8,128)(2,1)}, bf16[128,2048]{1,0:T(8,128)(2,1)S(1)}, u32[]{:S(2)}, u32[]{:S(2)}) collective-permute-start(bf16[128,2048]{1,0:T(8,128)(2,1)} %get-tuple-element.115), channel_id=1, source_target_pairs={{0,8},{8,0},{16,24},{24,16},{1,9},{9,1},{17,25},{25,17},{2,10},{10... | collective-permute-start | bytes 1572872 | tf_op jit(solution)/shard_map/ppermute | solution.py:618
  138.0 24.3 %collective-permute-start.15 = (bf16[128,2048]{1,0:T(8,128)(2,1)}, bf16[128,2048]{1,0:T(8,128)(2,1)S(1)}, u32[]{:S(2)}, u32[]{:S(2)}) collective-permute-start(bf16[128,2048]{1,0:T(8,128)(2,1)} %get-tuple-element.109), channel_id=1, source_target_pairs={{0,16},{8,24},{16,0},{24,8},{1,17},{9,25},{17,1},{25,9},{2,18},{10... | collective-permute-start | bytes 1572872 | tf_op jit(solution)/shard_map/ppermute | solution.py:618
  139.5 24.3 %collective-permute-start.18 = (bf16[128,2048]{1,0:T(8,128)(2,1)}, bf16[128,2048]{1,0:T(8,128)(2,1)S(1)}, u32[]{:S(2)}, u32[]{:S(2)}) collective-permute-start(bf16[128,2048]{1,0:T(8,128)(2,1)} %get-tuple-element.113), channel_id=1, source_target_pairs={{0,8},{8,0},{16,24},{24,16},{1,9},{9,1},{17,25},{25,17},{2,10},{10... | collective-permute-start | bytes 1572872 | tf_op jit(solution)/shard_map/ppermute | solution.py:618
  152.2 19.0 %collective-permute-start.17 = (bf16[128,2048]{1,0:T(8,128)(2,1)S(1)}, bf16[128,2048]{1,0:T(8,128)(2,1)S(1)}, u32[]{:S(2)}, u32[]{:S(2)}) collective-permute-start(bf16[128,2048]{1,0:T(8,128)(2,1)S(1)} %add_convert_fusion.5), channel_id=1, source_target_pairs={{0,8},{8,0},{16,24},{24,16},{1,9},{9,1},{17,25},{25,17},{2,10},{10... | collective-permute-start | bytes 1572872 | tf_op jit(solution)/shard_map/ppermute | solution.py:618
  154.0 17.3 %collective-permute-start.20 = (bf16[128,2048]{1,0:T(8,128)(2,1)S(1)}, bf16[128,2048]{1,0:T(8,128)(2,1)S(1)}, u32[]{:S(2)}, u32[]{:S(2)}) collective-permute-start(bf16[128,2048]{1,0:T(8,128)(2,1)S(1)} %add_convert_fusion.4), channel_id=1, source_target_pairs={{0,16},{8,24},{16,0},{24,8},{1,17},{9,25},{17,1},{25,9},{2,18},{10... | collective-permute-start | bytes 1572872 | tf_op jit(solution)/shard_map/ppermute | solution.py:618
  177.1 15.1 %collective-permute-start.21 = (bf16[128,2048]{1,0:T(8,128)(2,1)}, bf16[128,2048]{1,0:T(8,128)(2,1)S(1)}, u32[]{:S(2)}, u32[]{:S(2)}) collective-permute-start(bf16[128,2048]{1,0:T(8,128)(2,1)} %get-tuple-element.118.refs_0_), channel_id=1, source_target_pairs={{0,8},{8,0},{16,24},{24,16},{1,9},{9,1},{17,25},{25,17},{2,10},{10... | collective-permute-start | bytes 1572872 | tf_op jit(solution)/shard_map/ppermute | solution.py:618
  177.6 15.1 %collective-permute-start.24 = (bf16[128,2048]{1,0:T(8,128)(2,1)}, bf16[128,2048]{1,0:T(8,128)(2,1)S(1)}, u32[]{:S(2)}, u32[]{:S(2)}) collective-permute-start(bf16[128,2048]{1,0:T(8,128)(2,1)} %get-tuple-element.119.refs_1_), channel_id=1, source_target_pairs={{0,16},{8,24},{16,0},{24,8},{1,17},{9,25},{17,1},{25,9},{2,18},{10... | collective-permute-start | bytes 1572872 | tf_op jit(solution)/shard_map/ppermute | solution.py:618
  179.0 24.3 %collective-permute-start.22 = (bf16[128,2048]{1,0:T(8,128)(2,1)}, bf16[128,2048]{1,0:T(8,128)(2,1)S(1)}, u32[]{:S(2)}, u32[]{:S(2)}) collective-permute-start(bf16[128,2048]{1,0:T(8,128)(2,1)} %get-tuple-element.119.refs_1_), channel_id=1, source_target_pairs={{0,8},{8,0},{16,24},{24,16},{1,9},{9,1},{17,25},{25,17},{2,10},{10... | collective-permute-start | bytes 1572872 | tf_op jit(solution)/shard_map/ppermute | solution.py:618
  179.7 24.3 %collective-permute-start.23 = (bf16[128,2048]{1,0:T(8,128)(2,1)}, bf16[128,2048]{1,0:T(8,128)(2,1)S(1)}, u32[]{:S(2)}, u32[]{:S(2)}) collective-permute-start(bf16[128,2048]{1,0:T(8,128)(2,1)} %get-tuple-element.118.refs_0_), channel_id=1, source_target_pairs={{0,16},{8,24},{16,0},{24,8},{1,17},{9,25},{17,1},{25,9},{2,18},{10... | collective-permute-start | bytes 1572872 | tf_op jit(solution)/shard_map/ppermute | solution.py:618
  192.1 18.2 %collective-permute-start.25 = (bf16[128,2048]{1,0:T(8,128)(2,1)S(1)}, bf16[128,2048]{1,0:T(8,128)(2,1)S(1)}, u32[]{:S(2)}, u32[]{:S(2)}) collective-permute-start(bf16[128,2048]{1,0:T(8,128)(2,1)S(1)} %collective-permute-done.21.refs_2_), channel_id=1, source_target_pairs={{0,16},{8,24},{16,0},{24,8},{1,17},{9,25},{17,1},{25,9},{2,18},{10... | collective-permute-start | bytes 1572872 | tf_op jit(solution)/shard_map/ppermute | solution.py:618
  192.7 17.6 %collective-permute-start.26 = (bf16[128,2048]{1,0:T(8,128)(2,1)S(1)}, bf16[128,2048]{1,0:T(8,128)(2,1)S(1)}, u32[]{:S(2)}, u32[]{:S(2)}) collective-permute-start(bf16[128,2048]{1,0:T(8,128)(2,1)S(1)} %collective-permute-done.24.refs_5_), channel_id=1, source_target_pairs={{0,8},{8,0},{16,24},{24,16},{1,9},{9,1},{17,25},{25,17},{2,10},{10... | collective-permute-start | bytes 1572872 | tf_op jit(solution)/shard_map/ppermute | solution.py:618
  244.2 176.0 %reduce-scatter.6.cloned.1.call-start = ((), (), s32[]{:S(2)}) async-start(), calls=%async_computation.7 | async-start | bytes 7208960 | tf_op jit(solution)/shard_map/reduce_scatter | solution.py:667
  258.6 37.8 %collective-permute-start.30 = (bf16[1024,2816]{1,0:T(8,128)(2,1)}, bf16[1024,2816]{1,0:T(8,128)(2,1)}, u32[]{:S(2)}, u32[]{:S(2)}) collective-permute-start(bf16[1024,2816]{1,0:T(8,128)(2,1)} %grad_gate_up_of.1.grad_ref), channel_id=1, source_target_pairs={{0,1},{1,0},{2,3},{3,2},{4,5},{5,4},{6,7},{7,6},{8,9},{9,8},{10,11... | collective-permute-start | bytes 17301512 | tf_op jit(solution)/shard_map/ppermute | solution.py:664
  258.7 36.1 %collective-permute-start.29 = (bf16[1024,2048]{1,0:T(8,128)(2,1)}, bf16[1024,2048]{1,0:T(8,128)(2,1)}, u32[]{:S(2)}, u32[]{:S(2)}) collective-permute-start(bf16[1024,2048]{1,0:T(8,128)(2,1)} %get-tuple-element.132.left_ref), channel_id=1, source_target_pairs={{0,1},{1,0},{2,3},{3,2},{4,5},{5,4},{6,7},{7,6},{8,9},{9,8},{10,11... | collective-permute-start | bytes 12582920 | tf_op jit(solution)/shard_map/ppermute | solution.py:664
  278.0 16.0 %collective-permute-start.28 = (bf16[128,2048]{1,0:T(8,128)(2,1)}, bf16[128,2048]{1,0:T(8,128)(2,1)S(1)}, u32[]{:S(2)}, u32[]{:S(2)}) collective-permute-start(bf16[128,2048]{1,0:T(8,128)(2,1)} %get-tuple-element.131), channel_id=1, source_target_pairs={{0,8},{8,0},{16,24},{24,16},{1,9},{9,1},{17,25},{25,17},{2,10},{10... | collective-permute-start | bytes 1572872 | tf_op jit(solution)/shard_map/ppermute | solution.py:618
  278.4 36.8 %collective-permute-start.31 = (bf16[128,2048]{1,0:T(8,128)(2,1)}, bf16[128,2048]{1,0:T(8,128)(2,1)S(1)}, u32[]{:S(2)}, u32[]{:S(2)}) collective-permute-start(bf16[128,2048]{1,0:T(8,128)(2,1)} %get-tuple-element.134), channel_id=1, source_target_pairs={{0,16},{8,24},{16,0},{24,8},{1,17},{9,25},{17,1},{25,9},{2,18},{10... | collective-permute-start | bytes 1572872 | tf_op jit(solution)/shard_map/ppermute | solution.py:618
  291.4 23.7 %collective-permute-start.33 = (bf16[128,2048]{1,0:T(8,128)(2,1)}, bf16[128,2048]{1,0:T(8,128)(2,1)S(1)}, u32[]{:S(2)}, u32[]{:S(2)}) collective-permute-start(bf16[128,2048]{1,0:T(8,128)(2,1)} %get-tuple-element.136), channel_id=1, source_target_pairs={{0,8},{8,0},{16,24},{24,16},{1,9},{9,1},{17,25},{25,17},{2,10},{10... | collective-permute-start | bytes 1572872 | tf_op jit(solution)/shard_map/ppermute | solution.py:618
  294.0 21.2 %collective-permute-start.32 = (bf16[128,2048]{1,0:T(8,128)(2,1)S(1)}, bf16[128,2048]{1,0:T(8,128)(2,1)S(1)}, u32[]{:S(2)}, u32[]{:S(2)}) collective-permute-start(bf16[128,2048]{1,0:T(8,128)(2,1)S(1)} %add_convert_fusion.3), channel_id=1, source_target_pairs={{0,8},{8,0},{16,24},{24,16},{1,9},{9,1},{17,25},{25,17},{2,10},{10... | collective-permute-start | bytes 1572872 | tf_op jit(solution)/shard_map/ppermute | solution.py:618
  294.9 20.3 %collective-permute-start.34 = (bf16[128,2048]{1,0:T(8,128)(2,1)S(1)}, bf16[128,2048]{1,0:T(8,128)(2,1)S(1)}, u32[]{:S(2)}, u32[]{:S(2)}) collective-permute-start(bf16[128,2048]{1,0:T(8,128)(2,1)S(1)} %add_convert_fusion.2), channel_id=1, source_target_pairs={{0,16},{8,24},{16,0},{24,8},{1,17},{9,25},{17,1},{25,9},{2,18},{10... | collective-permute-start | bytes 1572872 | tf_op jit(solution)/shard_map/ppermute | solution.py:618
  316.5 162.7 %reduce-scatter.8.cloned.1.call-start = ((), (), s32[]{:S(2)}) async-start(), calls=%async_computation.8 | async-start | bytes 5308416 | tf_op jit(solution)/shard_map/reduce_scatter | solution.py:670
  322.5 15.1 %collective-permute-start.35 = (bf16[128,2048]{1,0:T(8,128)(2,1)}, bf16[128,2048]{1,0:T(8,128)(2,1)S(1)}, u32[]{:S(2)}, u32[]{:S(2)}) collective-permute-start(bf16[128,2048]{1,0:T(8,128)(2,1)} %get-tuple-element.144.refs_0_.refs_8_), channel_id=1, source_target_pairs={{0,8},{8,0},{16,24},{24,16},{1,9},{9,1},{17,25},{25,17},{2,10},{10... | collective-permute-start | bytes 1572872 | tf_op jit(solution)/shard_map/ppermute | solution.py:618
  323.2 15.3 %collective-permute-start.38 = (bf16[128,2048]{1,0:T(8,128)(2,1)}, bf16[128,2048]{1,0:T(8,128)(2,1)S(1)}, u32[]{:S(2)}, u32[]{:S(2)}) collective-permute-start(bf16[128,2048]{1,0:T(8,128)(2,1)} %get-tuple-element.145.refs_1_.refs_9_), channel_id=1, source_target_pairs={{0,16},{8,24},{16,0},{24,8},{1,17},{9,25},{17,1},{25,9},{2,18},{10... | collective-permute-start | bytes 1572872 | tf_op jit(solution)/shard_map/ppermute | solution.py:618
  324.1 27.0 %collective-permute-start.36 = (bf16[128,2048]{1,0:T(8,128)(2,1)}, bf16[128,2048]{1,0:T(8,128)(2,1)S(1)}, u32[]{:S(2)}, u32[]{:S(2)}) collective-permute-start(bf16[128,2048]{1,0:T(8,128)(2,1)} %get-tuple-element.145.refs_1_.refs_9_), channel_id=1, source_target_pairs={{0,8},{8,0},{16,24},{24,16},{1,9},{9,1},{17,25},{25,17},{2,10},{10... | collective-permute-start | bytes 1572872 | tf_op jit(solution)/shard_map/ppermute | solution.py:618
  325.4 25.7 %collective-permute-start.37 = (bf16[128,2048]{1,0:T(8,128)(2,1)}, bf16[128,2048]{1,0:T(8,128)(2,1)S(1)}, u32[]{:S(2)}, u32[]{:S(2)}) collective-permute-start(bf16[128,2048]{1,0:T(8,128)(2,1)} %get-tuple-element.144.refs_0_.refs_8_), channel_id=1, source_target_pairs={{0,16},{8,24},{16,0},{24,8},{1,17},{9,25},{17,1},{25,9},{2,18},{10... | collective-permute-start | bytes 1572872 | tf_op jit(solution)/shard_map/ppermute | solution.py:618
  337.6 19.4 %collective-permute-start.39 = (bf16[128,2048]{1,0:T(8,128)(2,1)S(1)}, bf16[128,2048]{1,0:T(8,128)(2,1)S(1)}, u32[]{:S(2)}, u32[]{:S(2)}) collective-permute-start(bf16[128,2048]{1,0:T(8,128)(2,1)S(1)} %collective-permute-done.35.refs_2_.refs_10_), channel_id=1, source_target_pairs={{0,16},{8,24},{16,0},{24,8},{1,17},{9,25},{17,1},{25,9},{2,18},{10... | collective-permute-start | bytes 1572872 | tf_op jit(solution)/shard_map/ppermute | solution.py:618
  338.5 18.5 %collective-permute-start.40 = (bf16[128,2048]{1,0:T(8,128)(2,1)S(1)}, bf16[128,2048]{1,0:T(8,128)(2,1)S(1)}, u32[]{:S(2)}, u32[]{:S(2)}) collective-permute-start(bf16[128,2048]{1,0:T(8,128)(2,1)S(1)} %collective-permute-done.38.refs_5_.refs_13_), channel_id=1, source_target_pairs={{0,8},{8,0},{16,24},{24,16},{1,9},{9,1},{17,25},{25,17},{2,10},{10... | collective-permute-start | bytes 1572872 | tf_op jit(solution)/shard_map/ppermute | solution.py:618
  357.0 38.4 %collective-permute-start.41 = (bf16[256,2048]{1,0:T(8,128)(2,1)}, bf16[256,2048]{1,0:T(8,128)(2,1)}, u32[]{:S(2)}, u32[]{:S(2)}) collective-permute-start(bf16[256,2048]{1,0:T(8,128)(2,1)} %get-tuple-element.158), channel_id=1, source_target_pairs={{0,8},{8,0},{16,24},{24,16},{1,9},{9,1},{17,25},{25,17},{2,10},{10... | collective-permute-start | bytes 3145736 | tf_op jit(solution)/shard_map/ppermute | solution.py:618
  358.3 43.8 %collective-permute-start.42 = (bf16[256,2048]{1,0:T(8,128)(2,1)}, bf16[256,2048]{1,0:T(8,128)(2,1)}, u32[]{:S(2)}, u32[]{:S(2)}) collective-permute-start(bf16[256,2048]{1,0:T(8,128)(2,1)} %get-tuple-element.159), channel_id=1, source_target_pairs={{0,16},{8,24},{16,0},{24,8},{1,17},{9,25},{17,1},{25,9},{2,18},{10... | collective-permute-start | bytes 3145736 | tf_op jit(solution)/shard_map/ppermute | solution.py:618
  359.3 42.8 %collective-permute-start.43 = (bf16[256,2048]{1,0:T(8,128)(2,1)}, bf16[256,2048]{1,0:T(8,128)(2,1)}, u32[]{:S(2)}, u32[]{:S(2)}) collective-permute-start(bf16[256,2048]{1,0:T(8,128)(2,1)} %get-tuple-element.160), channel_id=1, source_target_pairs={{0,24},{8,16},{16,8},{24,0},{1,25},{9,17},{17,9},{25,1},{2,26},{10... | collective-permute-start | bytes 3145736 | tf_op jit(solution)/shard_map/ppermute | solution.py:618
  423.5 23.9 %collective-permute-start.44 = (bf16[128,2048]{1,0:T(8,128)(2,1)S(1)}, bf16[128,2048]{1,0:T(8,128)(2,1)S(1)}, u32[]{:S(2)}, u32[]{:S(2)}) collective-permute-start(bf16[128,2048]{1,0:T(8,128)(2,1)S(1)} %copy-done.53), channel_id=1, source_target_pairs={{0,16},{8,24},{16,0},{24,8},{1,17},{9,25},{17,1},{25,9},{2,18},{10... | collective-permute-start | bytes 1572872 | tf_op jit(solution)/shard_map/ppermute | solution.py:618
  424.5 24.1 %collective-permute-start.47 = (bf16[128,2048]{1,0:T(8,128)(2,1)S(1)}, bf16[128,2048]{1,0:T(8,128)(2,1)S(1)}, u32[]{:S(2)}, u32[]{:S(2)}) collective-permute-start(bf16[128,2048]{1,0:T(8,128)(2,1)S(1)} %copy-done.52), channel_id=1, source_target_pairs={{0,8},{8,0},{16,24},{24,16},{1,9},{9,1},{17,25},{25,17},{2,10},{10... | collective-permute-start | bytes 1572872 | tf_op jit(solution)/shard_map/ppermute | solution.py:618
  436.3 20.2 %collective-permute-start.46 = (bf16[128,2048]{1,0:T(8,128)(2,1)S(1)}, bf16[128,2048]{1,0:T(8,128)(2,1)S(1)}, u32[]{:S(2)}, u32[]{:S(2)}) collective-permute-start(bf16[128,2048]{1,0:T(8,128)(2,1)S(1)} %add_convert_fusion.1), channel_id=1, source_target_pairs={{0,8},{8,0},{16,24},{24,16},{1,9},{9,1},{17,25},{25,17},{2,10},{10... | collective-permute-start | bytes 1572872 | tf_op jit(solution)/shard_map/ppermute | solution.py:618
  437.7 18.8 %collective-permute-start.49 = (bf16[128,2048]{1,0:T(8,128)(2,1)S(1)}, bf16[128,2048]{1,0:T(8,128)(2,1)S(1)}, u32[]{:S(2)}, u32[]{:S(2)}) collective-permute-start(bf16[128,2048]{1,0:T(8,128)(2,1)S(1)} %add_convert_fusion), channel_id=1, source_target_pairs={{0,16},{8,24},{16,0},{24,8},{1,17},{9,25},{17,1},{25,9},{2,18},{10... | collective-permute-start | bytes 1572872 | tf_op jit(solution)/shard_map/ppermute | solution.py:618
  459.1 15.1 %collective-permute-start.51 = (bf16[64,2816]{1,0:T(8,128)(2,1)S(1)}, bf16[64,2816]{1,0:T(8,128)(2,1)S(1)}, u32[]{:S(2)}, u32[]{:S(2)}) collective-permute-start(bf16[64,2816]{1,0:T(8,128)(2,1)S(1)} %get-tuple-element.190), channel_id=1, source_target_pairs={{0,16},{8,24},{16,0},{24,8},{1,17},{9,25},{17,1},{25,9},{2,18},{10... | collective-permute-start | bytes 1081352 | tf_op jit(solution)/shard_map/ppermute | solution.py:618
  (71 other events, 612.5 us)
Sparse Core Ops, SparseCore 0:
  20.4 52.0 all-gather.3
  74.7 106.8 all-gather.5
  183.2 58.7 all-gather.7
  244.4 65.2 reduce-scatter.3
  315.4 102.6 reduce-scatter.5
  420.5 55.5 reduce-scatter.7

commit v4 on v3

--- a/solution.py
+++ b/solution.py
@@ -132,8 +132,12 @@
         out_ref[at, :] = grad_ref[at, :] + grad - normed * jnp.mean(grad * normed, -1, keepdims=True)
 
 
-def block_out_kernel(middle_ref, *refs):
-    refs[-1][...] = (middle_ref[...] + added(refs[:-1])).astype(LOW)
+def block_out_kernel(parts, *refs):
+    middle_ref, refs, out_ref = refs[0], refs[1:-1], refs[-1]
+    per, rows = len(refs) // parts, out_ref.shape[0] // parts
+    for i in range(parts):
+        at = slice(i * rows, (i + 1) * rows)
+        out_ref[at, :] = (middle_ref[at, :] + added(refs[i * per:(i + 1) * per])).astype(LOW)
 
 
 def as_row(column):
@@ -199,11 +203,15 @@
 
 
 def hidden_kernel(count, chunk, *refs):
-    pieces, (weight_ref, slope_ref, hidden_ref, normed_ref, sems) = refs[:count], refs[count:]
-
-    @pl.when(pl.program_id(0) == 0)
+    pieces, refs = refs[:count], refs[count:]
+    weight_ref, slope_ref, hidden_ref, out_ref, normed_ref, sems, out_sem = refs
+    step = pl.program_id(0)
+    out_copy = pltpu.make_async_copy(normed_ref, out_ref, out_sem)
+
+    @pl.when(step == 0)
     def _():
         fetch(pieces, normed_ref, sems)
+        out_copy.start()
 
     both = dot(normed_ref[...], weight_ref[...])
     gate, up = both[:, :chunk], both[:, chunk:]
@@ -213,6 +221,10 @@
     slope_ref[...] = jnp.concatenate([slope, silu], 1).astype(LOW)
     hidden_ref[...] = (silu * up).T.astype(LOW)
 
+    @pl.when(step == pl.num_programs(0) - 1)
+    def _():
+        out_copy.wait()
+
 
 def hidden_of(pieces, weight, chunk):
     tokens, (width, both) = rows_of(pieces), weight.shape
@@ -220,9 +232,9 @@
         functools.partial(hidden_kernel, len(pieces), chunk),
         grid=(both // (2 * chunk),),
         in_specs=[ANY] * len(pieces) + [columns(width, 2 * chunk)],
-        out_specs=(columns(tokens, 2 * chunk), by_rows(chunk, tokens), whole((tokens, width))),
+        out_specs=(columns(tokens, 2 * chunk), by_rows(chunk, tokens), ANY),
         out_shape=(like((tokens, both)), like((both // 2, tokens)), like((tokens, width))),
-        scratch_shapes=[arrivals(len(pieces))],
+        scratch_shapes=[pltpu.VMEM((tokens, width), LOW), arrivals(len(pieces)), pltpu.SemaphoreType.DMA],
         compiler_params=PARAMS,
         name="hidden_of",
     )(*pieces, weight)
@@ -626,19 +638,22 @@
         ad, bd = swap(ax, 2), swap(by, 1)
         return [a, b, ax, bx, ay, by, ad, bd]
 
-    def seq_scatter(pieces):
+    def scatter_start(pieces):
         if parts == 1:
-            return (), [pieces[0]] + [swap(pieces[j], j) for j in range(1, seq_size)]
+            return [swap(pieces[j], j) for j in range(1, seq_size)]
         a, b = pieces[::2], pieces[1::2]
-        da, db = swap(a[3], 2), swap(b[3], 1)
-        ya, xb = swap(a[2], 2), swap(b[1], 1)
+        return [swap(a[3], 2), swap(b[3], 1), swap(a[2], 2), swap(b[1], 1)]
+
+    def scatter_end(pieces, came):
+        if parts == 1:
+            return (), [pieces[0], *came]
+        a, b, (da, db, ya, xb) = pieces[::2], pieces[1::2], came
         da = (a[1].astype(FULL) + da.astype(FULL)).astype(LOW)
         db = (b[2].astype(FULL) + db.astype(FULL)).astype(LOW)
-        xa, yb = swap(da, 1), swap(db, 2)
-        return (da, db), [a[0], ya, xa, b[0], xb, yb]
-
-    def direct_scatter(blocks):
-        return [blocks[0]] + [swap(blocks[j], j) for j in range(1, seq_size)]
+        return (da, db), [a[0], ya, swap(da, 1), b[0], xb, swap(db, 2)]
+
+    def seq_scatter(pieces):
+        return scatter_end(pieces, scatter_start(pieces))
 
     def spread(pieces_for):
         got = [pieces_for(here)] + [swap(pieces_for(here ^ j), j) for j in range(1, seq_size)]
@@ -745,20 +760,21 @@
     )
 
     branch_pieces = seq_gather(own_pieces)
-    out_pieces = rows_of_product(after(hidden, own_pieces[0]), down_full, span)
-    out_pieces = lax.optimization_barrier((*out_pieces, *branch_pieces))[:seq_size]
-    out_pieces = direct_scatter(out_pieces)
+    out_pieces = rows_of_product(after(hidden, own_pieces[0]), down_full, piece_rows)
+    out_pieces = lax.optimization_barrier((*out_pieces, *branch_pieces))[:len(out_pieces)]
+    out_came = scatter_start(out_pieces)
     grad_qkv, grad_qkv_turned = attend_back(
         order, rank, branch_pieces, projections.reshape(fsdp_size, seq_size, own_rows, -1), qrot, kv, mix, lse,
         cosine, sine, inv_one, heads, kvs, span,
     )
-    grad_qkv, *out_pieces = lax.optimization_barrier((grad_qkv, *out_pieces))
+    grad_qkv, grad_qkv_turned, *out_came = lax.optimization_barrier((grad_qkv, grad_qkv_turned, *out_came))
     part_projections = attention_weights_of(token_pieces, branch_pieces, grad_qkv, attended, into)
-    grad_pieces = grad_rows_of(after(grad_qkv_turned, part_projections), projections, piece_rows)
-    grad_projections = fsdp_scatter(after(part_projections, grad_gate_up_own, grad_pieces[0]))
-    grad_pieces = seq_scatter(grad_pieces)[1]
+    grad_pieces = grad_rows_of(grad_qkv_turned, projections, piece_rows)
+    first, grad_pieces = seq_scatter(grad_pieces)
+    grad_projections = fsdp_scatter(after(part_projections, grad_gate_up_own, *first))
     got = collect(after(grad_gate_up_own, *grad_pieces))
-    block_out = call_own(block_out_kernel, like((span, width)), middle, *out_pieces)
+    out_pieces = scatter_end(out_pieces, out_came)[1]
+    block_out = call_own(functools.partial(block_out_kernel, parts), like((span, width)), middle, *out_pieces)
 
 
     def whole_rows(x):

time: 506 us -> 503 us (level)
  waiting for transfers between devices: 179 us -> 171 us
    ppermute x54 -> x57, waiting for transfers between devices: 178 us -> 170 us  [swap(): return lax.ppermute(x, 'seq', [(i, i ^ j) for i in range(seq_size)])]
    ppermute x54 -> x57, starting transfers between devices: 60.2 us -> 62.9 us  [swap(): return lax.ppermute(x, 'seq', [(i, i ^ j) for i in range(seq_size)])]
  transfers between devices with their start and end apart: 62 -> 65, of which waited for: 29 -> 30; matrix products, arithmetic and copies ran while one was open for 3% -> 3% of each run, Pallas kernels for 43% -> 43%
where the time goes in v4:
time: 503 us; the launch traced here: 495 us
  Pallas kernels  218 us (43%)
  waiting for transfers between devices  171 us (34%)
  starting transfers between devices  63.6 us (13%)
  between operations  15.5 us (3%)
  local copies, waits for them, and re-layouts  13.8 us (3%)
  other arithmetic  13.7 us (3%)
    ppermute x57, waiting for transfers between devices, swap(): return lax.ppermute(x, 'seq', [(i, i ^ j) for i in range(seq_size)])  170 us
    ppermute x57, starting transfers between devices, swap(): return lax.ppermute(x, 'seq', [(i, i ^ j) for i in range(seq_size)])  62.9 us
    pallas_call x1, Pallas kernels, attend_back(): pl.pallas_call(functools.partial(attend_back_kernel, heads, kvs, span, le...  34.7 us
    pallas_call x1, Pallas kernels, attend(): pl.pallas_call(functools.partial(attend_kernel, heads, kvs, span, len(pie...  34.2 us
    pallas_call x7, Pallas kernels, call_own(): pl.pallas_call(kernel, out_shape=out_shape, in_specs=[SMEM] * len(scalars...  29.8 us
    pallas_call x2, Pallas kernels, grad_rows_of(): pl.pallas_call(functools.partial(grad_rows_kernel, weight.shape[1] - grad...  25.3 us
    pallas_call x1, Pallas kernels, hidden_of(): pl.pallas_call(functools.partial(hidden_kernel, len(pieces), chunk), grid...  20.2 us
    pallas_call x1, Pallas kernels, grad_weight_of(): pl.pallas_call(grad_weight_kernel, grid_spec=pltpu.PrefetchScalarGridSpec...  18.7 us
  transfers between devices with their start and end apart: 65, of which 30 were waited for; matrix products, arithmetic and copies ran while one was open for 3% of the time, Pallas kernels for 43%

profile of v4, /device:TPU:0, one launch (start us, length us, event | category | flops | bytes accessed | tf_op | source)
XLA Modules:
  0.0 495.0 jit_solution(10621942108840976236)
XLA Ops:
  10.2 3.9 collective-permute-start.8
  15.0 1.7 collective-permute-done.8
  16.7 1.9 collective-permute-done.7
  20.4 2.6 regroup_kernel.1
  27.9 8.8 %collective-permute-done.11 = bf16[64,2816]{1,0:T(8,128)(2,1)S(1)} collective-permute-done((bf16[64,2816]{1,0:T(8,128)(2,1)S(1)}, bf16[64,2816]{1,0:T(8,128)(2,1)S(1)}, u32[]{:S(2)}, u32[]{:S(2)}) %collective-permute-start.11) | collective-permute-done | bytes 360480 | tf_op jit(solution)/shard_map/ppermute | solution.py:630
  36.7 5.5 %collective-permute-done.10 = bf16[64,2816]{1,0:T(8,128)(2,1)S(1)} collective-permute-done((bf16[64,2816]{1,0:T(8,128)(2,1)S(1)}, bf16[64,2816]{1,0:T(8,128)(2,1)S(1)}, u32[]{:S(2)}, u32[]{:S(2)}) %collective-permute-start.10) | collective-permute-done | bytes 360480 | tf_op jit(solution)/shard_map/ppermute | solution.py:630
  49.1 10.8 %collective-permute-done.refs_2_ = bf16[128,2048]{1,0:T(8,128)(2,1)S(1)} collective-permute-done((bf16[128,2048]{1,0:T(8,128)(2,1)S(1)}, bf16[128,2048]{1,0:T(8,128)(2,1)S(1)}, u32[]{:S(2)}, u32[]{:S(2)}) %collective-permute-start) | collective-permute-done | bytes 524320 | tf_op jit(solution)/shard_map/ppermute | solution.py:630
  61.9 9.2 %collective-permute-done.1.refs_3_ = bf16[128,2048]{1,0:T(8,128)(2,1)S(1)} collective-permute-done((bf16[128,2048]{1,0:T(8,128)(2,1)S(1)}, bf16[128,2048]{1,0:T(8,128)(2,1)S(1)}, u32[]{:S(2)}, u32[]{:S(2)}) %collective-permute-start.1) | collective-permute-done | bytes 524320 | tf_op jit(solution)/shard_map/ppermute | solution.py:630
  72.4 10.1 %collective-permute-done.4.refs_6_ = bf16[128,2048]{1,0:T(8,128)(2,1)S(1)} collective-permute-done((bf16[128,2048]{1,0:T(8,128)(2,1)S(1)}, bf16[128,2048]{1,0:T(8,128)(2,1)S(1)}, u32[]{:S(2)}, u32[]{:S(2)}) %collective-permute-start.4) | collective-permute-done | bytes 524320 | tf_op jit(solution)/shard_map/ppermute | solution.py:630
  83.1 1.6 collective-permute-start.13
  89.6 34.2 %attend.1 = (bf16[512,1024]{1,0:T(8,128)(2,1)}, bf16[128,1024]{1,0:T(8,128)(2,1)}, bf16[512,1024]{1,0:T(8,128)(2,1)}, f32[512,1024]{1,0:T(8,128)}, f32[8,1024]{1,0:T(8,128)}, /*index=5*/f32[1,1024]{1,0:T(1,128)}) custom-call(s32[4]{0:T(128)} %get-tuple-element.108.order_ref, s32[4]{0:T(128)} %copy-done.58, bf16[128,2048]{1,0:T(8,128)(2,1)} %get-tuple-element.109.refs_0_, ...), custom_call_target="tpu_custom_call" | custom-call | tf_op jit(solution)/shard_map/attend/pallas_call | solution.py:489
  123.8 5.5 %collective-permute-done.13.refs_2_ = bf16[256,2048]{1,0:T(8,128)(2,1)S(1)} collective-permute-done((bf16[256,2048]{1,0:T(8,128)(2,1)S(1)}, bf16[256,2048]{1,0:T(8,128)(2,1)S(1)}, u32[]{:S(2)}, u32[]{:S(2)}) %collective-permute-start.13) | collective-permute-done | bytes 1048608 | tf_op jit(solution)/shard_map/ppermute | solution.py:630
  129.4 6.4 %rows_of_product.2 = (bf16[128,2048]{1,0:T(8,128)(2,1)}, bf16[128,2048]{1,0:T(8,128)(2,1)}, bf16[128,2048]{1,0:T(8,128)(2,1)}, bf16[128,2048]{1,0:T(8,128)(2,1)}...) custom-call(bf16[512,1024]{1,0:T(8,128)(2,1)} %get-tuple-element.115, ...), custom_call_target="tpu_custom_call" | custom-call | tf_op jit(solution)/shard_map/rows_of_product/pallas_call | solution.py:373
  135.8 1.6 collective-permute-start.16
  139.9 11.0 %collective-permute-done.16 = bf16[128,2048]{1,0:T(8,128)(2,1)S(1)} collective-permute-done((bf16[128,2048]{1,0:T(8,128)(2,1)}, bf16[128,2048]{1,0:T(8,128)(2,1)S(1)}, u32[]{:S(2)}, u32[]{:S(2)}) %collective-permute-start.16) | collective-permute-done | bytes 524320 | tf_op jit(solution)/shard_map/ppermute | solution.py:630
  152.2 1.6 collective-permute-start.17
  154.5 7.7 %collective-permute-done.15.refs_2_ = bf16[128,2048]{1,0:T(8,128)(2,1)S(1)} collective-permute-done((bf16[128,2048]{1,0:T(8,128)(2,1)}, bf16[128,2048]{1,0:T(8,128)(2,1)S(1)}, u32[]{:S(2)}, u32[]{:S(2)}) %collective-permute-start.15) | collective-permute-done | bytes 524320 | tf_op jit(solution)/shard_map/ppermute | solution.py:630
  163.7 7.4 %collective-permute-done.17.refs_3_ = bf16[128,2048]{1,0:T(8,128)(2,1)S(1)} collective-permute-done((bf16[128,2048]{1,0:T(8,128)(2,1)S(1)}, bf16[128,2048]{1,0:T(8,128)(2,1)S(1)}, u32[]{:S(2)}, u32[]{:S(2)}) %collective-permute-start.17) | collective-permute-done | bytes 524320 | tf_op jit(solution)/shard_map/ppermute | solution.py:630
  172.1 4.9 middle_kernel.1
  181.1 11.0 %collective-permute-done.21.refs_2_ = bf16[128,2048]{1,0:T(8,128)(2,1)S(1)} collective-permute-done((bf16[128,2048]{1,0:T(8,128)(2,1)}, bf16[128,2048]{1,0:T(8,128)(2,1)S(1)}, u32[]{:S(2)}, u32[]{:S(2)}) %collective-permute-start.21) | collective-permute-done | bytes 524320 | tf_op jit(solution)/shard_map/ppermute | solution.py:630
  194.1 9.2 %collective-permute-done.22.refs_3_ = bf16[128,2048]{1,0:T(8,128)(2,1)S(1)} collective-permute-done((bf16[128,2048]{1,0:T(8,128)(2,1)}, bf16[128,2048]{1,0:T(8,128)(2,1)S(1)}, u32[]{:S(2)}, u32[]{:S(2)}) %collective-permute-start.22) | collective-permute-done | bytes 524320 | tf_op jit(solution)/shard_map/ppermute | solution.py:630
  203.9 6.4 %collective-permute-done.25.refs_6_ = bf16[128,2048]{1,0:T(8,128)(2,1)S(1)} collective-permute-done((bf16[128,2048]{1,0:T(8,128)(2,1)S(1)}, bf16[128,2048]{1,0:T(8,128)(2,1)S(1)}, u32[]{:S(2)}, u32[]{:S(2)}) %collective-permute-start.25) | collective-permute-done | bytes 524320 | tf_op jit(solution)/shard_map/ppermute | solution.py:630
  211.3 20.2 %hidden_of.1 = (bf16[1024,2816]{1,0:T(8,128)(2,1)}, bf16[1408,1024]{1,0:T(8,128)(2,1)}, bf16[1024,2048]{1,0:T(8,128)(2,1)}) custom-call(bf16[128,2048]{1,0:T(8,128)(2,1)} %get-tuple-element.125.refs_0_, bf16[128,2048]{1,0:T(8,128)(2,1)} %get-tuple-element.126.refs_1_, bf16[128,2048]{1,0:T(8,128)(2,1)} %copy-done.37, bf16[128,2048]{1,0:T(8,128)(2,1)} %copy-done.41, ...), custom_call_target="tpu_custom_call" | custom-call | tf_op jit(solution)/shard_map/hidden_of/pallas_call | solution.py:231
  231.6 11.8 %grad_down_of.1 = bf16[1408,2048]{1,0:T(8,128)(2,1)} custom-call(bf16[256,2048]{1,0:T(8,128)(2,1)} %bitcast.71, bf16[256,2048]{1,0:T(8,128)(2,1)} %copy-done.1, bf16[256,2048]{1,0:T(8,128)(2,1)} %copy-done.2, bf16[256,2048]{1,0:T(8,128)(2,1)} %collective-permute-done.14.refs_3_, bf16[1408,1024]{1,0:T(8,128)(2,1)} %get-tuple-element.153.refs_4_.left_ref), custom_call_target="tpu_custom_call" | custom-call | tf_op jit(solution)/shard_map/grad_down_of/pallas_call | solution.py:251
  243.5 14.3 %grad_gate_up_of.1.grad_ref = bf16[1024,2816]{1,0:T(8,128)(2,1)} custom-call(bf16[256,2048]{1,0:T(8,128)(2,1)} %bitcast.72, bf16[256,2048]{1,0:T(8,128)(2,1)} %copy-done.1, bf16[256,2048]{1,0:T(8,128)(2,1)} %copy-done.2, bf16[256,2048]{1,0:T(8,128)(2,1)} %collective-permute-done.14.refs_3_, ...), custom_call_target="tpu_custom_call" | custom-call | tf_op jit(solution)/shard_map/grad_gate_up_of/pallas_call | solution.py:290
  258.4 17.2 %grad_rows_of.2 = (bf16[128,2048]{1,0:T(8,128)(2,1)}, bf16[128,2048]{1,0:T(8,128)(2,1)}, bf16[128,2048]{1,0:T(8,128)(2,1)}, bf16[128,2048]{1,0:T(8,128)(2,1)}, b...) custom-call(bf16[1024,2816]{1,0:T(8,128)(2,1)} %grad_gate_up_of.1.gr, ...), custom_call_target="tpu_custom_call" | custom-call | tf_op jit(solution)/shard_map/grad_rows_of/pallas_call | solution.py:312
  275.6 1.7 collective-permute-start.27
  277.5 1.6 collective-permute-start.31
  279.1 11.5 %collective-permute-done.27 = bf16[128,2048]{1,0:T(8,128)(2,1)S(1)} collective-permute-done((bf16[128,2048]{1,0:T(8,128)(2,1)}, bf16[128,2048]{1,0:T(8,128)(2,1)S(1)}, u32[]{:S(2)}, u32[]{:S(2)}) %collective-permute-start.27) | collective-permute-done | bytes 524320 | tf_op jit(solution)/shard_map/ppermute | solution.py:630
  294.1 1.6 collective-permute-start.34
  295.8 18.7 %grad_weight_of.1 = bf16[1024,2816]{1,0:T(8,128)(2,1)} custom-call(s32[1]{0:T(128)} %bitcast.21.core_ref, bf16[1024,2048]{1,0:T(8,128)(2,1)} %get-tuple-element.140.left_ref, bf16[1024,2048]{1,0:T(8,128)(2,1)} %collective-permute-done.29.other_left_ref, bf16[1024,2816]{1,0:T(8,128)(2,1)} %grad_gate_up_of.1.grad_ref, ...), custom_call_target="tpu_custom_call" | custom-call | tf_op jit(solution)/shard_map/grad_weight_of/pallas_call | solution.py:333
  315.8 6.0 %grad_middle_kernel.1 = (f32[256,2048]{1,0:T(8,128)}, bf16[128,2048]{1,0:T(8,128)(2,1)}, bf16[128,2048]{1,0:T(8,128)(2,1)}) custom-call(bf16[256,2048]{1,0:T(8,128)(2,1)} %bitcast.73, f32[256,2048]{1,0:T(8,128)} %get-tuple-element.124.refs_1_.refs_0_, f32[256,1]{1,0:T(8,128)} %get-tuple-element.128.refs_2_, bf16[128,2048]{1,0:T(8,128)(2,1)} %get-tuple-element.146.refs_3_, ...), custom_call_target="tpu_custom_call" | custom-call | tf_op jit(solution)/shard_map/grad_middle_kernel/pallas_call | solution.py:73
  325.8 11.0 %collective-permute-done.35.refs_2_.refs_10_ = bf16[128,2048]{1,0:T(8,128)(2,1)S(1)} collective-permute-done((bf16[128,2048]{1,0:T(8,128)(2,1)}, bf16[128,2048]{1,0:T(8,128)(2,1)S(1)}, u32[]{:S(2)}, u32[]{:S(2)}) %collective-permute-start.35) | collective-permute-done | bytes 524320 | tf_op jit(solution)/shard_map/ppermute | solution.py:630
  338.9 11.7 %rows_of_product.3 = (bf16[128,2048]{1,0:T(8,128)(2,1)}, bf16[128,2048]{1,0:T(8,128)(2,1)}, bf16[128,2048]{1,0:T(8,128)(2,1)}, bf16[128,2048]{1,0:T(8,128)(2,1)}...) custom-call(bf16[1408,1024]{1,0:T(8,128)(2,1)} %get-tuple-element.15, ...), custom_call_target="tpu_custom_call" | custom-call | tf_op jit(solution)/shard_map/rows_of_product/pallas_call | solution.py:373
  350.6 6.3 %collective-permute-done.39.refs_6_.refs_14_ = bf16[128,2048]{1,0:T(8,128)(2,1)S(1)} collective-permute-done((bf16[128,2048]{1,0:T(8,128)(2,1)S(1)}, bf16[128,2048]{1,0:T(8,128)(2,1)S(1)}, u32[]{:S(2)}, u32[]{:S(2)}) %collective-permute-start.39) | collective-permute-done | bytes 524320 | tf_op jit(solution)/shard_map/ppermute | solution.py:630
  361.1 34.7 %attend_back.1 = (bf16[640,1024]{1,0:T(8,128)(2,1)}, bf16[1024,640]{1,0:T(8,128)(2,1)}) custom-call(s32[4]{0:T(128)} %get-tuple-element.108.order_ref, s32[4]{0:T(128)} %copy-done.58, bf16[128,2048]{1,0:T(8,128)(2,1)} %get-tuple-element.152.refs_0_.refs_8_, bf16[128,2048]{1,0:T(8,128)(2,1)} %get-tuple-element.162.refs_1_.refs_9_, ...), custom_call_target="tpu_custom_call" | custom-call | tf_op jit(solution)/shard_map/attend_back/pallas_call | solution.py:592
  395.9 8.1 %grad_rows_of.3 = (bf16[128,2048]{1,0:T(8,128)(2,1)}, bf16[128,2048]{1,0:T(8,128)(2,1)}, bf16[128,2048]{1,0:T(8,128)(2,1)}, bf16[128,2048]{1,0:T(8,128)(2,1)}, b...) custom-call(bf16[1024,640]{1,0:T(8,128)(2,1)} %get-tuple-element.183, ...), custom_call_target="tpu_custom_call" | custom-call | tf_op jit(solution)/shard_map/grad_rows_of/pallas_call | solution.py:312
  406.3 10.6 %attention_weights_of.1 = bf16[2048,1152]{1,0:T(8,128)(2,1)} custom-call(bf16[128,2048]{1,0:T(8,128)(2,1)} %get-tuple-element.109.refs_0_, bf16[128,2048]{1,0:T(8,128)(2,1)} %get-tuple-element.110.refs_1_, bf16[128,2048]{1,0:T(8,128)(2,1)} %copy-done.7, bf16[128,2048]{1,0:T(8,128)(2,1)} %copy-done.9, bf16[128,2048]{1,0:T(8,128)(2,1)} %copy-done.10, ...), custom_call_target="tpu_custom_call" | custom-call | tf_op jit(solution)/shard_map/attention_weights_of/pallas_call | solution.py:407
  425.4 8.6 %collective-permute-done.47.refs_3_ = bf16[128,2048]{1,0:T(8,128)(2,1)S(1)} collective-permute-done((bf16[128,2048]{1,0:T(8,128)(2,1)S(1)}, bf16[128,2048]{1,0:T(8,128)(2,1)S(1)}, u32[]{:S(2)}, u32[]{:S(2)}) %collective-permute-start.47) | collective-permute-done | bytes 524320 | tf_op jit(solution)/shard_map/ppermute | solution.py:630
  435.3 11.2 %collective-permute-done.49.refs_4_ = bf16[128,2048]{1,0:T(8,128)(2,1)S(1)} collective-permute-done((bf16[128,2048]{1,0:T(8,128)(2,1)S(1)}, bf16[128,2048]{1,0:T(8,128)(2,1)S(1)}, u32[]{:S(2)}, u32[]{:S(2)}) %collective-permute-start.49) | collective-permute-done | bytes 524320 | tf_op jit(solution)/shard_map/ppermute | solution.py:630
  449.5 1.8 collective-permute-start.55
  452.1 5.7 %collective-permute-done.45.refs_3_ = bf16[128,2048]{1,0:T(8,128)(2,1)S(1)} collective-permute-done((bf16[128,2048]{1,0:T(8,128)(2,1)S(1)}, bf16[128,2048]{1,0:T(8,128)(2,1)S(1)}, u32[]{:S(2)}, u32[]{:S(2)}) %collective-permute-start.45) | collective-permute-done | bytes 524320 | tf_op jit(solution)/shard_map/ppermute | solution.py:630
  459.4 3.9 block_out_kernel.1
  463.3 5.6 %grad_tokens_kernel.1 = f32[256,2048]{1,0:T(8,128)} custom-call(bf16[256,2048]{1,0:T(8,128)(2,1)} %bitcast.70, f32[256,2048]{1,0:T(8,128)} %get-tuple-element.182.refs_1_, bf16[128,2048]{1,0:T(8,128)(2,1)} %get-tuple-element.184.refs_2_, bf16[128,2048]{1,0:T(8,128)(2,1)} %copy-done.27, bf16[128,2048]{1,0:T(8,128)(2,1)} %copy-done.30, ...), custom_call_target="tpu_custom_call" | custom-call | tf_op jit(solution)/shard_map/grad_tokens_kernel/pallas_call | solution.py:73
  468.9 1.6 collective-permute-done.55.refs_3_
  470.5 4.2 finish_gate_up_kernel.1
  482.5 2.4 collective-permute-done.58.refs_3_
  485.4 2.5 finish_projections_kernel.1
  (296 shorter events, 81.8 us)
Async XLA Ops:
  7.2 82.4 %all-gather.4.cloned.1.call-start = ((), (), s32[]{:S(2)}) async-start(), calls=%async_computation.3 | async-start | bytes 5308416 | tf_op jit(solution)/shard_map/all_gather | solution.py:676
  20.3 190.1 %all-gather.6.cloned.1.call-start = ((), (), s32[]{:S(2)}) async-start(), calls=%async_computation.4 | async-start | bytes 12976128 | tf_op jit(solution)/shard_map/all_gather | solution.py:676
  25.9 16.3 %collective-permute-start.10 = (bf16[64,2816]{1,0:T(8,128)(2,1)S(1)}, bf16[64,2816]{1,0:T(8,128)(2,1)S(1)}, u32[]{:S(2)}, u32[]{:S(2)}) collective-permute-start(bf16[64,2816]{1,0:T(8,128)(2,1)S(1)} %get-tuple-element.295), channel_id=1, source_target_pairs={{0,16},{8,24},{16,0},{24,8},{1,17},{9,25},{17,1},{25,9},{2,18},{10... | collective-permute-start | bytes 1081352 | tf_op jit(solution)/shard_map/ppermute | solution.py:630
  26.7 15.7 %collective-permute-start.9 = (bf16[64,2816]{1,0:T(8,128)(2,1)S(1)}, bf16[64,2816]{1,0:T(8,128)(2,1)S(1)}, u32[]{:S(2)}, u32[]{:S(2)}) collective-permute-start(bf16[64,2816]{1,0:T(8,128)(2,1)S(1)} %get-tuple-element.293), channel_id=1, source_target_pairs={{0,8},{8,0},{16,24},{24,16},{1,9},{9,1},{17,25},{25,17},{2,10},{10... | collective-permute-start | bytes 1081352 | tf_op jit(solution)/shard_map/ppermute | solution.py:630
  44.0 199.5 %all-gather.8.cloned.1.call-start = ((), (), s32[]{:S(2)}) async-start(), calls=%async_computation.5 | async-start | bytes 6488064 | tf_op jit(solution)/shard_map/all_gather | solution.py:676
  44.7 271.1 %reduce-scatter.4.cloned.1.call-start = ((), (), s32[]{:S(2)}) async-start(), calls=%async_computation.6 | async-start | bytes 6488064 | tf_op jit(solution)/shard_map/reduce_scatter | solution.py:685
  47.0 24.0 %collective-permute-start.1 = (bf16[128,2048]{1,0:T(8,128)(2,1)S(1)}, bf16[128,2048]{1,0:T(8,128)(2,1)S(1)}, u32[]{:S(2)}, u32[]{:S(2)}) collective-permute-start(bf16[128,2048]{1,0:T(8,128)(2,1)S(1)} %copy-done.6), channel_id=1, source_target_pairs={{0,8},{8,0},{16,24},{24,16},{1,9},{9,1},{17,25},{25,17},{2,10},{10... | collective-permute-start | bytes 1572872 | tf_op jit(solution)/shard_map/ppermute | solution.py:630
  48.4 24.0 %collective-permute-start.2 = (bf16[128,2048]{1,0:T(8,128)(2,1)S(1)}, bf16[128,2048]{1,0:T(8,128)(2,1)S(1)}, u32[]{:S(2)}, u32[]{:S(2)}) collective-permute-start(bf16[128,2048]{1,0:T(8,128)(2,1)S(1)} %copy-done.5), channel_id=1, source_target_pairs={{0,16},{8,24},{16,0},{24,8},{1,17},{9,25},{17,1},{25,9},{2,18},{10... | collective-permute-start | bytes 1572872 | tf_op jit(solution)/shard_map/ppermute | solution.py:630
  59.8 22.7 %collective-permute-start.4 = (bf16[128,2048]{1,0:T(8,128)(2,1)S(1)}, bf16[128,2048]{1,0:T(8,128)(2,1)S(1)}, u32[]{:S(2)}, u32[]{:S(2)}) collective-permute-start(bf16[128,2048]{1,0:T(8,128)(2,1)S(1)} %collective-permute-done.refs_2_), channel_id=1, source_target_pairs={{0,16},{8,24},{16,0},{24,8},{1,17},{9,25},{17,1},{25,9},{2,18},{10... | collective-permute-start | bytes 1572872 | tf_op jit(solution)/shard_map/ppermute | solution.py:630
  61.2 21.3 %collective-permute-start.5 = (bf16[128,2048]{1,0:T(8,128)(2,1)S(1)}, bf16[128,2048]{1,0:T(8,128)(2,1)S(1)}, u32[]{:S(2)}, u32[]{:S(2)}) collective-permute-start(bf16[128,2048]{1,0:T(8,128)(2,1)S(1)} %collective-permute-done.3.refs_5_), channel_id=1, source_target_pairs={{0,8},{8,0},{16,24},{24,16},{1,9},{9,1},{17,25},{25,17},{2,10},{10... | collective-permute-start | bytes 1572872 | tf_op jit(solution)/shard_map/ppermute | solution.py:630
  82.5 41.3 %collective-permute-start.12 = (bf16[256,2048]{1,0:T(8,128)(2,1)S(1)}, bf16[256,2048]{1,0:T(8,128)(2,1)S(1)}, u32[]{:S(2)}, u32[]{:S(2)}) collective-permute-start(bf16[256,2048]{1,0:T(8,128)(2,1)S(1)} %bitcast.74), channel_id=1, source_target_pairs={{0,8},{8,0},{16,24},{24,16},{1,9},{9,1},{17,25},{25,17},{2,10},{10... | collective-permute-start | bytes 3145736 | tf_op jit(solution)/shard_map/ppermute | solution.py:630
  83.1 46.3 %collective-permute-start.13 = (bf16[256,2048]{1,0:T(8,128)(2,1)S(1)}, bf16[256,2048]{1,0:T(8,128)(2,1)S(1)}, u32[]{:S(2)}, u32[]{:S(2)}) collective-permute-start(bf16[256,2048]{1,0:T(8,128)(2,1)S(1)} %bitcast.75), channel_id=1, source_target_pairs={{0,16},{8,24},{16,0},{24,8},{1,17},{9,25},{17,1},{25,9},{2,18},{10... | collective-permute-start | bytes 3145736 | tf_op jit(solution)/shard_map/ppermute | solution.py:630
  84.7 44.7 %collective-permute-start.14 = (bf16[256,2048]{1,0:T(8,128)(2,1)S(1)}, bf16[256,2048]{1,0:T(8,128)(2,1)}, u32[]{:S(2)}, u32[]{:S(2)}) collective-permute-start(bf16[256,2048]{1,0:T(8,128)(2,1)S(1)} %bitcast.76), channel_id=1, source_target_pairs={{0,24},{8,16},{16,8},{24,0},{1,25},{9,17},{17,9},{25,1},{2,26},{10... | collective-permute-start | bytes 3145736 | tf_op jit(solution)/shard_map/ppermute | solution.py:630
  135.8 15.1 %collective-permute-start.16 = (bf16[128,2048]{1,0:T(8,128)(2,1)}, bf16[128,2048]{1,0:T(8,128)(2,1)S(1)}, u32[]{:S(2)}, u32[]{:S(2)}) collective-permute-start(bf16[128,2048]{1,0:T(8,128)(2,1)} %get-tuple-element.119), channel_id=1, source_target_pairs={{0,16},{8,24},{16,0},{24,8},{1,17},{9,25},{17,1},{25,9},{2,18},{10... | collective-permute-start | bytes 1572872 | tf_op jit(solution)/shard_map/ppermute | solution.py:630
  137.4 16.4 %collective-permute-start.19 = (bf16[128,2048]{1,0:T(8,128)(2,1)}, bf16[128,2048]{1,0:T(8,128)(2,1)S(1)}, u32[]{:S(2)}, u32[]{:S(2)}) collective-permute-start(bf16[128,2048]{1,0:T(8,128)(2,1)} %get-tuple-element.123), channel_id=1, source_target_pairs={{0,8},{8,0},{16,24},{24,16},{1,9},{9,1},{17,25},{25,17},{2,10},{10... | collective-permute-start | bytes 1572872 | tf_op jit(solution)/shard_map/ppermute | solution.py:630
  137.9 24.2 %collective-permute-start.15 = (bf16[128,2048]{1,0:T(8,128)(2,1)}, bf16[128,2048]{1,0:T(8,128)(2,1)S(1)}, u32[]{:S(2)}, u32[]{:S(2)}) collective-permute-start(bf16[128,2048]{1,0:T(8,128)(2,1)} %get-tuple-element.117), channel_id=1, source_target_pairs={{0,16},{8,24},{16,0},{24,8},{1,17},{9,25},{17,1},{25,9},{2,18},{10... | collective-permute-start | bytes 1572872 | tf_op jit(solution)/shard_map/ppermute | solution.py:630
  139.4 24.3 %collective-permute-start.18 = (bf16[128,2048]{1,0:T(8,128)(2,1)}, bf16[128,2048]{1,0:T(8,128)(2,1)S(1)}, u32[]{:S(2)}, u32[]{:S(2)}) collective-permute-start(bf16[128,2048]{1,0:T(8,128)(2,1)} %get-tuple-element.121), channel_id=1, source_target_pairs={{0,8},{8,0},{16,24},{24,16},{1,9},{9,1},{17,25},{25,17},{2,10},{10... | collective-permute-start | bytes 1572872 | tf_op jit(solution)/shard_map/ppermute | solution.py:630
  152.2 19.0 %collective-permute-start.17 = (bf16[128,2048]{1,0:T(8,128)(2,1)S(1)}, bf16[128,2048]{1,0:T(8,128)(2,1)S(1)}, u32[]{:S(2)}, u32[]{:S(2)}) collective-permute-start(bf16[128,2048]{1,0:T(8,128)(2,1)S(1)} %add_convert_fusion.7), channel_id=1, source_target_pairs={{0,8},{8,0},{16,24},{24,16},{1,9},{9,1},{17,25},{25,17},{2,10},{10... | collective-permute-start | bytes 1572872 | tf_op jit(solution)/shard_map/ppermute | solution.py:630
  153.9 17.3 %collective-permute-start.20 = (bf16[128,2048]{1,0:T(8,128)(2,1)S(1)}, bf16[128,2048]{1,0:T(8,128)(2,1)S(1)}, u32[]{:S(2)}, u32[]{:S(2)}) collective-permute-start(bf16[128,2048]{1,0:T(8,128)(2,1)S(1)} %add_convert_fusion.6), channel_id=1, source_target_pairs={{0,16},{8,24},{16,0},{24,8},{1,17},{9,25},{17,1},{25,9},{2,18},{10... | collective-permute-start | bytes 1572872 | tf_op jit(solution)/shard_map/ppermute | solution.py:630
  179.0 24.3 %collective-permute-start.22 = (bf16[128,2048]{1,0:T(8,128)(2,1)}, bf16[128,2048]{1,0:T(8,128)(2,1)S(1)}, u32[]{:S(2)}, u32[]{:S(2)}) collective-permute-start(bf16[128,2048]{1,0:T(8,128)(2,1)} %get-tuple-element.126.refs_1_), channel_id=1, source_target_pairs={{0,8},{8,0},{16,24},{24,16},{1,9},{9,1},{17,25},{25,17},{2,10},{10... | collective-permute-start | bytes 1572872 | tf_op jit(solution)/shard_map/ppermute | solution.py:630
  179.7 24.3 %collective-permute-start.23 = (bf16[128,2048]{1,0:T(8,128)(2,1)}, bf16[128,2048]{1,0:T(8,128)(2,1)S(1)}, u32[]{:S(2)}, u32[]{:S(2)}) collective-permute-start(bf16[128,2048]{1,0:T(8,128)(2,1)} %get-tuple-element.125.refs_0_), channel_id=1, source_target_pairs={{0,16},{8,24},{16,0},{24,8},{1,17},{9,25},{17,1},{25,9},{2,18},{10... | collective-permute-start | bytes 1572872 | tf_op jit(solution)/shard_map/ppermute | solution.py:630
  192.1 18.2 %collective-permute-start.25 = (bf16[128,2048]{1,0:T(8,128)(2,1)S(1)}, bf16[128,2048]{1,0:T(8,128)(2,1)S(1)}, u32[]{:S(2)}, u32[]{:S(2)}) collective-permute-start(bf16[128,2048]{1,0:T(8,128)(2,1)S(1)} %collective-permute-done.21.refs_2_), channel_id=1, source_target_pairs={{0,16},{8,24},{16,0},{24,8},{1,17},{9,25},{17,1},{25,9},{2,18},{10... | collective-permute-start | bytes 1572872 | tf_op jit(solution)/shard_map/ppermute | solution.py:630
  192.7 17.6 %collective-permute-start.26 = (bf16[128,2048]{1,0:T(8,128)(2,1)S(1)}, bf16[128,2048]{1,0:T(8,128)(2,1)S(1)}, u32[]{:S(2)}, u32[]{:S(2)}) collective-permute-start(bf16[128,2048]{1,0:T(8,128)(2,1)S(1)} %collective-permute-done.24.refs_5_), channel_id=1, source_target_pairs={{0,8},{8,0},{16,24},{24,16},{1,9},{9,1},{17,25},{25,17},{2,10},{10... | collective-permute-start | bytes 1572872 | tf_op jit(solution)/shard_map/ppermute | solution.py:630
  243.4 174.7 %reduce-scatter.6.cloned.1.call-start = ((), (), s32[]{:S(2)}) async-start(), calls=%async_computation.7 | async-start | bytes 7208960 | tf_op jit(solution)/shard_map/reduce_scatter | solution.py:682
  257.8 37.9 %collective-permute-start.30 = (bf16[1024,2816]{1,0:T(8,128)(2,1)}, bf16[1024,2816]{1,0:T(8,128)(2,1)}, u32[]{:S(2)}, u32[]{:S(2)}) collective-permute-start(bf16[1024,2816]{1,0:T(8,128)(2,1)} %grad_gate_up_of.1.grad_ref), channel_id=1, source_target_pairs={{0,1},{1,0},{2,3},{3,2},{4,5},{5,4},{6,7},{7,6},{8,9},{9,8},{10,11... | collective-permute-start | bytes 17301512 | tf_op jit(solution)/shard_map/ppermute | solution.py:679
  257.9 36.2 %collective-permute-start.29 = (bf16[1024,2048]{1,0:T(8,128)(2,1)}, bf16[1024,2048]{1,0:T(8,128)(2,1)}, u32[]{:S(2)}, u32[]{:S(2)}) collective-permute-start(bf16[1024,2048]{1,0:T(8,128)(2,1)} %get-tuple-element.140.left_ref), channel_id=1, source_target_pairs={{0,1},{1,0},{2,3},{3,2},{4,5},{5,4},{6,7},{7,6},{8,9},{9,8},{10,11... | collective-permute-start | bytes 12582920 | tf_op jit(solution)/shard_map/ppermute | solution.py:679
  277.2 16.1 %collective-permute-start.28 = (bf16[128,2048]{1,0:T(8,128)(2,1)}, bf16[128,2048]{1,0:T(8,128)(2,1)S(1)}, u32[]{:S(2)}, u32[]{:S(2)}) collective-permute-start(bf16[128,2048]{1,0:T(8,128)(2,1)} %get-tuple-element.139), channel_id=1, source_target_pairs={{0,8},{8,0},{16,24},{24,16},{1,9},{9,1},{17,25},{25,17},{2,10},{10... | collective-permute-start | bytes 1572872 | tf_op jit(solution)/shard_map/ppermute | solution.py:630
  277.5 36.9 %collective-permute-start.31 = (bf16[128,2048]{1,0:T(8,128)(2,1)}, bf16[128,2048]{1,0:T(8,128)(2,1)S(1)}, u32[]{:S(2)}, u32[]{:S(2)}) collective-permute-start(bf16[128,2048]{1,0:T(8,128)(2,1)} %get-tuple-element.142), channel_id=1, source_target_pairs={{0,16},{8,24},{16,0},{24,8},{1,17},{9,25},{17,1},{25,9},{2,18},{10... | collective-permute-start | bytes 1572872 | tf_op jit(solution)/shard_map/ppermute | solution.py:630
  290.6 23.8 %collective-permute-start.33 = (bf16[128,2048]{1,0:T(8,128)(2,1)}, bf16[128,2048]{1,0:T(8,128)(2,1)S(1)}, u32[]{:S(2)}, u32[]{:S(2)}) collective-permute-start(bf16[128,2048]{1,0:T(8,128)(2,1)} %get-tuple-element.144), channel_id=1, source_target_pairs={{0,8},{8,0},{16,24},{24,16},{1,9},{9,1},{17,25},{25,17},{2,10},{10... | collective-permute-start | bytes 1572872 | tf_op jit(solution)/shard_map/ppermute | solution.py:630
  293.3 21.1 %collective-permute-start.32 = (bf16[128,2048]{1,0:T(8,128)(2,1)S(1)}, bf16[128,2048]{1,0:T(8,128)(2,1)S(1)}, u32[]{:S(2)}, u32[]{:S(2)}) collective-permute-start(bf16[128,2048]{1,0:T(8,128)(2,1)S(1)} %add_convert_fusion.5), channel_id=1, source_target_pairs={{0,8},{8,0},{16,24},{24,16},{1,9},{9,1},{17,25},{25,17},{2,10},{10... | collective-permute-start | bytes 1572872 | tf_op jit(solution)/shard_map/ppermute | solution.py:630
  294.1 20.4 %collective-permute-start.34 = (bf16[128,2048]{1,0:T(8,128)(2,1)S(1)}, bf16[128,2048]{1,0:T(8,128)(2,1)S(1)}, u32[]{:S(2)}, u32[]{:S(2)}) collective-permute-start(bf16[128,2048]{1,0:T(8,128)(2,1)S(1)} %add_convert_fusion.4), channel_id=1, source_target_pairs={{0,16},{8,24},{16,0},{24,8},{1,17},{9,25},{17,1},{25,9},{2,18},{10... | collective-permute-start | bytes 1572872 | tf_op jit(solution)/shard_map/ppermute | solution.py:630
  315.8 159.1 %reduce-scatter.8.cloned.1.call-start = ((), (), s32[]{:S(2)}) async-start(), calls=%async_computation.8 | async-start | bytes 5308416 | tf_op jit(solution)/shard_map/reduce_scatter | solution.py:685
  322.5 15.2 %collective-permute-start.38 = (bf16[128,2048]{1,0:T(8,128)(2,1)}, bf16[128,2048]{1,0:T(8,128)(2,1)S(1)}, u32[]{:S(2)}, u32[]{:S(2)}) collective-permute-start(bf16[128,2048]{1,0:T(8,128)(2,1)} %get-tuple-element.162.refs_1_.refs_9_), channel_id=1, source_target_pairs={{0,16},{8,24},{16,0},{24,8},{1,17},{9,25},{17,1},{25,9},{2,18},{10... | collective-permute-start | bytes 1572872 | tf_op jit(solution)/shard_map/ppermute | solution.py:630
  323.4 27.2 %collective-permute-start.36 = (bf16[128,2048]{1,0:T(8,128)(2,1)}, bf16[128,2048]{1,0:T(8,128)(2,1)S(1)}, u32[]{:S(2)}, u32[]{:S(2)}) collective-permute-start(bf16[128,2048]{1,0:T(8,128)(2,1)} %get-tuple-element.162.refs_1_.refs_9_), channel_id=1, source_target_pairs={{0,8},{8,0},{16,24},{24,16},{1,9},{9,1},{17,25},{25,17},{2,10},{10... | collective-permute-start | bytes 1572872 | tf_op jit(solution)/shard_map/ppermute | solution.py:630
  324.7 25.9 %collective-permute-start.37 = (bf16[128,2048]{1,0:T(8,128)(2,1)}, bf16[128,2048]{1,0:T(8,128)(2,1)S(1)}, u32[]{:S(2)}, u32[]{:S(2)}) collective-permute-start(bf16[128,2048]{1,0:T(8,128)(2,1)} %get-tuple-element.152.refs_0_.refs_8_), channel_id=1, source_target_pairs={{0,16},{8,24},{16,0},{24,8},{1,17},{9,25},{17,1},{25,9},{2,18},{10... | collective-permute-start | bytes 1572872 | tf_op jit(solution)/shard_map/ppermute | solution.py:630
  336.8 20.1 %collective-permute-start.39 = (bf16[128,2048]{1,0:T(8,128)(2,1)S(1)}, bf16[128,2048]{1,0:T(8,128)(2,1)S(1)}, u32[]{:S(2)}, u32[]{:S(2)}) collective-permute-start(bf16[128,2048]{1,0:T(8,128)(2,1)S(1)} %collective-permute-done.35.refs_2_.refs_10_), channel_id=1, source_target_pairs={{0,16},{8,24},{16,0},{24,8},{1,17},{9,25},{17,1},{25,9},{2,18},{10... | collective-permute-start | bytes 1572872 | tf_op jit(solution)/shard_map/ppermute | solution.py:630
  337.7 19.2 %collective-permute-start.40 = (bf16[128,2048]{1,0:T(8,128)(2,1)S(1)}, bf16[128,2048]{1,0:T(8,128)(2,1)S(1)}, u32[]{:S(2)}, u32[]{:S(2)}) collective-permute-start(bf16[128,2048]{1,0:T(8,128)(2,1)S(1)} %collective-permute-done.38.refs_5_.refs_13_), channel_id=1, source_target_pairs={{0,8},{8,0},{16,24},{24,16},{1,9},{9,1},{17,25},{25,17},{2,10},{10... | collective-permute-start | bytes 1572872 | tf_op jit(solution)/shard_map/ppermute | solution.py:630
  356.9 38.9 %collective-permute-start.41 = (bf16[128,2048]{1,0:T(8,128)(2,1)}, bf16[128,2048]{1,0:T(8,128)(2,1)}, u32[]{:S(2)}, u32[]{:S(2)}) collective-permute-start(bf16[128,2048]{1,0:T(8,128)(2,1)} %get-tuple-element.171), channel_id=1, source_target_pairs={{0,16},{8,24},{16,0},{24,8},{1,17},{9,25},{17,1},{25,9},{2,18},{10... | collective-permute-start | bytes 1572872 | tf_op jit(solution)/shard_map/ppermute | solution.py:630
  357.8 38.0 %collective-permute-start.42 = (bf16[128,2048]{1,0:T(8,128)(2,1)}, bf16[128,2048]{1,0:T(8,128)(2,1)S(1)}, u32[]{:S(2)}, u32[]{:S(2)}) collective-permute-start(bf16[128,2048]{1,0:T(8,128)(2,1)} %get-tuple-element.172), channel_id=1, source_target_pairs={{0,8},{8,0},{16,24},{24,16},{1,9},{9,1},{17,25},{25,17},{2,10},{10... | collective-permute-start | bytes 1572872 | tf_op jit(solution)/shard_map/ppermute | solution.py:630
  359.1 36.7 %collective-permute-start.43 = (bf16[128,2048]{1,0:T(8,128)(2,1)}, bf16[128,2048]{1,0:T(8,128)(2,1)S(1)}, u32[]{:S(2)}, u32[]{:S(2)}) collective-permute-start(bf16[128,2048]{1,0:T(8,128)(2,1)} %get-tuple-element.173), channel_id=1, source_target_pairs={{0,16},{8,24},{16,0},{24,8},{1,17},{9,25},{17,1},{25,9},{2,18},{10... | collective-permute-start | bytes 1572872 | tf_op jit(solution)/shard_map/ppermute | solution.py:630
  360.3 35.6 %collective-permute-start.44 = (bf16[128,2048]{1,0:T(8,128)(2,1)}, bf16[128,2048]{1,0:T(8,128)(2,1)S(1)}, u32[]{:S(2)}, u32[]{:S(2)}) collective-permute-start(bf16[128,2048]{1,0:T(8,128)(2,1)} %get-tuple-element.174), channel_id=1, source_target_pairs={{0,8},{8,0},{16,24},{24,16},{1,9},{9,1},{17,25},{25,17},{2,10},{10... | collective-permute-start | bytes 1572872 | tf_op jit(solution)/shard_map/ppermute | solution.py:630
  421.0 25.5 %collective-permute-start.49 = (bf16[128,2048]{1,0:T(8,128)(2,1)S(1)}, bf16[128,2048]{1,0:T(8,128)(2,1)S(1)}, u32[]{:S(2)}, u32[]{:S(2)}) collective-permute-start(bf16[128,2048]{1,0:T(8,128)(2,1)S(1)} %add_convert_fusion.1), channel_id=1, source_target_pairs={{0,8},{8,0},{16,24},{24,16},{1,9},{9,1},{17,25},{25,17},{2,10},{10... | collective-permute-start | bytes 1572872 | tf_op jit(solution)/shard_map/ppermute | solution.py:630
  422.2 24.3 %collective-permute-start.52 = (bf16[128,2048]{1,0:T(8,128)(2,1)S(1)}, bf16[128,2048]{1,0:T(8,128)(2,1)S(1)}, u32[]{:S(2)}, u32[]{:S(2)}) collective-permute-start(bf16[128,2048]{1,0:T(8,128)(2,1)S(1)} %add_convert_fusion), channel_id=1, source_target_pairs={{0,16},{8,24},{16,0},{24,8},{1,17},{9,25},{17,1},{25,9},{2,18},{10... | collective-permute-start | bytes 1572872 | tf_op jit(solution)/shard_map/ppermute | solution.py:630
  424.4 33.4 %collective-permute-start.45 = (bf16[128,2048]{1,0:T(8,128)(2,1)S(1)}, bf16[128,2048]{1,0:T(8,128)(2,1)S(1)}, u32[]{:S(2)}, u32[]{:S(2)}) collective-permute-start(bf16[128,2048]{1,0:T(8,128)(2,1)S(1)} %add_convert_fusion.3), channel_id=1, source_target_pairs={{0,8},{8,0},{16,24},{24,16},{1,9},{9,1},{17,25},{25,17},{2,10},{10... | collective-permute-start | bytes 1572872 | tf_op jit(solution)/shard_map/ppermute | solution.py:630
  434.0 23.8 %collective-permute-start.46 = (bf16[128,2048]{1,0:T(8,128)(2,1)S(1)}, bf16[128,2048]{1,0:T(8,128)(2,1)S(1)}, u32[]{:S(2)}, u32[]{:S(2)}) collective-permute-start(bf16[128,2048]{1,0:T(8,128)(2,1)S(1)} %add_convert_fusion.2), channel_id=1, source_target_pairs={{0,16},{8,24},{16,0},{24,8},{1,17},{9,25},{17,1},{25,9},{2,18},{10... | collective-permute-start | bytes 1572872 | tf_op jit(solution)/shard_map/ppermute | solution.py:630
  447.9 21.0 %collective-permute-start.53 = (bf16[64,2816]{1,0:T(8,128)(2,1)}, bf16[64,2816]{1,0:T(8,128)(2,1)S(1)}, u32[]{:S(2)}, u32[]{:S(2)}) collective-permute-start(bf16[64,2816]{1,0:T(8,128)(2,1)} %get-tuple-element.207), channel_id=1, source_target_pairs={{0,8},{8,0},{16,24},{24,16},{1,9},{9,1},{17,25},{25,17},{2,10},{10... | collective-permute-start | bytes 1081352 | tf_op jit(solution)/shard_map/ppermute | solution.py:630
  448.7 20.2 %collective-permute-start.54 = (bf16[64,2816]{1,0:T(8,128)(2,1)}, bf16[64,2816]{1,0:T(8,128)(2,1)S(1)}, u32[]{:S(2)}, u32[]{:S(2)}) collective-permute-start(bf16[64,2816]{1,0:T(8,128)(2,1)} %get-tuple-element.206), channel_id=1, source_target_pairs={{0,16},{8,24},{16,0},{24,8},{1,17},{9,25},{17,1},{25,9},{2,18},{10... | collective-permute-start | bytes 1081352 | tf_op jit(solution)/shard_map/ppermute | solution.py:630
  449.5 21.0 %collective-permute-start.55 = (bf16[64,2816]{1,0:T(8,128)(2,1)S(1)}, bf16[64,2816]{1,0:T(8,128)(2,1)}, u32[]{:S(2)}, u32[]{:S(2)}) collective-permute-start(bf16[64,2816]{1,0:T(8,128)(2,1)S(1)} %get-tuple-element.205), channel_id=1, source_target_pairs={{0,24},{8,16},{16,8},{24,0},{1,25},{9,17},{17,9},{25,1},{2,26},{10... | collective-permute-start | bytes 1081352 | tf_op jit(solution)/shard_map/ppermute | solution.py:630
  (78 other events, 687.6 us)
Sparse Core Ops, SparseCore 0:
  20.4 52.0 all-gather.3
  74.7 106.8 all-gather.5
  183.2 58.7 all-gather.7
  244.2 64.6 reduce-scatter.3
  314.7 102.5 reduce-scatter.5
  419.4 55.4 reduce-scatter.7

commit v5 on v4

--- a/solution.py
+++ b/solution.py
@@ -699,6 +699,13 @@
             lax.dynamic_slice_in_dim(value_low, first, kw, 1),
         ], 1)
 
+    count = positions.shape[1] // span
+    where_at = positions[0].reshape(count, span)
+    where_at = jnp.stack([lax.dynamic_index_in_dim(where_at, here ^ j, 0, False) for j in range(count)])
+    rank = where_at[:, 0] // span
+    order = jnp.argsort(rank).astype(jnp.int32)
+    cosine, sine = rope_tables(where_at.reshape(-1))
+
     own_tokens = tokens[0]
     own_pieces = call_own(
         functools.partial(regroup_kernel, into), (like((piece_rows, width)),) * parts, own_tokens
@@ -706,7 +713,7 @@
     token_pieces = seq_gather(own_pieces)
     output_own = output_weight.reshape(own_rows, seq_size, -1).swapaxes(0, 1).reshape(seq_size * own_rows, -1)
     projections = fsdp_gather(jnp.concatenate([output_own, spread(qkv_for)], 1))
-    gate_weight, up_weight = lax.optimization_barrier((gate_weight, up_weight, *own_pieces))[:2]
+    gate_weight, up_weight = lax.optimization_barrier((gate_weight, up_weight, *own_pieces, order, cosine, sine))[:2]
     gate_low, up_low = with_gain(gate_weight, gain_two), with_gain(up_weight, gain_two)
 
     def gate_up_for(t):
@@ -722,18 +729,12 @@
     own_upstream = after(cotangent[0], gate_up_own, *token_pieces)
     upstream = [own_upstream] + [swap(own_upstream, j) for j in range(1, seq_size)]
 
-    count = positions.shape[1] // span
-    where_at = positions[0].reshape(count, span)
-    where_at = jnp.stack([lax.dynamic_index_in_dim(where_at, here ^ j, 0, False) for j in range(count)])
-    rank = where_at[:, 0] // span
-    order = jnp.argsort(rank).astype(jnp.int32)
-    cosine, sine = rope_tables(where_at.reshape(-1))
-
     qrot, kv, attended, mix, lse, inv_one = attend(
         order, rank, token_pieces, projections, cosine, sine, heads, kvs, span
     )
-    attended, *upstream = lax.optimization_barrier((attended, *upstream))
-    branch = seq_scatter(rows_of_product(attended, projections, piece_rows, into))[1]
+    branch = rows_of_product(attended, projections, piece_rows, into)
+    branch, upstream = lax.optimization_barrier((branch, upstream))
+    branch = seq_scatter(branch)[1]
     middle, inv_two, *own_pieces = call_own(
         functools.partial(middle_kernel, into, parts),
         (like((span, width), FULL), like((span, 1), FULL)) + (like((piece_rows, width)),) * parts,

time: 503 us -> 501 us (level)
  transfers between devices with their start and end apart: 65 -> 65, of which waited for: 30 -> 32; matrix products, arithmetic and copies ran while one was open for 3% -> 3% of each run, Pallas kernels for 43% -> 44%
where the time goes in v5:
time: 501 us; the launch traced here: 493 us
  Pallas kernels  217 us (43%)
  waiting for transfers between devices  169 us (34%)
  starting transfers between devices  63.6 us (13%)
  between operations  15.5 us (3%)
  other arithmetic  13.6 us (3%)
  local copies, waits for them, and re-layouts  13.3 us (3%)
    ppermute x57, waiting for transfers between devices, swap(): return lax.ppermute(x, 'seq', [(i, i ^ j) for i in range(seq_size)])  168 us
    ppermute x57, starting transfers between devices, swap(): return lax.ppermute(x, 'seq', [(i, i ^ j) for i in range(seq_size)])  62.8 us
    pallas_call x1, Pallas kernels, attend_back(): pl.pallas_call(functools.partial(attend_back_kernel, heads, kvs, span, le...  34.7 us
    pallas_call x1, Pallas kernels, attend(): pl.pallas_call(functools.partial(attend_kernel, heads, kvs, span, len(pie...  34.2 us
    pallas_call x7, Pallas kernels, call_own(): pl.pallas_call(kernel, out_shape=out_shape, in_specs=[SMEM] * len(scalars...  29.5 us
    pallas_call x2, Pallas kernels, grad_rows_of(): pl.pallas_call(functools.partial(grad_rows_kernel, weight.shape[1] - grad...  25.2 us
    pallas_call x1, Pallas kernels, hidden_of(): pl.pallas_call(functools.partial(hidden_kernel, len(pieces), chunk), grid...  20.4 us
    pallas_call x1, Pallas kernels, grad_weight_of(): pl.pallas_call(grad_weight_kernel, grid_spec=pltpu.PrefetchScalarGridSpec...  18.7 us
  transfers between devices with their start and end apart: 65, of which 32 were waited for; matrix products, arithmetic and copies ran while one was open for 3% of the time, Pallas kernels for 44%

profile of v5, /device:TPU:0, one launch (start us, length us, event | category | flops | bytes accessed | tf_op | source)
XLA Modules:
  0.0 492.8 jit_solution(13896258415957658711)
XLA Ops:
  10.2 3.9 collective-permute-start.8
  15.0 1.7 collective-permute-done.8
  16.7 1.9 collective-permute-done.7
  21.6 2.6 regroup_kernel.1
  27.8 1.6 collective-permute-start.11
  31.3 8.8 %collective-permute-done.11 = bf16[64,2816]{1,0:T(8,128)(2,1)S(1)} collective-permute-done((bf16[64,2816]{1,0:T(8,128)(2,1)S(1)}, bf16[64,2816]{1,0:T(8,128)(2,1)S(1)}, u32[]{:S(2)}, u32[]{:S(2)}) %collective-permute-start.11) | collective-permute-done | bytes 360480 | tf_op jit(solution)/shard_map/ppermute | solution.py:630
  40.1 5.5 %collective-permute-done.10 = bf16[64,2816]{1,0:T(8,128)(2,1)S(1)} collective-permute-done((bf16[64,2816]{1,0:T(8,128)(2,1)S(1)}, bf16[64,2816]{1,0:T(8,128)(2,1)S(1)}, u32[]{:S(2)}, u32[]{:S(2)}) %collective-permute-start.10) | collective-permute-done | bytes 360480 | tf_op jit(solution)/shard_map/ppermute | solution.py:630
  52.5 10.8 %collective-permute-done.refs_2_ = bf16[128,2048]{1,0:T(8,128)(2,1)S(1)} collective-permute-done((bf16[128,2048]{1,0:T(8,128)(2,1)S(1)}, bf16[128,2048]{1,0:T(8,128)(2,1)S(1)}, u32[]{:S(2)}, u32[]{:S(2)}) %collective-permute-start) | collective-permute-done | bytes 524320 | tf_op jit(solution)/shard_map/ppermute | solution.py:630
  65.3 9.2 %collective-permute-done.1.refs_3_ = bf16[128,2048]{1,0:T(8,128)(2,1)S(1)} collective-permute-done((bf16[128,2048]{1,0:T(8,128)(2,1)S(1)}, bf16[128,2048]{1,0:T(8,128)(2,1)S(1)}, u32[]{:S(2)}, u32[]{:S(2)}) %collective-permute-start.1) | collective-permute-done | bytes 524320 | tf_op jit(solution)/shard_map/ppermute | solution.py:630
  75.9 10.1 %collective-permute-done.4.refs_6_ = bf16[128,2048]{1,0:T(8,128)(2,1)S(1)} collective-permute-done((bf16[128,2048]{1,0:T(8,128)(2,1)S(1)}, bf16[128,2048]{1,0:T(8,128)(2,1)S(1)}, u32[]{:S(2)}, u32[]{:S(2)}) %collective-permute-start.4) | collective-permute-done | bytes 524320 | tf_op jit(solution)/shard_map/ppermute | solution.py:630
  86.5 1.6 collective-permute-start.13
  89.6 34.2 %attend.1 = (bf16[512,1024]{1,0:T(8,128)(2,1)}, bf16[128,1024]{1,0:T(8,128)(2,1)}, bf16[512,1024]{1,0:T(8,128)(2,1)}, f32[512,1024]{1,0:T(8,128)}, f32[8,1024]{1,0:T(8,128)}, /*index=5*/f32[1,1024]{1,0:T(1,128)}) custom-call(s32[4]{0:T(128)} %get-tuple-element.115.order_ref, s32[4]{0:T(128)} %copy-done.57, bf16[128,2048]{1,0:T(8,128)(2,1)} %get-tuple-element.116.refs_0_, ...), custom_call_target="tpu_custom_call" | custom-call | tf_op jit(solution)/shard_map/attend/pallas_call | solution.py:489
  123.8 6.1 %rows_of_product.2 = (bf16[128,2048]{1,0:T(8,128)(2,1)}, bf16[128,2048]{1,0:T(8,128)(2,1)}, bf16[128,2048]{1,0:T(8,128)(2,1)}, bf16[128,2048]{1,0:T(8,128)(2,1)}...) custom-call(bf16[512,1024]{1,0:T(8,128)(2,1)} %get-tuple-element.118, ...), custom_call_target="tpu_custom_call" | custom-call | tf_op jit(solution)/shard_map/rows_of_product/pallas_call | solution.py:373
  129.9 2.8 collective-permute-done.13.refs_2_
  136.8 11.0 %collective-permute-done.16 = bf16[128,2048]{1,0:T(8,128)(2,1)S(1)} collective-permute-done((bf16[128,2048]{1,0:T(8,128)(2,1)}, bf16[128,2048]{1,0:T(8,128)(2,1)S(1)}, u32[]{:S(2)}, u32[]{:S(2)}) %collective-permute-start.16) | collective-permute-done | bytes 524320 | tf_op jit(solution)/shard_map/ppermute | solution.py:630
  149.0 1.6 collective-permute-start.17
  151.4 7.7 %collective-permute-done.15.refs_2_ = bf16[128,2048]{1,0:T(8,128)(2,1)S(1)} collective-permute-done((bf16[128,2048]{1,0:T(8,128)(2,1)}, bf16[128,2048]{1,0:T(8,128)(2,1)S(1)}, u32[]{:S(2)}, u32[]{:S(2)}) %collective-permute-start.15) | collective-permute-done | bytes 524320 | tf_op jit(solution)/shard_map/ppermute | solution.py:630
  160.6 7.8 %collective-permute-done.17.refs_3_ = bf16[128,2048]{1,0:T(8,128)(2,1)S(1)} collective-permute-done((bf16[128,2048]{1,0:T(8,128)(2,1)S(1)}, bf16[128,2048]{1,0:T(8,128)(2,1)S(1)}, u32[]{:S(2)}, u32[]{:S(2)}) %collective-permute-start.17) | collective-permute-done | bytes 524320 | tf_op jit(solution)/shard_map/ppermute | solution.py:630
  169.2 4.9 middle_kernel.1
  178.2 11.0 %collective-permute-done.21.refs_2_ = bf16[128,2048]{1,0:T(8,128)(2,1)S(1)} collective-permute-done((bf16[128,2048]{1,0:T(8,128)(2,1)}, bf16[128,2048]{1,0:T(8,128)(2,1)S(1)}, u32[]{:S(2)}, u32[]{:S(2)}) %collective-permute-start.21) | collective-permute-done | bytes 524320 | tf_op jit(solution)/shard_map/ppermute | solution.py:630
  191.2 9.2 %collective-permute-done.22.refs_3_ = bf16[128,2048]{1,0:T(8,128)(2,1)S(1)} collective-permute-done((bf16[128,2048]{1,0:T(8,128)(2,1)}, bf16[128,2048]{1,0:T(8,128)(2,1)S(1)}, u32[]{:S(2)}, u32[]{:S(2)}) %collective-permute-start.22) | collective-permute-done | bytes 524320 | tf_op jit(solution)/shard_map/ppermute | solution.py:630
  201.0 6.8 %collective-permute-done.25.refs_6_ = bf16[128,2048]{1,0:T(8,128)(2,1)S(1)} collective-permute-done((bf16[128,2048]{1,0:T(8,128)(2,1)S(1)}, bf16[128,2048]{1,0:T(8,128)(2,1)S(1)}, u32[]{:S(2)}, u32[]{:S(2)}) %collective-permute-start.25) | collective-permute-done | bytes 524320 | tf_op jit(solution)/shard_map/ppermute | solution.py:630
  208.8 20.4 %hidden_of.1 = (bf16[1024,2816]{1,0:T(8,128)(2,1)}, bf16[1408,1024]{1,0:T(8,128)(2,1)}, bf16[1024,2048]{1,0:T(8,128)(2,1)}) custom-call(bf16[128,2048]{1,0:T(8,128)(2,1)} %get-tuple-element.139.refs_0_, bf16[128,2048]{1,0:T(8,128)(2,1)} %get-tuple-element.140.refs_1_, bf16[128,2048]{1,0:T(8,128)(2,1)} %copy-done.37, bf16[128,2048]{1,0:T(8,128)(2,1)} %copy-done.42, ...), custom_call_target="tpu_custom_call" | custom-call | tf_op jit(solution)/shard_map/hidden_of/pallas_call | solution.py:231
  229.2 11.9 %grad_down_of.1 = bf16[1408,2048]{1,0:T(8,128)(2,1)} custom-call(bf16[256,2048]{1,0:T(8,128)(2,1)} %bitcast.71, bf16[256,2048]{1,0:T(8,128)(2,1)} %copy-done.1, bf16[256,2048]{1,0:T(8,128)(2,1)} %copy-done.2, bf16[256,2048]{1,0:T(8,128)(2,1)} %collective-permute-done.14.refs_3_, bf16[1408,1024]{1,0:T(8,128)(2,1)} %get-tuple-element.167.refs_4_.left_ref), custom_call_target="tpu_custom_call" | custom-call | tf_op jit(solution)/shard_map/grad_down_of/pallas_call | solution.py:251
  242.0 14.6 %grad_gate_up_of.1.grad_ref = bf16[1024,2816]{1,0:T(8,128)(2,1)} custom-call(bf16[256,2048]{1,0:T(8,128)(2,1)} %bitcast.72, bf16[256,2048]{1,0:T(8,128)(2,1)} %copy-done.1, bf16[256,2048]{1,0:T(8,128)(2,1)} %copy-done.2, bf16[256,2048]{1,0:T(8,128)(2,1)} %collective-permute-done.14.refs_3_, ...), custom_call_target="tpu_custom_call" | custom-call | tf_op jit(solution)/shard_map/grad_gate_up_of/pallas_call | solution.py:290
  257.2 17.2 %grad_rows_of.2 = (bf16[128,2048]{1,0:T(8,128)(2,1)}, bf16[128,2048]{1,0:T(8,128)(2,1)}, bf16[128,2048]{1,0:T(8,128)(2,1)}, bf16[128,2048]{1,0:T(8,128)(2,1)}, b...) custom-call(bf16[1024,2816]{1,0:T(8,128)(2,1)} %grad_gate_up_of.1.gr, ...), custom_call_target="tpu_custom_call" | custom-call | tf_op jit(solution)/shard_map/grad_rows_of/pallas_call | solution.py:312
  277.6 11.9 %collective-permute-done.27 = bf16[128,2048]{1,0:T(8,128)(2,1)S(1)} collective-permute-done((bf16[128,2048]{1,0:T(8,128)(2,1)}, bf16[128,2048]{1,0:T(8,128)(2,1)S(1)}, u32[]{:S(2)}, u32[]{:S(2)}) %collective-permute-start.27) | collective-permute-done | bytes 524320 | tf_op jit(solution)/shard_map/ppermute | solution.py:630
  294.0 18.7 %grad_weight_of.1 = bf16[1024,2816]{1,0:T(8,128)(2,1)} custom-call(s32[1]{0:T(128)} %bitcast.21.core_ref, bf16[1024,2048]{1,0:T(8,128)(2,1)} %get-tuple-element.154.left_ref, bf16[1024,2048]{1,0:T(8,128)(2,1)} %collective-permute-done.29.other_left_ref, bf16[1024,2816]{1,0:T(8,128)(2,1)} %grad_gate_up_of.1.grad_ref, ...), custom_call_target="tpu_custom_call" | custom-call | tf_op jit(solution)/shard_map/grad_weight_of/pallas_call | solution.py:333
  314.3 5.7 %grad_middle_kernel.1 = (f32[256,2048]{1,0:T(8,128)}, bf16[128,2048]{1,0:T(8,128)(2,1)}, bf16[128,2048]{1,0:T(8,128)(2,1)}) custom-call(bf16[256,2048]{1,0:T(8,128)(2,1)} %bitcast.73, f32[256,2048]{1,0:T(8,128)} %get-tuple-element.138.refs_1_.refs_0_, f32[256,1]{1,0:T(8,128)} %get-tuple-element.142.refs_2_, bf16[128,2048]{1,0:T(8,128)(2,1)} %get-tuple-element.160.refs_3_, ...), custom_call_target="tpu_custom_call" | custom-call | tf_op jit(solution)/shard_map/grad_middle_kernel/pallas_call | solution.py:73
  324.0 11.0 %collective-permute-done.35.refs_2_.refs_10_ = bf16[128,2048]{1,0:T(8,128)(2,1)S(1)} collective-permute-done((bf16[128,2048]{1,0:T(8,128)(2,1)}, bf16[128,2048]{1,0:T(8,128)(2,1)S(1)}, u32[]{:S(2)}, u32[]{:S(2)}) %collective-permute-start.35) | collective-permute-done | bytes 524320 | tf_op jit(solution)/shard_map/ppermute | solution.py:630
  335.1 1.5 collective-permute-start.39
  338.1 11.4 %rows_of_product.3 = (bf16[128,2048]{1,0:T(8,128)(2,1)}, bf16[128,2048]{1,0:T(8,128)(2,1)}, bf16[128,2048]{1,0:T(8,128)(2,1)}, bf16[128,2048]{1,0:T(8,128)(2,1)}...) custom-call(bf16[1408,1024]{1,0:T(8,128)(2,1)} %get-tuple-element.16, ...), custom_call_target="tpu_custom_call" | custom-call | tf_op jit(solution)/shard_map/rows_of_product/pallas_call | solution.py:373
  349.5 6.4 %collective-permute-done.39.refs_6_.refs_14_ = bf16[128,2048]{1,0:T(8,128)(2,1)S(1)} collective-permute-done((bf16[128,2048]{1,0:T(8,128)(2,1)S(1)}, bf16[128,2048]{1,0:T(8,128)(2,1)S(1)}, u32[]{:S(2)}, u32[]{:S(2)}) %collective-permute-start.39) | collective-permute-done | bytes 524320 | tf_op jit(solution)/shard_map/ppermute | solution.py:630
  355.9 1.5 collective-permute-start.41
  360.0 34.7 %attend_back.1 = (bf16[640,1024]{1,0:T(8,128)(2,1)}, bf16[1024,640]{1,0:T(8,128)(2,1)}) custom-call(s32[4]{0:T(128)} %get-tuple-element.115.order_ref, s32[4]{0:T(128)} %copy-done.57, bf16[128,2048]{1,0:T(8,128)(2,1)} %get-tuple-element.166.refs_0_.refs_8_, bf16[128,2048]{1,0:T(8,128)(2,1)} %get-tuple-element.176.refs_1_.refs_9_, ...), custom_call_target="tpu_custom_call" | custom-call | tf_op jit(solution)/shard_map/attend_back/pallas_call | solution.py:592
  394.9 8.0 %grad_rows_of.3 = (bf16[128,2048]{1,0:T(8,128)(2,1)}, bf16[128,2048]{1,0:T(8,128)(2,1)}, bf16[128,2048]{1,0:T(8,128)(2,1)}, bf16[128,2048]{1,0:T(8,128)(2,1)}, b...) custom-call(bf16[1024,640]{1,0:T(8,128)(2,1)} %get-tuple-element.197, ...), custom_call_target="tpu_custom_call" | custom-call | tf_op jit(solution)/shard_map/grad_rows_of/pallas_call | solution.py:312
  402.9 1.6 collective-permute-start.48
  405.1 10.7 %attention_weights_of.1 = bf16[2048,1152]{1,0:T(8,128)(2,1)} custom-call(bf16[128,2048]{1,0:T(8,128)(2,1)} %get-tuple-element.116.refs_0_, bf16[128,2048]{1,0:T(8,128)(2,1)} %get-tuple-element.117.refs_1_, bf16[128,2048]{1,0:T(8,128)(2,1)} %copy-done.7, bf16[128,2048]{1,0:T(8,128)(2,1)} %copy-done.9, bf16[128,2048]{1,0:T(8,128)(2,1)} %copy-done.10, ...), custom_call_target="tpu_custom_call" | custom-call | tf_op jit(solution)/shard_map/attention_weights_of/pallas_call | solution.py:407
  420.5 1.6 collective-permute-start.52
  424.9 8.0 %collective-permute-done.47.refs_3_ = bf16[128,2048]{1,0:T(8,128)(2,1)S(1)} collective-permute-done((bf16[128,2048]{1,0:T(8,128)(2,1)S(1)}, bf16[128,2048]{1,0:T(8,128)(2,1)S(1)}, u32[]{:S(2)}, u32[]{:S(2)}) %collective-permute-start.47) | collective-permute-done | bytes 524320 | tf_op jit(solution)/shard_map/ppermute | solution.py:630
  433.5 11.2 %collective-permute-done.49.refs_4_ = bf16[128,2048]{1,0:T(8,128)(2,1)S(1)} collective-permute-done((bf16[128,2048]{1,0:T(8,128)(2,1)S(1)}, bf16[128,2048]{1,0:T(8,128)(2,1)S(1)}, u32[]{:S(2)}, u32[]{:S(2)}) %collective-permute-start.49) | collective-permute-done | bytes 524320 | tf_op jit(solution)/shard_map/ppermute | solution.py:630
  447.6 1.5 collective-permute-start.54
  450.3 5.7 %collective-permute-done.45.refs_3_ = bf16[128,2048]{1,0:T(8,128)(2,1)S(1)} collective-permute-done((bf16[128,2048]{1,0:T(8,128)(2,1)S(1)}, bf16[128,2048]{1,0:T(8,128)(2,1)S(1)}, u32[]{:S(2)}, u32[]{:S(2)}) %collective-permute-start.45) | collective-permute-done | bytes 524320 | tf_op jit(solution)/shard_map/ppermute | solution.py:630
  457.6 3.9 block_out_kernel.1
  461.5 5.6 %grad_tokens_kernel.1 = f32[256,2048]{1,0:T(8,128)} custom-call(bf16[256,2048]{1,0:T(8,128)(2,1)} %bitcast.70, f32[256,2048]{1,0:T(8,128)} %get-tuple-element.196.refs_1_, bf16[128,2048]{1,0:T(8,128)(2,1)} %get-tuple-element.198.refs_2_, bf16[128,2048]{1,0:T(8,128)(2,1)} %copy-done.27, bf16[128,2048]{1,0:T(8,128)(2,1)} %copy-done.30, ...), custom_call_target="tpu_custom_call" | custom-call | tf_op jit(solution)/shard_map/grad_tokens_kernel/pallas_call | solution.py:73
  468.2 4.2 finish_gate_up_kernel.1
  480.1 2.4 collective-permute-done.58.refs_3_
  483.2 2.5 finish_projections_kernel.1
  (294 shorter events, 82.6 us)
Async XLA Ops:
  7.2 82.4 %all-gather.4.cloned.1.call-start = ((), (), s32[]{:S(2)}) async-start(), calls=%async_computation.3 | async-start | bytes 5308416 | tf_op jit(solution)/shard_map/all_gather | solution.py:676
  20.3 187.6 %all-gather.6.cloned.1.call-start = ((), (), s32[]{:S(2)}) async-start(), calls=%async_computation.4 | async-start | bytes 12976128 | tf_op jit(solution)/shard_map/all_gather | solution.py:676
  29.3 16.3 %collective-permute-start.10 = (bf16[64,2816]{1,0:T(8,128)(2,1)S(1)}, bf16[64,2816]{1,0:T(8,128)(2,1)S(1)}, u32[]{:S(2)}, u32[]{:S(2)}) collective-permute-start(bf16[64,2816]{1,0:T(8,128)(2,1)S(1)} %get-tuple-element.309), channel_id=1, source_target_pairs={{0,16},{8,24},{16,0},{24,8},{1,17},{9,25},{17,1},{25,9},{2,18},{10... | collective-permute-start | bytes 1081352 | tf_op jit(solution)/shard_map/ppermute | solution.py:630
  30.1 15.7 %collective-permute-start.9 = (bf16[64,2816]{1,0:T(8,128)(2,1)S(1)}, bf16[64,2816]{1,0:T(8,128)(2,1)S(1)}, u32[]{:S(2)}, u32[]{:S(2)}) collective-permute-start(bf16[64,2816]{1,0:T(8,128)(2,1)S(1)} %get-tuple-element.307), channel_id=1, source_target_pairs={{0,8},{8,0},{16,24},{24,16},{1,9},{9,1},{17,25},{25,17},{2,10},{10... | collective-permute-start | bytes 1081352 | tf_op jit(solution)/shard_map/ppermute | solution.py:630
  47.4 194.6 %all-gather.8.cloned.1.call-start = ((), (), s32[]{:S(2)}) async-start(), calls=%async_computation.5 | async-start | bytes 6488064 | tf_op jit(solution)/shard_map/all_gather | solution.py:676
  48.1 266.1 %reduce-scatter.4.cloned.1.call-start = ((), (), s32[]{:S(2)}) async-start(), calls=%async_computation.6 | async-start | bytes 6488064 | tf_op jit(solution)/shard_map/reduce_scatter | solution.py:685
  50.4 24.0 %collective-permute-start.1 = (bf16[128,2048]{1,0:T(8,128)(2,1)S(1)}, bf16[128,2048]{1,0:T(8,128)(2,1)S(1)}, u32[]{:S(2)}, u32[]{:S(2)}) collective-permute-start(bf16[128,2048]{1,0:T(8,128)(2,1)S(1)} %copy-done.6), channel_id=1, source_target_pairs={{0,8},{8,0},{16,24},{24,16},{1,9},{9,1},{17,25},{25,17},{2,10},{10... | collective-permute-start | bytes 1572872 | tf_op jit(solution)/shard_map/ppermute | solution.py:630
  51.9 24.0 %collective-permute-start.2 = (bf16[128,2048]{1,0:T(8,128)(2,1)S(1)}, bf16[128,2048]{1,0:T(8,128)(2,1)S(1)}, u32[]{:S(2)}, u32[]{:S(2)}) collective-permute-start(bf16[128,2048]{1,0:T(8,128)(2,1)S(1)} %copy-done.5), channel_id=1, source_target_pairs={{0,16},{8,24},{16,0},{24,8},{1,17},{9,25},{17,1},{25,9},{2,18},{10... | collective-permute-start | bytes 1572872 | tf_op jit(solution)/shard_map/ppermute | solution.py:630
  63.2 22.7 %collective-permute-start.4 = (bf16[128,2048]{1,0:T(8,128)(2,1)S(1)}, bf16[128,2048]{1,0:T(8,128)(2,1)S(1)}, u32[]{:S(2)}, u32[]{:S(2)}) collective-permute-start(bf16[128,2048]{1,0:T(8,128)(2,1)S(1)} %collective-permute-done.refs_2_), channel_id=1, source_target_pairs={{0,16},{8,24},{16,0},{24,8},{1,17},{9,25},{17,1},{25,9},{2,18},{10... | collective-permute-start | bytes 1572872 | tf_op jit(solution)/shard_map/ppermute | solution.py:630
  64.6 21.3 %collective-permute-start.5 = (bf16[128,2048]{1,0:T(8,128)(2,1)S(1)}, bf16[128,2048]{1,0:T(8,128)(2,1)S(1)}, u32[]{:S(2)}, u32[]{:S(2)}) collective-permute-start(bf16[128,2048]{1,0:T(8,128)(2,1)S(1)} %collective-permute-done.3.refs_5_), channel_id=1, source_target_pairs={{0,8},{8,0},{16,24},{24,16},{1,9},{9,1},{17,25},{25,17},{2,10},{10... | collective-permute-start | bytes 1572872 | tf_op jit(solution)/shard_map/ppermute | solution.py:630
  86.0 44.0 %collective-permute-start.12 = (bf16[256,2048]{1,0:T(8,128)(2,1)S(1)}, bf16[256,2048]{1,0:T(8,128)(2,1)S(1)}, u32[]{:S(2)}, u32[]{:S(2)}) collective-permute-start(bf16[256,2048]{1,0:T(8,128)(2,1)S(1)} %bitcast.74), channel_id=1, source_target_pairs={{0,8},{8,0},{16,24},{24,16},{1,9},{9,1},{17,25},{25,17},{2,10},{10... | collective-permute-start | bytes 3145736 | tf_op jit(solution)/shard_map/ppermute | solution.py:630
  86.5 46.3 %collective-permute-start.13 = (bf16[256,2048]{1,0:T(8,128)(2,1)S(1)}, bf16[256,2048]{1,0:T(8,128)(2,1)S(1)}, u32[]{:S(2)}, u32[]{:S(2)}) collective-permute-start(bf16[256,2048]{1,0:T(8,128)(2,1)S(1)} %bitcast.75), channel_id=1, source_target_pairs={{0,16},{8,24},{16,0},{24,8},{1,17},{9,25},{17,1},{25,9},{2,18},{10... | collective-permute-start | bytes 3145736 | tf_op jit(solution)/shard_map/ppermute | solution.py:630
  88.1 44.7 %collective-permute-start.14 = (bf16[256,2048]{1,0:T(8,128)(2,1)S(1)}, bf16[256,2048]{1,0:T(8,128)(2,1)}, u32[]{:S(2)}, u32[]{:S(2)}) collective-permute-start(bf16[256,2048]{1,0:T(8,128)(2,1)S(1)} %bitcast.76), channel_id=1, source_target_pairs={{0,24},{8,16},{16,8},{24,0},{1,25},{9,17},{17,9},{25,1},{2,26},{10... | collective-permute-start | bytes 3145736 | tf_op jit(solution)/shard_map/ppermute | solution.py:630
  134.3 16.3 %collective-permute-start.19 = (bf16[128,2048]{1,0:T(8,128)(2,1)}, bf16[128,2048]{1,0:T(8,128)(2,1)S(1)}, u32[]{:S(2)}, u32[]{:S(2)}) collective-permute-start(bf16[128,2048]{1,0:T(8,128)(2,1)} %get-tuple-element.137), channel_id=1, source_target_pairs={{0,8},{8,0},{16,24},{24,16},{1,9},{9,1},{17,25},{25,17},{2,10},{10... | collective-permute-start | bytes 1572872 | tf_op jit(solution)/shard_map/ppermute | solution.py:630
  134.8 24.3 %collective-permute-start.15 = (bf16[128,2048]{1,0:T(8,128)(2,1)}, bf16[128,2048]{1,0:T(8,128)(2,1)S(1)}, u32[]{:S(2)}, u32[]{:S(2)}) collective-permute-start(bf16[128,2048]{1,0:T(8,128)(2,1)} %get-tuple-element.131), channel_id=1, source_target_pairs={{0,16},{8,24},{16,0},{24,8},{1,17},{9,25},{17,1},{25,9},{2,18},{10... | collective-permute-start | bytes 1572872 | tf_op jit(solution)/shard_map/ppermute | solution.py:630
  136.3 24.3 %collective-permute-start.18 = (bf16[128,2048]{1,0:T(8,128)(2,1)}, bf16[128,2048]{1,0:T(8,128)(2,1)S(1)}, u32[]{:S(2)}, u32[]{:S(2)}) collective-permute-start(bf16[128,2048]{1,0:T(8,128)(2,1)} %get-tuple-element.135), channel_id=1, source_target_pairs={{0,8},{8,0},{16,24},{24,16},{1,9},{9,1},{17,25},{25,17},{2,10},{10... | collective-permute-start | bytes 1572872 | tf_op jit(solution)/shard_map/ppermute | solution.py:630
  149.0 19.4 %collective-permute-start.17 = (bf16[128,2048]{1,0:T(8,128)(2,1)S(1)}, bf16[128,2048]{1,0:T(8,128)(2,1)S(1)}, u32[]{:S(2)}, u32[]{:S(2)}) collective-permute-start(bf16[128,2048]{1,0:T(8,128)(2,1)S(1)} %add_convert_fusion.7), channel_id=1, source_target_pairs={{0,8},{8,0},{16,24},{24,16},{1,9},{9,1},{17,25},{25,17},{2,10},{10... | collective-permute-start | bytes 1572872 | tf_op jit(solution)/shard_map/ppermute | solution.py:630
  150.7 17.7 %collective-permute-start.20 = (bf16[128,2048]{1,0:T(8,128)(2,1)S(1)}, bf16[128,2048]{1,0:T(8,128)(2,1)}, u32[]{:S(2)}, u32[]{:S(2)}) collective-permute-start(bf16[128,2048]{1,0:T(8,128)(2,1)S(1)} %add_convert_fusion.6), channel_id=1, source_target_pairs={{0,16},{8,24},{16,0},{24,8},{1,17},{9,25},{17,1},{25,9},{2,18},{10... | collective-permute-start | bytes 1572872 | tf_op jit(solution)/shard_map/ppermute | solution.py:630
  174.7 15.1 %collective-permute-start.24 = (bf16[128,2048]{1,0:T(8,128)(2,1)}, bf16[128,2048]{1,0:T(8,128)(2,1)S(1)}, u32[]{:S(2)}, u32[]{:S(2)}) collective-permute-start(bf16[128,2048]{1,0:T(8,128)(2,1)} %get-tuple-element.140.refs_1_), channel_id=1, source_target_pairs={{0,16},{8,24},{16,0},{24,8},{1,17},{9,25},{17,1},{25,9},{2,18},{10... | collective-permute-start | bytes 1572872 | tf_op jit(solution)/shard_map/ppermute | solution.py:630
  176.1 24.3 %collective-permute-start.22 = (bf16[128,2048]{1,0:T(8,128)(2,1)}, bf16[128,2048]{1,0:T(8,128)(2,1)S(1)}, u32[]{:S(2)}, u32[]{:S(2)}) collective-permute-start(bf16[128,2048]{1,0:T(8,128)(2,1)} %get-tuple-element.140.refs_1_), channel_id=1, source_target_pairs={{0,8},{8,0},{16,24},{24,16},{1,9},{9,1},{17,25},{25,17},{2,10},{10... | collective-permute-start | bytes 1572872 | tf_op jit(solution)/shard_map/ppermute | solution.py:630
  176.8 24.3 %collective-permute-start.23 = (bf16[128,2048]{1,0:T(8,128)(2,1)}, bf16[128,2048]{1,0:T(8,128)(2,1)S(1)}, u32[]{:S(2)}, u32[]{:S(2)}) collective-permute-start(bf16[128,2048]{1,0:T(8,128)(2,1)} %get-tuple-element.139.refs_0_), channel_id=1, source_target_pairs={{0,16},{8,24},{16,0},{24,8},{1,17},{9,25},{17,1},{25,9},{2,18},{10... | collective-permute-start | bytes 1572872 | tf_op jit(solution)/shard_map/ppermute | solution.py:630
  189.2 18.6 %collective-permute-start.25 = (bf16[128,2048]{1,0:T(8,128)(2,1)S(1)}, bf16[128,2048]{1,0:T(8,128)(2,1)S(1)}, u32[]{:S(2)}, u32[]{:S(2)}) collective-permute-start(bf16[128,2048]{1,0:T(8,128)(2,1)S(1)} %collective-permute-done.21.refs_2_), channel_id=1, source_target_pairs={{0,16},{8,24},{16,0},{24,8},{1,17},{9,25},{17,1},{25,9},{2,18},{10... | collective-permute-start | bytes 1572872 | tf_op jit(solution)/shard_map/ppermute | solution.py:630
  189.8 18.0 %collective-permute-start.26 = (bf16[128,2048]{1,0:T(8,128)(2,1)S(1)}, bf16[128,2048]{1,0:T(8,128)(2,1)S(1)}, u32[]{:S(2)}, u32[]{:S(2)}) collective-permute-start(bf16[128,2048]{1,0:T(8,128)(2,1)S(1)} %collective-permute-done.24.refs_5_), channel_id=1, source_target_pairs={{0,8},{8,0},{16,24},{24,16},{1,9},{9,1},{17,25},{25,17},{2,10},{10... | collective-permute-start | bytes 1572872 | tf_op jit(solution)/shard_map/ppermute | solution.py:630
  241.1 175.9 %reduce-scatter.6.cloned.1.call-start = ((), (), s32[]{:S(2)}) async-start(), calls=%async_computation.7 | async-start | bytes 7208960 | tf_op jit(solution)/shard_map/reduce_scatter | solution.py:682
  256.7 37.4 %collective-permute-start.30 = (bf16[1024,2816]{1,0:T(8,128)(2,1)}, bf16[1024,2816]{1,0:T(8,128)(2,1)}, u32[]{:S(2)}, u32[]{:S(2)}) collective-permute-start(bf16[1024,2816]{1,0:T(8,128)(2,1)} %grad_gate_up_of.1.grad_ref), channel_id=1, source_target_pairs={{0,1},{1,0},{2,3},{3,2},{4,5},{5,4},{6,7},{7,6},{8,9},{9,8},{10,11... | collective-permute-start | bytes 17301512 | tf_op jit(solution)/shard_map/ppermute | solution.py:679
  256.9 36.0 %collective-permute-start.29 = (bf16[1024,2048]{1,0:T(8,128)(2,1)}, bf16[1024,2048]{1,0:T(8,128)(2,1)}, u32[]{:S(2)}, u32[]{:S(2)}) collective-permute-start(bf16[1024,2048]{1,0:T(8,128)(2,1)} %get-tuple-element.154.left_ref), channel_id=1, source_target_pairs={{0,1},{1,0},{2,3},{3,2},{4,5},{5,4},{6,7},{7,6},{8,9},{9,8},{10,11... | collective-permute-start | bytes 12582920 | tf_op jit(solution)/shard_map/ppermute | solution.py:679
  275.6 16.1 %collective-permute-start.28 = (bf16[128,2048]{1,0:T(8,128)(2,1)}, bf16[128,2048]{1,0:T(8,128)(2,1)S(1)}, u32[]{:S(2)}, u32[]{:S(2)}) collective-permute-start(bf16[128,2048]{1,0:T(8,128)(2,1)} %get-tuple-element.153), channel_id=1, source_target_pairs={{0,8},{8,0},{16,24},{24,16},{1,9},{9,1},{17,25},{25,17},{2,10},{10... | collective-permute-start | bytes 1572872 | tf_op jit(solution)/shard_map/ppermute | solution.py:630
  277.0 35.7 %collective-permute-start.31 = (bf16[128,2048]{1,0:T(8,128)(2,1)}, bf16[128,2048]{1,0:T(8,128)(2,1)S(1)}, u32[]{:S(2)}, u32[]{:S(2)}) collective-permute-start(bf16[128,2048]{1,0:T(8,128)(2,1)} %get-tuple-element.156), channel_id=1, source_target_pairs={{0,16},{8,24},{16,0},{24,8},{1,17},{9,25},{17,1},{25,9},{2,18},{10... | collective-permute-start | bytes 1572872 | tf_op jit(solution)/shard_map/ppermute | solution.py:630
  289.5 23.3 %collective-permute-start.33 = (bf16[128,2048]{1,0:T(8,128)(2,1)}, bf16[128,2048]{1,0:T(8,128)(2,1)S(1)}, u32[]{:S(2)}, u32[]{:S(2)}) collective-permute-start(bf16[128,2048]{1,0:T(8,128)(2,1)} %get-tuple-element.158), channel_id=1, source_target_pairs={{0,8},{8,0},{16,24},{24,16},{1,9},{9,1},{17,25},{25,17},{2,10},{10... | collective-permute-start | bytes 1572872 | tf_op jit(solution)/shard_map/ppermute | solution.py:630
  291.7 21.6 %collective-permute-start.32 = (bf16[128,2048]{1,0:T(8,128)(2,1)S(1)}, bf16[128,2048]{1,0:T(8,128)(2,1)S(1)}, u32[]{:S(2)}, u32[]{:S(2)}) collective-permute-start(bf16[128,2048]{1,0:T(8,128)(2,1)S(1)} %add_convert_fusion.5), channel_id=1, source_target_pairs={{0,8},{8,0},{16,24},{24,16},{1,9},{9,1},{17,25},{25,17},{2,10},{10... | collective-permute-start | bytes 1572872 | tf_op jit(solution)/shard_map/ppermute | solution.py:630
  292.9 20.4 %collective-permute-start.34 = (bf16[128,2048]{1,0:T(8,128)(2,1)S(1)}, bf16[128,2048]{1,0:T(8,128)(2,1)S(1)}, u32[]{:S(2)}, u32[]{:S(2)}) collective-permute-start(bf16[128,2048]{1,0:T(8,128)(2,1)S(1)} %add_convert_fusion.4), channel_id=1, source_target_pairs={{0,16},{8,24},{16,0},{24,8},{1,17},{9,25},{17,1},{25,9},{2,18},{10... | collective-permute-start | bytes 1572872 | tf_op jit(solution)/shard_map/ppermute | solution.py:630
  314.3 158.3 %reduce-scatter.8.cloned.1.call-start = ((), (), s32[]{:S(2)}) async-start(), calls=%async_computation.8 | async-start | bytes 5308416 | tf_op jit(solution)/shard_map/reduce_scatter | solution.py:685
  321.5 15.1 %collective-permute-start.38 = (bf16[128,2048]{1,0:T(8,128)(2,1)}, bf16[128,2048]{1,0:T(8,128)(2,1)S(1)}, u32[]{:S(2)}, u32[]{:S(2)}) collective-permute-start(bf16[128,2048]{1,0:T(8,128)(2,1)} %get-tuple-element.176.refs_1_.refs_9_), channel_id=1, source_target_pairs={{0,16},{8,24},{16,0},{24,8},{1,17},{9,25},{17,1},{25,9},{2,18},{10... | collective-permute-start | bytes 1572872 | tf_op jit(solution)/shard_map/ppermute | solution.py:630
  323.0 26.5 %collective-permute-start.36 = (bf16[128,2048]{1,0:T(8,128)(2,1)}, bf16[128,2048]{1,0:T(8,128)(2,1)S(1)}, u32[]{:S(2)}, u32[]{:S(2)}) collective-permute-start(bf16[128,2048]{1,0:T(8,128)(2,1)} %get-tuple-element.176.refs_1_.refs_9_), channel_id=1, source_target_pairs={{0,8},{8,0},{16,24},{24,16},{1,9},{9,1},{17,25},{25,17},{2,10},{10... | collective-permute-start | bytes 1572872 | tf_op jit(solution)/shard_map/ppermute | solution.py:630
  323.6 25.9 %collective-permute-start.37 = (bf16[128,2048]{1,0:T(8,128)(2,1)}, bf16[128,2048]{1,0:T(8,128)(2,1)S(1)}, u32[]{:S(2)}, u32[]{:S(2)}) collective-permute-start(bf16[128,2048]{1,0:T(8,128)(2,1)} %get-tuple-element.166.refs_0_.refs_8_), channel_id=1, source_target_pairs={{0,16},{8,24},{16,0},{24,8},{1,17},{9,25},{17,1},{25,9},{2,18},{10... | collective-permute-start | bytes 1572872 | tf_op jit(solution)/shard_map/ppermute | solution.py:630
  335.1 20.8 %collective-permute-start.39 = (bf16[128,2048]{1,0:T(8,128)(2,1)S(1)}, bf16[128,2048]{1,0:T(8,128)(2,1)S(1)}, u32[]{:S(2)}, u32[]{:S(2)}) collective-permute-start(bf16[128,2048]{1,0:T(8,128)(2,1)S(1)} %collective-permute-done.35.refs_2_.refs_10_), channel_id=1, source_target_pairs={{0,16},{8,24},{16,0},{24,8},{1,17},{9,25},{17,1},{25,9},{2,18},{10... | collective-permute-start | bytes 1572872 | tf_op jit(solution)/shard_map/ppermute | solution.py:630
  336.6 19.3 %collective-permute-start.40 = (bf16[128,2048]{1,0:T(8,128)(2,1)S(1)}, bf16[128,2048]{1,0:T(8,128)(2,1)S(1)}, u32[]{:S(2)}, u32[]{:S(2)}) collective-permute-start(bf16[128,2048]{1,0:T(8,128)(2,1)S(1)} %collective-permute-done.38.refs_5_.refs_13_), channel_id=1, source_target_pairs={{0,8},{8,0},{16,24},{24,16},{1,9},{9,1},{17,25},{25,17},{2,10},{10... | collective-permute-start | bytes 1572872 | tf_op jit(solution)/shard_map/ppermute | solution.py:630
  355.9 38.9 %collective-permute-start.41 = (bf16[128,2048]{1,0:T(8,128)(2,1)}, bf16[128,2048]{1,0:T(8,128)(2,1)}, u32[]{:S(2)}, u32[]{:S(2)}) collective-permute-start(bf16[128,2048]{1,0:T(8,128)(2,1)} %get-tuple-element.185), channel_id=1, source_target_pairs={{0,16},{8,24},{16,0},{24,8},{1,17},{9,25},{17,1},{25,9},{2,18},{10... | collective-permute-start | bytes 1572872 | tf_op jit(solution)/shard_map/ppermute | solution.py:630
  357.5 37.4 %collective-permute-start.42 = (bf16[128,2048]{1,0:T(8,128)(2,1)}, bf16[128,2048]{1,0:T(8,128)(2,1)S(1)}, u32[]{:S(2)}, u32[]{:S(2)}) collective-permute-start(bf16[128,2048]{1,0:T(8,128)(2,1)} %get-tuple-element.186), channel_id=1, source_target_pairs={{0,8},{8,0},{16,24},{24,16},{1,9},{9,1},{17,25},{25,17},{2,10},{10... | collective-permute-start | bytes 1572872 | tf_op jit(solution)/shard_map/ppermute | solution.py:630
  358.0 36.8 %collective-permute-start.43 = (bf16[128,2048]{1,0:T(8,128)(2,1)}, bf16[128,2048]{1,0:T(8,128)(2,1)S(1)}, u32[]{:S(2)}, u32[]{:S(2)}) collective-permute-start(bf16[128,2048]{1,0:T(8,128)(2,1)} %get-tuple-element.187), channel_id=1, source_target_pairs={{0,16},{8,24},{16,0},{24,8},{1,17},{9,25},{17,1},{25,9},{2,18},{10... | collective-permute-start | bytes 1572872 | tf_op jit(solution)/shard_map/ppermute | solution.py:630
  358.5 36.4 %collective-permute-start.44 = (bf16[128,2048]{1,0:T(8,128)(2,1)}, bf16[128,2048]{1,0:T(8,128)(2,1)S(1)}, u32[]{:S(2)}, u32[]{:S(2)}) collective-permute-start(bf16[128,2048]{1,0:T(8,128)(2,1)} %get-tuple-element.188), channel_id=1, source_target_pairs={{0,8},{8,0},{16,24},{24,16},{1,9},{9,1},{17,25},{25,17},{2,10},{10... | collective-permute-start | bytes 1572872 | tf_op jit(solution)/shard_map/ppermute | solution.py:630
  419.9 24.9 %collective-permute-start.49 = (bf16[128,2048]{1,0:T(8,128)(2,1)S(1)}, bf16[128,2048]{1,0:T(8,128)(2,1)S(1)}, u32[]{:S(2)}, u32[]{:S(2)}) collective-permute-start(bf16[128,2048]{1,0:T(8,128)(2,1)S(1)} %add_convert_fusion.1), channel_id=1, source_target_pairs={{0,8},{8,0},{16,24},{24,16},{1,9},{9,1},{17,25},{25,17},{2,10},{10... | collective-permute-start | bytes 1572872 | tf_op jit(solution)/shard_map/ppermute | solution.py:630
  420.5 24.3 %collective-permute-start.52 = (bf16[128,2048]{1,0:T(8,128)(2,1)S(1)}, bf16[128,2048]{1,0:T(8,128)(2,1)S(1)}, u32[]{:S(2)}, u32[]{:S(2)}) collective-permute-start(bf16[128,2048]{1,0:T(8,128)(2,1)S(1)} %add_convert_fusion), channel_id=1, source_target_pairs={{0,16},{8,24},{16,0},{24,8},{1,17},{9,25},{17,1},{25,9},{2,18},{10... | collective-permute-start | bytes 1572872 | tf_op jit(solution)/shard_map/ppermute | solution.py:630
  423.2 32.8 %collective-permute-start.45 = (bf16[128,2048]{1,0:T(8,128)(2,1)S(1)}, bf16[128,2048]{1,0:T(8,128)(2,1)S(1)}, u32[]{:S(2)}, u32[]{:S(2)}) collective-permute-start(bf16[128,2048]{1,0:T(8,128)(2,1)S(1)} %add_convert_fusion.3), channel_id=1, source_target_pairs={{0,8},{8,0},{16,24},{24,16},{1,9},{9,1},{17,25},{25,17},{2,10},{10... | collective-permute-start | bytes 1572872 | tf_op jit(solution)/shard_map/ppermute | solution.py:630
  432.9 23.2 %collective-permute-start.46 = (bf16[128,2048]{1,0:T(8,128)(2,1)S(1)}, bf16[128,2048]{1,0:T(8,128)(2,1)S(1)}, u32[]{:S(2)}, u32[]{:S(2)}) collective-permute-start(bf16[128,2048]{1,0:T(8,128)(2,1)S(1)} %add_convert_fusion.2), channel_id=1, source_target_pairs={{0,16},{8,24},{16,0},{24,8},{1,17},{9,25},{17,1},{25,9},{2,18},{10... | collective-permute-start | bytes 1572872 | tf_op jit(solution)/shard_map/ppermute | solution.py:630
  446.1 21.0 %collective-permute-start.53 = (bf16[64,2816]{1,0:T(8,128)(2,1)}, bf16[64,2816]{1,0:T(8,128)(2,1)S(1)}, u32[]{:S(2)}, u32[]{:S(2)}) collective-permute-start(bf16[64,2816]{1,0:T(8,128)(2,1)} %get-tuple-element.221), channel_id=1, source_target_pairs={{0,8},{8,0},{16,24},{24,16},{1,9},{9,1},{17,25},{25,17},{2,10},{10... | collective-permute-start | bytes 1081352 | tf_op jit(solution)/shard_map/ppermute | solution.py:630
  447.6 19.6 %collective-permute-start.54 = (bf16[64,2816]{1,0:T(8,128)(2,1)}, bf16[64,2816]{1,0:T(8,128)(2,1)S(1)}, u32[]{:S(2)}, u32[]{:S(2)}) collective-permute-start(bf16[64,2816]{1,0:T(8,128)(2,1)} %get-tuple-element.220), channel_id=1, source_target_pairs={{0,16},{8,24},{16,0},{24,8},{1,17},{9,25},{17,1},{25,9},{2,18},{10... | collective-permute-start | bytes 1081352 | tf_op jit(solution)/shard_map/ppermute | solution.py:630
  449.1 19.1 %collective-permute-start.55 = (bf16[64,2816]{1,0:T(8,128)(2,1)S(1)}, bf16[64,2816]{1,0:T(8,128)(2,1)}, u32[]{:S(2)}, u32[]{:S(2)}) collective-permute-start(bf16[64,2816]{1,0:T(8,128)(2,1)S(1)} %get-tuple-element.219), channel_id=1, source_target_pairs={{0,24},{8,16},{16,8},{24,0},{1,25},{9,17},{17,9},{25,1},{2,26},{10... | collective-permute-start | bytes 1081352 | tf_op jit(solution)/shard_map/ppermute | solution.py:630
  (77 other events, 679.5 us)
Sparse Core Ops, SparseCore 0:
  20.4 52.0 all-gather.3
  74.7 106.8 all-gather.5
  183.3 58.7 all-gather.7
  244.2 63.5 reduce-scatter.3
  313.4 101.4 reduce-scatter.5
  417.1 55.3 reduce-scatter.7

commit v6 on v5

--- a/solution.py
+++ b/solution.py
@@ -23,6 +23,7 @@
 ANY = pl.BlockSpec(memory_space=pltpu.HBM)
 SMEM = pl.BlockSpec(memory_space=pltpu.SMEM)
 PARAMS = pltpu.CompilerParams(vmem_limit_bytes=60 << 20)
+SMALL = pltpu.CompilerParams(vmem_limit_bytes=20 << 20)
 NN, NT, TN = ((1,), (0,)), ((1,), (1,)), ((0,), (0,))
 
 
@@ -69,10 +70,10 @@
     return pltpu.SemaphoreType.DMA((count,))
 
 
-def call_own(kernel, out_shape, *args, scalars=()):
+def call_own(kernel, out_shape, *args, scalars=(), params=PARAMS):
     return pl.pallas_call(
         kernel, out_shape=out_shape, in_specs=[SMEM] * len(scalars) + [VMEM] * len(args),
-        out_specs=jax.tree.map(lambda _: VMEM, out_shape), compiler_params=PARAMS,
+        out_specs=jax.tree.map(lambda _: VMEM, out_shape), compiler_params=params,
         name=getattr(kernel, "func", kernel).__name__,
     )(*scalars, *args)
 
@@ -738,7 +739,7 @@
     middle, inv_two, *own_pieces = call_own(
         functools.partial(middle_kernel, into, parts),
         (like((span, width), FULL), like((span, 1), FULL)) + (like((piece_rows, width)),) * parts,
-        own_tokens, *branch,
+        own_tokens, *branch, params=SMALL,
     )
 
     normed_pieces = seq_gather(own_pieces)
@@ -803,7 +804,7 @@
             finish_projections_kernel,
             tuple(like(w.shape, FULL) for w in (query_weight, key_weight, value_weight, output_weight))
             + (like((1, own_rows), FULL),),
-            *got, grad_projections, query_weight, key_weight, value_weight, gain_one, scalars=(place,),
+            *got, grad_projections, query_weight, key_weight, value_weight, gain_one, scalars=(place,), params=SMALL,
         )
     else:
         grad_output = grad_projections[:, :-qw - 2 * kw].reshape(seq_size, own_rows, -1).swapaxes(0, 1)

time: 501 us -> 498 us (level)
    pallas_call x7, Pallas kernels: 29.5 us -> 24.5 us  [call_own(): pl.pallas_call(kernel, out_shape=out_shape, in_specs=[SMEM] * len(scalars...]
  transfers between devices with their start and end apart: 65 -> 65, of which waited for: 32 -> 31; matrix products, arithmetic and copies ran while one was open for 3% -> 3% of each run, Pallas kernels for 44% -> 43%
where the time goes in v6:
time: 498 us; the launch traced here: 490 us
  Pallas kernels  212 us (43%)
  waiting for transfers between devices  172 us (35%)
  starting transfers between devices  63.3 us (13%)
  between operations  15.6 us (3%)
  other arithmetic  13.7 us (3%)
  local copies, waits for them, and re-layouts  13 us (3%)
    ppermute x57, waiting for transfers between devices, swap(): return lax.ppermute(x, 'seq', [(i, i ^ j) for i in range(seq_size)])  167 us
    ppermute x57, starting transfers between devices, swap(): return lax.ppermute(x, 'seq', [(i, i ^ j) for i in range(seq_size)])  62.6 us
    pallas_call x1, Pallas kernels, attend_back(): pl.pallas_call(functools.partial(attend_back_kernel, heads, kvs, span, le...  34.8 us
    pallas_call x1, Pallas kernels, attend(): pl.pallas_call(functools.partial(attend_kernel, heads, kvs, span, len(pie...  34.2 us
    pallas_call x2, Pallas kernels, grad_rows_of(): pl.pallas_call(functools.partial(grad_rows_kernel, weight.shape[1] - grad...  25.3 us
    pallas_call x7, Pallas kernels, call_own(): pl.pallas_call(kernel, out_shape=out_shape, in_specs=[SMEM] * len(scalars...  24.5 us
    pallas_call x1, Pallas kernels, hidden_of(): pl.pallas_call(functools.partial(hidden_kernel, len(pieces), chunk), grid...  20.4 us
    pallas_call x1, Pallas kernels, grad_weight_of(): pl.pallas_call(grad_weight_kernel, grid_spec=pltpu.PrefetchScalarGridSpec...  18.7 us
  transfers between devices with their start and end apart: 65, of which 31 were waited for; matrix products, arithmetic and copies ran while one was open for 3% of the time, Pallas kernels for 43%

profile of v6, /device:TPU:0, one launch (start us, length us, event | category | flops | bytes accessed | tf_op | source)
XLA Modules:
  0.0 489.8 jit_solution(612338397462256404)
XLA Ops:
  10.2 3.9 collective-permute-start.8
  15.0 1.7 collective-permute-done.8
  16.7 1.9 collective-permute-done.7
  21.6 2.6 regroup_kernel.1
  27.8 1.6 collective-permute-start.11
  31.3 8.8 %collective-permute-done.11 = bf16[64,2816]{1,0:T(8,128)(2,1)S(1)} collective-permute-done((bf16[64,2816]{1,0:T(8,128)(2,1)S(1)}, bf16[64,2816]{1,0:T(8,128)(2,1)S(1)}, u32[]{:S(2)}, u32[]{:S(2)}) %collective-permute-start.11) | collective-permute-done | bytes 360480 | tf_op jit(solution)/shard_map/ppermute | solution.py:631
  40.1 5.5 %collective-permute-done.10 = bf16[64,2816]{1,0:T(8,128)(2,1)S(1)} collective-permute-done((bf16[64,2816]{1,0:T(8,128)(2,1)S(1)}, bf16[64,2816]{1,0:T(8,128)(2,1)S(1)}, u32[]{:S(2)}, u32[]{:S(2)}) %collective-permute-start.10) | collective-permute-done | bytes 360480 | tf_op jit(solution)/shard_map/ppermute | solution.py:631
  52.5 10.8 %collective-permute-done.refs_2_ = bf16[128,2048]{1,0:T(8,128)(2,1)S(1)} collective-permute-done((bf16[128,2048]{1,0:T(8,128)(2,1)S(1)}, bf16[128,2048]{1,0:T(8,128)(2,1)S(1)}, u32[]{:S(2)}, u32[]{:S(2)}) %collective-permute-start) | collective-permute-done | bytes 524320 | tf_op jit(solution)/shard_map/ppermute | solution.py:631
  65.3 9.2 %collective-permute-done.1.refs_3_ = bf16[128,2048]{1,0:T(8,128)(2,1)S(1)} collective-permute-done((bf16[128,2048]{1,0:T(8,128)(2,1)S(1)}, bf16[128,2048]{1,0:T(8,128)(2,1)S(1)}, u32[]{:S(2)}, u32[]{:S(2)}) %collective-permute-start.1) | collective-permute-done | bytes 524320 | tf_op jit(solution)/shard_map/ppermute | solution.py:631
  75.9 10.1 %collective-permute-done.4.refs_6_ = bf16[128,2048]{1,0:T(8,128)(2,1)S(1)} collective-permute-done((bf16[128,2048]{1,0:T(8,128)(2,1)S(1)}, bf16[128,2048]{1,0:T(8,128)(2,1)S(1)}, u32[]{:S(2)}, u32[]{:S(2)}) %collective-permute-start.4) | collective-permute-done | bytes 524320 | tf_op jit(solution)/shard_map/ppermute | solution.py:631
  86.5 1.6 collective-permute-start.13
  89.6 34.2 %attend.1 = (bf16[512,1024]{1,0:T(8,128)(2,1)}, bf16[128,1024]{1,0:T(8,128)(2,1)}, bf16[512,1024]{1,0:T(8,128)(2,1)}, f32[512,1024]{1,0:T(8,128)}, f32[8,1024]{1,0:T(8,128)}, /*index=5*/f32[1,1024]{1,0:T(1,128)}) custom-call(s32[4]{0:T(128)} %get-tuple-element.115.order_ref, s32[4]{0:T(128)} %copy-done.61, bf16[128,2048]{1,0:T(8,128)(2,1)} %get-tuple-element.116.refs_0_, ...), custom_call_target="tpu_custom_call" | custom-call | tf_op jit(solution)/shard_map/attend/pallas_call | solution.py:490
  123.8 6.1 %rows_of_product.2 = (bf16[128,2048]{1,0:T(8,128)(2,1)}, bf16[128,2048]{1,0:T(8,128)(2,1)}, bf16[128,2048]{1,0:T(8,128)(2,1)}, bf16[128,2048]{1,0:T(8,128)(2,1)}...) custom-call(bf16[512,1024]{1,0:T(8,128)(2,1)} %get-tuple-element.118, ...), custom_call_target="tpu_custom_call" | custom-call | tf_op jit(solution)/shard_map/rows_of_product/pallas_call | solution.py:374
  129.9 2.8 collective-permute-done.13.refs_2_
  132.8 1.6 collective-permute-start.16
  136.9 11.0 %collective-permute-done.16 = bf16[128,2048]{1,0:T(8,128)(2,1)S(1)} collective-permute-done((bf16[128,2048]{1,0:T(8,128)(2,1)}, bf16[128,2048]{1,0:T(8,128)(2,1)S(1)}, u32[]{:S(2)}, u32[]{:S(2)}) %collective-permute-start.16) | collective-permute-done | bytes 524320 | tf_op jit(solution)/shard_map/ppermute | solution.py:631
  149.1 1.6 collective-permute-start.17
  151.5 7.7 %collective-permute-done.15.refs_2_ = bf16[128,2048]{1,0:T(8,128)(2,1)S(1)} collective-permute-done((bf16[128,2048]{1,0:T(8,128)(2,1)}, bf16[128,2048]{1,0:T(8,128)(2,1)S(1)}, u32[]{:S(2)}, u32[]{:S(2)}) %collective-permute-start.15) | collective-permute-done | bytes 524320 | tf_op jit(solution)/shard_map/ppermute | solution.py:631
  159.2 1.5 collective-permute-done.18.refs_5_
  160.7 7.7 %collective-permute-done.17.refs_3_ = bf16[128,2048]{1,0:T(8,128)(2,1)S(1)} collective-permute-done((bf16[128,2048]{1,0:T(8,128)(2,1)S(1)}, bf16[128,2048]{1,0:T(8,128)(2,1)S(1)}, u32[]{:S(2)}, u32[]{:S(2)}) %collective-permute-start.17) | collective-permute-done | bytes 524320 | tf_op jit(solution)/shard_map/ppermute | solution.py:631
  175.7 10.8 %collective-permute-done.21.refs_2_ = bf16[128,2048]{1,0:T(8,128)(2,1)S(1)} collective-permute-done((bf16[128,2048]{1,0:T(8,128)(2,1)S(1)}, bf16[128,2048]{1,0:T(8,128)(2,1)S(1)}, u32[]{:S(2)}, u32[]{:S(2)}) %collective-permute-start.21) | collective-permute-done | bytes 524320 | tf_op jit(solution)/shard_map/ppermute | solution.py:631
  188.6 9.2 %collective-permute-done.22.refs_3_ = bf16[128,2048]{1,0:T(8,128)(2,1)S(1)} collective-permute-done((bf16[128,2048]{1,0:T(8,128)(2,1)S(1)}, bf16[128,2048]{1,0:T(8,128)(2,1)S(1)}, u32[]{:S(2)}, u32[]{:S(2)}) %collective-permute-start.22) | collective-permute-done | bytes 524320 | tf_op jit(solution)/shard_map/ppermute | solution.py:631
  198.3 6.7 %collective-permute-done.25.refs_6_ = bf16[128,2048]{1,0:T(8,128)(2,1)S(1)} collective-permute-done((bf16[128,2048]{1,0:T(8,128)(2,1)S(1)}, bf16[128,2048]{1,0:T(8,128)(2,1)S(1)}, u32[]{:S(2)}, u32[]{:S(2)}) %collective-permute-start.25) | collective-permute-done | bytes 524320 | tf_op jit(solution)/shard_map/ppermute | solution.py:631
  205.9 20.4 %hidden_of.1 = (bf16[1024,2816]{1,0:T(8,128)(2,1)}, bf16[1408,1024]{1,0:T(8,128)(2,1)}, bf16[1024,2048]{1,0:T(8,128)(2,1)}) custom-call(bf16[128,2048]{1,0:T(8,128)(2,1)} %copy-done.4, bf16[128,2048]{1,0:T(8,128)(2,1)} %copy-done.5, bf16[128,2048]{1,0:T(8,128)(2,1)} %copy-done.48, bf16[128,2048]{1,0:T(8,128)(2,1)} %copy-done.53, ...), custom_call_target="tpu_custom_call" | custom-call | tf_op jit(solution)/shard_map/hidden_of/pallas_call | solution.py:232
  226.3 11.8 %grad_down_of.1 = bf16[1408,2048]{1,0:T(8,128)(2,1)} custom-call(bf16[256,2048]{1,0:T(8,128)(2,1)} %bitcast.71, bf16[256,2048]{1,0:T(8,128)(2,1)} %copy-done.12, bf16[256,2048]{1,0:T(8,128)(2,1)} %copy-done.13, bf16[256,2048]{1,0:T(8,128)(2,1)} %collective-permute-done.14.refs_3_, bf16[1408,1024]{1,0:T(8,128)(2,1)} %get-tuple-element.167.refs_4_.left_ref), custom_call_target="tpu_custom_call" | custom-call | tf_op jit(solution)/shard_map/grad_down_of/pallas_call | solution.py:252
  238.2 3.8 all-gather.8.cloned.1.call-done.refs_4_.weight_ref
  242.0 14.5 %grad_gate_up_of.1.grad_ref = bf16[1024,2816]{1,0:T(8,128)(2,1)} custom-call(bf16[256,2048]{1,0:T(8,128)(2,1)} %bitcast.72, bf16[256,2048]{1,0:T(8,128)(2,1)} %copy-done.12, bf16[256,2048]{1,0:T(8,128)(2,1)} %copy-done.13, bf16[256,2048]{1,0:T(8,128)(2,1)} %collective-permute-done.14.refs_3_, ...), custom_call_target="tpu_custom_call" | custom-call | tf_op jit(solution)/shard_map/grad_gate_up_of/pallas_call | solution.py:291
  257.1 17.2 %grad_rows_of.2 = (bf16[128,2048]{1,0:T(8,128)(2,1)}, bf16[128,2048]{1,0:T(8,128)(2,1)}, bf16[128,2048]{1,0:T(8,128)(2,1)}, bf16[128,2048]{1,0:T(8,128)(2,1)}, b...) custom-call(bf16[1024,2816]{1,0:T(8,128)(2,1)} %grad_gate_up_of.1.gr, ...), custom_call_target="tpu_custom_call" | custom-call | tf_op jit(solution)/shard_map/grad_rows_of/pallas_call | solution.py:313
  277.5 11.9 %collective-permute-done.27 = bf16[128,2048]{1,0:T(8,128)(2,1)S(1)} collective-permute-done((bf16[128,2048]{1,0:T(8,128)(2,1)}, bf16[128,2048]{1,0:T(8,128)(2,1)S(1)}, u32[]{:S(2)}, u32[]{:S(2)}) %collective-permute-start.27) | collective-permute-done | bytes 524320 | tf_op jit(solution)/shard_map/ppermute | solution.py:631
  293.9 18.7 %grad_weight_of.1 = bf16[1024,2816]{1,0:T(8,128)(2,1)} custom-call(s32[1]{0:T(128)} %bitcast.21.core_ref, bf16[1024,2048]{1,0:T(8,128)(2,1)} %get-tuple-element.154.left_ref, bf16[1024,2048]{1,0:T(8,128)(2,1)} %collective-permute-done.29.other_left_ref, bf16[1024,2816]{1,0:T(8,128)(2,1)} %grad_gate_up_of.1.grad_ref, ...), custom_call_target="tpu_custom_call" | custom-call | tf_op jit(solution)/shard_map/grad_weight_of/pallas_call | solution.py:334
  314.2 5.7 %grad_middle_kernel.1 = (f32[256,2048]{1,0:T(8,128)}, bf16[128,2048]{1,0:T(8,128)(2,1)}, bf16[128,2048]{1,0:T(8,128)(2,1)}) custom-call(bf16[256,2048]{1,0:T(8,128)(2,1)} %bitcast.73, f32[256,2048]{1,0:T(8,128)} %copy-done.1, f32[256,1]{1,0:T(8,128)} %copy-done.8, bf16[128,2048]{1,0:T(8,128)(2,1)} %get-tuple-element.160.refs_3_, ...), custom_call_target="tpu_custom_call" | custom-call | tf_op jit(solution)/shard_map/grad_middle_kernel/pallas_call | solution.py:74
  324.0 11.0 %collective-permute-done.35.refs_2_.refs_10_ = bf16[128,2048]{1,0:T(8,128)(2,1)S(1)} collective-permute-done((bf16[128,2048]{1,0:T(8,128)(2,1)}, bf16[128,2048]{1,0:T(8,128)(2,1)S(1)}, u32[]{:S(2)}, u32[]{:S(2)}) %collective-permute-start.35) | collective-permute-done | bytes 524320 | tf_op jit(solution)/shard_map/ppermute | solution.py:631
  337.8 11.4 %rows_of_product.3 = (bf16[128,2048]{1,0:T(8,128)(2,1)}, bf16[128,2048]{1,0:T(8,128)(2,1)}, bf16[128,2048]{1,0:T(8,128)(2,1)}, bf16[128,2048]{1,0:T(8,128)(2,1)}...) custom-call(bf16[1408,1024]{1,0:T(8,128)(2,1)} %get-tuple-element.16, ...), custom_call_target="tpu_custom_call" | custom-call | tf_op jit(solution)/shard_map/rows_of_product/pallas_call | solution.py:374
  349.3 6.4 %collective-permute-done.39.refs_6_.refs_14_ = bf16[128,2048]{1,0:T(8,128)(2,1)S(1)} collective-permute-done((bf16[128,2048]{1,0:T(8,128)(2,1)S(1)}, bf16[128,2048]{1,0:T(8,128)(2,1)S(1)}, u32[]{:S(2)}, u32[]{:S(2)}) %collective-permute-start.39) | collective-permute-done | bytes 524320 | tf_op jit(solution)/shard_map/ppermute | solution.py:631
  359.8 34.8 %attend_back.1 = (bf16[640,1024]{1,0:T(8,128)(2,1)}, bf16[1024,640]{1,0:T(8,128)(2,1)}) custom-call(s32[4]{0:T(128)} %get-tuple-element.115.order_ref, s32[4]{0:T(128)} %copy-done.61, bf16[128,2048]{1,0:T(8,128)(2,1)} %get-tuple-element.166.refs_0_.refs_8_, bf16[128,2048]{1,0:T(8,128)(2,1)} %get-tuple-element.176.refs_1_.refs_9_, ...), custom_call_target="tpu_custom_call" | custom-call | tf_op jit(solution)/shard_map/attend_back/pallas_call | solution.py:593
  394.7 8.1 %grad_rows_of.3 = (bf16[128,2048]{1,0:T(8,128)(2,1)}, bf16[128,2048]{1,0:T(8,128)(2,1)}, bf16[128,2048]{1,0:T(8,128)(2,1)}, bf16[128,2048]{1,0:T(8,128)(2,1)}, b...) custom-call(bf16[1024,640]{1,0:T(8,128)(2,1)} %get-tuple-element.197, ...), custom_call_target="tpu_custom_call" | custom-call | tf_op jit(solution)/shard_map/grad_rows_of/pallas_call | solution.py:313
  402.7 1.5 collective-permute-start.48
  404.9 10.7 %attention_weights_of.1 = bf16[2048,1152]{1,0:T(8,128)(2,1)} custom-call(bf16[128,2048]{1,0:T(8,128)(2,1)} %get-tuple-element.116.refs_0_, bf16[128,2048]{1,0:T(8,128)(2,1)} %get-tuple-element.117.refs_1_, bf16[128,2048]{1,0:T(8,128)(2,1)} %copy-done.18, bf16[128,2048]{1,0:T(8,128)(2,1)} %copy-done.20, bf16[128,2048]{1,0:T(8,128)(2,1)} %copy-done.21, ...), custom_call_target="tpu_custom_call" | custom-call | tf_op jit(solution)/shard_map/attention_weights_of/pallas_call | solution.py:408
  420.4 1.5 collective-permute-start.52
  424.7 8.0 %collective-permute-done.47.refs_3_ = bf16[128,2048]{1,0:T(8,128)(2,1)S(1)} collective-permute-done((bf16[128,2048]{1,0:T(8,128)(2,1)S(1)}, bf16[128,2048]{1,0:T(8,128)(2,1)S(1)}, u32[]{:S(2)}, u32[]{:S(2)}) %collective-permute-start.47) | collective-permute-done | bytes 524320 | tf_op jit(solution)/shard_map/ppermute | solution.py:631
  433.4 11.2 %collective-permute-done.49.refs_4_ = bf16[128,2048]{1,0:T(8,128)(2,1)S(1)} collective-permute-done((bf16[128,2048]{1,0:T(8,128)(2,1)S(1)}, bf16[128,2048]{1,0:T(8,128)(2,1)S(1)}, u32[]{:S(2)}, u32[]{:S(2)}) %collective-permute-start.49) | collective-permute-done | bytes 524320 | tf_op jit(solution)/shard_map/ppermute | solution.py:631
  447.4 1.5 collective-permute-start.54
  450.2 5.7 %collective-permute-done.45.refs_3_ = bf16[128,2048]{1,0:T(8,128)(2,1)S(1)} collective-permute-done((bf16[128,2048]{1,0:T(8,128)(2,1)S(1)}, bf16[128,2048]{1,0:T(8,128)(2,1)S(1)}, u32[]{:S(2)}, u32[]{:S(2)}) %collective-permute-start.45) | collective-permute-done | bytes 524320 | tf_op jit(solution)/shard_map/ppermute | solution.py:631
  457.5 3.9 block_out_kernel.1
  461.4 5.6 %grad_tokens_kernel.1 = f32[256,2048]{1,0:T(8,128)} custom-call(bf16[256,2048]{1,0:T(8,128)(2,1)} %bitcast.67, f32[256,2048]{1,0:T(8,128)} %get-tuple-element.196.refs_1_, bf16[128,2048]{1,0:T(8,128)(2,1)} %get-tuple-element.198.refs_2_, bf16[128,2048]{1,0:T(8,128)(2,1)} %copy-done.38, bf16[128,2048]{1,0:T(8,128)(2,1)} %copy-done.41, ...), custom_call_target="tpu_custom_call" | custom-call | tf_op jit(solution)/shard_map/grad_tokens_kernel/pallas_call | solution.py:74
  467.9 4.2 finish_gate_up_kernel.1
  474.6 1.6 collective-permute-start.57
  479.1 2.5 collective-permute-done.58.refs_3_
  (302 shorter events, 81.9 us)
Async XLA Ops:
  7.2 82.4 %all-gather.4.cloned.1.call-start = ((), (), s32[]{:S(2)}) async-start(), calls=%async_computation.3 | async-start | bytes 5308416 | tf_op jit(solution)/shard_map/all_gather | solution.py:677
  20.3 185.6 %all-gather.6.cloned.1.call-start = ((), (), s32[]{:S(2)}) async-start(), calls=%async_computation.4 | async-start | bytes 12976128 | tf_op jit(solution)/shard_map/all_gather | solution.py:677
  29.3 16.3 %collective-permute-start.10 = (bf16[64,2816]{1,0:T(8,128)(2,1)S(1)}, bf16[64,2816]{1,0:T(8,128)(2,1)S(1)}, u32[]{:S(2)}, u32[]{:S(2)}) collective-permute-start(bf16[64,2816]{1,0:T(8,128)(2,1)S(1)} %get-tuple-element.309), channel_id=1, source_target_pairs={{0,16},{8,24},{16,0},{24,8},{1,17},{9,25},{17,1},{25,9},{2,18},{10... | collective-permute-start | bytes 1081352 | tf_op jit(solution)/shard_map/ppermute | solution.py:631
  30.1 15.7 %collective-permute-start.9 = (bf16[64,2816]{1,0:T(8,128)(2,1)S(1)}, bf16[64,2816]{1,0:T(8,128)(2,1)S(1)}, u32[]{:S(2)}, u32[]{:S(2)}) collective-permute-start(bf16[64,2816]{1,0:T(8,128)(2,1)S(1)} %get-tuple-element.307), channel_id=1, source_target_pairs={{0,8},{8,0},{16,24},{24,16},{1,9},{9,1},{17,25},{25,17},{2,10},{10... | collective-permute-start | bytes 1081352 | tf_op jit(solution)/shard_map/ppermute | solution.py:631
  47.4 194.6 %all-gather.8.cloned.1.call-start = ((), (), s32[]{:S(2)}) async-start(), calls=%async_computation.5 | async-start | bytes 6488064 | tf_op jit(solution)/shard_map/all_gather | solution.py:677
  48.1 266.1 %reduce-scatter.4.cloned.1.call-start = ((), (), s32[]{:S(2)}) async-start(), calls=%async_computation.6 | async-start | bytes 6488064 | tf_op jit(solution)/shard_map/reduce_scatter | solution.py:686
  50.4 24.0 %collective-permute-start.1 = (bf16[128,2048]{1,0:T(8,128)(2,1)S(1)}, bf16[128,2048]{1,0:T(8,128)(2,1)S(1)}, u32[]{:S(2)}, u32[]{:S(2)}) collective-permute-start(bf16[128,2048]{1,0:T(8,128)(2,1)S(1)} %copy-done.17), channel_id=1, source_target_pairs={{0,8},{8,0},{16,24},{24,16},{1,9},{9,1},{17,25},{25,17},{2,10},{10... | collective-permute-start | bytes 1572872 | tf_op jit(solution)/shard_map/ppermute | solution.py:631
  51.9 24.0 %collective-permute-start.2 = (bf16[128,2048]{1,0:T(8,128)(2,1)S(1)}, bf16[128,2048]{1,0:T(8,128)(2,1)S(1)}, u32[]{:S(2)}, u32[]{:S(2)}) collective-permute-start(bf16[128,2048]{1,0:T(8,128)(2,1)S(1)} %copy-done.16), channel_id=1, source_target_pairs={{0,16},{8,24},{16,0},{24,8},{1,17},{9,25},{17,1},{25,9},{2,18},{10... | collective-permute-start | bytes 1572872 | tf_op jit(solution)/shard_map/ppermute | solution.py:631
  63.2 22.7 %collective-permute-start.4 = (bf16[128,2048]{1,0:T(8,128)(2,1)S(1)}, bf16[128,2048]{1,0:T(8,128)(2,1)S(1)}, u32[]{:S(2)}, u32[]{:S(2)}) collective-permute-start(bf16[128,2048]{1,0:T(8,128)(2,1)S(1)} %collective-permute-done.refs_2_), channel_id=1, source_target_pairs={{0,16},{8,24},{16,0},{24,8},{1,17},{9,25},{17,1},{25,9},{2,18},{10... | collective-permute-start | bytes 1572872 | tf_op jit(solution)/shard_map/ppermute | solution.py:631
  64.6 21.3 %collective-permute-start.5 = (bf16[128,2048]{1,0:T(8,128)(2,1)S(1)}, bf16[128,2048]{1,0:T(8,128)(2,1)S(1)}, u32[]{:S(2)}, u32[]{:S(2)}) collective-permute-start(bf16[128,2048]{1,0:T(8,128)(2,1)S(1)} %collective-permute-done.3.refs_5_), channel_id=1, source_target_pairs={{0,8},{8,0},{16,24},{24,16},{1,9},{9,1},{17,25},{25,17},{2,10},{10... | collective-permute-start | bytes 1572872 | tf_op jit(solution)/shard_map/ppermute | solution.py:631
  86.0 44.0 %collective-permute-start.12 = (bf16[256,2048]{1,0:T(8,128)(2,1)S(1)}, bf16[256,2048]{1,0:T(8,128)(2,1)S(1)}, u32[]{:S(2)}, u32[]{:S(2)}) collective-permute-start(bf16[256,2048]{1,0:T(8,128)(2,1)S(1)} %bitcast.74), channel_id=1, source_target_pairs={{0,8},{8,0},{16,24},{24,16},{1,9},{9,1},{17,25},{25,17},{2,10},{10... | collective-permute-start | bytes 3145736 | tf_op jit(solution)/shard_map/ppermute | solution.py:631
  86.5 46.3 %collective-permute-start.13 = (bf16[256,2048]{1,0:T(8,128)(2,1)S(1)}, bf16[256,2048]{1,0:T(8,128)(2,1)S(1)}, u32[]{:S(2)}, u32[]{:S(2)}) collective-permute-start(bf16[256,2048]{1,0:T(8,128)(2,1)S(1)} %bitcast.75), channel_id=1, source_target_pairs={{0,16},{8,24},{16,0},{24,8},{1,17},{9,25},{17,1},{25,9},{2,18},{10... | collective-permute-start | bytes 3145736 | tf_op jit(solution)/shard_map/ppermute | solution.py:631
  88.1 44.7 %collective-permute-start.14 = (bf16[256,2048]{1,0:T(8,128)(2,1)S(1)}, bf16[256,2048]{1,0:T(8,128)(2,1)}, u32[]{:S(2)}, u32[]{:S(2)}) collective-permute-start(bf16[256,2048]{1,0:T(8,128)(2,1)S(1)} %bitcast.76), channel_id=1, source_target_pairs={{0,24},{8,16},{16,8},{24,0},{1,25},{9,17},{17,9},{25,1},{2,26},{10... | collective-permute-start | bytes 3145736 | tf_op jit(solution)/shard_map/ppermute | solution.py:631
  132.8 15.1 %collective-permute-start.16 = (bf16[128,2048]{1,0:T(8,128)(2,1)}, bf16[128,2048]{1,0:T(8,128)(2,1)S(1)}, u32[]{:S(2)}, u32[]{:S(2)}) collective-permute-start(bf16[128,2048]{1,0:T(8,128)(2,1)} %get-tuple-element.133), channel_id=1, source_target_pairs={{0,16},{8,24},{16,0},{24,8},{1,17},{9,25},{17,1},{25,9},{2,18},{10... | collective-permute-start | bytes 1572872 | tf_op jit(solution)/shard_map/ppermute | solution.py:631
  134.4 16.3 %collective-permute-start.19 = (bf16[128,2048]{1,0:T(8,128)(2,1)}, bf16[128,2048]{1,0:T(8,128)(2,1)S(1)}, u32[]{:S(2)}, u32[]{:S(2)}) collective-permute-start(bf16[128,2048]{1,0:T(8,128)(2,1)} %get-tuple-element.137), channel_id=1, source_target_pairs={{0,8},{8,0},{16,24},{24,16},{1,9},{9,1},{17,25},{25,17},{2,10},{10... | collective-permute-start | bytes 1572872 | tf_op jit(solution)/shard_map/ppermute | solution.py:631
  134.9 24.3 %collective-permute-start.15 = (bf16[128,2048]{1,0:T(8,128)(2,1)}, bf16[128,2048]{1,0:T(8,128)(2,1)S(1)}, u32[]{:S(2)}, u32[]{:S(2)}) collective-permute-start(bf16[128,2048]{1,0:T(8,128)(2,1)} %get-tuple-element.131), channel_id=1, source_target_pairs={{0,16},{8,24},{16,0},{24,8},{1,17},{9,25},{17,1},{25,9},{2,18},{10... | collective-permute-start | bytes 1572872 | tf_op jit(solution)/shard_map/ppermute | solution.py:631
  136.4 24.3 %collective-permute-start.18 = (bf16[128,2048]{1,0:T(8,128)(2,1)}, bf16[128,2048]{1,0:T(8,128)(2,1)S(1)}, u32[]{:S(2)}, u32[]{:S(2)}) collective-permute-start(bf16[128,2048]{1,0:T(8,128)(2,1)} %get-tuple-element.135), channel_id=1, source_target_pairs={{0,8},{8,0},{16,24},{24,16},{1,9},{9,1},{17,25},{25,17},{2,10},{10... | collective-permute-start | bytes 1572872 | tf_op jit(solution)/shard_map/ppermute | solution.py:631
  149.1 19.3 %collective-permute-start.17 = (bf16[128,2048]{1,0:T(8,128)(2,1)S(1)}, bf16[128,2048]{1,0:T(8,128)(2,1)S(1)}, u32[]{:S(2)}, u32[]{:S(2)}) collective-permute-start(bf16[128,2048]{1,0:T(8,128)(2,1)S(1)} %add_convert_fusion.7), channel_id=1, source_target_pairs={{0,8},{8,0},{16,24},{24,16},{1,9},{9,1},{17,25},{25,17},{2,10},{10... | collective-permute-start | bytes 1572872 | tf_op jit(solution)/shard_map/ppermute | solution.py:631
  150.9 17.5 %collective-permute-start.20 = (bf16[128,2048]{1,0:T(8,128)(2,1)S(1)}, bf16[128,2048]{1,0:T(8,128)(2,1)S(1)}, u32[]{:S(2)}, u32[]{:S(2)}) collective-permute-start(bf16[128,2048]{1,0:T(8,128)(2,1)S(1)} %add_convert_fusion.6), channel_id=1, source_target_pairs={{0,16},{8,24},{16,0},{24,8},{1,17},{9,25},{17,1},{25,9},{2,18},{10... | collective-permute-start | bytes 1572872 | tf_op jit(solution)/shard_map/ppermute | solution.py:631
  173.7 24.0 %collective-permute-start.22 = (bf16[128,2048]{1,0:T(8,128)(2,1)S(1)}, bf16[128,2048]{1,0:T(8,128)(2,1)S(1)}, u32[]{:S(2)}, u32[]{:S(2)}) collective-permute-start(bf16[128,2048]{1,0:T(8,128)(2,1)S(1)} %get-tuple-element.140.refs_1_), channel_id=1, source_target_pairs={{0,8},{8,0},{16,24},{24,16},{1,9},{9,1},{17,25},{25,17},{2,10},{10... | collective-permute-start | bytes 1572872 | tf_op jit(solution)/shard_map/ppermute | solution.py:631
  174.3 24.0 %collective-permute-start.23 = (bf16[128,2048]{1,0:T(8,128)(2,1)S(1)}, bf16[128,2048]{1,0:T(8,128)(2,1)S(1)}, u32[]{:S(2)}, u32[]{:S(2)}) collective-permute-start(bf16[128,2048]{1,0:T(8,128)(2,1)S(1)} %get-tuple-element.139.refs_0_), channel_id=1, source_target_pairs={{0,16},{8,24},{16,0},{24,8},{1,17},{9,25},{17,1},{25,9},{2,18},{10... | collective-permute-start | bytes 1572872 | tf_op jit(solution)/shard_map/ppermute | solution.py:631
  186.5 18.6 %collective-permute-start.25 = (bf16[128,2048]{1,0:T(8,128)(2,1)S(1)}, bf16[128,2048]{1,0:T(8,128)(2,1)S(1)}, u32[]{:S(2)}, u32[]{:S(2)}) collective-permute-start(bf16[128,2048]{1,0:T(8,128)(2,1)S(1)} %collective-permute-done.21.refs_2_), channel_id=1, source_target_pairs={{0,16},{8,24},{16,0},{24,8},{1,17},{9,25},{17,1},{25,9},{2,18},{10... | collective-permute-start | bytes 1572872 | tf_op jit(solution)/shard_map/ppermute | solution.py:631
  187.1 18.7 %collective-permute-start.26 = (bf16[128,2048]{1,0:T(8,128)(2,1)S(1)}, bf16[128,2048]{1,0:T(8,128)(2,1)}, u32[]{:S(2)}, u32[]{:S(2)}) collective-permute-start(bf16[128,2048]{1,0:T(8,128)(2,1)S(1)} %collective-permute-done.24.refs_5_), channel_id=1, source_target_pairs={{0,8},{8,0},{16,24},{24,16},{1,9},{9,1},{17,25},{25,17},{2,10},{10... | collective-permute-start | bytes 1572872 | tf_op jit(solution)/shard_map/ppermute | solution.py:631
  238.2 178.7 %reduce-scatter.6.cloned.1.call-start = ((), (), s32[]{:S(2)}) async-start(), calls=%async_computation.7 | async-start | bytes 7208960 | tf_op jit(solution)/shard_map/reduce_scatter | solution.py:683
  256.5 37.4 %collective-permute-start.30 = (bf16[1024,2816]{1,0:T(8,128)(2,1)}, bf16[1024,2816]{1,0:T(8,128)(2,1)}, u32[]{:S(2)}, u32[]{:S(2)}) collective-permute-start(bf16[1024,2816]{1,0:T(8,128)(2,1)} %grad_gate_up_of.1.grad_ref), channel_id=1, source_target_pairs={{0,1},{1,0},{2,3},{3,2},{4,5},{5,4},{6,7},{7,6},{8,9},{9,8},{10,11... | collective-permute-start | bytes 17301512 | tf_op jit(solution)/shard_map/ppermute | solution.py:680
  256.8 36.0 %collective-permute-start.29 = (bf16[1024,2048]{1,0:T(8,128)(2,1)}, bf16[1024,2048]{1,0:T(8,128)(2,1)}, u32[]{:S(2)}, u32[]{:S(2)}) collective-permute-start(bf16[1024,2048]{1,0:T(8,128)(2,1)} %get-tuple-element.154.left_ref), channel_id=1, source_target_pairs={{0,1},{1,0},{2,3},{3,2},{4,5},{5,4},{6,7},{7,6},{8,9},{9,8},{10,11... | collective-permute-start | bytes 12582920 | tf_op jit(solution)/shard_map/ppermute | solution.py:680
  275.5 16.1 %collective-permute-start.28 = (bf16[128,2048]{1,0:T(8,128)(2,1)}, bf16[128,2048]{1,0:T(8,128)(2,1)S(1)}, u32[]{:S(2)}, u32[]{:S(2)}) collective-permute-start(bf16[128,2048]{1,0:T(8,128)(2,1)} %get-tuple-element.153), channel_id=1, source_target_pairs={{0,8},{8,0},{16,24},{24,16},{1,9},{9,1},{17,25},{25,17},{2,10},{10... | collective-permute-start | bytes 1572872 | tf_op jit(solution)/shard_map/ppermute | solution.py:631
  276.9 35.7 %collective-permute-start.31 = (bf16[128,2048]{1,0:T(8,128)(2,1)}, bf16[128,2048]{1,0:T(8,128)(2,1)S(1)}, u32[]{:S(2)}, u32[]{:S(2)}) collective-permute-start(bf16[128,2048]{1,0:T(8,128)(2,1)} %get-tuple-element.156), channel_id=1, source_target_pairs={{0,16},{8,24},{16,0},{24,8},{1,17},{9,25},{17,1},{25,9},{2,18},{10... | collective-permute-start | bytes 1572872 | tf_op jit(solution)/shard_map/ppermute | solution.py:631
  289.4 23.3 %collective-permute-start.33 = (bf16[128,2048]{1,0:T(8,128)(2,1)}, bf16[128,2048]{1,0:T(8,128)(2,1)S(1)}, u32[]{:S(2)}, u32[]{:S(2)}) collective-permute-start(bf16[128,2048]{1,0:T(8,128)(2,1)} %get-tuple-element.158), channel_id=1, source_target_pairs={{0,8},{8,0},{16,24},{24,16},{1,9},{9,1},{17,25},{25,17},{2,10},{10... | collective-permute-start | bytes 1572872 | tf_op jit(solution)/shard_map/ppermute | solution.py:631
  291.6 21.6 %collective-permute-start.32 = (bf16[128,2048]{1,0:T(8,128)(2,1)S(1)}, bf16[128,2048]{1,0:T(8,128)(2,1)S(1)}, u32[]{:S(2)}, u32[]{:S(2)}) collective-permute-start(bf16[128,2048]{1,0:T(8,128)(2,1)S(1)} %add_convert_fusion.5), channel_id=1, source_target_pairs={{0,8},{8,0},{16,24},{24,16},{1,9},{9,1},{17,25},{25,17},{2,10},{10... | collective-permute-start | bytes 1572872 | tf_op jit(solution)/shard_map/ppermute | solution.py:631
  292.8 20.4 %collective-permute-start.34 = (bf16[128,2048]{1,0:T(8,128)(2,1)S(1)}, bf16[128,2048]{1,0:T(8,128)(2,1)S(1)}, u32[]{:S(2)}, u32[]{:S(2)}) collective-permute-start(bf16[128,2048]{1,0:T(8,128)(2,1)S(1)} %add_convert_fusion.4), channel_id=1, source_target_pairs={{0,16},{8,24},{16,0},{24,8},{1,17},{9,25},{17,1},{25,9},{2,18},{10... | collective-permute-start | bytes 1572872 | tf_op jit(solution)/shard_map/ppermute | solution.py:631
  314.2 157.9 %reduce-scatter.8.cloned.1.call-start = ((), (), s32[]{:S(2)}) async-start(), calls=%async_computation.8 | async-start | bytes 5308416 | tf_op jit(solution)/shard_map/reduce_scatter | solution.py:686
  321.3 15.1 %collective-permute-start.38 = (bf16[128,2048]{1,0:T(8,128)(2,1)}, bf16[128,2048]{1,0:T(8,128)(2,1)S(1)}, u32[]{:S(2)}, u32[]{:S(2)}) collective-permute-start(bf16[128,2048]{1,0:T(8,128)(2,1)} %get-tuple-element.176.refs_1_.refs_9_), channel_id=1, source_target_pairs={{0,16},{8,24},{16,0},{24,8},{1,17},{9,25},{17,1},{25,9},{2,18},{10... | collective-permute-start | bytes 1572872 | tf_op jit(solution)/shard_map/ppermute | solution.py:631
  322.7 26.5 %collective-permute-start.36 = (bf16[128,2048]{1,0:T(8,128)(2,1)}, bf16[128,2048]{1,0:T(8,128)(2,1)S(1)}, u32[]{:S(2)}, u32[]{:S(2)}) collective-permute-start(bf16[128,2048]{1,0:T(8,128)(2,1)} %get-tuple-element.176.refs_1_.refs_9_), channel_id=1, source_target_pairs={{0,8},{8,0},{16,24},{24,16},{1,9},{9,1},{17,25},{25,17},{2,10},{10... | collective-permute-start | bytes 1572872 | tf_op jit(solution)/shard_map/ppermute | solution.py:631
  323.3 25.9 %collective-permute-start.37 = (bf16[128,2048]{1,0:T(8,128)(2,1)}, bf16[128,2048]{1,0:T(8,128)(2,1)S(1)}, u32[]{:S(2)}, u32[]{:S(2)}) collective-permute-start(bf16[128,2048]{1,0:T(8,128)(2,1)} %get-tuple-element.166.refs_0_.refs_8_), channel_id=1, source_target_pairs={{0,16},{8,24},{16,0},{24,8},{1,17},{9,25},{17,1},{25,9},{2,18},{10... | collective-permute-start | bytes 1572872 | tf_op jit(solution)/shard_map/ppermute | solution.py:631
  335.0 20.7 %collective-permute-start.39 = (bf16[128,2048]{1,0:T(8,128)(2,1)S(1)}, bf16[128,2048]{1,0:T(8,128)(2,1)S(1)}, u32[]{:S(2)}, u32[]{:S(2)}) collective-permute-start(bf16[128,2048]{1,0:T(8,128)(2,1)S(1)} %collective-permute-done.35.refs_2_.refs_10_), channel_id=1, source_target_pairs={{0,16},{8,24},{16,0},{24,8},{1,17},{9,25},{17,1},{25,9},{2,18},{10... | collective-permute-start | bytes 1572872 | tf_op jit(solution)/shard_map/ppermute | solution.py:631
  336.4 19.3 %collective-permute-start.40 = (bf16[128,2048]{1,0:T(8,128)(2,1)S(1)}, bf16[128,2048]{1,0:T(8,128)(2,1)S(1)}, u32[]{:S(2)}, u32[]{:S(2)}) collective-permute-start(bf16[128,2048]{1,0:T(8,128)(2,1)S(1)} %collective-permute-done.38.refs_5_.refs_13_), channel_id=1, source_target_pairs={{0,8},{8,0},{16,24},{24,16},{1,9},{9,1},{17,25},{25,17},{2,10},{10... | collective-permute-start | bytes 1572872 | tf_op jit(solution)/shard_map/ppermute | solution.py:631
  355.7 38.9 %collective-permute-start.41 = (bf16[128,2048]{1,0:T(8,128)(2,1)}, bf16[128,2048]{1,0:T(8,128)(2,1)}, u32[]{:S(2)}, u32[]{:S(2)}) collective-permute-start(bf16[128,2048]{1,0:T(8,128)(2,1)} %get-tuple-element.185), channel_id=1, source_target_pairs={{0,16},{8,24},{16,0},{24,8},{1,17},{9,25},{17,1},{25,9},{2,18},{10... | collective-permute-start | bytes 1572872 | tf_op jit(solution)/shard_map/ppermute | solution.py:631
  357.2 37.4 %collective-permute-start.42 = (bf16[128,2048]{1,0:T(8,128)(2,1)}, bf16[128,2048]{1,0:T(8,128)(2,1)S(1)}, u32[]{:S(2)}, u32[]{:S(2)}) collective-permute-start(bf16[128,2048]{1,0:T(8,128)(2,1)} %get-tuple-element.186), channel_id=1, source_target_pairs={{0,8},{8,0},{16,24},{24,16},{1,9},{9,1},{17,25},{25,17},{2,10},{10... | collective-permute-start | bytes 1572872 | tf_op jit(solution)/shard_map/ppermute | solution.py:631
  357.8 36.8 %collective-permute-start.43 = (bf16[128,2048]{1,0:T(8,128)(2,1)}, bf16[128,2048]{1,0:T(8,128)(2,1)S(1)}, u32[]{:S(2)}, u32[]{:S(2)}) collective-permute-start(bf16[128,2048]{1,0:T(8,128)(2,1)} %get-tuple-element.187), channel_id=1, source_target_pairs={{0,16},{8,24},{16,0},{24,8},{1,17},{9,25},{17,1},{25,9},{2,18},{10... | collective-permute-start | bytes 1572872 | tf_op jit(solution)/shard_map/ppermute | solution.py:631
  358.4 36.2 %collective-permute-start.44 = (bf16[128,2048]{1,0:T(8,128)(2,1)}, bf16[128,2048]{1,0:T(8,128)(2,1)S(1)}, u32[]{:S(2)}, u32[]{:S(2)}) collective-permute-start(bf16[128,2048]{1,0:T(8,128)(2,1)} %get-tuple-element.188), channel_id=1, source_target_pairs={{0,8},{8,0},{16,24},{24,16},{1,9},{9,1},{17,25},{25,17},{2,10},{10... | collective-permute-start | bytes 1572872 | tf_op jit(solution)/shard_map/ppermute | solution.py:631
  419.7 24.9 %collective-permute-start.49 = (bf16[128,2048]{1,0:T(8,128)(2,1)S(1)}, bf16[128,2048]{1,0:T(8,128)(2,1)S(1)}, u32[]{:S(2)}, u32[]{:S(2)}) collective-permute-start(bf16[128,2048]{1,0:T(8,128)(2,1)S(1)} %add_convert_fusion.1), channel_id=1, source_target_pairs={{0,8},{8,0},{16,24},{24,16},{1,9},{9,1},{17,25},{25,17},{2,10},{10... | collective-permute-start | bytes 1572872 | tf_op jit(solution)/shard_map/ppermute | solution.py:631
  420.4 24.3 %collective-permute-start.52 = (bf16[128,2048]{1,0:T(8,128)(2,1)S(1)}, bf16[128,2048]{1,0:T(8,128)(2,1)S(1)}, u32[]{:S(2)}, u32[]{:S(2)}) collective-permute-start(bf16[128,2048]{1,0:T(8,128)(2,1)S(1)} %add_convert_fusion), channel_id=1, source_target_pairs={{0,16},{8,24},{16,0},{24,8},{1,17},{9,25},{17,1},{25,9},{2,18},{10... | collective-permute-start | bytes 1572872 | tf_op jit(solution)/shard_map/ppermute | solution.py:631
  423.2 32.7 %collective-permute-start.45 = (bf16[128,2048]{1,0:T(8,128)(2,1)S(1)}, bf16[128,2048]{1,0:T(8,128)(2,1)S(1)}, u32[]{:S(2)}, u32[]{:S(2)}) collective-permute-start(bf16[128,2048]{1,0:T(8,128)(2,1)S(1)} %add_convert_fusion.3), channel_id=1, source_target_pairs={{0,8},{8,0},{16,24},{24,16},{1,9},{9,1},{17,25},{25,17},{2,10},{10... | collective-permute-start | bytes 1572872 | tf_op jit(solution)/shard_map/ppermute | solution.py:631
  432.7 23.2 %collective-permute-start.46 = (bf16[128,2048]{1,0:T(8,128)(2,1)S(1)}, bf16[128,2048]{1,0:T(8,128)(2,1)S(1)}, u32[]{:S(2)}, u32[]{:S(2)}) collective-permute-start(bf16[128,2048]{1,0:T(8,128)(2,1)S(1)} %add_convert_fusion.2), channel_id=1, source_target_pairs={{0,16},{8,24},{16,0},{24,8},{1,17},{9,25},{17,1},{25,9},{2,18},{10... | collective-permute-start | bytes 1572872 | tf_op jit(solution)/shard_map/ppermute | solution.py:631
  446.0 21.0 %collective-permute-start.53 = (bf16[64,2816]{1,0:T(8,128)(2,1)}, bf16[64,2816]{1,0:T(8,128)(2,1)S(1)}, u32[]{:S(2)}, u32[]{:S(2)}) collective-permute-start(bf16[64,2816]{1,0:T(8,128)(2,1)} %get-tuple-element.221), channel_id=1, source_target_pairs={{0,8},{8,0},{16,24},{24,16},{1,9},{9,1},{17,25},{25,17},{2,10},{10... | collective-permute-start | bytes 1081352 | tf_op jit(solution)/shard_map/ppermute | solution.py:631
  447.4 19.6 %collective-permute-start.54 = (bf16[64,2816]{1,0:T(8,128)(2,1)}, bf16[64,2816]{1,0:T(8,128)(2,1)S(1)}, u32[]{:S(2)}, u32[]{:S(2)}) collective-permute-start(bf16[64,2816]{1,0:T(8,128)(2,1)} %get-tuple-element.220), channel_id=1, source_target_pairs={{0,16},{8,24},{16,0},{24,8},{1,17},{9,25},{17,1},{25,9},{2,18},{10... | collective-permute-start | bytes 1081352 | tf_op jit(solution)/shard_map/ppermute | solution.py:631
  448.9 18.6 %collective-permute-start.55 = (bf16[64,2816]{1,0:T(8,128)(2,1)S(1)}, bf16[64,2816]{1,0:T(8,128)(2,1)}, u32[]{:S(2)}, u32[]{:S(2)}) collective-permute-start(bf16[64,2816]{1,0:T(8,128)(2,1)S(1)} %get-tuple-element.219), channel_id=1, source_target_pairs={{0,24},{8,16},{16,8},{24,0},{1,25},{9,17},{17,9},{25,1},{2,26},{10... | collective-permute-start | bytes 1081352 | tf_op jit(solution)/shard_map/ppermute | solution.py:631
  (81 other events, 866.3 us)
Sparse Core Ops, SparseCore 0:
  20.4 52.0 all-gather.3
  74.7 106.8 all-gather.5
  183.3 58.7 all-gather.7
  244.2 63.5 reduce-scatter.3
  313.4 100.8 reduce-scatter.5
  417.0 54.8 reduce-scatter.7

commit v7 on v6

--- a/solution.py
+++ b/solution.py
@@ -772,8 +772,9 @@
     grad_qkv, grad_qkv_turned, *out_came = lax.optimization_barrier((grad_qkv, grad_qkv_turned, *out_came))
     part_projections = attention_weights_of(token_pieces, branch_pieces, grad_qkv, attended, into)
     grad_pieces = grad_rows_of(grad_qkv_turned, projections, piece_rows)
-    first, grad_pieces = seq_scatter(grad_pieces)
-    grad_projections = fsdp_scatter(after(part_projections, grad_gate_up_own, *first))
+    came = scatter_start(grad_pieces)
+    grad_projections = fsdp_scatter(after(part_projections, grad_gate_up_own, *came[:2]))
+    grad_pieces = scatter_end(grad_pieces, came)[1]
     got = collect(after(grad_gate_up_own, *grad_pieces))
     out_pieces = scatter_end(out_pieces, out_came)[1]
     block_out = call_own(functools.partial(block_out_kernel, parts), like((span, width)), middle, *out_pieces)

time: 498 us -> 498 us (level)
  transfers between devices with their start and end apart: 65 -> 65, of which waited for: 31 -> 30; matrix products, arithmetic and copies ran while one was open for 3% -> 3% of each run, Pallas kernels for 43% -> 43%
where the time goes in v7:
time: 498 us; the launch traced here: 490 us
  Pallas kernels  212 us (43%)
  waiting for transfers between devices  173 us (35%)
  starting transfers between devices  63.7 us (13%)
  between operations  15.5 us (3%)
  other arithmetic  14.5 us (3%)
  local copies, waits for them, and re-layouts  10.7 us (2%)
    ppermute x57, waiting for transfers between devices, swap(): return lax.ppermute(x, 'seq', [(i, i ^ j) for i in range(seq_size)])  169 us
    ppermute x57, starting transfers between devices, swap(): return lax.ppermute(x, 'seq', [(i, i ^ j) for i in range(seq_size)])  62.9 us
    pallas_call x1, Pallas kernels, attend_back(): pl.pallas_call(functools.partial(attend_back_kernel, heads, kvs, span, le...  34.8 us
    pallas_call x1, Pallas kernels, attend(): pl.pallas_call(functools.partial(attend_kernel, heads, kvs, span, len(pie...  34.2 us
    pallas_call x2, Pallas kernels, grad_rows_of(): pl.pallas_call(functools.partial(grad_rows_kernel, weight.shape[1] - grad...  25.2 us
    pallas_call x7, Pallas kernels, call_own(): pl.pallas_call(kernel, out_shape=out_shape, in_specs=[SMEM] * len(scalars...  24.4 us
    pallas_call x1, Pallas kernels, hidden_of(): pl.pallas_call(functools.partial(hidden_kernel, len(pieces), chunk), grid...  20.4 us
    pallas_call x1, Pallas kernels, grad_weight_of(): pl.pallas_call(grad_weight_kernel, grid_spec=pltpu.PrefetchScalarGridSpec...  18.7 us
  transfers between devices with their start and end apart: 65, of which 30 were waited for; matrix products, arithmetic and copies ran while one was open for 3% of the time, Pallas kernels for 43%

profile of v7, /device:TPU:0, one launch (start us, length us, event | category | flops | bytes accessed | tf_op | source)
XLA Modules:
  0.0 490.0 jit_solution(12720395631176312476)
XLA Ops:
  10.2 3.9 collective-permute-start.8
  15.0 1.7 collective-permute-done.8
  16.7 1.9 collective-permute-done.7
  21.6 2.6 regroup_kernel.1
  27.8 1.6 collective-permute-start.11
  31.3 8.8 %collective-permute-done.11 = bf16[64,2816]{1,0:T(8,128)(2,1)S(1)} collective-permute-done((bf16[64,2816]{1,0:T(8,128)(2,1)S(1)}, bf16[64,2816]{1,0:T(8,128)(2,1)S(1)}, u32[]{:S(2)}, u32[]{:S(2)}) %collective-permute-start.11) | collective-permute-done | bytes 360480 | tf_op jit(solution)/shard_map/ppermute | solution.py:631
  40.1 5.5 %collective-permute-done.10 = bf16[64,2816]{1,0:T(8,128)(2,1)S(1)} collective-permute-done((bf16[64,2816]{1,0:T(8,128)(2,1)S(1)}, bf16[64,2816]{1,0:T(8,128)(2,1)S(1)}, u32[]{:S(2)}, u32[]{:S(2)}) %collective-permute-start.10) | collective-permute-done | bytes 360480 | tf_op jit(solution)/shard_map/ppermute | solution.py:631
  52.5 10.8 %collective-permute-done.refs_2_ = bf16[128,2048]{1,0:T(8,128)(2,1)S(1)} collective-permute-done((bf16[128,2048]{1,0:T(8,128)(2,1)S(1)}, bf16[128,2048]{1,0:T(8,128)(2,1)S(1)}, u32[]{:S(2)}, u32[]{:S(2)}) %collective-permute-start) | collective-permute-done | bytes 524320 | tf_op jit(solution)/shard_map/ppermute | solution.py:631
  65.3 9.2 %collective-permute-done.1.refs_3_ = bf16[128,2048]{1,0:T(8,128)(2,1)S(1)} collective-permute-done((bf16[128,2048]{1,0:T(8,128)(2,1)S(1)}, bf16[128,2048]{1,0:T(8,128)(2,1)S(1)}, u32[]{:S(2)}, u32[]{:S(2)}) %collective-permute-start.1) | collective-permute-done | bytes 524320 | tf_op jit(solution)/shard_map/ppermute | solution.py:631
  75.9 10.1 %collective-permute-done.4.refs_6_ = bf16[128,2048]{1,0:T(8,128)(2,1)S(1)} collective-permute-done((bf16[128,2048]{1,0:T(8,128)(2,1)S(1)}, bf16[128,2048]{1,0:T(8,128)(2,1)S(1)}, u32[]{:S(2)}, u32[]{:S(2)}) %collective-permute-start.4) | collective-permute-done | bytes 524320 | tf_op jit(solution)/shard_map/ppermute | solution.py:631
  86.5 1.6 collective-permute-start.13
  89.6 34.2 %attend.1 = (bf16[512,1024]{1,0:T(8,128)(2,1)}, bf16[128,1024]{1,0:T(8,128)(2,1)}, bf16[512,1024]{1,0:T(8,128)(2,1)}, f32[512,1024]{1,0:T(8,128)}, f32[8,1024]{1,0:T(8,128)}, /*index=5*/f32[1,1024]{1,0:T(1,128)}) custom-call(s32[4]{0:T(128)} %get-tuple-element.115.order_ref, s32[4]{0:T(128)} %copy-done.61, bf16[128,2048]{1,0:T(8,128)(2,1)} %get-tuple-element.116.refs_0_, ...), custom_call_target="tpu_custom_call" | custom-call | tf_op jit(solution)/shard_map/attend/pallas_call | solution.py:490
  123.8 6.1 %rows_of_product.2 = (bf16[128,2048]{1,0:T(8,128)(2,1)}, bf16[128,2048]{1,0:T(8,128)(2,1)}, bf16[128,2048]{1,0:T(8,128)(2,1)}, bf16[128,2048]{1,0:T(8,128)(2,1)}...) custom-call(bf16[512,1024]{1,0:T(8,128)(2,1)} %get-tuple-element.118, ...), custom_call_target="tpu_custom_call" | custom-call | tf_op jit(solution)/shard_map/rows_of_product/pallas_call | solution.py:374
  129.9 2.9 collective-permute-done.13.refs_2_
  132.8 1.6 collective-permute-start.16
  136.9 11.0 %collective-permute-done.16 = bf16[128,2048]{1,0:T(8,128)(2,1)S(1)} collective-permute-done((bf16[128,2048]{1,0:T(8,128)(2,1)}, bf16[128,2048]{1,0:T(8,128)(2,1)S(1)}, u32[]{:S(2)}, u32[]{:S(2)}) %collective-permute-start.16) | collective-permute-done | bytes 524320 | tf_op jit(solution)/shard_map/ppermute | solution.py:631
  149.2 1.6 collective-permute-start.17
  151.5 7.7 %collective-permute-done.15.refs_2_ = bf16[128,2048]{1,0:T(8,128)(2,1)S(1)} collective-permute-done((bf16[128,2048]{1,0:T(8,128)(2,1)}, bf16[128,2048]{1,0:T(8,128)(2,1)S(1)}, u32[]{:S(2)}, u32[]{:S(2)}) %collective-permute-start.15) | collective-permute-done | bytes 524320 | tf_op jit(solution)/shard_map/ppermute | solution.py:631
  159.2 1.5 collective-permute-done.18.refs_5_
  160.7 7.7 %collective-permute-done.17.refs_3_ = bf16[128,2048]{1,0:T(8,128)(2,1)S(1)} collective-permute-done((bf16[128,2048]{1,0:T(8,128)(2,1)S(1)}, bf16[128,2048]{1,0:T(8,128)(2,1)S(1)}, u32[]{:S(2)}, u32[]{:S(2)}) %collective-permute-start.17) | collective-permute-done | bytes 524320 | tf_op jit(solution)/shard_map/ppermute | solution.py:631
  175.7 10.8 %collective-permute-done.21.refs_2_ = bf16[128,2048]{1,0:T(8,128)(2,1)S(1)} collective-permute-done((bf16[128,2048]{1,0:T(8,128)(2,1)S(1)}, bf16[128,2048]{1,0:T(8,128)(2,1)S(1)}, u32[]{:S(2)}, u32[]{:S(2)}) %collective-permute-start.21) | collective-permute-done | bytes 524320 | tf_op jit(solution)/shard_map/ppermute | solution.py:631
  188.6 9.2 %collective-permute-done.22.refs_3_ = bf16[128,2048]{1,0:T(8,128)(2,1)S(1)} collective-permute-done((bf16[128,2048]{1,0:T(8,128)(2,1)S(1)}, bf16[128,2048]{1,0:T(8,128)(2,1)S(1)}, u32[]{:S(2)}, u32[]{:S(2)}) %collective-permute-start.22) | collective-permute-done | bytes 524320 | tf_op jit(solution)/shard_map/ppermute | solution.py:631
  198.4 6.7 %collective-permute-done.25.refs_6_ = bf16[128,2048]{1,0:T(8,128)(2,1)S(1)} collective-permute-done((bf16[128,2048]{1,0:T(8,128)(2,1)S(1)}, bf16[128,2048]{1,0:T(8,128)(2,1)S(1)}, u32[]{:S(2)}, u32[]{:S(2)}) %collective-permute-start.25) | collective-permute-done | bytes 524320 | tf_op jit(solution)/shard_map/ppermute | solution.py:631
  205.9 20.4 %hidden_of.1 = (bf16[1024,2816]{1,0:T(8,128)(2,1)}, bf16[1408,1024]{1,0:T(8,128)(2,1)}, bf16[1024,2048]{1,0:T(8,128)(2,1)}) custom-call(bf16[128,2048]{1,0:T(8,128)(2,1)} %copy-done.4, bf16[128,2048]{1,0:T(8,128)(2,1)} %copy-done.5, bf16[128,2048]{1,0:T(8,128)(2,1)} %copy-done.49, bf16[128,2048]{1,0:T(8,128)(2,1)} %copy-done.52, ...), custom_call_target="tpu_custom_call" | custom-call | tf_op jit(solution)/shard_map/hidden_of/pallas_call | solution.py:232
  226.3 11.8 %grad_down_of.1 = bf16[1408,2048]{1,0:T(8,128)(2,1)} custom-call(bf16[256,2048]{1,0:T(8,128)(2,1)} %bitcast.71, bf16[256,2048]{1,0:T(8,128)(2,1)} %copy-done.12, bf16[256,2048]{1,0:T(8,128)(2,1)} %copy-done.13, bf16[256,2048]{1,0:T(8,128)(2,1)} %collective-permute-done.14.refs_3_, bf16[1408,1024]{1,0:T(8,128)(2,1)} %get-tuple-element.167.refs_4_.left_ref), custom_call_target="tpu_custom_call" | custom-call | tf_op jit(solution)/shard_map/grad_down_of/pallas_call | solution.py:252
  238.2 3.8 all-gather.8.cloned.1.call-done.refs_4_.weight_ref
  242.0 14.5 %grad_gate_up_of.1.grad_ref = bf16[1024,2816]{1,0:T(8,128)(2,1)} custom-call(bf16[256,2048]{1,0:T(8,128)(2,1)} %bitcast.72, bf16[256,2048]{1,0:T(8,128)(2,1)} %copy-done.12, bf16[256,2048]{1,0:T(8,128)(2,1)} %copy-done.13, bf16[256,2048]{1,0:T(8,128)(2,1)} %collective-permute-done.14.refs_3_, ...), custom_call_target="tpu_custom_call" | custom-call | tf_op jit(solution)/shard_map/grad_gate_up_of/pallas_call | solution.py:291
  257.1 17.2 %grad_rows_of.2 = (bf16[128,2048]{1,0:T(8,128)(2,1)}, bf16[128,2048]{1,0:T(8,128)(2,1)}, bf16[128,2048]{1,0:T(8,128)(2,1)}, bf16[128,2048]{1,0:T(8,128)(2,1)}, b...) custom-call(bf16[1024,2816]{1,0:T(8,128)(2,1)} %grad_gate_up_of.1.gr, ...), custom_call_target="tpu_custom_call" | custom-call | tf_op jit(solution)/shard_map/grad_rows_of/pallas_call | solution.py:313
  277.5 11.9 %collective-permute-done.27 = bf16[128,2048]{1,0:T(8,128)(2,1)S(1)} collective-permute-done((bf16[128,2048]{1,0:T(8,128)(2,1)}, bf16[128,2048]{1,0:T(8,128)(2,1)S(1)}, u32[]{:S(2)}, u32[]{:S(2)}) %collective-permute-start.27) | collective-permute-done | bytes 524320 | tf_op jit(solution)/shard_map/ppermute | solution.py:631
  293.9 18.7 %grad_weight_of.1 = bf16[1024,2816]{1,0:T(8,128)(2,1)} custom-call(s32[1]{0:T(128)} %bitcast.21.core_ref, bf16[1024,2048]{1,0:T(8,128)(2,1)} %get-tuple-element.154.left_ref, bf16[1024,2048]{1,0:T(8,128)(2,1)} %collective-permute-done.29.other_left_ref, bf16[1024,2816]{1,0:T(8,128)(2,1)} %grad_gate_up_of.1.grad_ref, ...), custom_call_target="tpu_custom_call" | custom-call | tf_op jit(solution)/shard_map/grad_weight_of/pallas_call | solution.py:334
  314.1 5.7 %grad_middle_kernel.1 = (f32[256,2048]{1,0:T(8,128)}, bf16[128,2048]{1,0:T(8,128)(2,1)}, bf16[128,2048]{1,0:T(8,128)(2,1)}) custom-call(bf16[256,2048]{1,0:T(8,128)(2,1)} %bitcast.73, f32[256,2048]{1,0:T(8,128)} %copy-done.1, f32[256,1]{1,0:T(8,128)} %copy-done.8, bf16[128,2048]{1,0:T(8,128)(2,1)} %get-tuple-element.160.refs_3_, ...), custom_call_target="tpu_custom_call" | custom-call | tf_op jit(solution)/shard_map/grad_middle_kernel/pallas_call | solution.py:74
  323.9 11.0 %collective-permute-done.35.refs_2_.refs_10_ = bf16[128,2048]{1,0:T(8,128)(2,1)S(1)} collective-permute-done((bf16[128,2048]{1,0:T(8,128)(2,1)}, bf16[128,2048]{1,0:T(8,128)(2,1)S(1)}, u32[]{:S(2)}, u32[]{:S(2)}) %collective-permute-start.35) | collective-permute-done | bytes 524320 | tf_op jit(solution)/shard_map/ppermute | solution.py:631
  337.7 11.5 %rows_of_product.3 = (bf16[128,2048]{1,0:T(8,128)(2,1)}, bf16[128,2048]{1,0:T(8,128)(2,1)}, bf16[128,2048]{1,0:T(8,128)(2,1)}, bf16[128,2048]{1,0:T(8,128)(2,1)}...) custom-call(bf16[1408,1024]{1,0:T(8,128)(2,1)} %get-tuple-element.16, ...), custom_call_target="tpu_custom_call" | custom-call | tf_op jit(solution)/shard_map/rows_of_product/pallas_call | solution.py:374
  349.3 6.3 %collective-permute-done.39.refs_6_.refs_14_ = bf16[128,2048]{1,0:T(8,128)(2,1)S(1)} collective-permute-done((bf16[128,2048]{1,0:T(8,128)(2,1)S(1)}, bf16[128,2048]{1,0:T(8,128)(2,1)S(1)}, u32[]{:S(2)}, u32[]{:S(2)}) %collective-permute-start.39) | collective-permute-done | bytes 524320 | tf_op jit(solution)/shard_map/ppermute | solution.py:631
  359.8 34.8 %attend_back.1 = (bf16[640,1024]{1,0:T(8,128)(2,1)}, bf16[1024,640]{1,0:T(8,128)(2,1)}) custom-call(s32[4]{0:T(128)} %get-tuple-element.115.order_ref, s32[4]{0:T(128)} %copy-done.61, bf16[128,2048]{1,0:T(8,128)(2,1)} %get-tuple-element.166.refs_0_.refs_8_, bf16[128,2048]{1,0:T(8,128)(2,1)} %get-tuple-element.176.refs_1_.refs_9_, ...), custom_call_target="tpu_custom_call" | custom-call | tf_op jit(solution)/shard_map/attend_back/pallas_call | solution.py:593
  394.6 8.1 %grad_rows_of.3 = (bf16[128,2048]{1,0:T(8,128)(2,1)}, bf16[128,2048]{1,0:T(8,128)(2,1)}, bf16[128,2048]{1,0:T(8,128)(2,1)}, bf16[128,2048]{1,0:T(8,128)(2,1)}, b...) custom-call(bf16[1024,640]{1,0:T(8,128)(2,1)} %get-tuple-element.197, ...), custom_call_target="tpu_custom_call" | custom-call | tf_op jit(solution)/shard_map/grad_rows_of/pallas_call | solution.py:313
  404.8 10.7 %attention_weights_of.1 = bf16[2048,1152]{1,0:T(8,128)(2,1)} custom-call(bf16[128,2048]{1,0:T(8,128)(2,1)} %get-tuple-element.116.refs_0_, bf16[128,2048]{1,0:T(8,128)(2,1)} %get-tuple-element.117.refs_1_, bf16[128,2048]{1,0:T(8,128)(2,1)} %copy-done.18, bf16[128,2048]{1,0:T(8,128)(2,1)} %copy-done.20, bf16[128,2048]{1,0:T(8,128)(2,1)} %copy-done.21, ...), custom_call_target="tpu_custom_call" | custom-call | tf_op jit(solution)/shard_map/attention_weights_of/pallas_call | solution.py:408
  418.6 1.6 collective-permute-start.52
  423.8 7.0 %collective-permute-done.47.refs_3_ = bf16[128,2048]{1,0:T(8,128)(2,1)S(1)} collective-permute-done((bf16[128,2048]{1,0:T(8,128)(2,1)}, bf16[128,2048]{1,0:T(8,128)(2,1)S(1)}, u32[]{:S(2)}, u32[]{:S(2)}) %collective-permute-start.47) | collective-permute-done | bytes 524320 | tf_op jit(solution)/shard_map/ppermute | solution.py:631
  431.3 11.2 %collective-permute-done.49.refs_4_ = bf16[128,2048]{1,0:T(8,128)(2,1)S(1)} collective-permute-done((bf16[128,2048]{1,0:T(8,128)(2,1)S(1)}, bf16[128,2048]{1,0:T(8,128)(2,1)S(1)}, u32[]{:S(2)}, u32[]{:S(2)}) %collective-permute-start.49) | collective-permute-done | bytes 524320 | tf_op jit(solution)/shard_map/ppermute | solution.py:631
  445.2 1.6 collective-permute-start.54
  448.1 5.7 %collective-permute-done.45.refs_3_ = bf16[128,2048]{1,0:T(8,128)(2,1)S(1)} collective-permute-done((bf16[128,2048]{1,0:T(8,128)(2,1)S(1)}, bf16[128,2048]{1,0:T(8,128)(2,1)S(1)}, u32[]{:S(2)}, u32[]{:S(2)}) %collective-permute-start.45) | collective-permute-done | bytes 524320 | tf_op jit(solution)/shard_map/ppermute | solution.py:631
  454.6 3.9 block_out_kernel.1
  458.5 5.6 %grad_tokens_kernel.1 = f32[256,2048]{1,0:T(8,128)} custom-call(bf16[256,2048]{1,0:T(8,128)(2,1)} %bitcast.67, f32[256,2048]{1,0:T(8,128)} %get-tuple-element.196.refs_1_, bf16[128,2048]{1,0:T(8,128)(2,1)} %get-tuple-element.198.refs_2_, bf16[128,2048]{1,0:T(8,128)(2,1)} %copy-done.38, bf16[128,2048]{1,0:T(8,128)(2,1)} %copy-done.41, ...), custom_call_target="tpu_custom_call" | custom-call | tf_op jit(solution)/shard_map/grad_tokens_kernel/pallas_call | solution.py:74
  464.1 3.2 collective-permute-done.55.refs_3_
  468.0 4.2 finish_gate_up_kernel.1
  473.3 1.5 collective-permute-start.56
  479.7 2.0 collective-permute-done.58.refs_3_
  (300 shorter events, 82.0 us)
Async XLA Ops:
  7.2 82.4 %all-gather.4.cloned.1.call-start = ((), (), s32[]{:S(2)}) async-start(), calls=%async_computation.3 | async-start | bytes 5308416 | tf_op jit(solution)/shard_map/all_gather | solution.py:677
  20.3 185.6 %all-gather.6.cloned.1.call-start = ((), (), s32[]{:S(2)}) async-start(), calls=%async_computation.4 | async-start | bytes 12976128 | tf_op jit(solution)/shard_map/all_gather | solution.py:677
  29.4 16.3 %collective-permute-start.10 = (bf16[64,2816]{1,0:T(8,128)(2,1)S(1)}, bf16[64,2816]{1,0:T(8,128)(2,1)S(1)}, u32[]{:S(2)}, u32[]{:S(2)}) collective-permute-start(bf16[64,2816]{1,0:T(8,128)(2,1)S(1)} %get-tuple-element.309), channel_id=1, source_target_pairs={{0,16},{8,24},{16,0},{24,8},{1,17},{9,25},{17,1},{25,9},{2,18},{10... | collective-permute-start | bytes 1081352 | tf_op jit(solution)/shard_map/ppermute | solution.py:631
  30.1 15.7 %collective-permute-start.9 = (bf16[64,2816]{1,0:T(8,128)(2,1)S(1)}, bf16[64,2816]{1,0:T(8,128)(2,1)S(1)}, u32[]{:S(2)}, u32[]{:S(2)}) collective-permute-start(bf16[64,2816]{1,0:T(8,128)(2,1)S(1)} %get-tuple-element.307), channel_id=1, source_target_pairs={{0,8},{8,0},{16,24},{24,16},{1,9},{9,1},{17,25},{25,17},{2,10},{10... | collective-permute-start | bytes 1081352 | tf_op jit(solution)/shard_map/ppermute | solution.py:631
  47.4 194.6 %all-gather.8.cloned.1.call-start = ((), (), s32[]{:S(2)}) async-start(), calls=%async_computation.5 | async-start | bytes 6488064 | tf_op jit(solution)/shard_map/all_gather | solution.py:677
  48.1 266.0 %reduce-scatter.4.cloned.1.call-start = ((), (), s32[]{:S(2)}) async-start(), calls=%async_computation.6 | async-start | bytes 6488064 | tf_op jit(solution)/shard_map/reduce_scatter | solution.py:686
  50.4 24.0 %collective-permute-start.1 = (bf16[128,2048]{1,0:T(8,128)(2,1)S(1)}, bf16[128,2048]{1,0:T(8,128)(2,1)S(1)}, u32[]{:S(2)}, u32[]{:S(2)}) collective-permute-start(bf16[128,2048]{1,0:T(8,128)(2,1)S(1)} %copy-done.17), channel_id=1, source_target_pairs={{0,8},{8,0},{16,24},{24,16},{1,9},{9,1},{17,25},{25,17},{2,10},{10... | collective-permute-start | bytes 1572872 | tf_op jit(solution)/shard_map/ppermute | solution.py:631
  51.9 24.0 %collective-permute-start.2 = (bf16[128,2048]{1,0:T(8,128)(2,1)S(1)}, bf16[128,2048]{1,0:T(8,128)(2,1)S(1)}, u32[]{:S(2)}, u32[]{:S(2)}) collective-permute-start(bf16[128,2048]{1,0:T(8,128)(2,1)S(1)} %copy-done.16), channel_id=1, source_target_pairs={{0,16},{8,24},{16,0},{24,8},{1,17},{9,25},{17,1},{25,9},{2,18},{10... | collective-permute-start | bytes 1572872 | tf_op jit(solution)/shard_map/ppermute | solution.py:631
  63.2 22.7 %collective-permute-start.4 = (bf16[128,2048]{1,0:T(8,128)(2,1)S(1)}, bf16[128,2048]{1,0:T(8,128)(2,1)S(1)}, u32[]{:S(2)}, u32[]{:S(2)}) collective-permute-start(bf16[128,2048]{1,0:T(8,128)(2,1)S(1)} %collective-permute-done.refs_2_), channel_id=1, source_target_pairs={{0,16},{8,24},{16,0},{24,8},{1,17},{9,25},{17,1},{25,9},{2,18},{10... | collective-permute-start | bytes 1572872 | tf_op jit(solution)/shard_map/ppermute | solution.py:631
  64.6 21.3 %collective-permute-start.5 = (bf16[128,2048]{1,0:T(8,128)(2,1)S(1)}, bf16[128,2048]{1,0:T(8,128)(2,1)S(1)}, u32[]{:S(2)}, u32[]{:S(2)}) collective-permute-start(bf16[128,2048]{1,0:T(8,128)(2,1)S(1)} %collective-permute-done.3.refs_5_), channel_id=1, source_target_pairs={{0,8},{8,0},{16,24},{24,16},{1,9},{9,1},{17,25},{25,17},{2,10},{10... | collective-permute-start | bytes 1572872 | tf_op jit(solution)/shard_map/ppermute | solution.py:631
  86.0 43.9 %collective-permute-start.12 = (bf16[256,2048]{1,0:T(8,128)(2,1)S(1)}, bf16[256,2048]{1,0:T(8,128)(2,1)S(1)}, u32[]{:S(2)}, u32[]{:S(2)}) collective-permute-start(bf16[256,2048]{1,0:T(8,128)(2,1)S(1)} %bitcast.74), channel_id=1, source_target_pairs={{0,8},{8,0},{16,24},{24,16},{1,9},{9,1},{17,25},{25,17},{2,10},{10... | collective-permute-start | bytes 3145736 | tf_op jit(solution)/shard_map/ppermute | solution.py:631
  86.5 46.3 %collective-permute-start.13 = (bf16[256,2048]{1,0:T(8,128)(2,1)S(1)}, bf16[256,2048]{1,0:T(8,128)(2,1)S(1)}, u32[]{:S(2)}, u32[]{:S(2)}) collective-permute-start(bf16[256,2048]{1,0:T(8,128)(2,1)S(1)} %bitcast.75), channel_id=1, source_target_pairs={{0,16},{8,24},{16,0},{24,8},{1,17},{9,25},{17,1},{25,9},{2,18},{10... | collective-permute-start | bytes 3145736 | tf_op jit(solution)/shard_map/ppermute | solution.py:631
  88.1 44.7 %collective-permute-start.14 = (bf16[256,2048]{1,0:T(8,128)(2,1)S(1)}, bf16[256,2048]{1,0:T(8,128)(2,1)}, u32[]{:S(2)}, u32[]{:S(2)}) collective-permute-start(bf16[256,2048]{1,0:T(8,128)(2,1)S(1)} %bitcast.76), channel_id=1, source_target_pairs={{0,24},{8,16},{16,8},{24,0},{1,25},{9,17},{17,9},{25,1},{2,26},{10... | collective-permute-start | bytes 3145736 | tf_op jit(solution)/shard_map/ppermute | solution.py:631
  132.8 15.1 %collective-permute-start.16 = (bf16[128,2048]{1,0:T(8,128)(2,1)}, bf16[128,2048]{1,0:T(8,128)(2,1)S(1)}, u32[]{:S(2)}, u32[]{:S(2)}) collective-permute-start(bf16[128,2048]{1,0:T(8,128)(2,1)} %get-tuple-element.133), channel_id=1, source_target_pairs={{0,16},{8,24},{16,0},{24,8},{1,17},{9,25},{17,1},{25,9},{2,18},{10... | collective-permute-start | bytes 1572872 | tf_op jit(solution)/shard_map/ppermute | solution.py:631
  134.4 16.3 %collective-permute-start.19 = (bf16[128,2048]{1,0:T(8,128)(2,1)}, bf16[128,2048]{1,0:T(8,128)(2,1)S(1)}, u32[]{:S(2)}, u32[]{:S(2)}) collective-permute-start(bf16[128,2048]{1,0:T(8,128)(2,1)} %get-tuple-element.137), channel_id=1, source_target_pairs={{0,8},{8,0},{16,24},{24,16},{1,9},{9,1},{17,25},{25,17},{2,10},{10... | collective-permute-start | bytes 1572872 | tf_op jit(solution)/shard_map/ppermute | solution.py:631
  134.9 24.3 %collective-permute-start.15 = (bf16[128,2048]{1,0:T(8,128)(2,1)}, bf16[128,2048]{1,0:T(8,128)(2,1)S(1)}, u32[]{:S(2)}, u32[]{:S(2)}) collective-permute-start(bf16[128,2048]{1,0:T(8,128)(2,1)} %get-tuple-element.131), channel_id=1, source_target_pairs={{0,16},{8,24},{16,0},{24,8},{1,17},{9,25},{17,1},{25,9},{2,18},{10... | collective-permute-start | bytes 1572872 | tf_op jit(solution)/shard_map/ppermute | solution.py:631
  136.4 24.3 %collective-permute-start.18 = (bf16[128,2048]{1,0:T(8,128)(2,1)}, bf16[128,2048]{1,0:T(8,128)(2,1)S(1)}, u32[]{:S(2)}, u32[]{:S(2)}) collective-permute-start(bf16[128,2048]{1,0:T(8,128)(2,1)} %get-tuple-element.135), channel_id=1, source_target_pairs={{0,8},{8,0},{16,24},{24,16},{1,9},{9,1},{17,25},{25,17},{2,10},{10... | collective-permute-start | bytes 1572872 | tf_op jit(solution)/shard_map/ppermute | solution.py:631
  149.2 19.3 %collective-permute-start.17 = (bf16[128,2048]{1,0:T(8,128)(2,1)S(1)}, bf16[128,2048]{1,0:T(8,128)(2,1)S(1)}, u32[]{:S(2)}, u32[]{:S(2)}) collective-permute-start(bf16[128,2048]{1,0:T(8,128)(2,1)S(1)} %add_convert_fusion.7), channel_id=1, source_target_pairs={{0,8},{8,0},{16,24},{24,16},{1,9},{9,1},{17,25},{25,17},{2,10},{10... | collective-permute-start | bytes 1572872 | tf_op jit(solution)/shard_map/ppermute | solution.py:631
  150.9 17.5 %collective-permute-start.20 = (bf16[128,2048]{1,0:T(8,128)(2,1)S(1)}, bf16[128,2048]{1,0:T(8,128)(2,1)S(1)}, u32[]{:S(2)}, u32[]{:S(2)}) collective-permute-start(bf16[128,2048]{1,0:T(8,128)(2,1)S(1)} %add_convert_fusion.6), channel_id=1, source_target_pairs={{0,16},{8,24},{16,0},{24,8},{1,17},{9,25},{17,1},{25,9},{2,18},{10... | collective-permute-start | bytes 1572872 | tf_op jit(solution)/shard_map/ppermute | solution.py:631
  173.7 24.0 %collective-permute-start.22 = (bf16[128,2048]{1,0:T(8,128)(2,1)S(1)}, bf16[128,2048]{1,0:T(8,128)(2,1)S(1)}, u32[]{:S(2)}, u32[]{:S(2)}) collective-permute-start(bf16[128,2048]{1,0:T(8,128)(2,1)S(1)} %get-tuple-element.140.refs_1_), channel_id=1, source_target_pairs={{0,8},{8,0},{16,24},{24,16},{1,9},{9,1},{17,25},{25,17},{2,10},{10... | collective-permute-start | bytes 1572872 | tf_op jit(solution)/shard_map/ppermute | solution.py:631
  174.3 24.0 %collective-permute-start.23 = (bf16[128,2048]{1,0:T(8,128)(2,1)S(1)}, bf16[128,2048]{1,0:T(8,128)(2,1)S(1)}, u32[]{:S(2)}, u32[]{:S(2)}) collective-permute-start(bf16[128,2048]{1,0:T(8,128)(2,1)S(1)} %get-tuple-element.139.refs_0_), channel_id=1, source_target_pairs={{0,16},{8,24},{16,0},{24,8},{1,17},{9,25},{17,1},{25,9},{2,18},{10... | collective-permute-start | bytes 1572872 | tf_op jit(solution)/shard_map/ppermute | solution.py:631
  186.5 18.6 %collective-permute-start.25 = (bf16[128,2048]{1,0:T(8,128)(2,1)S(1)}, bf16[128,2048]{1,0:T(8,128)(2,1)S(1)}, u32[]{:S(2)}, u32[]{:S(2)}) collective-permute-start(bf16[128,2048]{1,0:T(8,128)(2,1)S(1)} %collective-permute-done.21.refs_2_), channel_id=1, source_target_pairs={{0,16},{8,24},{16,0},{24,8},{1,17},{9,25},{17,1},{25,9},{2,18},{10... | collective-permute-start | bytes 1572872 | tf_op jit(solution)/shard_map/ppermute | solution.py:631
  187.2 18.7 %collective-permute-start.26 = (bf16[128,2048]{1,0:T(8,128)(2,1)S(1)}, bf16[128,2048]{1,0:T(8,128)(2,1)}, u32[]{:S(2)}, u32[]{:S(2)}) collective-permute-start(bf16[128,2048]{1,0:T(8,128)(2,1)S(1)} %collective-permute-done.24.refs_5_), channel_id=1, source_target_pairs={{0,8},{8,0},{16,24},{24,16},{1,9},{9,1},{17,25},{25,17},{2,10},{10... | collective-permute-start | bytes 1572872 | tf_op jit(solution)/shard_map/ppermute | solution.py:631
  238.1 177.5 %reduce-scatter.6.cloned.1.call-start = ((), (), s32[]{:S(2)}) async-start(), calls=%async_computation.7 | async-start | bytes 7208960 | tf_op jit(solution)/shard_map/reduce_scatter | solution.py:683
  256.5 37.4 %collective-permute-start.30 = (bf16[1024,2816]{1,0:T(8,128)(2,1)}, bf16[1024,2816]{1,0:T(8,128)(2,1)}, u32[]{:S(2)}, u32[]{:S(2)}) collective-permute-start(bf16[1024,2816]{1,0:T(8,128)(2,1)} %grad_gate_up_of.1.grad_ref), channel_id=1, source_target_pairs={{0,1},{1,0},{2,3},{3,2},{4,5},{5,4},{6,7},{7,6},{8,9},{9,8},{10,11... | collective-permute-start | bytes 17301512 | tf_op jit(solution)/shard_map/ppermute | solution.py:680
  256.7 36.0 %collective-permute-start.29 = (bf16[1024,2048]{1,0:T(8,128)(2,1)}, bf16[1024,2048]{1,0:T(8,128)(2,1)}, u32[]{:S(2)}, u32[]{:S(2)}) collective-permute-start(bf16[1024,2048]{1,0:T(8,128)(2,1)} %get-tuple-element.154.left_ref), channel_id=1, source_target_pairs={{0,1},{1,0},{2,3},{3,2},{4,5},{5,4},{6,7},{7,6},{8,9},{9,8},{10,11... | collective-permute-start | bytes 12582920 | tf_op jit(solution)/shard_map/ppermute | solution.py:680
  275.4 16.1 %collective-permute-start.28 = (bf16[128,2048]{1,0:T(8,128)(2,1)}, bf16[128,2048]{1,0:T(8,128)(2,1)S(1)}, u32[]{:S(2)}, u32[]{:S(2)}) collective-permute-start(bf16[128,2048]{1,0:T(8,128)(2,1)} %get-tuple-element.153), channel_id=1, source_target_pairs={{0,8},{8,0},{16,24},{24,16},{1,9},{9,1},{17,25},{25,17},{2,10},{10... | collective-permute-start | bytes 1572872 | tf_op jit(solution)/shard_map/ppermute | solution.py:631
  276.9 35.7 %collective-permute-start.31 = (bf16[128,2048]{1,0:T(8,128)(2,1)}, bf16[128,2048]{1,0:T(8,128)(2,1)S(1)}, u32[]{:S(2)}, u32[]{:S(2)}) collective-permute-start(bf16[128,2048]{1,0:T(8,128)(2,1)} %get-tuple-element.156), channel_id=1, source_target_pairs={{0,16},{8,24},{16,0},{24,8},{1,17},{9,25},{17,1},{25,9},{2,18},{10... | collective-permute-start | bytes 1572872 | tf_op jit(solution)/shard_map/ppermute | solution.py:631
  289.3 23.3 %collective-permute-start.33 = (bf16[128,2048]{1,0:T(8,128)(2,1)}, bf16[128,2048]{1,0:T(8,128)(2,1)S(1)}, u32[]{:S(2)}, u32[]{:S(2)}) collective-permute-start(bf16[128,2048]{1,0:T(8,128)(2,1)} %get-tuple-element.158), channel_id=1, source_target_pairs={{0,8},{8,0},{16,24},{24,16},{1,9},{9,1},{17,25},{25,17},{2,10},{10... | collective-permute-start | bytes 1572872 | tf_op jit(solution)/shard_map/ppermute | solution.py:631
  291.6 21.6 %collective-permute-start.32 = (bf16[128,2048]{1,0:T(8,128)(2,1)S(1)}, bf16[128,2048]{1,0:T(8,128)(2,1)S(1)}, u32[]{:S(2)}, u32[]{:S(2)}) collective-permute-start(bf16[128,2048]{1,0:T(8,128)(2,1)S(1)} %add_convert_fusion.5), channel_id=1, source_target_pairs={{0,8},{8,0},{16,24},{24,16},{1,9},{9,1},{17,25},{25,17},{2,10},{10... | collective-permute-start | bytes 1572872 | tf_op jit(solution)/shard_map/ppermute | solution.py:631
  292.8 20.4 %collective-permute-start.34 = (bf16[128,2048]{1,0:T(8,128)(2,1)S(1)}, bf16[128,2048]{1,0:T(8,128)(2,1)S(1)}, u32[]{:S(2)}, u32[]{:S(2)}) collective-permute-start(bf16[128,2048]{1,0:T(8,128)(2,1)S(1)} %add_convert_fusion.4), channel_id=1, source_target_pairs={{0,16},{8,24},{16,0},{24,8},{1,17},{9,25},{17,1},{25,9},{2,18},{10... | collective-permute-start | bytes 1572872 | tf_op jit(solution)/shard_map/ppermute | solution.py:631
  314.1 158.1 %reduce-scatter.8.cloned.1.call-start = ((), (), s32[]{:S(2)}) async-start(), calls=%async_computation.8 | async-start | bytes 5308416 | tf_op jit(solution)/shard_map/reduce_scatter | solution.py:686
  322.7 26.6 %collective-permute-start.36 = (bf16[128,2048]{1,0:T(8,128)(2,1)}, bf16[128,2048]{1,0:T(8,128)(2,1)S(1)}, u32[]{:S(2)}, u32[]{:S(2)}) collective-permute-start(bf16[128,2048]{1,0:T(8,128)(2,1)} %get-tuple-element.176.refs_1_.refs_9_), channel_id=1, source_target_pairs={{0,8},{8,0},{16,24},{24,16},{1,9},{9,1},{17,25},{25,17},{2,10},{10... | collective-permute-start | bytes 1572872 | tf_op jit(solution)/shard_map/ppermute | solution.py:631
  323.3 26.0 %collective-permute-start.37 = (bf16[128,2048]{1,0:T(8,128)(2,1)}, bf16[128,2048]{1,0:T(8,128)(2,1)S(1)}, u32[]{:S(2)}, u32[]{:S(2)}) collective-permute-start(bf16[128,2048]{1,0:T(8,128)(2,1)} %get-tuple-element.166.refs_0_.refs_8_), channel_id=1, source_target_pairs={{0,16},{8,24},{16,0},{24,8},{1,17},{9,25},{17,1},{25,9},{2,18},{10... | collective-permute-start | bytes 1572872 | tf_op jit(solution)/shard_map/ppermute | solution.py:631
  334.9 20.7 %collective-permute-start.39 = (bf16[128,2048]{1,0:T(8,128)(2,1)S(1)}, bf16[128,2048]{1,0:T(8,128)(2,1)S(1)}, u32[]{:S(2)}, u32[]{:S(2)}) collective-permute-start(bf16[128,2048]{1,0:T(8,128)(2,1)S(1)} %collective-permute-done.35.refs_2_.refs_10_), channel_id=1, source_target_pairs={{0,16},{8,24},{16,0},{24,8},{1,17},{9,25},{17,1},{25,9},{2,18},{10... | collective-permute-start | bytes 1572872 | tf_op jit(solution)/shard_map/ppermute | solution.py:631
  336.3 19.3 %collective-permute-start.40 = (bf16[128,2048]{1,0:T(8,128)(2,1)S(1)}, bf16[128,2048]{1,0:T(8,128)(2,1)S(1)}, u32[]{:S(2)}, u32[]{:S(2)}) collective-permute-start(bf16[128,2048]{1,0:T(8,128)(2,1)S(1)} %collective-permute-done.38.refs_5_.refs_13_), channel_id=1, source_target_pairs={{0,8},{8,0},{16,24},{24,16},{1,9},{9,1},{17,25},{25,17},{2,10},{10... | collective-permute-start | bytes 1572872 | tf_op jit(solution)/shard_map/ppermute | solution.py:631
  355.6 38.9 %collective-permute-start.41 = (bf16[128,2048]{1,0:T(8,128)(2,1)}, bf16[128,2048]{1,0:T(8,128)(2,1)}, u32[]{:S(2)}, u32[]{:S(2)}) collective-permute-start(bf16[128,2048]{1,0:T(8,128)(2,1)} %get-tuple-element.185), channel_id=1, source_target_pairs={{0,16},{8,24},{16,0},{24,8},{1,17},{9,25},{17,1},{25,9},{2,18},{10... | collective-permute-start | bytes 1572872 | tf_op jit(solution)/shard_map/ppermute | solution.py:631
  357.1 37.4 %collective-permute-start.42 = (bf16[128,2048]{1,0:T(8,128)(2,1)}, bf16[128,2048]{1,0:T(8,128)(2,1)S(1)}, u32[]{:S(2)}, u32[]{:S(2)}) collective-permute-start(bf16[128,2048]{1,0:T(8,128)(2,1)} %get-tuple-element.186), channel_id=1, source_target_pairs={{0,8},{8,0},{16,24},{24,16},{1,9},{9,1},{17,25},{25,17},{2,10},{10... | collective-permute-start | bytes 1572872 | tf_op jit(solution)/shard_map/ppermute | solution.py:631
  357.7 36.8 %collective-permute-start.43 = (bf16[128,2048]{1,0:T(8,128)(2,1)}, bf16[128,2048]{1,0:T(8,128)(2,1)S(1)}, u32[]{:S(2)}, u32[]{:S(2)}) collective-permute-start(bf16[128,2048]{1,0:T(8,128)(2,1)} %get-tuple-element.187), channel_id=1, source_target_pairs={{0,16},{8,24},{16,0},{24,8},{1,17},{9,25},{17,1},{25,9},{2,18},{10... | collective-permute-start | bytes 1572872 | tf_op jit(solution)/shard_map/ppermute | solution.py:631
  358.3 36.2 %collective-permute-start.44 = (bf16[128,2048]{1,0:T(8,128)(2,1)}, bf16[128,2048]{1,0:T(8,128)(2,1)S(1)}, u32[]{:S(2)}, u32[]{:S(2)}) collective-permute-start(bf16[128,2048]{1,0:T(8,128)(2,1)} %get-tuple-element.188), channel_id=1, source_target_pairs={{0,8},{8,0},{16,24},{24,16},{1,9},{9,1},{17,25},{25,17},{2,10},{10... | collective-permute-start | bytes 1572872 | tf_op jit(solution)/shard_map/ppermute | solution.py:631
  415.7 15.1 %collective-permute-start.47 = (bf16[128,2048]{1,0:T(8,128)(2,1)}, bf16[128,2048]{1,0:T(8,128)(2,1)S(1)}, u32[]{:S(2)}, u32[]{:S(2)}) collective-permute-start(bf16[128,2048]{1,0:T(8,128)(2,1)} %get-tuple-element.199), channel_id=1, source_target_pairs={{0,16},{8,24},{16,0},{24,8},{1,17},{9,25},{17,1},{25,9},{2,18},{10... | collective-permute-start | bytes 1572872 | tf_op jit(solution)/shard_map/ppermute | solution.py:631
  417.7 24.8 %collective-permute-start.49 = (bf16[128,2048]{1,0:T(8,128)(2,1)S(1)}, bf16[128,2048]{1,0:T(8,128)(2,1)S(1)}, u32[]{:S(2)}, u32[]{:S(2)}) collective-permute-start(bf16[128,2048]{1,0:T(8,128)(2,1)S(1)} %add_convert_fusion.1), channel_id=1, source_target_pairs={{0,8},{8,0},{16,24},{24,16},{1,9},{9,1},{17,25},{25,17},{2,10},{10... | collective-permute-start | bytes 1572872 | tf_op jit(solution)/shard_map/ppermute | solution.py:631
  418.6 23.9 %collective-permute-start.52 = (bf16[128,2048]{1,0:T(8,128)(2,1)S(1)}, bf16[128,2048]{1,0:T(8,128)(2,1)S(1)}, u32[]{:S(2)}, u32[]{:S(2)}) collective-permute-start(bf16[128,2048]{1,0:T(8,128)(2,1)S(1)} %add_convert_fusion), channel_id=1, source_target_pairs={{0,16},{8,24},{16,0},{24,8},{1,17},{9,25},{17,1},{25,9},{2,18},{10... | collective-permute-start | bytes 1572872 | tf_op jit(solution)/shard_map/ppermute | solution.py:631
  421.4 32.3 %collective-permute-start.45 = (bf16[128,2048]{1,0:T(8,128)(2,1)S(1)}, bf16[128,2048]{1,0:T(8,128)(2,1)S(1)}, u32[]{:S(2)}, u32[]{:S(2)}) collective-permute-start(bf16[128,2048]{1,0:T(8,128)(2,1)S(1)} %add_convert_fusion.3), channel_id=1, source_target_pairs={{0,8},{8,0},{16,24},{24,16},{1,9},{9,1},{17,25},{25,17},{2,10},{10... | collective-permute-start | bytes 1572872 | tf_op jit(solution)/shard_map/ppermute | solution.py:631
  430.8 23.0 %collective-permute-start.46 = (bf16[128,2048]{1,0:T(8,128)(2,1)}, bf16[128,2048]{1,0:T(8,128)(2,1)}, u32[]{:S(2)}, u32[]{:S(2)}) collective-permute-start(bf16[128,2048]{1,0:T(8,128)(2,1)} %add_convert_fusion.2), channel_id=1, source_target_pairs={{0,16},{8,24},{16,0},{24,8},{1,17},{9,25},{17,1},{25,9},{2,18},{10... | collective-permute-start | bytes 1572872 | tf_op jit(solution)/shard_map/ppermute | solution.py:631
  443.9 20.2 %collective-permute-start.53 = (bf16[64,2816]{1,0:T(8,128)(2,1)}, bf16[64,2816]{1,0:T(8,128)(2,1)S(1)}, u32[]{:S(2)}, u32[]{:S(2)}) collective-permute-start(bf16[64,2816]{1,0:T(8,128)(2,1)} %get-tuple-element.221), channel_id=1, source_target_pairs={{0,8},{8,0},{16,24},{24,16},{1,9},{9,1},{17,25},{25,17},{2,10},{10... | collective-permute-start | bytes 1081352 | tf_op jit(solution)/shard_map/ppermute | solution.py:631
  445.2 18.9 %collective-permute-start.54 = (bf16[64,2816]{1,0:T(8,128)(2,1)}, bf16[64,2816]{1,0:T(8,128)(2,1)S(1)}, u32[]{:S(2)}, u32[]{:S(2)}) collective-permute-start(bf16[64,2816]{1,0:T(8,128)(2,1)} %get-tuple-element.220), channel_id=1, source_target_pairs={{0,16},{8,24},{16,0},{24,8},{1,17},{9,25},{17,1},{25,9},{2,18},{10... | collective-permute-start | bytes 1081352 | tf_op jit(solution)/shard_map/ppermute | solution.py:631
  446.8 20.5 %collective-permute-start.55 = (bf16[64,2816]{1,0:T(8,128)(2,1)S(1)}, bf16[64,2816]{1,0:T(8,128)(2,1)S(1)}, u32[]{:S(2)}, u32[]{:S(2)}) collective-permute-start(bf16[64,2816]{1,0:T(8,128)(2,1)S(1)} %get-tuple-element.219), channel_id=1, source_target_pairs={{0,24},{8,16},{16,8},{24,0},{1,25},{9,17},{17,9},{25,1},{2,26},{10... | collective-permute-start | bytes 1081352 | tf_op jit(solution)/shard_map/ppermute | solution.py:631
  (80 other events, 851.6 us)
Sparse Core Ops, SparseCore 0:
  20.4 52.0 all-gather.3
  74.7 106.8 all-gather.5
  183.3 58.7 all-gather.7
  244.2 63.5 reduce-scatter.3
  313.3 100.8 reduce-scatter.5
  416.3 55.4 reduce-scatter.7
